TPU v7x, 256 devices: a whole 4x4x8 slice. The times are simulated.
256 devices in a mesh: wide: 64 (over x, z, core), narrow: 4 (over y).
Axes of the slice: x: 4, y: 4, z: 8, core: 2. Of those that a mesh axis runs over, the one named last changes fastest.
Arguments:
- grid_latent: bfloat16 [131072, 512], P(('wide', 'narrow')), may hold values from -24 to 24
- enc_edge_latent: bfloat16 [131072, 512], P(('wide', 'narrow')), may hold values from -24 to 24
- enc_source: int32 [131072], P(('wide', 'narrow')), may hold values from 0 to 511
- enc_target_device: int32 [131072, 1], P(('wide', 'narrow')), may hold values from 0 to 255; in each aligned block of 512 rows (0 to 511, 512 to 1023, ...) at most 4 rows name the same one
- enc_target_row: int32 [131072], P(('wide', 'narrow')), may hold values from 0 to 159
- mesh_static: bfloat16 [40960, 512], P(('wide', 'narrow')), may hold values from -6 to 6
- mesh_edge_latent: bfloat16 [327680, 512], P(('wide', 'narrow')), may hold values from -24 to 24
- mesh_source: int32 [327680], P(('wide', 'narrow')), may hold values from 0 to 479
- mesh_target: int32 [327680], P(('wide', 'narrow')), may hold values from 0 to 159
- w_enc_edge: bfloat16 [512, 512], replicated, may hold values from -0.25 to 0.25
- w_enc_grid: bfloat16 [512, 512], replicated, may hold values from -0.25 to 0.25
- w_enc_out: bfloat16 [512, 512], replicated, may hold values from -0.25 to 0.25
- w_proc_edge: bfloat16 [512, 512], replicated, may hold values from -0.25 to 0.25
- w_proc_src: bfloat16 [512, 512], replicated, may hold values from -0.25 to 0.25
- w_proc_dst: bfloat16 [512, 512], replicated, may hold values from -0.25 to 0.25
- w_proc_out: bfloat16 [512, 512], replicated, may hold values from -0.25 to 0.25
- w_node_self: bfloat16 [512, 512], replicated, may hold values from -0.25 to 0.25
- w_node_agg: bfloat16 [512, 512], replicated, may hold values from -0.25 to 0.25
- w_node_out: bfloat16 [512, 512], replicated, may hold values from -0.25 to 0.25
- cotangent: bfloat16 [40960, 512], P(('wide', 'narrow')), may hold values from -6 to 6
Outputs:
- mesh_out: bfloat16 [40960, 512], P(('wide', 'narrow'))
- grid_grad: float32 [131072, 512], P(('wide', 'narrow'))
- weight_grads: float32 [2621440], P(('wide', 'narrow'))
- mesh_grad: float32 [40960, 512], P(('wide', 'narrow'))
Inputs may be any that keep to these rules, and one draw needn't show every extreme that they name: `enc_target_device`: among the 512 rows of one device no device is named more than 4 times, and that many in some device's rows. `mesh_source`: table rows 0 to 159 are the mesh rows of the device one index lower along wide (wrapping), the next 160 the device's own, the last 160 those of the device one index higher.
All inputs are finite; a program needn't handle non-finite values.
Results may differ from a plain program's by a relative error of at most 0.029.
Values may be sent and summed in bfloat16 or wider, within the bound.
No kernel may reach another device: no remote copies, remote signals or barrier semaphores. Data moves between devices by JAX's collectives and lax.ppermute only.
A program may use at most 128 MiB of HBM per device.

v0:
```python
import functools

import jax
import jax.numpy as jnp
from jax import lax
from jax.experimental import pallas as pl
from jax.experimental.pallas import tpu as pltpu
from jax.sharding import PartitionSpec as P

BF = jnp.bfloat16
F32 = jnp.float32
I32 = jnp.int32
LANE = 128


def dot(left, right):
    return jnp.dot(left, right, preferred_element_type=F32)


def dot_rt(left, right):
    return lax.dot_general(left, right, (((1,), (1,)), ((), ())), preferred_element_type=F32)


def dot_lt(left, right):
    return lax.dot_general(left, right, (((0,), (0,)), ((), ())), preferred_element_type=F32)


def silu_pair(value):
    sig = jax.nn.sigmoid(value)
    act = value * sig
    return act, sig + act * (1.0 - sig)


def columns(row):
    return jnp.broadcast_to(row.astype(F32), (LANE, row.shape[1])).T


def same(cols, width, shift=0):
    wide = jnp.concatenate([cols] * (-(-width // LANE)), axis=1)
    lane = lax.broadcasted_iota(I32, wide.shape, 1) + shift
    return jnp.where(wide == lane.astype(F32), 1.0, 0.0).astype(BF)


def same_t(row, height, shift=0):
    sub = lax.broadcasted_iota(I32, (height, row.shape[1]), 0) + shift
    return jnp.where(sub == row, 1.0, 0.0).astype(BF)


def enc_forward(
    capacity, grid_ref, edge_ref, src_ref, tdev_ref, trow_ref, we_ref, wg_ref, out_ref, sg_ref, slot_ref
):
    edges, width = edge_ref.shape
    slots = out_ref.shape[0]
    tdev = tdev_ref[...]
    member = same_t(tdev, slots // capacity)
    before = lax.broadcasted_iota(I32, (edges, edges), 0) < lax.broadcasted_iota(
        I32, (edges, edges), 1
    )
    ahead = dot(member, jnp.where(before, 1.0, 0.0).astype(BF))
    rank = jnp.sum(member.astype(F32) * ahead, axis=0, keepdims=True)
    slot = tdev * capacity + rank.astype(I32)
    slot_ref[...] = slot
    tag = columns(trow_ref[...] + 1).astype(BF)
    gathered = dot(same(columns(src_ref[...]), grid_ref.shape[0]), grid_ref[...]).astype(BF)
    pre = dot(edge_ref[...], we_ref[...]) + dot(gathered, wg_ref[...])
    act, grad = silu_pair(pre)
    sg_ref[...] = grad.astype(BF)
    payload = jnp.concatenate([act.astype(BF), tag], axis=1)
    step = 256
    for at in range(0, slots, step):
        place = same_t(slot, step, at)
        out_ref[pl.ds(at, step), :] = dot(place, payload).astype(BF)


def mesh_forward(
    recv_ref, static_ref, wout_ref, wsrc_ref, wdst_ref, h0_ref, a0_ref, psrc_ref, pdst_ref, pick_ref
):
    rows, width = static_ref.shape
    padded = pick_ref.shape[1]
    tag = recv_ref[:, width:].astype(F32)
    pick = same(tag, padded, 1)
    pick_ref[...] = pick
    a0 = dot_lt(pick, recv_ref[:, :width])[:rows].astype(BF)
    a0_ref[...] = a0
    h0 = (static_ref[...].astype(F32) + dot(a0, wout_ref[...])).astype(BF)
    h0_ref[...] = h0
    psrc_ref[...] = dot(h0, wsrc_ref[...]).astype(BF)
    pdst_ref[...] = dot(h0, wdst_ref[...]).astype(BF)


def processor(
    scales,
    mel_ref,
    msrc_ref,
    mtgt_ref,
    pb_ref,
    po_ref,
    pa_ref,
    pd_ref,
    h0_ref,
    cot_ref,
    we_ref,
    wpo_ref,
    wns_ref,
    wna_ref,
    wno_ref,
    wdst_ref,
    out_ref,
    sb_ref,
    so_ref,
    sa_ref,
    mg_ref,
    gpe_ref,
    gpd_ref,
    gpo_ref,
    gns_ref,
    gna_ref,
    gno_ref,
    table,
    hot,
    sg,
    zsum,
    back,
    gacc,
):
    proc_scale, node_scale = scales
    edges, width = mel_ref.shape
    rows = h0_ref.shape[0]
    reach = table.shape[0]
    first = reach - 256
    step = 256
    steps = edges // step
    table[pl.ds(0, rows), :] = pb_ref[...]
    table[pl.ds(rows, rows), :] = po_ref[...]
    table[pl.ds(2 * rows, rows), :] = pa_ref[...]
    table[pl.ds(3 * rows, reach - 3 * rows), :] = jnp.zeros((reach - 3 * rows, width), BF)
    table[pl.ds(first, rows), :] = pd_ref[...]
    zsum[...] = jnp.zeros_like(zsum)

    def ahead(i, carry):
        at = pl.multiple_of(i * step, step)
        src = columns(msrc_ref[pl.ds(i, 1), :])
        tgt = columns(mtgt_ref[pl.ds(i, 1), :] + first)
        src = jnp.concatenate([src] * (reach // LANE), axis=1)
        tgt = jnp.concatenate([tgt] * (reach // LANE), axis=1)
        lane = lax.broadcasted_iota(I32, (step, reach), 1).astype(F32)
        chosen = jnp.where((src == lane) | (tgt == lane), 1.0, 0.0).astype(BF)
        hot[pl.ds(at, step), :] = chosen
        pre = dot(mel_ref[pl.ds(at, step), :], we_ref[...]) + dot(chosen, table[...])
        act, grad = silu_pair(pre)
        sg[pl.ds(at, step), :] = grad.astype(BF)
        zsum[...] += dot_lt(chosen[:, first:], act.astype(BF))
        return carry

    lax.fori_loop(0, steps, ahead, 0)
    zeta = zsum[pl.ds(0, rows), :].astype(BF)
    h0 = h0_ref[...]
    cot = cot_ref[...]
    agg = dot(zeta, wpo_ref[...]).astype(BF)
    pre_node = dot(h0, wns_ref[...]) + dot(agg, wna_ref[...])
    act, grad = silu_pair(pre_node)
    unit = act.astype(BF)
    out_ref[...] = (h0.astype(F32) + dot(unit, wno_ref[...])).astype(BF)
    gno_ref[...] = (dot_lt(unit, cot) * node_scale).astype(BF)
    d_node = (dot_rt(cot, wno_ref[...]) * grad).astype(BF)
    gns_ref[...] = (dot_lt(h0, d_node) * node_scale).astype(BF)
    gna_ref[...] = (dot_lt(agg, d_node) * node_scale).astype(BF)
    d_agg = dot_rt(d_node, wna_ref[...]).astype(BF)
    gpo_ref[...] = (dot_lt(zeta, d_agg) * proc_scale).astype(BF)
    d_zeta = dot_rt(d_agg, wpo_ref[...]).astype(BF)
    mg_ref[...] = cot.astype(F32) + dot_rt(d_node, wns_ref[...])
    back[...] = jnp.zeros_like(back)
    gacc[...] = jnp.zeros_like(gacc)
    table[pl.ds(first, rows), :] = d_zeta

    def behind(i, carry):
        at = pl.multiple_of(i * step, step)
        chosen = hot[pl.ds(at, step), :]
        d_edge = dot(chosen[:, first:], table[pl.ds(first, 256), :])
        d_proc = (d_edge * sg[pl.ds(at, step), :].astype(F32)).astype(BF)
        back[...] += dot_lt(chosen, d_proc)
        gacc[...] += dot_lt(mel_ref[pl.ds(at, step), :], d_proc)
        return carry

    lax.fori_loop(0, steps, behind, 0)
    gpe_ref[...] = (gacc[...] * proc_scale).astype(BF)
    sb_ref[...] = back[pl.ds(0, rows), :].astype(BF)
    so_ref[...] = back[pl.ds(rows, rows), :].astype(BF)
    sa_ref[...] = back[pl.ds(2 * rows, rows), :].astype(BF)
    dst_sum = back[pl.ds(first, rows), :].astype(BF)
    mg_ref[...] += dot_rt(dst_sum, wdst_ref[...])
    gpd_ref[...] = (dot_lt(h0, dst_sum) * proc_scale).astype(BF)


def mesh_backward(
    scales, so_ref, sb_ref, sa_ref, mg_ref, h0_ref, a0_ref, pick_ref, wsrc_ref, wout_ref,
    out_ref, ret_ref, gps_ref, geo_ref, padded,
):
    proc_scale, enc_scale = scales
    rows = h0_ref.shape[0]
    total = (so_ref[...].astype(F32) + sb_ref[...].astype(F32) + sa_ref[...].astype(F32)).astype(BF)
    grad = mg_ref[...] + dot_rt(total, wsrc_ref[...])
    out_ref[...] = grad
    d_mesh = grad.astype(BF)
    padded[...] = jnp.zeros_like(padded)
    padded[pl.ds(0, rows), :] = dot_rt(d_mesh, wout_ref[...]).astype(BF)
    step = 256
    for at in range(0, ret_ref.shape[0], step):
        ret_ref[pl.ds(at, step), :] = dot(pick_ref[pl.ds(at, step), :], padded[...]).astype(BF)
    gps_ref[...] = (dot_lt(h0_ref[...], total) * proc_scale).astype(BF)
    geo_ref[...] = (dot_lt(a0_ref[...], d_mesh) * enc_scale).astype(BF)


def enc_backward(
    enc_scale, ret_ref, slot_ref, src_ref, sg_ref, edge_ref, grid_ref, wg_ref,
    out_ref, gee_ref, geg_ref,
):
    chosen = same(columns(slot_ref[...]), ret_ref.shape[0])
    d_enc = (dot(chosen, ret_ref[...]) * sg_ref[...].astype(F32)).astype(BF)
    gee_ref[...] = (dot_lt(edge_ref[...], d_enc) * enc_scale).astype(BF)
    grid_sum = dot(same_t(src_ref[...], grid_ref.shape[0]), d_enc).astype(BF)
    geg_ref[...] = (dot_lt(grid_ref[...], grid_sum) * enc_scale).astype(BF)
    out_ref[...] = dot_rt(grid_sum, wg_ref[...])


def call(body, outs, scratch=(), flops=0, moved=0, limit=48 << 20):
    return pl.pallas_call(
        body,
        out_shape=[jax.ShapeDtypeStruct(shape, kind) for shape, kind in outs],
        scratch_shapes=[pltpu.VMEM(shape, kind) for shape, kind in scratch],
        compiler_params=pltpu.CompilerParams(vmem_limit_bytes=limit),
        cost_estimate=pl.CostEstimate(flops=flops, bytes_accessed=moved, transcendentals=0),
    )


def partner_sum(grads, core, wide):
    kept = lax.dynamic_index_in_dim(grads, core, 1, keepdims=False)
    sent = lax.dynamic_index_in_dim(grads, 1 - core, 1, keepdims=False)
    came = lax.ppermute(sent, "wide", [(i, i ^ 1) for i in range(wide)])
    return (kept.astype(F32) + came.astype(F32)).astype(BF)


def on_device(
    grid_latent,
    enc_edge_latent,
    enc_source,
    enc_target_device,
    enc_target_row,
    mesh_static,
    mesh_edge_latent,
    mesh_source,
    mesh_target,
    w_enc_edge,
    w_enc_grid,
    w_enc_out,
    w_proc_edge,
    w_proc_src,
    w_proc_dst,
    w_proc_out,
    w_node_self,
    w_node_agg,
    w_node_out,
    cotangent,
):
    wide = lax.axis_size("wide")
    narrow = lax.axis_size("narrow")
    devices = wide * narrow
    edges, width = enc_edge_latent.shape
    grid_rows = grid_latent.shape[0]
    rows = mesh_static.shape[0]
    mesh_edges = mesh_source.shape[0]
    capacity = 2 * edges // devices
    slots = devices * capacity
    enc_scale = float(edges * devices) ** (-0.5)
    proc_scale = float(mesh_edges * devices) ** (-0.5)
    node_scale = float(rows * devices) ** (-0.5)
    core = lax.axis_index("wide") % 2

    source = enc_source.reshape(1, edges)
    payload, enc_sg, slot = call(
        functools.partial(enc_forward, capacity),
        [((slots, width + LANE), BF), ((edges, width), BF), ((1, edges), I32)],
    )(
        grid_latent,
        enc_edge_latent,
        source,
        enc_target_device.reshape(1, edges),
        enc_target_row.reshape(1, edges),
        w_enc_edge,
        w_enc_grid,
    )
    received = lax.all_to_all(
        payload.reshape(devices, capacity, width + LANE),
        ("wide", "narrow"),
        split_axis=0,
        concat_axis=0,
        tiled=True,
    ).reshape(slots, width + LANE)
    h0, a0, p_src, p_dst, pick = call(
        mesh_forward,
        [((rows, width), BF)] * 4 + [((slots, 256), BF)],
    )(received, mesh_static, w_enc_out, w_proc_src, w_proc_dst)
    up = [(i, (i + 1) % wide) for i in range(wide)]
    down = [(j, i) for i, j in up]
    p_before = lax.ppermute(p_src, "wide", up)
    p_after = lax.ppermute(p_src, "wide", down)
    square = ((width, width), BF)
    block = ((rows, width), BF)
    reach = -(-3 * rows // LANE) * LANE + 256
    mesh_out, s_before, s_own, s_after, partial_grad, gpe, gpd, gpo, gns, gna, gno = call(
        functools.partial(processor, (proc_scale, node_scale)),
        [block] * 4 + [((rows, width), F32)] + [square] * 6,
        [
            ((reach, width), BF),
            ((mesh_edges, reach), BF),
            ((mesh_edges, width), BF),
            ((256, width), F32),
            ((reach, width), F32),
            ((width, width), F32),
        ],
    )(
        mesh_edge_latent,
        mesh_source.reshape(-1, 256),
        mesh_target.reshape(-1, 256),
        p_before,
        p_src,
        p_after,
        p_dst,
        h0,
        cotangent,
        w_proc_edge,
        w_proc_out,
        w_node_self,
        w_node_agg,
        w_node_out,
        w_proc_dst,
    )
    from_after = lax.ppermute(s_before, "wide", down)
    from_before = lax.ppermute(s_after, "wide", up)
    mesh_grad, returning, gps, geo = call(
        functools.partial(mesh_backward, (proc_scale, enc_scale)),
        [((rows, width), F32), ((slots, width), BF), square, square],
        [((256, width), BF)],
    )(s_own, from_after, from_before, partial_grad, h0, a0, pick, w_proc_src, w_enc_out)

    pair = 2 * narrow
    chunk = 10 * width // devices
    span = pair * chunk
    late = 2 * width
    late_groups = -(-late // span)
    first = late // span
    early = jnp.concatenate([geo, gpe, gps, gpd, gpo, gns, gna, gno], axis=0)
    early = jnp.pad(early, ((late - first * span, 0), (0, 0)))
    groups = wide // 2 - first
    early = partner_sum(early.reshape(groups, 2, narrow * chunk, width), core, wide)
    early = early.reshape(groups, narrow, chunk, width).transpose(1, 0, 2, 3)
    early = lax.psum_scatter(
        early.reshape(narrow, groups * chunk, width), "narrow", scatter_dimension=0, tiled=True
    ).reshape(groups, chunk, width)

    returned = lax.all_to_all(
        returning.reshape(devices, capacity, width),
        ("wide", "narrow"),
        split_axis=0,
        concat_axis=0,
        tiled=True,
    ).reshape(slots, width)
    grid_grad, gee, geg = call(
        functools.partial(enc_backward, enc_scale),
        [((grid_rows, width), F32), square, square],
    )(returned, slot, source, enc_sg, enc_edge_latent, grid_latent, w_enc_grid)

    last = jnp.concatenate([gee, geg], axis=0)
    last = jnp.pad(last, ((0, late_groups * span - late), (0, 0)))
    last = partner_sum(last.reshape(late_groups, 2, narrow * chunk, width), core, wide)
    last = last.reshape(late_groups, narrow, chunk, width).transpose(1, 0, 2, 3)
    last = lax.all_to_all(
        last.reshape(narrow, late_groups * chunk, width),
        "narrow",
        split_axis=0,
        concat_axis=0,
        tiled=True,
    )
    last = jnp.sum(last.astype(F32), axis=0).reshape(late_groups, chunk, width)
    shared = late_groups - first
    both = jnp.concatenate(
        [last[:first], last[first:] + early[:shared].astype(F32), early[shared:].astype(F32)], axis=0
    ).astype(BF)
    both = lax.all_to_all(
        both,
        "wide",
        split_axis=0,
        concat_axis=0,
        tiled=True,
        axis_index_groups=[[i for i in range(wide) if i % 2 == c] for c in range(2)],
    )
    summed = jnp.sum(both.astype(F32), axis=0).reshape(-1)
    return (mesh_out, grid_grad, summed, mesh_grad)


def solution(mesh):
    in_specs = (
        P(("wide", "narrow"), None),
        P(("wide", "narrow"), None),
        P(("wide", "narrow")),
        P(("wide", "narrow"), None),
        P(("wide", "narrow")),
        P(("wide", "narrow"), None),
        P(("wide", "narrow"), None),
        P(("wide", "narrow")),
        P(("wide", "narrow")),
        P(),
        P(),
        P(),
        P(),
        P(),
        P(),
        P(),
        P(),
        P(),
        P(),
        P(("wide", "narrow"), None),
    )
    out_specs = (
        P(("wide", "narrow"), None),
        P(("wide", "narrow"), None),
        P(("wide", "narrow")),
        P(("wide", "narrow"), None),
    )
    return jax.shard_map(
        on_device, mesh=mesh, in_specs=in_specs, out_specs=out_specs, check_vma=False
    )
```

profile of v0, /device:TPU:8, one launch (start us, length us, event | category | flops | bytes accessed | tf_op | source)
XLA Modules:
  0.0 234.4 jit_solution(15695813899929056507)
XLA Ops:
  7.2 1.0 copy-done
  8.3 1.0 copy-done.2
  9.3 1.0 copy-done.4
  10.3 1.0 copy-done.9
  13.4 2.2 shard_map.219
  15.7 0.8 copy-done.20
  16.5 1.3 reshape.80
  17.7 52.2 %all_to_all.20 = bf16[256,4,640]{2,1,0:T(4,128)(2,1)} all-to-all(bf16[256,4,640]{2,1,0:T(4,128)(2,1)} %reshape.80), channel_id=1, replica_groups=mesh['wide'=64,'narrow'=4] {'wide','narrow'}, dimensions={0} | all-to-all | bytes 2621440 | tf_op jit(solution)/shard_map/all_to_all | solution.py:292
  69.9 2.5 %reshape.81.recv_ref = bf16[1024,640]{1,0:T(8,128)(2,1)S(1)} reshape(bf16[256,4,640]{2,1,0:T(4,128)(2,1)} %all_to_all.20) | data formatting | bytes 2621440 | tf_op jit(solution)/shard_map/reshape | solution.py:298
  72.5 0.9 shard_map.220
  73.4 0.8 copy-done.22
  76.1 0.7 reshape.76.mtgt_ref
  76.8 1.0 collective-permute-done.1.pa_ref
  77.7 5.2 %collective-permute-done.pb_ref = bf16[160,512]{1,0:T(8,128)(2,1)S(1)} collective-permute-done((bf16[160,512]{1,0:T(8,128)(2,1)S(1)}, bf16[160,512]{1,0:T(8,128)(2,1)S(1)}, u32[]{:S(2)}, u32[]{:S(2)}) %collective-permute-start) | collective-permute-done | bytes 163872 | tf_op jit(solution)/shard_map/ppermute | solution.py:305
  83.0 1.0 copy-done.24
  84.0 1.0 copy-done.25
  85.0 0.9 copy-done.31
  86.0 0.9 copy-done.33
  86.9 0.9 copy-done.35
  87.8 12.7 %shard_map.221 = (bf16[160,512]{1,0:T(8,128)(2,1)}, bf16[160,512]{1,0:T(8,128)(2,1)S(1)}, bf16[160,512]{1,0:T(8,128)(2,1)S(1)}, bf16[160,512]{1,0:T(8,128)(2,1)S...) custom-call(bf16[1280,512]{1,0:T(8,128)(2,1)} %mel_ref.1, ...), custom_call_target="tpu_custom_call" | custom-call | tf_op jit(solution)/shard_map/pallas_call | solution.py:310
  100.5 0.8 copy-done.10
  101.3 0.8 copy-done.12
  102.2 0.8 copy-done.14
  103.0 0.8 copy-done.16
  103.8 0.8 copy-done.18
  105.1 2.3 collective-permute-done.2.sb_ref
  108.1 4.6 %collective-permute-done.3.sa_ref = bf16[160,512]{1,0:T(8,128)(2,1)S(1)} collective-permute-done((bf16[160,512]{1,0:T(8,128)(2,1)S(1)}, bf16[160,512]{1,0:T(8,128)(2,1)S(1)}, u32[]{:S(2)}, u32[]{:S(2)}) %collective-permute-start.3) | collective-permute-done | bytes 163872 | tf_op jit(solution)/shard_map/ppermute | solution.py:339
  113.3 1.0 copy-done.23
  114.3 0.9 copy-done.28
  115.3 0.9 copy-done.30
  116.2 1.7 shard_map.222
  118.1 0.8 copy-done.15
  119.3 2.3 pad.9
  121.6 1.7 dynamic-slice_bitcast_fusion
  123.4 4.3 %collective-permute-done.5 = bf16[26,80,512]{2,1,0:T(8,128)(2,1)} collective-permute-done((bf16[26,80,512]{2,1,0:T(8,128)(2,1)S(1)}, bf16[26,80,512]{2,1,0:T(8,128)(2,1)}, u32[]{:S(2)}, u32[]{:S(2)}) %collective-permute-start.5) | collective-permute-done | bytes 2129952 | tf_op jit(solution)/shard_map/ppermute | solution.py:239
  127.7 2.9 %fusion = bf16[26,80,512]{2,1,0:T(8,128)(2,1)S(1)} fusion(bf16[26,80,512]{2,1,0:T(8,128)(2,1)} %collective-permute-done.5, bf16[26,2,80,512]{3,2,1,0:T(8,128)(2,1)} %bitcast.8, s32[]{:T(128)S(6)} %select_n.18), kind=kLoop, calls=%fused_computation.1 | loop fusion | flops 4259840 | bytes 6389764 | tf_op jit(solution)/shard_map/convert_element_type | solution.py:240
  130.7 2.2 reshape.88
  132.9 2.8 %copy.36 = bf16[4,26,20,512]{3,0,2,1:T(4,128)(2,1)S(1)} copy(bf16[4,26,20,512]{3,2,0,1:T(8,128)(2,1)} %bitcast.34) | data formatting | bytes 4259840 | tf_op jit(solution)/shard_map/transpose | solution.py:356
  135.7 1.8 copy.37
  137.5 1.1 reshape.82
  138.6 39.8 %all_to_all.21 = bf16[256,4,512]{2,1,0:T(4,128)(2,1)} all-to-all(bf16[256,4,512]{2,1,0:T(4,128)(2,1)} %reshape.82), channel_id=1, replica_groups=mesh['wide'=64,'narrow'=4] {'wide','narrow'}, dimensions={0} | all-to-all | bytes 2097152 | tf_op jit(solution)/shard_map/all_to_all | solution.py:361
  178.4 1.3 reshape.83.ret_ref
  179.8 3.0 %shard_map.223 = (f32[512,512]{1,0:T(8,128)}, bf16[512,512]{1,0:T(8,128)(2,1)S(1)}, bf16[512,512]{1,0:T(8,128)(2,1)S(1)}) custom-call(bf16[1024,512]{1,0:T(8,128)(2,1)S(1)} %reshape.83.ret_ref, s32[1,512]{1,0:T(1,128)S(1)} %get-tuple-element.42.slot_ref, s32[1,512]{1,0:T(1,128)S(1)} %bitcast.31, bf16[512,512]{1,0:T(8,128)(2,1)S(1)} %copy-done.21, ...), custom_call_target="tpu_custom_call" | custom-call | tf_op jit(solution)/shard_map/pallas_call | solution.py:368
  183.0 2.0 collective-permute-done.4
  185.7 13.1 %all_to_all.22 = bf16[4,140,512]{2,1,0:T(8,128)(2,1)S(1)} all-to-all(bf16[4,140,512]{2,1,0:T(8,128)(2,1)S(1)} %copy.34), channel_id=1, replica_groups=mesh['wide'=64,'narrow'=4] {'narrow'}, dimensions={0} | all-to-all | bytes 1146880 | tf_op jit(solution)/shard_map/all_to_all | solution.py:377
  198.9 1.2 slice.27
  200.2 0.7 fusion.6
  201.0 25.8 %all_to_all.23 = bf16[32,20,512]{2,1,0:T(8,128)(2,1)S(1)} all-to-all(bf16[32,20,512]{2,1,0:T(8,128)(2,1)S(1)} %pad_maximum_fusion), channel_id=1, replica_groups={{0,8,16,24,32,40,48,56,64,72,80,88,96,104,112,120,128,136,144,152,160,1..., dimensions={0} | all-to-all | bytes 1310720 | tf_op jit(solution)/shard_map/all_to_all | solution.py:389
  (93 shorter events, 8.5 us)
Async XLA Ops:
  7.2 191.7 %reduce-scatter.2.cloned.1.call-start = ((), (), s32[]{:S(2)}) async-start(), calls=%async_computation.5 | async-start | bytes 2662400 | tf_op jit(solution)/shard_map/reduce_scatter | solution.py:357
  7.2 1.0 copy-start
  8.3 1.0 copy-start.2
  9.3 1.0 copy-start.4
  10.3 1.0 copy-start.9
  11.4 0.7 copy-start.36
  12.1 0.7 copy-start.38
  12.7 0.7 copy-start.39
  15.6 0.8 copy-start.20
  17.7 54.7 %copy-start.6 = (bf16[512,512]{1,0:T(8,128)(2,1)S(1)}, bf16[512,512]{1,0:T(8,128)(2,1)}, u32[]{:S(2)}) copy-start(bf16[512,512]{1,0:T(8,128)(2,1)} %wout_ref.3) | copy-start | bytes 1572868
  17.7 54.7 %copy-start.7 = (bf16[512,512]{1,0:T(8,128)(2,1)S(1)}, bf16[512,512]{1,0:T(8,128)(2,1)}, u32[]{:S(2)}) copy-start(bf16[512,512]{1,0:T(8,128)(2,1)} %wsrc_ref.3) | copy-start | bytes 1572868
  17.7 54.7 %copy-start.8 = (bf16[512,512]{1,0:T(8,128)(2,1)S(1)}, bf16[512,512]{1,0:T(8,128)(2,1)}, u32[]{:S(2)}) copy-start(bf16[512,512]{1,0:T(8,128)(2,1)} %wdst_ref.3) | copy-start | bytes 1572868
  17.7 54.8 %copy-start.26 = (bf16[160,512]{1,0:T(8,128)(2,1)S(1)}, bf16[160,512]{1,0:T(8,128)(2,1)}, u32[]{:S(2)}) copy-start(bf16[160,512]{1,0:T(8,128)(2,1)} %static_ref.1) | copy-start | bytes 491524
  69.9 6.1 %copy-start.40 = (s32[1280]{0:T(1024)S(1)}, s32[1280]{0:T(1024)}, u32[]{:S(2)}) copy-start(s32[1280]{0:T(1024)} %param.27) | copy-start | bytes 15364
  73.4 0.8 copy-start.22
  74.2 0.7 copy-start.34
  74.9 2.8 %collective-permute-start.1 = (bf16[160,512]{1,0:T(8,128)(2,1)S(1)}, bf16[160,512]{1,0:T(8,128)(2,1)S(1)}, u32[]{:S(2)}, u32[]{:S(2)}) collective-permute-start(bf16[160,512]{1,0:T(8,128)(2,1)S(1)} %get-tuple-element.31.po_ref), channel_id=1, source_target_pairs={{4,0},{8,4},{12,8},{16,12},{20,16},{24,20},{28,24},{32,28},{36,32}... | collective-permute-start | bytes 491528 | tf_op jit(solution)/shard_map/ppermute | solution.py:306
  74.9 8.1 %collective-permute-start = (bf16[160,512]{1,0:T(8,128)(2,1)S(1)}, bf16[160,512]{1,0:T(8,128)(2,1)S(1)}, u32[]{:S(2)}, u32[]{:S(2)}) collective-permute-start(bf16[160,512]{1,0:T(8,128)(2,1)S(1)} %get-tuple-element.31.po_ref), channel_id=1, source_target_pairs={{0,4},{4,8},{8,12},{12,16},{16,20},{20,24},{24,28},{28,32},{32,36}... | collective-permute-start | bytes 491528 | tf_op jit(solution)/shard_map/ppermute | solution.py:305
  75.4 0.7 copy-start.32
  83.0 1.0 copy-start.24
  84.0 1.0 copy-start.25
  85.0 0.9 copy-start.31
  86.0 0.9 copy-start.33
  86.9 0.9 copy-start.35
  100.5 0.8 copy-start.10
  101.3 0.8 copy-start.12
  102.2 0.8 copy-start.14
  103.0 0.8 copy-start.16
  103.8 0.8 copy-start.18
  104.6 2.8 %collective-permute-start.2 = (bf16[160,512]{1,0:T(8,128)(2,1)S(1)}, bf16[160,512]{1,0:T(8,128)(2,1)S(1)}, u32[]{:S(2)}, u32[]{:S(2)}) collective-permute-start(bf16[160,512]{1,0:T(8,128)(2,1)S(1)} %get-tuple-element.36), channel_id=1, source_target_pairs={{4,0},{8,4},{12,8},{16,12},{20,16},{24,20},{28,24},{32,28},{36,32}... | collective-permute-start | bytes 491528 | tf_op jit(solution)/shard_map/ppermute | solution.py:338
  104.6 8.1 %collective-permute-start.3 = (bf16[160,512]{1,0:T(8,128)(2,1)S(1)}, bf16[160,512]{1,0:T(8,128)(2,1)S(1)}, u32[]{:S(2)}, u32[]{:S(2)}) collective-permute-start(bf16[160,512]{1,0:T(8,128)(2,1)S(1)} %get-tuple-element.37), channel_id=1, source_target_pairs={{0,4},{4,8},{8,12},{12,16},{16,20},{20,24},{24,28},{28,32},{32,36}... | collective-permute-start | bytes 491528 | tf_op jit(solution)/shard_map/ppermute | solution.py:339
  105.1 12.8 %copy-start.19 = (bf16[512,512]{1,0:T(8,128)(2,1)S(1)}, bf16[512,512]{1,0:T(8,128)(2,1)}, u32[]{:S(2)}) copy-start(bf16[512,512]{1,0:T(8,128)(2,1)} %copy-done.18) | copy-start | bytes 1572868
  107.4 0.7 copy-start.27
  112.6 0.7 copy-start.29
  113.3 1.0 copy-start.23
  114.3 0.9 copy-start.28
  115.3 0.9 copy-start.30
  116.2 1.8 copy-start.17
  117.9 1.0 copy-start.15
  117.9 1.2 copy-start.13
  118.0 1.3 copy-start.11
  123.3 4.4 %collective-permute-start.5 = (bf16[26,80,512]{2,1,0:T(8,128)(2,1)S(1)}, bf16[26,80,512]{2,1,0:T(8,128)(2,1)}, u32[]{:S(2)}, u32[]{:S(2)}) collective-permute-start(bf16[26,80,512]{2,1,0:T(8,128)(2,1)S(1)} %dynamic-slice_bitcast_fusion), channel_id=1, source_target_pairs={{0,4},{4,0},{8,12},{12,8},{16,20},{20,16},{24,28},{28,24},{32,36},... | collective-permute-start | bytes 6389768 | tf_op jit(solution)/shard_map/ppermute | solution.py:239
  138.6 41.2 %copy-start.1 = (bf16[512,512]{1,0:T(8,128)(2,1)S(1)}, bf16[512,512]{1,0:T(8,128)(2,1)}, u32[]{:S(2)}) copy-start(bf16[512,512]{1,0:T(8,128)(2,1)} %grid_ref.3) | copy-start | bytes 1572868
  138.6 41.2 %copy-start.3 = (bf16[512,512]{1,0:T(8,128)(2,1)S(1)}, bf16[512,512]{1,0:T(8,128)(2,1)}, u32[]{:S(2)}) copy-start(bf16[512,512]{1,0:T(8,128)(2,1)} %edge_ref.3) | copy-start | bytes 1572868
  138.6 41.2 %copy-start.5 = (bf16[512,512]{1,0:T(8,128)(2,1)S(1)}, bf16[512,512]{1,0:T(8,128)(2,1)}, u32[]{:S(2)}) copy-start(bf16[512,512]{1,0:T(8,128)(2,1)} %wg_ref.3) | copy-start | bytes 1572868
  138.6 41.2 %copy-start.21 = (bf16[512,512]{1,0:T(8,128)(2,1)S(1)}, bf16[512,512]{1,0:T(8,128)(2,1)}, u32[]{:S(2)}) copy-start(bf16[512,512]{1,0:T(8,128)(2,1)} %copy-done.20) | copy-start | bytes 1572868
  138.6 41.2 %copy-start.37 = (s32[512]{0:T(512)S(1)}, s32[512]{0:T(512)}, u32[]{:S(2)}) copy-start(s32[512]{0:T(512)} %param.22) | copy-start | bytes 6148
  182.9 2.1 collective-permute-start.4
Sparse Core Ops, SparseCore 0:
  137.6 33.2 reduce-scatter.1
where the time goes:
time: 236 us; the launch traced here: 234 us
  blocking collectives  131 us (56%)
  local copies, waits for them, and re-layouts  43.8 us (19%)
  Pallas kernels  20.5 us (9%)
  waiting for transfers between devices  19.4 us (8%)
  between operations  14.4 us (6%)
  other arithmetic  4.22 us (2%)
    all_to_all x1, blocking collectives, on_device(): lax.all_to_all(payload.reshape(devices, capacity, width + LANE), ('wide',...  52.2 us
    all_to_all x1, blocking collectives, on_device(): lax.all_to_all(returning.reshape(devices, capacity, width), ('wide', 'nar...  39.8 us
    all_to_all x1, blocking collectives, on_device(): lax.all_to_all(both, 'wide', split_axis=0, concat_axis=0, tiled=True, axi...  25.8 us
    unnamed x89, local copies, waits for them, and re-layouts  23.6 us
    all_to_all x1, blocking collectives, on_device(): lax.all_to_all(last.reshape(narrow, late_groups * chunk, width), 'narrow'...  13.1 us
    pallas_call x1, Pallas kernels, on_device(): call(functools.partial(processor, (proc_scale, node_scale)), [block] * 4...  12.7 us
    ppermute x2, waiting for transfers between devices, partner_sum(): came = lax.ppermute(sent, 'wide', [(i, i ^ 1) for i in range(wide)])  6.28 us
    ppermute x1, waiting for transfers between devices, on_device(): p_before = lax.ppermute(p_src, 'wide', up)  5.23 us
  transfers between devices with their start and end apart: 7, of which 6 were waited for; matrix products, arithmetic and copies ran while one was open for 2% of the time, Pallas kernels for 1%

commit v1 on v0

--- a/solution.py
+++ b/solution.py
@@ -2,6 +2,7 @@
 
 import jax
 import jax.numpy as jnp
+import numpy as np
 from jax import lax
 from jax.experimental import pallas as pl
 from jax.experimental.pallas import tpu as pltpu
@@ -192,9 +193,29 @@
     gpd_ref[...] = (dot_lt(h0, dst_sum) * proc_scale).astype(BF)
 
 
+def split_halves(core, held, layout, kept_ref, sent_ref):
+    first, groups, half = layout
+    width = kept_ref.shape[1]
+    even = core == 0
+    step = 16
+
+    def piece(row):
+        ref = held[row // width] if row < 10 * width else None
+        return jnp.zeros((step, width), BF) if ref is None else ref[pl.ds(row % width, step), :]
+
+    for group in range(groups):
+        for part in range(0, half, step):
+            row = (first + group) * 2 * half + part
+            at = pl.ds(group * half + part, step)
+            left, right = piece(row), piece(row + half)
+            kept_ref[at, :] = jnp.where(even, left, right)
+            sent_ref[at, :] = jnp.where(even, right, left)
+
+
 def mesh_backward(
-    scales, so_ref, sb_ref, sa_ref, mg_ref, h0_ref, a0_ref, pick_ref, wsrc_ref, wout_ref,
-    out_ref, ret_ref, gps_ref, geo_ref, padded,
+    scales, layout, core_ref, so_ref, sb_ref, sa_ref, mg_ref, h0_ref, a0_ref, pick_ref, wsrc_ref,
+    wout_ref, gpe_ref, gpd_ref, gpo_ref, gns_ref, gna_ref, gno_ref,
+    out_ref, ret_ref, kept_ref, sent_ref, padded, geo, gps,
 ):
     proc_scale, enc_scale = scales
     rows = h0_ref.shape[0]
@@ -202,42 +223,67 @@
     grad = mg_ref[...] + dot_rt(total, wsrc_ref[...])
     out_ref[...] = grad
     d_mesh = grad.astype(BF)
-    padded[...] = jnp.zeros_like(padded)
+    padded[pl.ds(rows, 256 - rows), :] = jnp.zeros((256 - rows, padded.shape[1]), BF)
     padded[pl.ds(0, rows), :] = dot_rt(d_mesh, wout_ref[...]).astype(BF)
     step = 256
     for at in range(0, ret_ref.shape[0], step):
         ret_ref[pl.ds(at, step), :] = dot(pick_ref[pl.ds(at, step), :], padded[...]).astype(BF)
-    gps_ref[...] = (dot_lt(h0_ref[...], total) * proc_scale).astype(BF)
-    geo_ref[...] = (dot_lt(a0_ref[...], d_mesh) * enc_scale).astype(BF)
+    gps[...] = (dot_lt(h0_ref[...], total) * proc_scale).astype(BF)
+    geo[...] = (dot_lt(a0_ref[...], d_mesh) * enc_scale).astype(BF)
+    held = [None, None, geo, gpe_ref, gps, gpd_ref, gpo_ref, gns_ref, gna_ref, gno_ref]
+    split_halves(core_ref[0], held, layout, kept_ref, sent_ref)
 
 
 def enc_backward(
-    enc_scale, ret_ref, slot_ref, src_ref, sg_ref, edge_ref, grid_ref, wg_ref,
-    out_ref, gee_ref, geg_ref,
+    enc_scale, layout, core_ref, ret_ref, slot_ref, src_ref, sg_ref, edge_ref, grid_ref, wg_ref,
+    out_ref, kept_ref, sent_ref, gee, geg,
 ):
     chosen = same(columns(slot_ref[...]), ret_ref.shape[0])
     d_enc = (dot(chosen, ret_ref[...]) * sg_ref[...].astype(F32)).astype(BF)
-    gee_ref[...] = (dot_lt(edge_ref[...], d_enc) * enc_scale).astype(BF)
+    gee[...] = (dot_lt(edge_ref[...], d_enc) * enc_scale).astype(BF)
     grid_sum = dot(same_t(src_ref[...], grid_ref.shape[0]), d_enc).astype(BF)
-    geg_ref[...] = (dot_lt(grid_ref[...], grid_sum) * enc_scale).astype(BF)
+    geg[...] = (dot_lt(grid_ref[...], grid_sum) * enc_scale).astype(BF)
     out_ref[...] = dot_rt(grid_sum, wg_ref[...])
-
-
-def call(body, outs, scratch=(), flops=0, moved=0, limit=48 << 20):
+    split_halves(core_ref[0], [gee, geg] + [None] * 8, layout, kept_ref, sent_ref)
+
+
+def add_halves(chunk, turn_ref, kept_ref, came_ref, out_ref):
+    narrow, length, width = out_ref.shape
+    blocks = turn_ref.shape[0]
+    step = blocks // narrow
+    skip = length - kept_ref.shape[0] // narrow
+    if skip:
+        for y in range(narrow):
+            out_ref[y, pl.ds(0, skip), :] = jnp.zeros((skip, width), BF)
+    for at in range(0, kept_ref.shape[0], blocks):
+        total = kept_ref[pl.ds(at, blocks), :].astype(F32) + came_ref[pl.ds(at, blocks), :].astype(F32)
+        total = total.astype(BF)
+        if step > chunk:
+            total = dot(turn_ref[...], total).astype(BF)
+        for y in range(narrow):
+            out_ref[y, pl.ds(skip + at // narrow, step), :] = total[y * step : (y + 1) * step]
+
+
+def turned(narrow, chunk, groups):
+    rows = np.arange(groups * narrow * chunk).reshape(groups, narrow, chunk)
+    rows = rows.transpose(1, 0, 2).reshape(-1)
+    return jnp.asarray(rows[:, None] == np.arange(rows.size)[None, :], BF)
+
+
+def call(body, outs, scratch=(), flops=0, moved=0, limit=16, scalars=0):
+    ins = {}
+    if scalars:
+        ins["in_specs"] = [pl.BlockSpec(memory_space=pltpu.SMEM)] + [
+            pl.BlockSpec(memory_space=pltpu.VMEM)
+        ] * scalars
     return pl.pallas_call(
         body,
+        **ins,
         out_shape=[jax.ShapeDtypeStruct(shape, kind) for shape, kind in outs],
         scratch_shapes=[pltpu.VMEM(shape, kind) for shape, kind in scratch],
-        compiler_params=pltpu.CompilerParams(vmem_limit_bytes=limit),
+        compiler_params=pltpu.CompilerParams(vmem_limit_bytes=limit << 20),
         cost_estimate=pl.CostEstimate(flops=flops, bytes_accessed=moved, transcendentals=0),
     )
-
-
-def partner_sum(grads, core, wide):
-    kept = lax.dynamic_index_in_dim(grads, core, 1, keepdims=False)
-    sent = lax.dynamic_index_in_dim(grads, 1 - core, 1, keepdims=False)
-    came = lax.ppermute(sent, "wide", [(i, i ^ 1) for i in range(wide)])
-    return (kept.astype(F32) + came.astype(F32)).astype(BF)
 
 
 def on_device(
@@ -318,6 +364,7 @@
             ((reach, width), F32),
             ((width, width), F32),
         ],
+        limit=24,
     )(
         mesh_edge_latent,
         mesh_source.reshape(-1, 256),
@@ -337,27 +384,43 @@
     )
     from_after = lax.ppermute(s_before, "wide", down)
     from_before = lax.ppermute(s_after, "wide", up)
-    mesh_grad, returning, gps, geo = call(
-        functools.partial(mesh_backward, (proc_scale, enc_scale)),
-        [((rows, width), F32), ((slots, width), BF), square, square],
-        [((256, width), BF)],
-    )(s_own, from_after, from_before, partial_grad, h0, a0, pick, w_proc_src, w_enc_out)
-
-    pair = 2 * narrow
+    chips = wide // 2
     chunk = 10 * width // devices
-    span = pair * chunk
+    half = narrow * chunk
     late = 2 * width
-    late_groups = -(-late // span)
-    first = late // span
-    early = jnp.concatenate([geo, gpe, gps, gpd, gpo, gns, gna, gno], axis=0)
-    early = jnp.pad(early, ((late - first * span, 0), (0, 0)))
-    groups = wide // 2 - first
-    early = partner_sum(early.reshape(groups, 2, narrow * chunk, width), core, wide)
-    early = early.reshape(groups, narrow, chunk, width).transpose(1, 0, 2, 3)
+    block = 4 if chunk % 16 else 1
+    span = 2 * half * block
+    late_layout = (0, -(-late // span) * block, half)
+    early_layout = (late // span * block, chips - late // span * block, half)
+    turn = turned(narrow, chunk, block)
+    late_block = ((late_layout[1] * half, width), BF)
+    early_block = ((early_layout[1] * half, width), BF)
+    where = core.reshape(1)
+    swap = [(i, i ^ 1) for i in range(wide)]
+    mesh_grad, returning, kept, sent = call(
+        functools.partial(mesh_backward, (proc_scale, enc_scale), early_layout),
+        [((rows, width), F32), ((slots, width), BF), early_block, early_block],
+        [((256, width), BF), square, square],
+        scalars=15,
+    )(
+        where, s_own, from_after, from_before, partial_grad, h0, a0, pick, w_proc_src, w_enc_out,
+        gpe, gpd, gpo, gns, gna, gno,
+    )
+    came = lax.ppermute(sent, "wide", swap)
+    far = 4 if chips > 4 else 2
+    near = chips // far
+    line = [[i + j * 2 * near for j in range(far)] for i in range(2 * near)]
+    plane = [[i * 2 * near + 2 * j + c for j in range(near)] for i in range(far) for c in range(2)]
+    turning = functools.partial(add_halves, chunk)
+    (early,) = call(turning, [((narrow, chips * chunk, width), BF)])(turn, kept, came)
+    early = lax.psum_scatter(early, "narrow", scatter_dimension=0, tiled=True)
     early = lax.psum_scatter(
-        early.reshape(narrow, groups * chunk, width), "narrow", scatter_dimension=0, tiled=True
-    ).reshape(groups, chunk, width)
-
+        early.reshape(far, near * chunk, width),
+        "wide",
+        scatter_dimension=0,
+        tiled=True,
+        axis_index_groups=line,
+    ).reshape(near * chunk, width)
     returned = lax.all_to_all(
         returning.reshape(devices, capacity, width),
         ("wide", "narrow"),
@@ -365,34 +428,31 @@
         concat_axis=0,
         tiled=True,
     ).reshape(slots, width)
-    grid_grad, gee, geg = call(
-        functools.partial(enc_backward, enc_scale),
-        [((grid_rows, width), F32), square, square],
-    )(returned, slot, source, enc_sg, enc_edge_latent, grid_latent, w_enc_grid)
-
-    last = jnp.concatenate([gee, geg], axis=0)
-    last = jnp.pad(last, ((0, late_groups * span - late), (0, 0)))
-    last = partner_sum(last.reshape(late_groups, 2, narrow * chunk, width), core, wide)
-    last = last.reshape(late_groups, narrow, chunk, width).transpose(1, 0, 2, 3)
-    last = lax.all_to_all(
-        last.reshape(narrow, late_groups * chunk, width),
-        "narrow",
-        split_axis=0,
-        concat_axis=0,
-        tiled=True,
-    )
-    last = jnp.sum(last.astype(F32), axis=0).reshape(late_groups, chunk, width)
-    shared = late_groups - first
-    both = jnp.concatenate(
-        [last[:first], last[first:] + early[:shared].astype(F32), early[shared:].astype(F32)], axis=0
-    ).astype(BF)
+    grid_grad, kept, sent = call(
+        functools.partial(enc_backward, enc_scale, late_layout),
+        [((grid_rows, width), F32), late_block, late_block],
+        [square, square],
+        scalars=7,
+    )(where, returned, slot, source, enc_sg, enc_edge_latent, grid_latent, w_enc_grid)
+    came = lax.ppermute(sent, "wide", swap)
+    spread = late_layout[1] * chunk
+    (last,) = call(turning, [((narrow, spread, width), BF)])(turn, kept, came)
+    last = lax.all_to_all(last, "narrow", split_axis=0, concat_axis=0, tiled=True)
+    last = jnp.sum(last.astype(F32), axis=0).astype(BF)
+    parts = [
+        lax.ppermute(last, "wide", [(j * 2 * near + i, i) for i in range(2 * near)])
+        for j in range(1, far)
+    ]
+    at_first = lax.axis_index("wide") < 2 * near
+    last = jnp.where(at_first, last.astype(F32), 0.0) + sum(p.astype(F32) for p in parts)
+    both = early.astype(F32) + last[: near * chunk]
     both = lax.all_to_all(
-        both,
+        both.astype(BF).reshape(near, chunk, width),
         "wide",
         split_axis=0,
         concat_axis=0,
         tiled=True,
-        axis_index_groups=[[i for i in range(wide) if i % 2 == c] for c in range(2)],
+        axis_index_groups=plane,
     )
     summed = jnp.sum(both.astype(F32), axis=0).reshape(-1)
     return (mesh_out, grid_grad, summed, mesh_grad)

time: 236 us -> 230 us (0.975)
  blocking collectives: 131 us -> 118 us
  waiting for transfers between devices: 19.4 us -> 28.6 us
  local copies, waits for them, and re-layouts: 43.8 us -> 39.4 us
  starting transfers between devices: 1.24 us -> 4.98 us
  other arithmetic: 4.22 us -> 1.17 us
    all_to_all x2, blocking collectives: 38.9 us -> 27.4 us  [the longest x1 13.8 us: on_device(): lax.all_to_all(last, 'narrow', split_axis=0, concat_axis=0, tiled=True)]
    unnamed x89 -> x92, local copies, waits for them, and re-layouts: 23.6 us -> 33.3 us
    ppermute x2 -> x5, waiting for transfers between devices: 6.28 us -> 14.8 us  [the longest x3 8.13 us: on_device(): lax.ppermute(last, 'wide', [(j * 2 * near + i, i) for i in range(2 * near)])]
    reshape x4 -> x1, local copies, waits for them, and re-layouts: 4.14 us -> 0.04 us  [on_device(): both.astype(BF).reshape(near, chunk, width)]
    ppermute x2 -> x5, starting transfers between devices: 0.19 us -> 3.88 us  [the longest x3 3.88 us: on_device(): lax.ppermute(last, 'wide', [(j * 2 * near + i, i) for i in range(2 * near)])]
    pallas_call x2 -> x4, Pallas kernels: 4.64 us -> 8.28 us  [the longest x1 3.1 us: on_device(): call(functools.partial(enc_backward, enc_scale, late_layout), [((grid_row...]
    transpose x2 -> x0, local copies, waits for them, and re-layouts: 3.12 us -> none  [the longest x1 2.82 us: on_device(): early = early.reshape(groups, narrow, chunk, width).transpose(1, 0, 2, 3)]
  transfers between devices with their start and end apart: 7 -> 11, of which waited for: 6 -> 7; matrix products, arithmetic and copies ran while one was open for 2% -> 1% of each run, Pallas kernels for 1% -> 2%
where the time goes in v1:
time: 230 us; the launch traced here: 229 us
  blocking collectives  118 us (51%)
  local copies, waits for them, and re-layouts  39.4 us (17%)
  waiting for transfers between devices  28.6 us (12%)
  Pallas kernels  22.2 us (10%)
  between operations  14.3 us (6%)
  starting transfers between devices  4.98 us (2%)
    all_to_all x1, blocking collectives, on_device(): lax.all_to_all(payload.reshape(devices, capacity, width + LANE), ('wide',...  52 us
    all_to_all x1, blocking collectives, on_device(): lax.all_to_all(returning.reshape(devices, capacity, width), ('wide', 'nar...  38.8 us
    unnamed x92, local copies, waits for them, and re-layouts  33.3 us
    all_to_all x1, blocking collectives, on_device(): lax.all_to_all(last, 'narrow', split_axis=0, concat_axis=0, tiled=True)  13.8 us
    all_to_all x1, blocking collectives, on_device(): lax.all_to_all(both.astype(BF).reshape(near, chunk, width), 'wide', split...  13.6 us
    pallas_call x1, Pallas kernels, on_device(): call(functools.partial(processor, (proc_scale, node_scale)), [block] * 4...  10.7 us
    ppermute x3, waiting for transfers between devices, on_device(): lax.ppermute(last, 'wide', [(j * 2 * near + i, i) for i in range(2 * near)])  8.13 us
    ppermute x2, waiting for transfers between devices, on_device(): came = lax.ppermute(sent, 'wide', swap)  6.72 us
  transfers between devices with their start and end apart: 11, of which 7 were waited for; matrix products, arithmetic and copies ran while one was open for 1% of the time, Pallas kernels for 2%

profile of v1, /device:TPU:8, one launch (start us, length us, event | category | flops | bytes accessed | tf_op | source)
XLA Modules:
  0.0 228.8 jit_solution(3225756723447922549)
XLA Ops:
  7.2 1.0 copy-done.2
  8.3 1.0 copy-done.4
  9.3 1.0 copy-done.6
  10.3 1.0 copy-done.11
  13.4 2.2 shard_map.228
  15.7 0.8 copy-done.26
  16.8 52.0 %all_to_all.20 = bf16[256,4,640]{2,1,0:T(4,128)(2,1)} all-to-all(bf16[256,4,640]{2,1,0:T(4,128)(2,1)S(1)} %reshape.55), channel_id=1, replica_groups=mesh['wide'=64,'narrow'=4] {'wide','narrow'}, dimensions={0} | all-to-all | bytes 2621440 | tf_op jit(solution)/shard_map/all_to_all | solution.py:338
  68.8 2.6 %reshape.56.recv_ref = bf16[1024,640]{1,0:T(8,128)(2,1)S(1)} reshape(bf16[256,4,640]{2,1,0:T(4,128)(2,1)} %all_to_all.20) | data formatting | bytes 2621440 | tf_op jit(solution)/shard_map/reshape | solution.py:344
  71.5 0.9 shard_map.229
  75.8 1.0 collective-permute-done.1.pa_ref
  76.7 5.2 %collective-permute-done.pb_ref = bf16[160,512]{1,0:T(8,128)(2,1)S(1)} collective-permute-done((bf16[160,512]{1,0:T(8,128)(2,1)S(1)}, bf16[160,512]{1,0:T(8,128)(2,1)S(1)}, u32[]{:S(2)}, u32[]{:S(2)}) %collective-permute-start) | collective-permute-done | bytes 163872 | tf_op jit(solution)/shard_map/ppermute | solution.py:351
  82.0 1.3 copy-done.9
  83.3 1.0 copy-done.28
  84.3 1.0 copy-done.29
  85.4 1.0 copy-done.30
  86.4 1.0 copy-done.31
  87.4 1.0 copy-done.32
  88.5 0.9 copy-done.36
  89.4 0.9 copy-done.38
  90.3 0.9 copy-done.40
  91.2 10.7 %shard_map.230 = (bf16[160,512]{1,0:T(8,128)(2,1)}, bf16[160,512]{1,0:T(8,128)(2,1)S(1)}, bf16[160,512]{1,0:T(8,128)(2,1)S(1)}, bf16[160,512]{1,0:T(8,128)(2,1)S...) custom-call(bf16[1280,512]{1,0:T(8,128)(2,1)S(1)} %copy-done.9, ...), custom_call_target="tpu_custom_call" | custom-call | tf_op jit(solution)/shard_map/pallas_call | solution.py:356
  103.6 0.8 copy-done.18
  105.2 0.8 copy-done.22
  107.3 2.3 %collective-permute-done.2.sb_ref = bf16[160,512]{1,0:T(8,128)(2,1)S(1)} collective-permute-done((bf16[160,512]{1,0:T(8,128)(2,1)S(1)}, bf16[160,512]{1,0:T(8,128)(2,1)S(1)}, u32[]{:S(2)}, u32[]{:S(2)}) %collective-permute-start.2) | collective-permute-done | bytes 163872 | tf_op jit(solution)/shard_map/ppermute | solution.py:385
  109.6 5.2 %collective-permute-done.3.sa_ref = bf16[160,512]{1,0:T(8,128)(2,1)S(1)} collective-permute-done((bf16[160,512]{1,0:T(8,128)(2,1)S(1)}, bf16[160,512]{1,0:T(8,128)(2,1)S(1)}, u32[]{:S(2)}, u32[]{:S(2)}) %collective-permute-start.3) | collective-permute-done | bytes 163872 | tf_op jit(solution)/shard_map/ppermute | solution.py:386
  115.5 1.0 copy-done.13
  116.5 1.0 copy-done.15
  117.6 1.0 copy-done.17
  118.6 1.0 copy-done.19
  119.7 1.0 copy-done.21
  120.7 1.0 copy-done.23
  121.8 1.0 copy-done.25
  122.8 0.9 copy-done.35
  123.7 1.7 shard_map.231
  125.4 4.4 %collective-permute-done.4.came_ref = bf16[2240,512]{1,0:T(8,128)(2,1)S(1)} collective-permute-done((bf16[2240,512]{1,0:T(8,128)(2,1)S(1)}, bf16[2240,512]{1,0:T(8,128)(2,1)S(1)}, u32[]{:S(2)}, u32[]{:S(2)}) %collective-permute-start.4) | collective-permute-done | bytes 2293792 | tf_op jit(solution)/shard_map/ppermute | solution.py:409
  129.8 3.0 %shard_map.233 = bf16[4,640,512]{2,1,0:T(8,128)(2,1)} custom-call(bf16[320,320]{1,0:T(8,128)(2,1)S(1)} %copy-done.10, bf16[2240,512]{1,0:T(8,128)(2,1)S(1)} %get-tuple-element.51.kept_ref, bf16[2240,512]{1,0:T(8,128)(2,1)S(1)} %collective-permute-done.4.came_ref), custom_call_target="tpu_custom_call" | custom-call | tf_op jit(solution)/shard_map/pallas_call | solution.py:415
  133.2 38.8 %all_to_all.21 = bf16[256,4,512]{2,1,0:T(4,128)(2,1)} all-to-all(bf16[256,4,512]{2,1,0:T(4,128)(2,1)S(1)} %reshape.58), channel_id=1, replica_groups=mesh['wide'=64,'narrow'=4] {'wide','narrow'}, dimensions={0} | all-to-all | bytes 2097152 | tf_op jit(solution)/shard_map/all_to_all | solution.py:424
  172.0 1.5 reshape.59.ret_ref
  173.6 1.0 copy-done.27
  174.7 3.1 %shard_map.232 = (f32[512,512]{1,0:T(8,128)}, bf16[640,512]{1,0:T(8,128)(2,1)S(1)}, bf16[640,512]{1,0:T(8,128)(2,1)}) custom-call(s32[1]{0:T(128)} %bitcast.3.core_ref, bf16[1024,512]{1,0:T(8,128)(2,1)S(1)} %reshape.59.ret_ref, s32[1,512]{1,0:T(1,128)S(1)} %get-tuple-element.48.slot_ref, s32[1,512]{1,0:T(1,128)S(1)} %bitcast.9, ...), custom_call_target="tpu_custom_call" | custom-call | tf_op jit(solution)/shard_map/pallas_call | solution.py:431
  177.8 2.3 collective-permute-done.5.came_ref
  180.6 13.8 %all_to_all.22 = bf16[4,160,512]{2,1,0:T(8,128)(2,1)S(1)} all-to-all(bf16[4,160,512]{2,1,0:T(8,128)(2,1)S(1)} %shard_map.234), channel_id=1, replica_groups=mesh['wide'=64,'narrow'=4] {'narrow'}, dimensions={0} | all-to-all | bytes 1310720 | tf_op jit(solution)/shard_map/all_to_all | solution.py:440
  194.5 1.3 collective-permute-start.8
  195.8 1.3 collective-permute-start.7
  197.1 1.3 collective-permute-start.6
  198.4 8.1 %collective-permute-done.8 = bf16[160,512]{1,0:T(8,128)(2,1)S(1)} collective-permute-done((bf16[160,512]{1,0:T(8,128)(2,1)S(1)}, bf16[160,512]{1,0:T(8,128)(2,1)S(1)}, u32[]{:S(2)}, u32[]{:S(2)}) %collective-permute-start.8) | collective-permute-done | bytes 163872 | tf_op jit(solution)/shard_map/ppermute | solution.py:443
  206.6 1.0 fusion
  207.7 13.6 %all_to_all.23 = bf16[8,20,512]{2,1,0:T(8,128)(2,1)S(1)} all-to-all(bf16[8,20,512]{2,1,0:T(8,128)(2,1)S(1)} %reshape.61), channel_id=1, replica_groups={{0,8,16,24,32,40,48,56},{4,12,20,28,36,44,52,60},{64,72,80,88,96,104,11..., dimensions={0} | all-to-all | bytes 327680 | tf_op jit(solution)/shard_map/all_to_all | solution.py:449
  (90 shorter events, 12.0 us)
Async XLA Ops:
  7.2 170.6 %reduce-scatter.3.cloned.1.call-start = ((), (), s32[]{:S(2)}) async-start(), calls=%async_computation.6 | async-start | bytes 3276800 | tf_op jit(solution)/shard_map/reduce_scatter | solution.py:416
  7.2 1.0 copy-start.2
  8.3 1.0 copy-start.4
  9.3 1.0 copy-start.6
  10.3 1.0 copy-start.11
  15.6 0.8 copy-start.26
  68.8 2.6 %copy-start = (bf16[512,512]{1,0:T(8,128)(2,1)S(1)}, bf16[512,512]{1,0:T(8,128)(2,1)}, u32[]{:S(2)}) copy-start(bf16[512,512]{1,0:T(8,128)(2,1)} %wout_ref.3) | copy-start | bytes 1572868
  68.8 2.7 %copy-start.1 = (bf16[512,512]{1,0:T(8,128)(2,1)S(1)}, bf16[512,512]{1,0:T(8,128)(2,1)}, u32[]{:S(2)}) copy-start(bf16[512,512]{1,0:T(8,128)(2,1)} %wsrc_ref.3) | copy-start | bytes 1572868
  68.8 2.7 %copy-start.8 = (bf16[512,512]{1,0:T(8,128)(2,1)S(1)}, bf16[512,512]{1,0:T(8,128)(2,1)}, u32[]{:S(2)}) copy-start(bf16[512,512]{1,0:T(8,128)(2,1)} %wdst_ref.3) | copy-start | bytes 1572868
  68.8 2.7 %copy-start.33 = (bf16[160,512]{1,0:T(8,128)(2,1)S(1)}, bf16[160,512]{1,0:T(8,128)(2,1)}, u32[]{:S(2)}) copy-start(bf16[160,512]{1,0:T(8,128)(2,1)} %static_ref.1) | copy-start | bytes 491524
  71.5 3.6 %copy-start.45 = (s32[1280]{0:T(1024)S(1)}, s32[1280]{0:T(1024)}, u32[]{:S(2)}) copy-start(s32[1280]{0:T(1024)} %param.28) | copy-start | bytes 15364
  72.4 0.8 copy-start.12
  73.9 2.8 %collective-permute-start.1 = (bf16[160,512]{1,0:T(8,128)(2,1)S(1)}, bf16[160,512]{1,0:T(8,128)(2,1)S(1)}, u32[]{:S(2)}, u32[]{:S(2)}) collective-permute-start(bf16[160,512]{1,0:T(8,128)(2,1)S(1)} %get-tuple-element.31.po_ref), channel_id=1, source_target_pairs={{4,0},{8,4},{12,8},{16,12},{20,16},{24,20},{28,24},{32,28},{36,32}... | collective-permute-start | bytes 491528 | tf_op jit(solution)/shard_map/ppermute | solution.py:352
  73.9 8.1 %collective-permute-start = (bf16[160,512]{1,0:T(8,128)(2,1)S(1)}, bf16[160,512]{1,0:T(8,128)(2,1)S(1)}, u32[]{:S(2)}, u32[]{:S(2)}) collective-permute-start(bf16[160,512]{1,0:T(8,128)(2,1)S(1)} %get-tuple-element.31.po_ref), channel_id=1, source_target_pairs={{0,4},{4,8},{8,12},{12,16},{16,20},{20,24},{24,28},{28,32},{32,36}... | collective-permute-start | bytes 491528 | tf_op jit(solution)/shard_map/ppermute | solution.py:351
  82.0 1.3 copy-start.9
  83.3 1.0 copy-start.28
  84.3 1.0 copy-start.29
  85.4 1.0 copy-start.30
  86.4 1.0 copy-start.31
  87.4 1.0 copy-start.32
  88.5 0.9 copy-start.36
  89.4 0.9 copy-start.38
  90.3 0.9 copy-start.40
  102.0 0.8 copy-start.14
  103.6 0.8 copy-start.18
  105.2 0.8 copy-start.22
  106.8 2.8 %collective-permute-start.2 = (bf16[160,512]{1,0:T(8,128)(2,1)S(1)}, bf16[160,512]{1,0:T(8,128)(2,1)S(1)}, u32[]{:S(2)}, u32[]{:S(2)}) collective-permute-start(bf16[160,512]{1,0:T(8,128)(2,1)S(1)} %get-tuple-element.36), channel_id=1, source_target_pairs={{4,0},{8,4},{12,8},{16,12},{20,16},{24,20},{28,24},{32,28},{36,32}... | collective-permute-start | bytes 491528 | tf_op jit(solution)/shard_map/ppermute | solution.py:385
  106.8 8.1 %collective-permute-start.3 = (bf16[160,512]{1,0:T(8,128)(2,1)S(1)}, bf16[160,512]{1,0:T(8,128)(2,1)S(1)}, u32[]{:S(2)}, u32[]{:S(2)}) collective-permute-start(bf16[160,512]{1,0:T(8,128)(2,1)S(1)} %get-tuple-element.37), channel_id=1, source_target_pairs={{0,4},{4,8},{8,12},{12,16},{16,20},{20,24},{24,28},{28,32},{32,36}... | collective-permute-start | bytes 491528 | tf_op jit(solution)/shard_map/ppermute | solution.py:386
  115.5 1.0 copy-start.13
  116.5 1.0 copy-start.15
  117.6 1.0 copy-start.17
  118.6 1.0 copy-start.19
  119.7 1.0 copy-start.21
  120.7 1.0 copy-start.23
  121.8 1.0 copy-start.25
  122.8 0.9 copy-start.35
  123.7 6.1 %copy-start.10 = (bf16[320,320]{1,0:T(8,128)(2,1)S(1)}, bf16[320,320]{1,0:T(8,128)(2,1)}, u32[]{:S(2)}) copy-start(bf16[320,320]{1,0:T(8,128)(2,1)} %constant.27.clone.turn_ref) | copy-start | bytes 614404
  125.4 4.4 %collective-permute-start.4 = (bf16[2240,512]{1,0:T(8,128)(2,1)S(1)}, bf16[2240,512]{1,0:T(8,128)(2,1)S(1)}, u32[]{:S(2)}, u32[]{:S(2)}) collective-permute-start(bf16[2240,512]{1,0:T(8,128)(2,1)S(1)} %get-tuple-element.52), channel_id=1, source_target_pairs={{0,4},{4,0},{8,12},{12,8},{16,20},{20,16},{24,28},{28,24},{32,36},... | collective-permute-start | bytes 6881288 | tf_op jit(solution)/shard_map/ppermute | solution.py:409
  132.8 73.7 %reduce-scatter.5.cloned.1.call-start = ((), (), s32[]{:S(2)}) async-start(), calls=%async_computation.7 | async-start | bytes 819200 | tf_op jit(solution)/shard_map/reduce_scatter | solution.py:417
  171.9 1.5 copy-start.3
  172.0 1.5 copy-start.5
  172.0 1.7 copy-start.7
  172.0 1.7 copy-start.42
  173.6 1.0 copy-start.27
  177.8 2.3 %collective-permute-start.5 = (bf16[640,512]{1,0:T(8,128)(2,1)}, bf16[640,512]{1,0:T(8,128)(2,1)S(1)}, u32[]{:S(2)}, u32[]{:S(2)}) collective-permute-start(bf16[640,512]{1,0:T(8,128)(2,1)} %get-tuple-element.54), channel_id=1, source_target_pairs={{0,4},{4,0},{8,12},{12,8},{16,20},{20,16},{24,28},{28,24},{32,36},... | collective-permute-start | bytes 1966088 | tf_op jit(solution)/shard_map/ppermute | solution.py:437
  194.5 12.0 %collective-permute-start.8 = (bf16[160,512]{1,0:T(8,128)(2,1)S(1)}, bf16[160,512]{1,0:T(8,128)(2,1)S(1)}, u32[]{:S(2)}, u32[]{:S(2)}) collective-permute-start(bf16[160,512]{1,0:T(8,128)(2,1)S(1)} %reduce_sum.21), channel_id=1, source_target_pairs={{192,0},{196,4},{200,8},{204,12},{208,16},{212,20},{216,24},{220,2... | collective-permute-start | bytes 491528 | tf_op jit(solution)/shard_map/ppermute | solution.py:443
  195.8 10.7 %collective-permute-start.7 = (bf16[160,512]{1,0:T(8,128)(2,1)S(1)}, bf16[160,512]{1,0:T(8,128)(2,1)S(1)}, u32[]{:S(2)}, u32[]{:S(2)}) collective-permute-start(bf16[160,512]{1,0:T(8,128)(2,1)S(1)} %reduce_sum.21), channel_id=1, source_target_pairs={{128,0},{132,4},{136,8},{140,12},{144,16},{148,20},{152,24},{156,2... | collective-permute-start | bytes 491528 | tf_op jit(solution)/shard_map/ppermute | solution.py:443
  197.1 9.4 %collective-permute-start.6 = (bf16[160,512]{1,0:T(8,128)(2,1)S(1)}, bf16[160,512]{1,0:T(8,128)(2,1)S(1)}, u32[]{:S(2)}, u32[]{:S(2)}) collective-permute-start(bf16[160,512]{1,0:T(8,128)(2,1)S(1)} %reduce_sum.21), channel_id=1, source_target_pairs={{64,0},{68,4},{72,8},{76,12},{80,16},{84,20},{88,24},{92,28},{96,3... | collective-permute-start | bytes 491528 | tf_op jit(solution)/shard_map/ppermute | solution.py:443
  (9 other events, 6.4 us)
Sparse Core Ops, SparseCore 0:
  133.0 39.0 reduce-scatter.2
  177.9 22.1 reduce-scatter.4

commit v2 on v1

v2 whole, which is shorter than its diff:
```python
import functools

import jax
import jax.numpy as jnp
import numpy as np
from jax import lax
from jax.experimental import pallas as pl
from jax.experimental.pallas import tpu as pltpu
from jax.sharding import PartitionSpec as P

BF = jnp.bfloat16
F32 = jnp.float32
I32 = jnp.int32
LANE = 128


def dot(left, right):
    return jnp.dot(left, right, preferred_element_type=F32)


def dot_rt(left, right):
    return lax.dot_general(left, right, (((1,), (1,)), ((), ())), preferred_element_type=F32)


def dot_lt(left, right):
    return lax.dot_general(left, right, (((0,), (0,)), ((), ())), preferred_element_type=F32)


def silu_pair(value):
    sig = jax.nn.sigmoid(value)
    act = value * sig
    return act, sig + act * (1.0 - sig)


def columns(row):
    return jnp.broadcast_to(row.astype(F32), (LANE, row.shape[1])).T


def same(cols, width, shift=0):
    wide = jnp.concatenate([cols] * (-(-width // LANE)), axis=1)
    lane = lax.broadcasted_iota(I32, wide.shape, 1) + shift
    return jnp.where(wide == lane.astype(F32), 1.0, 0.0).astype(BF)


def same_t(row, height, shift=0):
    sub = lax.broadcasted_iota(I32, (height, row.shape[1]), 0) + shift
    return jnp.where(sub == row, 1.0, 0.0).astype(BF)


def enc_forward(
    capacity, tdev_ref, trow_ref, src_ref, grid_ref, edge_ref, we_ref, wg_ref, out_ref, sg_ref, slot_ref
):
    edges, width = edge_ref.buffer.shape
    slots = out_ref.buffer.shape[0]
    tdev = tdev_ref.get()[...]
    member = same_t(tdev, slots // capacity)
    before = lax.broadcasted_iota(I32, (edges, edges), 0) < lax.broadcasted_iota(
        I32, (edges, edges), 1
    )
    ahead = dot(member, jnp.where(before, 1.0, 0.0).astype(BF))
    rank = jnp.sum(member.astype(F32) * ahead, axis=0, keepdims=True)
    slot = tdev * capacity + rank.astype(I32)
    slot_ref.buffer[...] = slot
    slot_ref.send()
    tag = columns(trow_ref.get()[...] + 1).astype(BF)
    grid = grid_ref.get()[...]
    gathered = dot(same(columns(src_ref.get()[...]), grid.shape[0]), grid).astype(BF)
    pre = dot(edge_ref.get()[...], we_ref.get()[...]) + dot(gathered, wg_ref.get()[...])
    act, grad = silu_pair(pre)
    sg_ref.buffer[...] = grad.astype(BF)
    sg_ref.send()
    payload = jnp.concatenate([act.astype(BF), tag], axis=1)
    step = 256
    for at in range(0, slots, step):
        place = same_t(slot, step, at)
        out_ref.buffer[pl.ds(at, step), :] = dot(place, payload).astype(BF)


def mesh_forward(
    recv_ref, wout_ref, static_ref, wsrc_ref, wdst_ref, h0_ref, a0_ref, psrc_ref, pdst_ref, pick_ref
):
    rows, width = static_ref.buffer.shape
    padded = pick_ref.buffer.shape[1]
    tag = recv_ref.get()[:, width:].astype(F32)
    pick = same(tag, padded, 1)
    pick_ref.buffer[...] = pick
    pick_ref.send()
    a0 = dot_lt(pick, recv_ref.get()[:, :width])[:rows].astype(BF)
    a0_ref.buffer[...] = a0
    h0 = (static_ref.get()[...].astype(F32) + dot(a0, wout_ref.get()[...])).astype(BF)
    h0_ref.buffer[...] = h0
    psrc_ref.buffer[...] = dot(h0, wsrc_ref.get()[...]).astype(BF)
    pdst_ref.buffer[...] = dot(h0, wdst_ref.get()[...]).astype(BF)


def processor(
    scales,
    msrc_ref,
    mtgt_ref,
    pb_ref,
    po_ref,
    pa_ref,
    pd_ref,
    we_ref,
    mel_ref,
    wpo_ref,
    h0_ref,
    wns_ref,
    wna_ref,
    wno_ref,
    cot_ref,
    wdst_ref,
    out_ref,
    sb_ref,
    so_ref,
    sa_ref,
    mg_ref,
    gpe_ref,
    gpd_ref,
    gpo_ref,
    gns_ref,
    gna_ref,
    gno_ref,
    table,
    hot,
    sg,
    zsum,
    back,
    gacc,
):
    proc_scale, node_scale = scales
    edges, width = mel_ref.buffer.shape
    rows = h0_ref.buffer.shape[0]
    reach = table.shape[0]
    first = reach - 256
    step = 256
    steps = edges // step
    table[pl.ds(0, rows), :] = pb_ref.get()[...]
    table[pl.ds(rows, rows), :] = po_ref.get()[...]
    table[pl.ds(2 * rows, rows), :] = pa_ref.get()[...]
    table[pl.ds(3 * rows, reach - 3 * rows), :] = jnp.zeros((reach - 3 * rows, width), BF)
    table[pl.ds(first, rows), :] = pd_ref.get()[...]
    zsum[...] = jnp.zeros_like(zsum)
    for ref in (msrc_ref, mtgt_ref, we_ref, mel_ref):
        ref.get()

    def ahead(i, carry):
        at = pl.multiple_of(i * step, step)
        src = columns(msrc_ref.get()[pl.ds(i, 1), :])
        tgt = columns(mtgt_ref.get()[pl.ds(i, 1), :] + first)
        src = jnp.concatenate([src] * (reach // LANE), axis=1)
        tgt = jnp.concatenate([tgt] * (reach // LANE), axis=1)
        lane = lax.broadcasted_iota(I32, (step, reach), 1).astype(F32)
        chosen = jnp.where((src == lane) | (tgt == lane), 1.0, 0.0).astype(BF)
        hot[pl.ds(at, step), :] = chosen
        pre = dot(mel_ref.get()[pl.ds(at, step), :], we_ref.get()[...]) + dot(chosen, table[...])
        act, grad = silu_pair(pre)
        sg[pl.ds(at, step), :] = grad.astype(BF)
        zsum[...] += dot_lt(chosen[:, first:], act.astype(BF))
        return carry

    lax.fori_loop(0, steps, ahead, 0)
    zeta = zsum[pl.ds(0, rows), :].astype(BF)
    h0 = h0_ref.get()[...]
    cot = cot_ref.get()[...]
    agg = dot(zeta, wpo_ref.get()[...]).astype(BF)
    pre_node = dot(h0, wns_ref.get()[...]) + dot(agg, wna_ref.get()[...])
    act, grad = silu_pair(pre_node)
    unit = act.astype(BF)
    out_ref.buffer[...] = (h0.astype(F32) + dot(unit, wno_ref.get()[...])).astype(BF)
    out_ref.send()
    gno_ref.buffer[...] = (dot_lt(unit, cot) * node_scale).astype(BF)
    gno_ref.send()
    d_node = (dot_rt(cot, wno_ref.get()[...]) * grad).astype(BF)
    gns_ref.buffer[...] = (dot_lt(h0, d_node) * node_scale).astype(BF)
    gns_ref.send()
    gna_ref.buffer[...] = (dot_lt(agg, d_node) * node_scale).astype(BF)
    gna_ref.send()
    d_agg = dot_rt(d_node, wna_ref.get()[...]).astype(BF)
    gpo_ref.buffer[...] = (dot_lt(zeta, d_agg) * proc_scale).astype(BF)
    gpo_ref.send()
    d_zeta = dot_rt(d_agg, wpo_ref.get()[...]).astype(BF)
    mg_ref.buffer[...] = cot.astype(F32) + dot_rt(d_node, wns_ref.get()[...])
    back[...] = jnp.zeros_like(back)
    gacc[...] = jnp.zeros_like(gacc)
    table[pl.ds(first, rows), :] = d_zeta

    def behind(i, carry):
        at = pl.multiple_of(i * step, step)
        chosen = hot[pl.ds(at, step), :]
        d_edge = dot(chosen[:, first:], table[pl.ds(first, 256), :])
        d_proc = (d_edge * sg[pl.ds(at, step), :].astype(F32)).astype(BF)
        back[...] += dot_lt(chosen, d_proc)
        gacc[...] += dot_lt(mel_ref.get()[pl.ds(at, step), :], d_proc)
        return carry

    lax.fori_loop(0, steps, behind, 0)
    gpe_ref.buffer[...] = (gacc[...] * proc_scale).astype(BF)
    gpe_ref.send()
    sb_ref.buffer[...] = back[pl.ds(0, rows), :].astype(BF)
    so_ref.buffer[...] = back[pl.ds(rows, rows), :].astype(BF)
    sa_ref.buffer[...] = back[pl.ds(2 * rows, rows), :].astype(BF)
    sa_ref.send()
    sb_ref.send()
    so_ref.send()
    dst_sum = back[pl.ds(first, rows), :].astype(BF)
    mg_ref.buffer[...] += dot_rt(dst_sum, wdst_ref.get()[...])
    gpd_ref.buffer[...] = (dot_lt(h0, dst_sum) * proc_scale).astype(BF)


def split_halves(core, held, layout, kept_ref, sent_ref):
    first, groups, half = layout
    width = kept_ref.shape[1]
    even = core == 0
    step = 16

    def piece(row):
        ref = held[row // width] if row < 10 * width else None
        return jnp.zeros((step, width), BF) if ref is None else ref[pl.ds(row % width, step), :]

    for group in range(groups):
        for part in range(0, half, step):
            row = (first + group) * 2 * half + part
            at = pl.ds(group * half + part, step)
            left, right = piece(row), piece(row + half)
            kept_ref[at, :] = jnp.where(even, left, right)
            sent_ref[at, :] = jnp.where(even, right, left)


def mesh_backward(
    scales, layout, core_ref, so_ref, sb_ref, sa_ref, wsrc_ref, mg_ref, wout_ref, pick_ref, h0_ref,
    a0_ref, gpe_ref, gpd_ref, gpo_ref, gns_ref, gna_ref, gno_ref,
    out_ref, ret_ref, kept_ref, sent_ref, padded, geo, gps,
):
    proc_scale, enc_scale = scales
    rows = h0_ref.buffer.shape[0]
    total = sum(ref.get()[...].astype(F32) for ref in (so_ref, sb_ref, sa_ref)).astype(BF)
    grad = mg_ref.get()[...] + dot_rt(total, wsrc_ref.get()[...])
    out_ref.buffer[...] = grad
    out_ref.send()
    d_mesh = grad.astype(BF)
    padded[pl.ds(rows, 256 - rows), :] = jnp.zeros((256 - rows, padded.shape[1]), BF)
    padded[pl.ds(0, rows), :] = dot_rt(d_mesh, wout_ref.get()[...]).astype(BF)
    step = 256
    for at in range(0, ret_ref.buffer.shape[0], step):
        ret_ref.buffer[pl.ds(at, step), :] = dot(pick_ref.get()[pl.ds(at, step), :], padded[...]).astype(BF)
    ret_ref.send()
    gps[...] = (dot_lt(h0_ref.get()[...], total) * proc_scale).astype(BF)
    geo[...] = (dot_lt(a0_ref.get()[...], d_mesh) * enc_scale).astype(BF)
    held = [None, None, geo, gpe_ref.get(), gps, gpd_ref.get()] + [
        ref.get() for ref in (gpo_ref, gns_ref, gna_ref, gno_ref)
    ]
    split_halves(core_ref[0], held, layout, kept_ref.buffer, sent_ref.buffer)


def enc_backward(
    enc_scale, layout, core_ref, slot_ref, src_ref, ret_ref, sg_ref, edge_ref, grid_ref, wg_ref,
    out_ref, kept_ref, sent_ref, gee, geg,
):
    chosen = same(columns(slot_ref.get()[...]), ret_ref.buffer.shape[0])
    d_enc = (dot(chosen, ret_ref.get()[...]) * sg_ref.get()[...].astype(F32)).astype(BF)
    gee[...] = (dot_lt(edge_ref.get()[...], d_enc) * enc_scale).astype(BF)
    grid_sum = dot(same_t(src_ref.get()[...], grid_ref.buffer.shape[0]), d_enc).astype(BF)
    geg[...] = (dot_lt(grid_ref.get()[...], grid_sum) * enc_scale).astype(BF)
    out_ref.buffer[...] = dot_rt(grid_sum, wg_ref.get()[...])
    out_ref.send()
    split_halves(core_ref[0], [gee, geg] + [None] * 8, layout, kept_ref.buffer, sent_ref.buffer)


def add_halves(chunk, turn_ref, kept_ref, came_ref, out_ref):
    narrow, length, width = out_ref.buffer.shape
    blocks = turn_ref.buffer.shape[0]
    step = blocks // narrow
    skip = length - kept_ref.buffer.shape[0] // narrow
    if skip:
        for y in range(narrow):
            out_ref.buffer[y, pl.ds(0, skip), :] = jnp.zeros((skip, width), BF)
    for at in range(0, kept_ref.buffer.shape[0], blocks):
        total = kept_ref.get()[pl.ds(at, blocks), :].astype(F32) + came_ref.get()[pl.ds(at, blocks), :].astype(F32)
        total = total.astype(BF)
        if step > chunk:
            total = dot(turn_ref.get()[...], total).astype(BF)
        for y in range(narrow):
            out_ref.buffer[y, pl.ds(skip + at // narrow, step), :] = total[y * step : (y + 1) * step]


def turned(narrow, chunk, groups):
    rows = np.arange(groups * narrow * chunk).reshape(groups, narrow, chunk)
    rows = rows.transpose(1, 0, 2).reshape(-1)
    return jnp.asarray(rows[:, None] == np.arange(rows.size)[None, :], BF)


class Inward:
    def __init__(self, source, buffer, sem):
        self.copy = pltpu.make_async_copy(source, buffer, sem)
        self.copy.start()
        self.buffer = buffer
        self.waited = False

    def get(self):
        if not self.waited:
            self.copy.wait()
            self.waited = True
        return self.buffer


class Outward:
    def __init__(self, buffer, target, sem):
        self.copy = pltpu.make_async_copy(buffer, target, sem)
        self.buffer = buffer
        self.started = False

    def send(self):
        self.copy.start()
        self.started = True

    def finish(self):
        if not self.started:
            self.send()
        self.copy.wait()


def call(body, ins, outs, scratch=(), limit=16, scalar=None):
    count, made, extra = len(ins), len(outs), int(scalar is not None)

    def kernel(*refs):
        lead, refs = refs[:extra], refs[extra:]
        source, target, refs = refs[:count], refs[count : count + made], refs[count + made :]
        here, there, refs = refs[:count], refs[count : count + made], refs[count + made :]
        in_sem, out_sem = refs[:2]
        got = [Inward(source[i], here[i], in_sem.at[i]) for i in range(count)]
        put = [Outward(there[i], target[i], out_sem.at[i]) for i in range(made)]
        body(*lead, *got, *put, *refs[2:])
        for one in got:
            one.get()
        for one in put:
            one.finish()

    hbm = pl.BlockSpec(memory_space=pl.ANY)
    return pl.pallas_call(
        kernel,
        in_specs=[pl.BlockSpec(memory_space=pltpu.SMEM)] * extra + [hbm] * count,
        out_specs=[hbm] * made,
        out_shape=[jax.ShapeDtypeStruct(shape, kind) for shape, kind in outs],
        scratch_shapes=[pltpu.VMEM(one.shape, one.dtype) for one in ins]
        + [pltpu.VMEM(shape, kind) for shape, kind in outs]
        + [pltpu.SemaphoreType.DMA((count,)), pltpu.SemaphoreType.DMA((made,))]
        + [pltpu.VMEM(shape, kind) for shape, kind in scratch],
        compiler_params=pltpu.CompilerParams(vmem_limit_bytes=limit << 20),
    )(*([scalar] * extra), *ins)


def on_device(
    grid_latent,
    enc_edge_latent,
    enc_source,
    enc_target_device,
    enc_target_row,
    mesh_static,
    mesh_edge_latent,
    mesh_source,
    mesh_target,
    w_enc_edge,
    w_enc_grid,
    w_enc_out,
    w_proc_edge,
    w_proc_src,
    w_proc_dst,
    w_proc_out,
    w_node_self,
    w_node_agg,
    w_node_out,
    cotangent,
):
    wide = lax.axis_size("wide")
    narrow = lax.axis_size("narrow")
    devices = wide * narrow
    edges, width = enc_edge_latent.shape
    grid_rows = grid_latent.shape[0]
    rows = mesh_static.shape[0]
    mesh_edges = mesh_source.shape[0]
    capacity = 2 * edges // devices
    slots = devices * capacity
    enc_scale = float(edges * devices) ** (-0.5)
    proc_scale = float(mesh_edges * devices) ** (-0.5)
    node_scale = float(rows * devices) ** (-0.5)
    core = lax.axis_index("wide") % 2

    source = enc_source.reshape(1, edges)
    payload, enc_sg, slot = call(
        functools.partial(enc_forward, capacity),
        [
            enc_target_device.reshape(1, edges),
            enc_target_row.reshape(1, edges),
            source,
            grid_latent,
            enc_edge_latent,
            w_enc_edge,
            w_enc_grid,
        ],
        [((slots, width + LANE), BF), ((edges, width), BF), ((1, edges), I32)],
    )
    received = lax.all_to_all(
        payload.reshape(devices, capacity, width + LANE),
        ("wide", "narrow"),
        split_axis=0,
        concat_axis=0,
        tiled=True,
    ).reshape(slots, width + LANE)
    h0, a0, p_src, p_dst, pick = call(
        mesh_forward,
        [received, w_enc_out, mesh_static, w_proc_src, w_proc_dst],
        [((rows, width), BF)] * 4 + [((slots, 256), BF)],
    )
    up = [(i, (i + 1) % wide) for i in range(wide)]
    down = [(j, i) for i, j in up]
    p_before = lax.ppermute(p_src, "wide", up)
    p_after = lax.ppermute(p_src, "wide", down)
    square = ((width, width), BF)
    block = ((rows, width), BF)
    reach = -(-3 * rows // LANE) * LANE + 256
    mesh_out, s_before, s_own, s_after, partial_grad, gpe, gpd, gpo, gns, gna, gno = call(
        functools.partial(processor, (proc_scale, node_scale)),
        [
            mesh_source.reshape(-1, 256),
            mesh_target.reshape(-1, 256),
            p_before,
            p_src,
            p_after,
            p_dst,
            w_proc_edge,
            mesh_edge_latent,
            w_proc_out,
            h0,
            w_node_self,
            w_node_agg,
            w_node_out,
            cotangent,
            w_proc_dst,
        ],
        [block] * 4 + [((rows, width), F32)] + [square] * 6,
        [
            ((reach, width), BF),
            ((mesh_edges, reach), BF),
            ((mesh_edges, width), BF),
            ((256, width), F32),
            ((reach, width), F32),
            ((width, width), F32),
        ],
        limit=32,
    )
    from_after = lax.ppermute(s_before, "wide", down)
    from_before = lax.ppermute(s_after, "wide", up)
    chips = wide // 2
    chunk = 10 * width // devices
    half = narrow * chunk
    late = 2 * width
    block = 4 if chunk % 16 else 1
    span = 2 * half * block
    late_layout = (0, -(-late // span) * block, half)
    early_layout = (late // span * block, chips - late // span * block, half)
    turn = turned(narrow, chunk, block)
    late_block = ((late_layout[1] * half, width), BF)
    early_block = ((early_layout[1] * half, width), BF)
    where = core.reshape(1)
    swap = [(i, i ^ 1) for i in range(wide)]
    mesh_grad, returning, kept, sent = call(
        functools.partial(mesh_backward, (proc_scale, enc_scale), early_layout),
        [s_own, from_after, from_before, w_proc_src, partial_grad, w_enc_out, pick, h0, a0]
        + [gpe, gpd, gpo, gns, gna, gno],
        [((rows, width), F32), ((slots, width), BF), early_block, early_block],
        [((256, width), BF), square, square],
        limit=24,
        scalar=where,
    )
    came = lax.ppermute(sent, "wide", swap)
    far = 4 if chips > 4 else 2
    near = chips // far
    line = [[i + j * 2 * near for j in range(far)] for i in range(2 * near)]
    plane = [[i * 2 * near + 2 * j + c for j in range(near)] for i in range(far) for c in range(2)]
    turning = functools.partial(add_halves, chunk)
    (early,) = call(turning, [turn, kept, came], [((narrow, chips * chunk, width), BF)])
    early = lax.psum_scatter(early, "narrow", scatter_dimension=0, tiled=True)
    early = lax.psum_scatter(
        early.reshape(far, near * chunk, width),
        "wide",
        scatter_dimension=0,
        tiled=True,
        axis_index_groups=line,
    ).reshape(near * chunk, width)
    returned = lax.all_to_all(
        returning.reshape(devices, capacity, width),
        ("wide", "narrow"),
        split_axis=0,
        concat_axis=0,
        tiled=True,
    ).reshape(slots, width)
    grid_grad, kept, sent = call(
        functools.partial(enc_backward, enc_scale, late_layout),
        [slot, source, returned, enc_sg, enc_edge_latent, grid_latent, w_enc_grid],
        [((grid_rows, width), F32), late_block, late_block],
        [square, square],
        limit=24,
        scalar=where,
    )
    came = lax.ppermute(sent, "wide", swap)
    spread = late_layout[1] * chunk
    (last,) = call(turning, [turn, kept, came], [((narrow, spread, width), BF)])
    last = lax.all_to_all(last, "narrow", split_axis=0, concat_axis=0, tiled=True)
    last = jnp.sum(last.astype(F32), axis=0).astype(BF)
    parts = [
        lax.ppermute(last, "wide", [(j * 2 * near + i, i) for i in range(2 * near)])
        for j in range(1, far)
    ]
    at_first = lax.axis_index("wide") < 2 * near
    last = jnp.where(at_first, last.astype(F32), 0.0) + sum(p.astype(F32) for p in parts)
    both = early.astype(F32) + last[: near * chunk]
    both = lax.all_to_all(
        both.astype(BF).reshape(near, chunk, width),
        "wide",
        split_axis=0,
        concat_axis=0,
        tiled=True,
        axis_index_groups=plane,
    )
    summed = jnp.sum(both.astype(F32), axis=0).reshape(-1)
    return (mesh_out, grid_grad, summed, mesh_grad)


def solution(mesh):
    in_specs = (
        P(("wide", "narrow"), None),
        P(("wide", "narrow"), None),
        P(("wide", "narrow")),
        P(("wide", "narrow"), None),
        P(("wide", "narrow")),
        P(("wide", "narrow"), None),
        P(("wide", "narrow"), None),
        P(("wide", "narrow")),
        P(("wide", "narrow")),
        P(),
        P(),
        P(),
        P(),
        P(),
        P(),
        P(),
        P(),
        P(),
        P(),
        P(("wide", "narrow"), None),
    )
    out_specs = (
        P(("wide", "narrow"), None),
        P(("wide", "narrow"), None),
        P(("wide", "narrow")),
        P(("wide", "narrow"), None),
    )
    return jax.shard_map(
        on_device, mesh=mesh, in_specs=in_specs, out_specs=out_specs, check_vma=False
    )
```

time: 230 us -> 244 us (1.061)
  Pallas kernels: 22.2 us -> 36.6 us
    pallas_call x7, Pallas kernels: 22.2 us -> 36.6 us  [call(): pl.pallas_call(kernel, in_specs=[pl.BlockSpec(memory_space=pltpu.SMEM)] *...]
  transfers between devices with their start and end apart: 11 -> 11, of which waited for: 7 -> 7; matrix products, arithmetic and copies ran while one was open for 1% -> 1% of each run, Pallas kernels for 2% -> 3%
where the time goes in v2:
time: 244 us; the launch traced here: 242 us
  blocking collectives  117 us (48%)
  local copies, waits for them, and re-layouts  39.4 us (16%)
  Pallas kernels  36.6 us (15%)
  waiting for transfers between devices  28.6 us (12%)
  between operations  14.3 us (6%)
  starting transfers between devices  5.16 us (2%)
    all_to_all x1, blocking collectives, on_device(): lax.all_to_all(payload.reshape(devices, capacity, width + LANE), ('wide',...  52 us
    all_to_all x1, blocking collectives, on_device(): lax.all_to_all(returning.reshape(devices, capacity, width), ('wide', 'nar...  38.8 us
    pallas_call x7, Pallas kernels, call(): pl.pallas_call(kernel, in_specs=[pl.BlockSpec(memory_space=pltpu.SMEM)] *...  36.6 us
    unnamed x92, local copies, waits for them, and re-layouts  33.3 us
    all_to_all x1, blocking collectives, on_device(): lax.all_to_all(last, 'narrow', split_axis=0, concat_axis=0, tiled=True)  13.8 us
    all_to_all x1, blocking collectives, on_device(): lax.all_to_all(both.astype(BF).reshape(near, chunk, width), 'wide', split...  12.4 us
    ppermute x3, waiting for transfers between devices, on_device(): lax.ppermute(last, 'wide', [(j * 2 * near + i, i) for i in range(2 * near)])  8.11 us
    ppermute x2, waiting for transfers between devices, on_device(): came = lax.ppermute(sent, 'wide', swap)  6.67 us
  transfers between devices with their start and end apart: 11, of which 7 were waited for; matrix products, arithmetic and copies ran while one was open for 1% of the time, Pallas kernels for 3%

profile of v2, /device:TPU:8, one launch (start us, length us, event | category | flops | bytes accessed | tf_op | source)
XLA Modules:
  0.0 242.2 jit_solution(9694496359285461586)
XLA Ops:
  7.2 1.0 copy-done.2
  8.3 1.0 copy-done.4
  9.3 1.0 copy-done.6
  10.3 1.0 copy-done.11
  13.4 3.2 %shard_map.228 = (bf16[1024,640]{1,0:T(8,128)(2,1)S(1)}, bf16[512,512]{1,0:T(8,128)(2,1)S(1)}, s32[1,512]{1,0:T(1,128)S(1)}) custom-call(s32[1,512]{1,0:T(1,128)S(1)} %bitcast.10, s32[1,512]{1,0:T(1,128)S(1)} %bitcast.11, s32[1,512]{1,0:T(1,128)S(1)} %bitcast.8, bf16[512,512]{1,0:T(8,128)(2,1)S(1)} %copy-done.2, bf16[512,512]{1,0:T(8,128)(2,1)S(1)} %copy-done.4, ...), custom_call_target="tpu_custom_call" | custom-call | tf_op jit(solution)/shard_map/pallas_call | solution.py:340
  16.7 0.8 copy-done.26
  17.8 52.0 %all_to_all.20 = bf16[256,4,640]{2,1,0:T(4,128)(2,1)} all-to-all(bf16[256,4,640]{2,1,0:T(4,128)(2,1)S(1)} %reshape.55), channel_id=1, replica_groups=mesh['wide'=64,'narrow'=4] {'wide','narrow'}, dimensions={0} | all-to-all | bytes 2621440 | tf_op jit(solution)/shard_map/all_to_all | solution.py:403
  69.8 2.6 %reshape.56.refs_0_ = bf16[1024,640]{1,0:T(8,128)(2,1)S(1)} reshape(bf16[256,4,640]{2,1,0:T(4,128)(2,1)} %all_to_all.20) | data formatting | bytes 2621440 | tf_op jit(solution)/shard_map/reshape | solution.py:409
  72.5 2.7 %shard_map.229 = (bf16[160,512]{1,0:T(8,128)(2,1)S(1)}, bf16[160,512]{1,0:T(8,128)(2,1)S(1)}, bf16[160,512]{1,0:T(8,128)(2,1)S(1)}, bf16[160,512]{1,0:T(8,128)(2,1)S(1)}, bf16[1024,256]{1,0:T(8,128)(2,1)S(1)}) custom-call(bf16[1024,640]{1,0:T(8,128)(2,1)S(1)} %reshape.56.refs_0_, bf16[512,512]{1,0:T(8,128)(2,1)S(1)} %copy-done, ...), custom_call_target="tpu_custom_call" | custom-call | tf_op jit(solution)/shard_map/pallas_call | solution.py:340
  78.6 1.0 collective-permute-done.1.refs_4_
  79.6 5.2 %collective-permute-done.refs_2_ = bf16[160,512]{1,0:T(8,128)(2,1)S(1)} collective-permute-done((bf16[160,512]{1,0:T(8,128)(2,1)S(1)}, bf16[160,512]{1,0:T(8,128)(2,1)S(1)}, u32[]{:S(2)}, u32[]{:S(2)}) %collective-permute-start) | collective-permute-done | bytes 163872 | tf_op jit(solution)/shard_map/ppermute | solution.py:417
  84.8 1.3 copy-done.9
  86.1 1.0 copy-done.28
  87.2 1.0 copy-done.29
  88.2 1.0 copy-done.30
  89.2 1.0 copy-done.31
  90.3 1.0 copy-done.32
  91.3 0.9 copy-done.36
  92.2 0.9 copy-done.38
  93.2 0.9 copy-done.40
  94.1 14.9 %shard_map.230 = (bf16[160,512]{1,0:T(8,128)(2,1)}, bf16[160,512]{1,0:T(8,128)(2,1)S(1)}, bf16[160,512]{1,0:T(8,128)(2,1)S(1)}, bf16[160,512]{1,0:T(8,128)(2,1)S...) custom-call(s32[5,256]{1,0:T(8,128)S(1)} %reshape.50.refs_0_, ...), custom_call_target="tpu_custom_call" | custom-call | tf_op jit(solution)/shard_map/pallas_call | solution.py:340
  110.5 0.8 copy-done.18
  114.2 2.3 collective-permute-done.2.refs_2_
  116.6 5.2 %collective-permute-done.3.refs_3_ = bf16[160,512]{1,0:T(8,128)(2,1)S(1)} collective-permute-done((bf16[160,512]{1,0:T(8,128)(2,1)S(1)}, bf16[160,512]{1,0:T(8,128)(2,1)S(1)}, u32[]{:S(2)}, u32[]{:S(2)}) %collective-permute-start.3) | collective-permute-done | bytes 163872 | tf_op jit(solution)/shard_map/ppermute | solution.py:453
  122.5 1.0 copy-done.13
  123.5 1.0 copy-done.15
  124.5 1.0 copy-done.17
  125.6 1.0 copy-done.19
  126.6 1.0 copy-done.21
  127.7 1.0 copy-done.23
  128.7 1.0 copy-done.25
  129.8 0.9 copy-done.35
  130.7 4.8 %shard_map.231 = (f32[160,512]{1,0:T(8,128)}, bf16[1024,512]{1,0:T(8,128)(2,1)S(1)}, bf16[2240,512]{1,0:T(8,128)(2,1)S(1)}, bf16[2240,512]{1,0:T(8,128)(2,1)S(1)}) custom-call(s32[1]{0:T(128)} %bitcast.3.refs_0_, bf16[160,512]{1,0:T(8,128)(2,1)S(1)} %get-tuple-element.36.refs_1_, bf16[160,512]{1,0:T(8,128)(2,1)S(1)} %collective-permute-done.2.refs_2_, ...), custom_call_target="tpu_custom_call" | custom-call | tf_op jit(solution)/shard_map/pallas_call | solution.py:340
  135.6 4.4 %collective-permute-done.4.refs_2_ = bf16[2240,512]{1,0:T(8,128)(2,1)S(1)} collective-permute-done((bf16[2240,512]{1,0:T(8,128)(2,1)S(1)}, bf16[2240,512]{1,0:T(8,128)(2,1)S(1)}, u32[]{:S(2)}, u32[]{:S(2)}) %collective-permute-start.4) | collective-permute-done | bytes 2293792 | tf_op jit(solution)/shard_map/ppermute | solution.py:476
  140.0 4.1 %shard_map.233 = bf16[4,640,512]{2,1,0:T(8,128)(2,1)} custom-call(bf16[320,320]{1,0:T(8,128)(2,1)S(1)} %copy-done.10, bf16[2240,512]{1,0:T(8,128)(2,1)S(1)} %get-tuple-element.51.refs_1_, bf16[2240,512]{1,0:T(8,128)(2,1)S(1)} %collective-permute-done.4.refs_2_), custom_call_target="tpu_custom_call" | custom-call | tf_op jit(solution)/shard_map/pallas_call | solution.py:340
  144.5 38.8 %all_to_all.21 = bf16[256,4,512]{2,1,0:T(4,128)(2,1)} all-to-all(bf16[256,4,512]{2,1,0:T(4,128)(2,1)S(1)} %reshape.58), channel_id=1, replica_groups=mesh['wide'=64,'narrow'=4] {'wide','narrow'}, dimensions={0} | all-to-all | bytes 2097152 | tf_op jit(solution)/shard_map/all_to_all | solution.py:491
  183.3 1.5 reshape.59.refs_3_
  185.0 1.0 copy-done.27
  186.0 5.3 %shard_map.232 = (f32[512,512]{1,0:T(8,128)}, bf16[640,512]{1,0:T(8,128)(2,1)S(1)}, bf16[640,512]{1,0:T(8,128)(2,1)}) custom-call(s32[1]{0:T(128)} %bitcast.3.refs_0_, s32[1,512]{1,0:T(1,128)S(1)} %get-tuple-element.35.refs_1_, s32[1,512]{1,0:T(1,128)S(1)} %bitcast.9, bf16[1024,512]{1,0:T(8,128)(2,1)S(1)} %reshape.59.refs_3_, ...), custom_call_target="tpu_custom_call" | custom-call | tf_op jit(solution)/shard_map/pallas_call | solution.py:340
  191.4 2.2 collective-permute-done.5.refs_2_
  193.7 1.6 shard_map.234
  195.3 13.8 %all_to_all.22 = bf16[4,160,512]{2,1,0:T(8,128)(2,1)S(1)} all-to-all(bf16[4,160,512]{2,1,0:T(8,128)(2,1)S(1)} %shard_map.234), channel_id=1, replica_groups=mesh['wide'=64,'narrow'=4] {'narrow'}, dimensions={0} | all-to-all | bytes 1310720 | tf_op jit(solution)/shard_map/all_to_all | solution.py:509
  209.2 1.3 collective-permute-start.8
  210.5 1.3 collective-permute-start.7
  211.8 1.3 collective-permute-start.6
  213.1 8.1 %collective-permute-done.8 = bf16[160,512]{1,0:T(8,128)(2,1)S(1)} collective-permute-done((bf16[160,512]{1,0:T(8,128)(2,1)S(1)}, bf16[160,512]{1,0:T(8,128)(2,1)S(1)}, u32[]{:S(2)}, u32[]{:S(2)}) %collective-permute-start.8) | collective-permute-done | bytes 163872 | tf_op jit(solution)/shard_map/ppermute | solution.py:512
  221.2 1.0 fusion
  222.3 12.4 %all_to_all.23 = bf16[8,20,512]{2,1,0:T(8,128)(2,1)S(1)} all-to-all(bf16[8,20,512]{2,1,0:T(8,128)(2,1)S(1)} %reshape.61), channel_id=1, replica_groups={{0,8,16,24,32,40,48,56},{4,12,20,28,36,44,52,60},{64,72,80,88,96,104,11..., dimensions={0} | all-to-all | bytes 327680 | tf_op jit(solution)/shard_map/all_to_all | solution.py:518
  (90 shorter events, 12.5 us)
Async XLA Ops:
  7.2 184.2 %reduce-scatter.3.cloned.1.call-start = ((), (), s32[]{:S(2)}) async-start(), calls=%async_computation.6 | async-start | bytes 3276800 | tf_op jit(solution)/shard_map/reduce_scatter | solution.py:483
  7.2 1.0 copy-start.2
  8.3 1.0 copy-start.4
  9.3 1.0 copy-start.6
  10.3 1.0 copy-start.11
  16.7 0.8 copy-start.26
  69.8 2.6 %copy-start = (bf16[512,512]{1,0:T(8,128)(2,1)S(1)}, bf16[512,512]{1,0:T(8,128)(2,1)}, u32[]{:S(2)}) copy-start(bf16[512,512]{1,0:T(8,128)(2,1)} %refs_6_.6) | copy-start | bytes 1572868
  69.8 2.7 %copy-start.1 = (bf16[512,512]{1,0:T(8,128)(2,1)S(1)}, bf16[512,512]{1,0:T(8,128)(2,1)}, u32[]{:S(2)}) copy-start(bf16[512,512]{1,0:T(8,128)(2,1)} %refs_4_.5) | copy-start | bytes 1572868
  69.8 2.7 %copy-start.8 = (bf16[512,512]{1,0:T(8,128)(2,1)S(1)}, bf16[512,512]{1,0:T(8,128)(2,1)}, u32[]{:S(2)}) copy-start(bf16[512,512]{1,0:T(8,128)(2,1)} %refs_14_.1) | copy-start | bytes 1572868
  69.8 2.7 %copy-start.33 = (bf16[160,512]{1,0:T(8,128)(2,1)S(1)}, bf16[160,512]{1,0:T(8,128)(2,1)}, u32[]{:S(2)}) copy-start(bf16[160,512]{1,0:T(8,128)(2,1)} %refs_2_.1) | copy-start | bytes 491524
  72.5 5.4 %copy-start.45 = (s32[1280]{0:T(1024)S(1)}, s32[1280]{0:T(1024)}, u32[]{:S(2)}) copy-start(s32[1280]{0:T(1024)} %param.28) | copy-start | bytes 15364
  75.3 0.8 copy-start.12
  76.7 2.8 %collective-permute-start.1 = (bf16[160,512]{1,0:T(8,128)(2,1)S(1)}, bf16[160,512]{1,0:T(8,128)(2,1)S(1)}, u32[]{:S(2)}, u32[]{:S(2)}) collective-permute-start(bf16[160,512]{1,0:T(8,128)(2,1)S(1)} %get-tuple-element.31.refs_3_), channel_id=1, source_target_pairs={{4,0},{8,4},{12,8},{16,12},{20,16},{24,20},{28,24},{32,28},{36,32}... | collective-permute-start | bytes 491528 | tf_op jit(solution)/shard_map/ppermute | solution.py:418
  76.7 8.1 %collective-permute-start = (bf16[160,512]{1,0:T(8,128)(2,1)S(1)}, bf16[160,512]{1,0:T(8,128)(2,1)S(1)}, u32[]{:S(2)}, u32[]{:S(2)}) collective-permute-start(bf16[160,512]{1,0:T(8,128)(2,1)S(1)} %get-tuple-element.31.refs_3_), channel_id=1, source_target_pairs={{0,4},{4,8},{8,12},{12,16},{16,20},{20,24},{24,28},{28,32},{32,36}... | collective-permute-start | bytes 491528 | tf_op jit(solution)/shard_map/ppermute | solution.py:417
  84.8 1.3 copy-start.9
  86.1 1.0 copy-start.28
  87.2 1.0 copy-start.29
  88.2 1.0 copy-start.30
  89.2 1.0 copy-start.31
  90.3 1.0 copy-start.32
  91.3 0.9 copy-start.36
  92.2 0.9 copy-start.38
  93.2 0.9 copy-start.40
  108.9 0.8 copy-start.14
  110.5 0.8 copy-start.18
  112.1 0.8 copy-start.22
  113.7 2.8 %collective-permute-start.2 = (bf16[160,512]{1,0:T(8,128)(2,1)S(1)}, bf16[160,512]{1,0:T(8,128)(2,1)S(1)}, u32[]{:S(2)}, u32[]{:S(2)}) collective-permute-start(bf16[160,512]{1,0:T(8,128)(2,1)S(1)} %get-tuple-element.37), channel_id=1, source_target_pairs={{4,0},{8,4},{12,8},{16,12},{20,16},{24,20},{28,24},{32,28},{36,32}... | collective-permute-start | bytes 491528 | tf_op jit(solution)/shard_map/ppermute | solution.py:452
  113.7 8.1 %collective-permute-start.3 = (bf16[160,512]{1,0:T(8,128)(2,1)S(1)}, bf16[160,512]{1,0:T(8,128)(2,1)S(1)}, u32[]{:S(2)}, u32[]{:S(2)}) collective-permute-start(bf16[160,512]{1,0:T(8,128)(2,1)S(1)} %get-tuple-element.38), channel_id=1, source_target_pairs={{0,4},{4,8},{8,12},{12,16},{16,20},{20,24},{24,28},{28,32},{32,36}... | collective-permute-start | bytes 491528 | tf_op jit(solution)/shard_map/ppermute | solution.py:453
  122.5 1.0 copy-start.13
  123.5 1.0 copy-start.15
  124.5 1.0 copy-start.17
  125.6 1.0 copy-start.19
  126.6 1.0 copy-start.21
  127.7 1.0 copy-start.23
  128.7 1.0 copy-start.25
  129.8 0.9 copy-start.35
  130.7 9.4 %copy-start.10 = (bf16[320,320]{1,0:T(8,128)(2,1)S(1)}, bf16[320,320]{1,0:T(8,128)(2,1)}, u32[]{:S(2)}) copy-start(bf16[320,320]{1,0:T(8,128)(2,1)} %constant.27.clone.refs_0_) | copy-start | bytes 614404
  135.5 4.5 %collective-permute-start.4 = (bf16[2240,512]{1,0:T(8,128)(2,1)S(1)}, bf16[2240,512]{1,0:T(8,128)(2,1)S(1)}, u32[]{:S(2)}, u32[]{:S(2)}) collective-permute-start(bf16[2240,512]{1,0:T(8,128)(2,1)S(1)} %get-tuple-element.52), channel_id=1, source_target_pairs={{0,4},{4,0},{8,12},{12,8},{16,20},{20,16},{24,28},{28,24},{32,36},... | collective-permute-start | bytes 6881288 | tf_op jit(solution)/shard_map/ppermute | solution.py:476
  144.2 77.0 %reduce-scatter.5.cloned.1.call-start = ((), (), s32[]{:S(2)}) async-start(), calls=%async_computation.7 | async-start | bytes 819200 | tf_op jit(solution)/shard_map/reduce_scatter | solution.py:484
  183.3 1.5 copy-start.3
  183.3 1.5 copy-start.5
  183.3 1.7 copy-start.7
  183.3 1.7 copy-start.42
  185.0 1.0 copy-start.27
  191.3 2.4 collective-permute-start.5
  209.2 12.0 %collective-permute-start.8 = (bf16[160,512]{1,0:T(8,128)(2,1)S(1)}, bf16[160,512]{1,0:T(8,128)(2,1)S(1)}, u32[]{:S(2)}, u32[]{:S(2)}) collective-permute-start(bf16[160,512]{1,0:T(8,128)(2,1)S(1)} %reduce_sum.21), channel_id=1, source_target_pairs={{192,0},{196,4},{200,8},{204,12},{208,16},{212,20},{216,24},{220,2... | collective-permute-start | bytes 491528 | tf_op jit(solution)/shard_map/ppermute | solution.py:512
  210.5 10.7 %collective-permute-start.7 = (bf16[160,512]{1,0:T(8,128)(2,1)S(1)}, bf16[160,512]{1,0:T(8,128)(2,1)S(1)}, u32[]{:S(2)}, u32[]{:S(2)}) collective-permute-start(bf16[160,512]{1,0:T(8,128)(2,1)S(1)} %reduce_sum.21), channel_id=1, source_target_pairs={{128,0},{132,4},{136,8},{140,12},{144,16},{148,20},{152,24},{156,2... | collective-permute-start | bytes 491528 | tf_op jit(solution)/shard_map/ppermute | solution.py:512
  211.8 9.4 %collective-permute-start.6 = (bf16[160,512]{1,0:T(8,128)(2,1)S(1)}, bf16[160,512]{1,0:T(8,128)(2,1)S(1)}, u32[]{:S(2)}, u32[]{:S(2)}) collective-permute-start(bf16[160,512]{1,0:T(8,128)(2,1)S(1)} %reduce_sum.21), channel_id=1, source_target_pairs={{64,0},{68,4},{72,8},{76,12},{80,16},{84,20},{88,24},{92,28},{96,3... | collective-permute-start | bytes 491528 | tf_op jit(solution)/shard_map/ppermute | solution.py:512
  (9 other events, 6.4 us)
Sparse Core Ops, SparseCore 0:
  144.3 39.0 reduce-scatter.2
  191.6 19.8 reduce-scatter.4

commit v3 on v2

--- a/solution.py
+++ b/solution.py
@@ -320,7 +320,7 @@
         self.copy.wait()
 
 
-def call(body, ins, outs, scratch=(), limit=16, scalar=None):
+def call(body, ins, outs, scratch=(), scalar=None):
     count, made, extra = len(ins), len(outs), int(scalar is not None)
 
     def kernel(*refs):
@@ -346,7 +346,7 @@
         + [pltpu.VMEM(shape, kind) for shape, kind in outs]
         + [pltpu.SemaphoreType.DMA((count,)), pltpu.SemaphoreType.DMA((made,))]
         + [pltpu.VMEM(shape, kind) for shape, kind in scratch],
-        compiler_params=pltpu.CompilerParams(vmem_limit_bytes=limit << 20),
+        compiler_params=pltpu.CompilerParams(vmem_limit_bytes=60 << 20),
     )(*([scalar] * extra), *ins)
 
 
@@ -447,7 +447,6 @@
             ((reach, width), F32),
             ((width, width), F32),
         ],
-        limit=32,
     )
     from_after = lax.ppermute(s_before, "wide", down)
     from_before = lax.ppermute(s_after, "wide", up)
@@ -470,7 +469,6 @@
         + [gpe, gpd, gpo, gns, gna, gno],
         [((rows, width), F32), ((slots, width), BF), early_block, early_block],
         [((256, width), BF), square, square],
-        limit=24,
         scalar=where,
     )
     came = lax.ppermute(sent, "wide", swap)
@@ -500,7 +498,6 @@
         [slot, source, returned, enc_sg, enc_edge_latent, grid_latent, w_enc_grid],
         [((grid_rows, width), F32), late_block, late_block],
         [square, square],
-        limit=24,
         scalar=where,
     )
     came = lax.ppermute(sent, "wide", swap)

time: 244 us -> 226 us (0.926)
  local copies, waits for them, and re-layouts: 39.4 us -> 11.9 us
  Pallas kernels: 36.6 us -> 46.4 us
    unnamed x92 -> x18, local copies, waits for them, and re-layouts: 33.3 us -> 4.83 us
    pallas_call x7, Pallas kernels: 36.6 us -> 46.4 us  [call(): pl.pallas_call(kernel, in_specs=[pl.BlockSpec(memory_space=pltpu.SMEM)] *...]
  transfers between devices with their start and end apart: 11 -> 11, of which waited for: 7 -> 7; matrix products, arithmetic and copies ran while one was open for 1% -> 1% of each run, Pallas kernels for 3% -> 4%
where the time goes in v3:
time: 226 us
  blocking collectives  117 us (52%)
  Pallas kernels  46.4 us (21%)
  waiting for transfers between devices  29.8 us (13%)
  between operations  14.2 us (6%)
  local copies, waits for them, and re-layouts  11.9 us (5%)
  starting transfers between devices  5.3 us (2%)
    all_to_all x1, blocking collectives, on_device(): lax.all_to_all(payload.reshape(devices, capacity, width + LANE), ('wide',...  51.9 us
    pallas_call x7, Pallas kernels, call(): pl.pallas_call(kernel, in_specs=[pl.BlockSpec(memory_space=pltpu.SMEM)] *...  46.4 us
    all_to_all x1, blocking collectives, on_device(): lax.all_to_all(returning.reshape(devices, capacity, width), ('wide', 'nar...  38.1 us
    all_to_all x1, blocking collectives, on_device(): lax.all_to_all(last, 'narrow', split_axis=0, concat_axis=0, tiled=True)  14.8 us
    all_to_all x1, blocking collectives, on_device(): lax.all_to_all(both.astype(BF).reshape(near, chunk, width), 'wide', split...  12.2 us
    ppermute x3, waiting for transfers between devices, on_device(): lax.ppermute(last, 'wide', [(j * 2 * near + i, i) for i in range(2 * near)])  8.12 us
    ppermute x2, waiting for transfers between devices, on_device(): came = lax.ppermute(sent, 'wide', swap)  6.88 us
    ppermute x1, waiting for transfers between devices, on_device(): from_before = lax.ppermute(s_after, 'wide', up)  5.38 us
  transfers between devices with their start and end apart: 11, of which 7 were waited for; matrix products, arithmetic and copies ran while one was open for 1% of the time, Pallas kernels for 4%

profile of v3, /device:TPU:8, one launch (start us, length us, event | category | flops | bytes accessed | tf_op | source)
XLA Modules:
  0.0 225.7 jit_solution(8777079268493745282)
XLA Ops:
  7.2 0.0 reduce-scatter.3.cloned.1.call-start
  7.2 4.7 %shard_map.228 = (bf16[1024,640]{1,0:T(8,128)(2,1)}, bf16[512,512]{1,0:T(8,128)(2,1)}, s32[1,512]{1,0:T(1,128)}) custom-call(s32[1,512]{1,0:T(1,128)} %bitcast.11, s32[1,512]{1,0:T(1,128)} %bitcast.12, s32[1,512]{1,0:T(1,128)} %bitcast.9, bf16[512,512]{1,0:T(8,128)(2,1)} %refs_6_.7, bf16[512,512]{1,0:T(8,128)(2,1)} %refs_5_.3, bf16[512,512]{1,0:T(8,128)(2,1)} %refs_5_.2, ...), custom_call_target="tpu_custom_call" | custom-call | tf_op jit(solution)/shard_map/pallas_call | solution.py:340
  11.9 2.6 %reshape.55 = bf16[256,4,640]{2,1,0:T(4,128)(2,1)S(1)} reshape(bf16[1024,640]{1,0:T(8,128)(2,1)} %get-tuple-element.30) | data formatting | bytes 2621440 | tf_op jit(solution)/shard_map/reshape | solution.py:404
  14.5 51.9 %all_to_all.20 = bf16[256,4,640]{2,1,0:T(4,128)(2,1)S(1)} all-to-all(bf16[256,4,640]{2,1,0:T(4,128)(2,1)S(1)} %reshape.55), channel_id=1, replica_groups=mesh['wide'=64,'narrow'=4] {'wide','narrow'}, dimensions={0} | all-to-all | bytes 2621440 | tf_op jit(solution)/shard_map/all_to_all | solution.py:403
  66.4 1.2 reshape.56.refs_0_
  67.6 5.1 %shard_map.229 = (bf16[160,512]{1,0:T(8,128)(2,1)}, bf16[160,512]{1,0:T(8,128)(2,1)}, bf16[160,512]{1,0:T(8,128)(2,1)}, bf16[160,512]{1,0:T(8,128)(2,1)}, bf16[1024,256]{1,0:T(8,128)(2,1)}) custom-call(bf16[1024,640]{1,0:T(8,128)(2,1)} %reshape.56.refs_0_, bf16[512,512]{1,0:T(8,128)(2,1)} %refs_6_.6, bf16[160,512]{1,0:T(8,128)(2,1)} %refs_2_.1, ...), custom_call_target="tpu_custom_call" | custom-call | tf_op jit(solution)/shard_map/pallas_call | solution.py:340
  72.7 0.1 collective-permute-start.1
  72.8 0.5 collective-permute-start
  73.3 0.6 reshape.50.refs_0_
  73.9 0.6 reshape.51.refs_1_
  74.5 1.5 collective-permute-done.1.refs_4_
  76.0 5.2 %collective-permute-done.refs_2_ = bf16[160,512]{1,0:T(8,128)(2,1)S(1)} collective-permute-done((bf16[160,512]{1,0:T(8,128)(2,1)}, bf16[160,512]{1,0:T(8,128)(2,1)S(1)}, u32[]{:S(2)}, u32[]{:S(2)}) %collective-permute-start) | collective-permute-done | bytes 163872 | tf_op jit(solution)/shard_map/ppermute | solution.py:417
  81.2 0.7 copy-done.6
  81.9 15.0 %shard_map.230 = (bf16[160,512]{1,0:T(8,128)(2,1)}, bf16[160,512]{1,0:T(8,128)(2,1)}, bf16[160,512]{1,0:T(8,128)(2,1)}, bf16[160,512]{1,0:T(8,128)(2,1)}, f32[16...) custom-call(s32[5,256]{1,0:T(8,128)} %reshape.50.refs_0_, ...), custom_call_target="tpu_custom_call" | custom-call | tf_op jit(solution)/shard_map/pallas_call | solution.py:340
  96.9 0.1 collective-permute-start.2
  97.0 0.5 collective-permute-start.3
  97.4 2.6 %collective-permute-done.2.refs_2_ = bf16[160,512]{1,0:T(8,128)(2,1)S(1)} collective-permute-done((bf16[160,512]{1,0:T(8,128)(2,1)}, bf16[160,512]{1,0:T(8,128)(2,1)S(1)}, u32[]{:S(2)}, u32[]{:S(2)}) %collective-permute-start.2) | collective-permute-done | bytes 163872 | tf_op jit(solution)/shard_map/ppermute | solution.py:451
  100.1 5.4 %collective-permute-done.3.refs_3_ = bf16[160,512]{1,0:T(8,128)(2,1)S(1)} collective-permute-done((bf16[160,512]{1,0:T(8,128)(2,1)}, bf16[160,512]{1,0:T(8,128)(2,1)S(1)}, u32[]{:S(2)}, u32[]{:S(2)}) %collective-permute-start.3) | collective-permute-done | bytes 163872 | tf_op jit(solution)/shard_map/ppermute | solution.py:452
  105.5 0.7 copy-done.4
  106.1 6.5 %shard_map.231 = (f32[160,512]{1,0:T(8,128)}, bf16[1024,512]{1,0:T(8,128)(2,1)}, bf16[2240,512]{1,0:T(8,128)(2,1)}, bf16[2240,512]{1,0:T(8,128)(2,1)}) custom-call(s32[1]{0:T(128)} %bitcast.3.refs_0_, bf16[160,512]{1,0:T(8,128)(2,1)} %get-tuple-element.36.refs_1_, bf16[160,512]{1,0:T(8,128)(2,1)} %copy-done.3, bf16[160,512]{1,0:T(8,128)(2,1)} %copy-done.4, ...), custom_call_target="tpu_custom_call" | custom-call | tf_op jit(solution)/shard_map/pallas_call | solution.py:340
  112.7 0.1 collective-permute-start.4
  112.8 4.6 %collective-permute-done.4.refs_2_ = bf16[2240,512]{1,0:T(8,128)(2,1)S(1)} collective-permute-done((bf16[2240,512]{1,0:T(8,128)(2,1)}, bf16[2240,512]{1,0:T(8,128)(2,1)S(1)}, u32[]{:S(2)}, u32[]{:S(2)}) %collective-permute-start.4) | collective-permute-done | bytes 2293792 | tf_op jit(solution)/shard_map/ppermute | solution.py:474
  117.4 1.5 copy-done
  118.9 5.4 %shard_map.233 = bf16[4,640,512]{2,1,0:T(8,128)(2,1)} custom-call(bf16[320,320]{1,0:T(8,128)(2,1)} %constant.27.clone.refs_0_, bf16[2240,512]{1,0:T(8,128)(2,1)} %get-tuple-element.51.refs_1_, bf16[2240,512]{1,0:T(8,128)(2,1)} %copy-done), custom_call_target="tpu_custom_call" | custom-call | tf_op jit(solution)/shard_map/pallas_call | solution.py:340
  124.3 0.0 copy-start.1
  124.3 0.0 reduce-scatter.3.cloned.1.call-update
  124.4 0.0 reduce-scatter.5.cloned.1.call-start
  124.4 1.1 copy-done.1
  125.5 0.3 reshape.58
  125.8 38.1 %all_to_all.21 = bf16[256,4,512]{2,1,0:T(4,128)(2,1)S(1)} all-to-all(bf16[256,4,512]{2,1,0:T(4,128)(2,1)S(1)} %reshape.58), channel_id=1, replica_groups=mesh['wide'=64,'narrow'=4] {'wide','narrow'}, dimensions={0} | all-to-all | bytes 2097152 | tf_op jit(solution)/shard_map/all_to_all | solution.py:489
  163.9 1.1 reshape.59.refs_3_
  165.1 6.8 %shard_map.232 = (f32[512,512]{1,0:T(8,128)}, bf16[640,512]{1,0:T(8,128)(2,1)}, bf16[640,512]{1,0:T(8,128)(2,1)}) custom-call(s32[1]{0:T(128)} %bitcast.3.refs_0_, s32[1,512]{1,0:T(1,128)} %get-tuple-element.35.refs_1_, s32[1,512]{1,0:T(1,128)} %bitcast.10, bf16[1024,512]{1,0:T(8,128)(2,1)} %reshape.59.refs_3_, bf16[512,512]{1,0:T(8,128)(2,1)} %get-tuple-element.49.refs_4_, ...), custom_call_target="tpu_custom_call" | custom-call | tf_op jit(solution)/shard_map/pallas_call | solution.py:340
  171.8 0.1 collective-permute-start.5
  171.9 0.0 reduce-scatter.3.cloned.1.call-done
  171.9 0.0 reduce-scatter.5.cloned.1.call-update
  172.0 2.2 collective-permute-done.5.refs_2_
  174.2 0.9 copy-done.2
  175.1 2.9 %shard_map.234 = bf16[4,160,512]{2,1,0:T(8,128)(2,1)} custom-call(bf16[320,320]{1,0:T(8,128)(2,1)} %constant.27.clone.refs_0_, bf16[640,512]{1,0:T(8,128)(2,1)} %get-tuple-element.53.refs_1_, bf16[640,512]{1,0:T(8,128)(2,1)} %copy-done.2), custom_call_target="tpu_custom_call" | custom-call | tf_op jit(solution)/shard_map/pallas_call | solution.py:340
  178.0 14.8 %all_to_all.22 = bf16[4,160,512]{2,1,0:T(8,128)(2,1)S(1)} all-to-all(bf16[4,160,512]{2,1,0:T(8,128)(2,1)} %shard_map.234), channel_id=1, replica_groups=mesh['wide'=64,'narrow'=4] {'narrow'}, dimensions={0} | all-to-all | bytes 1310720 | tf_op jit(solution)/shard_map/all_to_all | solution.py:506
  192.8 0.1 reduce_sum.21
  192.9 1.3 collective-permute-start.8
  194.2 1.3 collective-permute-start.7
  195.5 1.3 collective-permute-start.6
  196.8 8.1 %collective-permute-done.8 = bf16[160,512]{1,0:T(8,128)(2,1)S(1)} collective-permute-done((bf16[160,512]{1,0:T(8,128)(2,1)S(1)}, bf16[160,512]{1,0:T(8,128)(2,1)S(1)}, u32[]{:S(2)}, u32[]{:S(2)}) %collective-permute-start.8) | collective-permute-done | bytes 163872 | tf_op jit(solution)/shard_map/ppermute | solution.py:509
  204.9 0.0 reduce-scatter.5.cloned.1.call-done
  205.0 1.0 fusion
  206.0 12.2 %all_to_all.23 = bf16[8,20,512]{2,1,0:T(8,128)(2,1)S(1)} all-to-all(bf16[8,20,512]{2,1,0:T(8,128)(2,1)S(1)} %reshape.61), channel_id=1, replica_groups={{0,8,16,24,32,40,48,56},{4,12,20,28,36,44,52,60},{64,72,80,88,96,104,11..., dimensions={0} | all-to-all | bytes 327680 | tf_op jit(solution)/shard_map/all_to_all | solution.py:515
  218.3 0.6 reshape.62
  (16 shorter events, 0.1 us)
Async XLA Ops:
  7.2 164.8 %reduce-scatter.3.cloned.1.call-start = ((), (), s32[]{:S(2)}) async-start(), calls=%async_computation.6 | async-start | bytes 3276800 | tf_op jit(solution)/shard_map/reduce_scatter | solution.py:481
  67.6 5.7 %copy-start.7 = (s32[1280]{0:T(1024)S(1)}, s32[1280]{0:T(1024)}, u32[]{:S(2)}) copy-start(s32[1280]{0:T(1024)} %param.28) | copy-start | bytes 15364
  67.6 6.3 %copy-start.8 = (s32[1280]{0:T(1024)S(1)}, s32[1280]{0:T(1024)}, u32[]{:S(2)}) copy-start(s32[1280]{0:T(1024)} %param.29) | copy-start | bytes 15364
  72.7 3.2 %collective-permute-start.1 = (bf16[160,512]{1,0:T(8,128)(2,1)}, bf16[160,512]{1,0:T(8,128)(2,1)S(1)}, u32[]{:S(2)}, u32[]{:S(2)}) collective-permute-start(bf16[160,512]{1,0:T(8,128)(2,1)} %get-tuple-element.31.refs_3_), channel_id=1, source_target_pairs={{4,0},{8,4},{12,8},{16,12},{20,16},{24,20},{28,24},{32,28},{36,32}... | collective-permute-start | bytes 491528 | tf_op jit(solution)/shard_map/ppermute | solution.py:418
  72.8 8.4 %collective-permute-start = (bf16[160,512]{1,0:T(8,128)(2,1)}, bf16[160,512]{1,0:T(8,128)(2,1)S(1)}, u32[]{:S(2)}, u32[]{:S(2)}) collective-permute-start(bf16[160,512]{1,0:T(8,128)(2,1)} %get-tuple-element.31.refs_3_), channel_id=1, source_target_pairs={{0,4},{4,8},{8,12},{12,16},{16,20},{20,24},{24,28},{28,32},{32,36}... | collective-permute-start | bytes 491528 | tf_op jit(solution)/shard_map/ppermute | solution.py:417
  76.0 5.2 %copy-start.5 = (bf16[160,512]{1,0:T(8,128)(2,1)}, bf16[160,512]{1,0:T(8,128)(2,1)S(1)}, u32[]{:S(2)}) copy-start(bf16[160,512]{1,0:T(8,128)(2,1)S(1)} %collective-permute-done.1.refs_4_) | copy-start | bytes 491524
  81.2 0.7 copy-start.6
  96.9 3.2 %collective-permute-start.2 = (bf16[160,512]{1,0:T(8,128)(2,1)}, bf16[160,512]{1,0:T(8,128)(2,1)S(1)}, u32[]{:S(2)}, u32[]{:S(2)}) collective-permute-start(bf16[160,512]{1,0:T(8,128)(2,1)} %get-tuple-element.37), channel_id=1, source_target_pairs={{4,0},{8,4},{12,8},{16,12},{20,16},{24,20},{28,24},{32,28},{36,32}... | collective-permute-start | bytes 491528 | tf_op jit(solution)/shard_map/ppermute | solution.py:451
  97.0 8.5 %collective-permute-start.3 = (bf16[160,512]{1,0:T(8,128)(2,1)}, bf16[160,512]{1,0:T(8,128)(2,1)S(1)}, u32[]{:S(2)}, u32[]{:S(2)}) collective-permute-start(bf16[160,512]{1,0:T(8,128)(2,1)} %get-tuple-element.38), channel_id=1, source_target_pairs={{0,4},{4,8},{8,12},{12,16},{16,20},{20,24},{24,28},{28,32},{32,36}... | collective-permute-start | bytes 491528 | tf_op jit(solution)/shard_map/ppermute | solution.py:452
  100.1 5.4 %copy-start.3 = (bf16[160,512]{1,0:T(8,128)(2,1)}, bf16[160,512]{1,0:T(8,128)(2,1)S(1)}, u32[]{:S(2)}) copy-start(bf16[160,512]{1,0:T(8,128)(2,1)S(1)} %collective-permute-done.2.refs_2_) | copy-start | bytes 491524
  105.5 0.7 copy-start.4
  112.7 4.7 %collective-permute-start.4 = (bf16[2240,512]{1,0:T(8,128)(2,1)}, bf16[2240,512]{1,0:T(8,128)(2,1)S(1)}, u32[]{:S(2)}, u32[]{:S(2)}) collective-permute-start(bf16[2240,512]{1,0:T(8,128)(2,1)} %get-tuple-element.52), channel_id=1, source_target_pairs={{0,4},{4,0},{8,12},{12,8},{16,20},{20,16},{24,28},{28,24},{32,36},... | collective-permute-start | bytes 6881288 | tf_op jit(solution)/shard_map/ppermute | solution.py:474
  117.4 1.5 copy-start
  124.3 1.2 copy-start.1
  124.4 80.6 %reduce-scatter.5.cloned.1.call-start = ((), (), s32[]{:S(2)}) async-start(), calls=%async_computation.7 | async-start | bytes 819200 | tf_op jit(solution)/shard_map/reduce_scatter | solution.py:482
  171.8 2.4 %collective-permute-start.5 = (bf16[640,512]{1,0:T(8,128)(2,1)}, bf16[640,512]{1,0:T(8,128)(2,1)S(1)}, u32[]{:S(2)}, u32[]{:S(2)}) collective-permute-start(bf16[640,512]{1,0:T(8,128)(2,1)} %get-tuple-element.54), channel_id=1, source_target_pairs={{0,4},{4,0},{8,12},{12,8},{16,20},{20,16},{24,28},{28,24},{32,36},... | collective-permute-start | bytes 1966088 | tf_op jit(solution)/shard_map/ppermute | solution.py:503
  174.2 0.9 copy-start.2
  192.9 12.0 %collective-permute-start.8 = (bf16[160,512]{1,0:T(8,128)(2,1)S(1)}, bf16[160,512]{1,0:T(8,128)(2,1)S(1)}, u32[]{:S(2)}, u32[]{:S(2)}) collective-permute-start(bf16[160,512]{1,0:T(8,128)(2,1)S(1)} %reduce_sum.21), channel_id=1, source_target_pairs={{192,0},{196,4},{200,8},{204,12},{208,16},{212,20},{216,24},{220,2... | collective-permute-start | bytes 491528 | tf_op jit(solution)/shard_map/ppermute | solution.py:509
  194.2 10.7 %collective-permute-start.7 = (bf16[160,512]{1,0:T(8,128)(2,1)S(1)}, bf16[160,512]{1,0:T(8,128)(2,1)S(1)}, u32[]{:S(2)}, u32[]{:S(2)}) collective-permute-start(bf16[160,512]{1,0:T(8,128)(2,1)S(1)} %reduce_sum.21), channel_id=1, source_target_pairs={{128,0},{132,4},{136,8},{140,12},{144,16},{148,20},{152,24},{156,2... | collective-permute-start | bytes 491528 | tf_op jit(solution)/shard_map/ppermute | solution.py:509
  195.5 9.4 %collective-permute-start.6 = (bf16[160,512]{1,0:T(8,128)(2,1)S(1)}, bf16[160,512]{1,0:T(8,128)(2,1)S(1)}, u32[]{:S(2)}, u32[]{:S(2)}) collective-permute-start(bf16[160,512]{1,0:T(8,128)(2,1)S(1)} %reduce_sum.21), channel_id=1, source_target_pairs={{64,0},{68,4},{72,8},{76,12},{80,16},{84,20},{88,24},{92,28},{96,3... | collective-permute-start | bytes 491528 | tf_op jit(solution)/shard_map/ppermute | solution.py:509
Sparse Core Ops, SparseCore 0:
  124.5 38.9 reduce-scatter.2
  172.1 19.3 reduce-scatter.4

commit v4 on v3

v4 whole, which is shorter than its diff:
```python
import functools

import jax
import jax.numpy as jnp
import numpy as np
from jax import lax
from jax.experimental import pallas as pl
from jax.experimental.pallas import tpu as pltpu
from jax.sharding import PartitionSpec as P

BF = jnp.bfloat16
F32 = jnp.float32
I32 = jnp.int32
LANE = 128


def dot(left, right):
    return jnp.dot(left, right, preferred_element_type=F32)


def dot_rt(left, right):
    return lax.dot_general(left, right, (((1,), (1,)), ((), ())), preferred_element_type=F32)


def dot_lt(left, right):
    return lax.dot_general(left, right, (((0,), (0,)), ((), ())), preferred_element_type=F32)


def silu_pair(value):
    sig = jax.nn.sigmoid(value)
    act = value * sig
    return act, sig + act * (1.0 - sig)


def columns(row):
    return jnp.broadcast_to(row.astype(F32), (LANE, row.shape[1])).T


def same(cols, width, shift=0):
    wide = jnp.concatenate([cols] * (-(-width // LANE)), axis=1)
    lane = lax.broadcasted_iota(I32, wide.shape, 1) + shift
    return jnp.where(wide == lane.astype(F32), 1.0, 0.0).astype(BF)


def same_t(row, height, shift=0):
    sub = lax.broadcasted_iota(I32, (height, row.shape[1]), 0) + shift
    return jnp.where(sub == row, 1.0, 0.0).astype(BF)


def enc_forward(
    capacity, tdev_ref, trow_ref, src_ref, grid_ref, edge_ref, we_ref, wg_ref, out_ref, sg_ref, slot_ref
):
    edges, width = edge_ref.buffer.shape
    slots = out_ref.buffer.shape[0]
    tdev = tdev_ref.get()[...]
    member = same_t(tdev, slots // capacity)
    before = lax.broadcasted_iota(I32, (edges, edges), 0) < lax.broadcasted_iota(
        I32, (edges, edges), 1
    )
    ahead = dot(member, jnp.where(before, 1.0, 0.0).astype(BF))
    rank = jnp.sum(member.astype(F32) * ahead, axis=0, keepdims=True)
    slot = tdev * capacity + rank.astype(I32)
    slot_ref.buffer[...] = slot
    slot_ref.send()
    tag = columns(trow_ref.get()[...] + 1).astype(BF)
    grid = grid_ref.get()[...]
    gathered = dot(same(columns(src_ref.get()[...]), grid.shape[0]), grid).astype(BF)
    pre = dot(edge_ref.get()[...], we_ref.get()[...]) + dot(gathered, wg_ref.get()[...])
    act, grad = silu_pair(pre)
    sg_ref.buffer[...] = grad.astype(BF)
    sg_ref.send()
    payload = jnp.concatenate([act.astype(BF), tag], axis=1)
    step = 256
    for at in range(0, slots, step):
        place = same_t(slot, step, at)
        out_ref.buffer[pl.ds(at, step), :] = dot(place, payload).astype(BF)


def mesh_forward(recv_ref, wout_ref, static_ref, wsrc_ref, h0_ref, a0_ref, psrc_ref):
    rows, width = static_ref.buffer.shape
    recv = recv_ref.get()
    pick = same(recv[:, width:].astype(F32), 256, 1)
    a0 = dot_lt(pick, recv[:, :width])[:rows].astype(BF)
    a0_ref.buffer[...] = a0
    a0_ref.send()
    h0 = (static_ref.get()[...].astype(F32) + dot(a0, wout_ref.get()[...])).astype(BF)
    h0_ref.buffer[...] = h0
    h0_ref.send()
    psrc_ref.buffer[...] = dot(h0, wsrc_ref.get()[...]).astype(BF)


def processor(
    proc_scale,
    msrc_ref,
    mtgt_ref,
    pb_ref,
    po_ref,
    pa_ref,
    h0_ref,
    wdst_ref,
    we_ref,
    mel_ref,
    wpo_ref,
    wns_ref,
    wna_ref,
    wno_ref,
    cot_ref,
    sb_ref,
    so_ref,
    sa_ref,
    dst_ref,
    unit_ref,
    dnode_ref,
    dagg_ref,
    agg_ref,
    zeta_ref,
    gpe_ref,
    table,
    hot,
    sg,
    zsum,
    back,
    gacc,
):
    edges, width = mel_ref.buffer.shape
    rows = h0_ref.buffer.shape[0]
    reach = table.shape[0]
    first = reach - 256
    step = 256
    steps = edges // step
    h0 = h0_ref.get()[...]
    table[pl.ds(3 * rows, reach - 3 * rows), :] = jnp.zeros((reach - 3 * rows, width), BF)
    table[pl.ds(first, rows), :] = dot(h0, wdst_ref.get()[...]).astype(BF)
    table[pl.ds(0, rows), :] = pb_ref.get()[...]
    table[pl.ds(rows, rows), :] = po_ref.get()[...]
    table[pl.ds(2 * rows, rows), :] = pa_ref.get()[...]
    zsum[...] = jnp.zeros_like(zsum)
    for ref in (msrc_ref, mtgt_ref, we_ref, mel_ref):
        ref.get()

    def ahead(i, carry):
        at = pl.multiple_of(i * step, step)
        src = columns(msrc_ref.buffer[pl.ds(i, 1), :])
        tgt = columns(mtgt_ref.buffer[pl.ds(i, 1), :] + first)
        src = jnp.concatenate([src] * (reach // LANE), axis=1)
        tgt = jnp.concatenate([tgt] * (reach // LANE), axis=1)
        lane = lax.broadcasted_iota(I32, (step, reach), 1).astype(F32)
        chosen = jnp.where((src == lane) | (tgt == lane), 1.0, 0.0).astype(BF)
        hot[pl.ds(at, step), :] = chosen
        pre = dot(mel_ref.buffer[pl.ds(at, step), :], we_ref.buffer[...])
        act, grad = silu_pair(pre + dot(chosen, table[...]))
        sg[pl.ds(at, step), :] = grad.astype(BF)
        zsum[...] += dot_lt(chosen[:, first:], act.astype(BF))
        return carry

    lax.fori_loop(0, steps, ahead, 0)
    zeta = zsum[pl.ds(0, rows), :].astype(BF)
    cot = cot_ref.get()[...]
    agg = dot(zeta, wpo_ref.get()[...]).astype(BF)
    pre_node = dot(h0, wns_ref.get()[...]) + dot(agg, wna_ref.get()[...])
    act, grad = silu_pair(pre_node)
    d_node = (dot_rt(cot, wno_ref.get()[...]) * grad).astype(BF)
    d_agg = dot_rt(d_node, wna_ref.get()[...]).astype(BF)
    table[pl.ds(first, rows), :] = dot_rt(d_agg, wpo_ref.get()[...]).astype(BF)
    for ref, value in (
        (unit_ref, act.astype(BF)),
        (dnode_ref, d_node),
        (dagg_ref, d_agg),
        (agg_ref, agg),
        (zeta_ref, zeta),
    ):
        ref.buffer[...] = value
        ref.send()
    back[...] = jnp.zeros_like(back)
    gacc[...] = jnp.zeros_like(gacc)

    def behind(i, carry):
        at = pl.multiple_of(i * step, step)
        chosen = hot[pl.ds(at, step), :]
        d_edge = dot(chosen[:, first:], table[pl.ds(first, 256), :])
        d_proc = (d_edge * sg[pl.ds(at, step), :].astype(F32)).astype(BF)
        back[...] += dot_lt(chosen, d_proc)
        gacc[...] += dot_lt(mel_ref.buffer[pl.ds(at, step), :], d_proc)
        return carry

    lax.fori_loop(0, steps, behind, 0)
    for ref, at in ((sa_ref, 2 * rows), (sb_ref, 0), (so_ref, rows), (dst_ref, first)):
        ref.buffer[...] = back[pl.ds(at, rows), :].astype(BF)
        ref.send()
    gpe_ref.buffer[...] = (gacc[...] * proc_scale).astype(BF)


def node_gradients(
    scales, h0_ref, unit_ref, wno_ref, cot_ref, dnode_ref, wns_ref, dagg_ref, agg_ref, zeta_ref,
    dst_ref, wdst_ref, turn_ref, out_ref, mg_ref, early_ref, gpd, gpo, gns, gna, gno,
):
    proc_scale, node_scale = scales
    h0 = h0_ref.get()[...]
    unit = unit_ref.get()[...]
    out_ref.buffer[...] = (h0.astype(F32) + dot(unit, wno_ref.get()[...])).astype(BF)
    out_ref.send()
    cot = cot_ref.get()[...]
    d_node = dnode_ref.get()[...]
    dst_sum = dst_ref.get()[...]
    mg_ref.buffer[...] = (
        cot.astype(F32) + dot_rt(d_node, wns_ref.get()[...]) + dot_rt(dst_sum, wdst_ref.get()[...])
    )
    mg_ref.send()
    gno[...] = (dot_lt(unit, cot) * node_scale).astype(BF)
    gns[...] = (dot_lt(h0, d_node) * node_scale).astype(BF)
    gna[...] = (dot_lt(agg_ref.get()[...], d_node) * node_scale).astype(BF)
    gpo[...] = (dot_lt(zeta_ref.get()[...], dagg_ref.get()[...]) * proc_scale).astype(BF)
    gpd[...] = (dot_lt(h0, dst_sum) * proc_scale).astype(BF)
    held = [None] * 5 + [gpd, gpo, gns, gna, gno]
    width = h0.shape[1]
    turn_rows(held, turn_ref.get()[...], 5 * width, 10 * width, early_ref.buffer)


def rows_of(held, start, count):
    width = next(ref for ref in held if ref is not None).shape[1]
    pieces = []
    while count:
        size = min(count, width - start % width)
        ref = held[start // width] if start < 10 * width else None
        pieces.append(
            jnp.zeros((size, width), BF) if ref is None else ref[pl.ds(start % width, size), :]
        )
        start, count = start + size, count - size
    return pieces[0] if len(pieces) == 1 else jnp.concatenate(pieces, axis=0)


def turn_rows(held, turn, start, stop, out):
    narrow = out.shape[0]
    block = turn.shape[0]
    slab = block // narrow
    for at in range(start, stop, block):
        value = dot(turn, rows_of(held, at, block)).astype(BF)
        for y in range(narrow):
            out[y, pl.ds((at - start) // narrow, slab), :] = value[y * slab : (y + 1) * slab]


def mesh_backward(
    scales, start, so_ref, sb_ref, sa_ref, wsrc_ref, mg_ref, wout_ref, tag_ref, h0_ref, a0_ref,
    gpe_ref, turn_ref, out_ref, ret_ref, early_ref, padded, geo, gps,
):
    proc_scale, enc_scale = scales
    rows, width = h0_ref.buffer.shape
    total = sum(ref.get()[...].astype(F32) for ref in (so_ref, sb_ref, sa_ref)).astype(BF)
    grad = mg_ref.get()[...] + dot_rt(total, wsrc_ref.get()[...])
    out_ref.buffer[...] = grad
    out_ref.send()
    d_mesh = grad.astype(BF)
    padded[pl.ds(rows, 256 - rows), :] = jnp.zeros((256 - rows, padded.shape[1]), BF)
    padded[pl.ds(0, rows), :] = dot_rt(d_mesh, wout_ref.get()[...]).astype(BF)
    tag = tag_ref.get()
    step = 256
    for at in range(0, ret_ref.buffer.shape[0], step):
        pick = same(tag[pl.ds(at, step), :].astype(F32), 256, 1)
        ret_ref.buffer[pl.ds(at, step), :] = dot(pick, padded[...]).astype(BF)
    ret_ref.send()
    gps[...] = (dot_lt(h0_ref.get()[...], total) * proc_scale).astype(BF)
    geo[...] = (dot_lt(a0_ref.get()[...], d_mesh) * enc_scale).astype(BF)
    held = [None, None, geo, gpe_ref.get(), gps] + [None] * 5
    turn_rows(held, turn_ref.get()[...], start, 5 * width, early_ref.buffer)


def enc_backward(
    enc_scale, half, core_ref, slot_ref, src_ref, ret_ref, sg_ref, edge_ref, grid_ref, turn_ref,
    wg_ref,
    out_ref, kept_ref, sent_ref, gee, geg,
):
    chosen = same(columns(slot_ref.get()[...]), ret_ref.buffer.shape[0])
    d_enc = (dot(chosen, ret_ref.get()[...]) * sg_ref.get()[...].astype(F32)).astype(BF)
    grid_sum = dot(same_t(src_ref.get()[...], grid_ref.buffer.shape[0]), d_enc).astype(BF)
    out_ref.buffer[...] = dot_rt(grid_sum, wg_ref.get()[...])
    out_ref.send()
    gee[...] = (dot_lt(edge_ref.get()[...], d_enc) * enc_scale).astype(BF)
    geg[...] = (dot_lt(grid_ref.get()[...], grid_sum) * enc_scale).astype(BF)
    held = [gee, geg] + [None] * 8
    even = core_ref[0] == 0
    turn = turn_ref.get()[...]
    narrow, length, _ = kept_ref.buffer.shape
    block = turn.shape[0]
    slab = block // narrow
    for at in range(0, length, slab):
        both = []
        for c in range(2):
            lead = range(2 * at * narrow, 2 * (at + slab) * narrow, 2 * half)
            rows = [rows_of(held, row + c * half, half) for row in lead]
            both.append(dot(turn, jnp.concatenate(rows, axis=0)).astype(BF))
        own, other = jnp.where(even, both[0], both[1]), jnp.where(even, both[1], both[0])
        for y in range(narrow):
            kept_ref.buffer[y, pl.ds(at, slab), :] = own[y * slab : (y + 1) * slab]
            sent_ref.buffer[y, pl.ds(at, slab), :] = other[y * slab : (y + 1) * slab]


def turned(narrow, chunk, groups):
    rows = np.arange(groups * narrow * chunk).reshape(groups, narrow, chunk)
    rows = rows.transpose(1, 0, 2).reshape(-1)
    return jnp.asarray(rows[:, None] == np.arange(rows.size)[None, :], BF)


class Inward:
    def __init__(self, source, buffer, sem):
        self.copy = pltpu.make_async_copy(source, buffer, sem)
        self.copy.start()
        self.buffer = buffer
        self.waited = False

    def get(self):
        if not self.waited:
            self.copy.wait()
            self.waited = True
        return self.buffer


class Outward:
    def __init__(self, buffer, target, sem):
        self.copy = pltpu.make_async_copy(buffer, target, sem)
        self.buffer = buffer
        self.started = False

    def send(self):
        self.copy.start()
        self.started = True

    def finish(self):
        if not self.started:
            self.send()
        self.copy.wait()


def call(body, ins, outs, scratch=(), scalar=None, cut=None, place=None, alias=None, flops=0):
    cut, place = cut or {}, place or {}
    extra, more = int(scalar is not None), int(alias is not None)
    count, made = len(ins), len(outs)
    held_in = [(one.shape[0], cut[i][1]) if i in cut else one.shape for i, one in enumerate(ins)]
    held_out = [
        (shape[0], place[i][1], shape[2]) if i in place else shape
        for i, (shape, _) in enumerate(outs)
    ]

    def kernel(*refs):
        lead, refs = refs[:extra], refs[extra:]
        source, refs = refs[:count], refs[count + more :]
        target, refs = refs[:made], refs[made:]
        here, there, refs = refs[:count], refs[count : count + made], refs[count + made :]
        in_sem, out_sem = refs[:2]
        got, put = [], []
        for i in range(count):
            part = source[i].at[:, pl.ds(*cut[i])] if i in cut else source[i]
            got.append(Inward(part, here[i], in_sem.at[i]))
        for i in range(made):
            part = target[i].at[:, pl.ds(*place[i]), :] if i in place else target[i]
            put.append(Outward(there[i], part, out_sem.at[i]))
        body(*lead, *got, *put, *refs[2:])
        for one in got:
            one.get()
        for one in put:
            one.finish()

    hbm = pl.BlockSpec(memory_space=pl.ANY)
    moved = sum(one.size * one.dtype.itemsize for one in ins)
    return pl.pallas_call(
        kernel,
        in_specs=[pl.BlockSpec(memory_space=pltpu.SMEM)] * extra + [hbm] * (count + more),
        out_specs=[hbm] * made,
        out_shape=[jax.ShapeDtypeStruct(shape, kind) for shape, kind in outs],
        scratch_shapes=[pltpu.VMEM(held_in[i], ins[i].dtype) for i in range(count)]
        + [pltpu.VMEM(held_out[i], outs[i][1]) for i in range(made)]
        + [pltpu.SemaphoreType.DMA((count,)), pltpu.SemaphoreType.DMA((made,))]
        + [pltpu.VMEM(shape, kind) for shape, kind in scratch],
        input_output_aliases={extra + count: next(iter(place))} if more else {},
        compiler_params=pltpu.CompilerParams(vmem_limit_bytes=60 << 20),
        cost_estimate=pl.CostEstimate(flops=flops, bytes_accessed=moved, transcendentals=0),
    )(*([scalar] * extra), *ins, *([alias] * more))


def on_device(
    grid_latent,
    enc_edge_latent,
    enc_source,
    enc_target_device,
    enc_target_row,
    mesh_static,
    mesh_edge_latent,
    mesh_source,
    mesh_target,
    w_enc_edge,
    w_enc_grid,
    w_enc_out,
    w_proc_edge,
    w_proc_src,
    w_proc_dst,
    w_proc_out,
    w_node_self,
    w_node_agg,
    w_node_out,
    cotangent,
):
    wide = lax.axis_size("wide")
    narrow = lax.axis_size("narrow")
    devices = wide * narrow
    edges, width = enc_edge_latent.shape
    grid_rows = grid_latent.shape[0]
    rows = mesh_static.shape[0]
    mesh_edges = mesh_source.shape[0]
    capacity = 2 * edges // devices
    slots = devices * capacity
    enc_scale = float(edges * devices) ** (-0.5)
    proc_scale = float(mesh_edges * devices) ** (-0.5)
    node_scale = float(rows * devices) ** (-0.5)
    core = lax.axis_index("wide") % 2

    source = enc_source.reshape(1, edges)
    payload, enc_sg, slot = call(
        functools.partial(enc_forward, capacity),
        [
            enc_target_device.reshape(1, edges),
            enc_target_row.reshape(1, edges),
            source,
            grid_latent,
            enc_edge_latent,
            w_enc_edge,
            w_enc_grid,
        ],
        [((slots, width + LANE), BF), ((edges, width), BF), ((1, edges), I32)],
    )
    received = lax.all_to_all(
        payload.reshape(devices, capacity, width + LANE),
        ("wide", "narrow"),
        split_axis=0,
        concat_axis=0,
        tiled=True,
    ).reshape(slots, width + LANE)
    h0, a0, p_src = call(
        mesh_forward,
        [received, w_enc_out, mesh_static, w_proc_src],
        [((rows, width), BF)] * 3,
    )
    up = [(i, (i + 1) % wide) for i in range(wide)]
    down = [(j, i) for i, j in up]
    p_before = lax.ppermute(p_src, "wide", up)
    p_after = lax.ppermute(p_src, "wide", down)
    square = ((width, width), BF)
    block = ((rows, width), BF)
    reach = -(-3 * rows // LANE) * LANE + 256
    s_before, s_own, s_after, dst_sum, unit, d_node, d_agg, agg, zeta, gpe = call(
        functools.partial(processor, proc_scale),
        [
            mesh_source.reshape(-1, 256),
            mesh_target.reshape(-1, 256),
            p_before,
            p_src,
            p_after,
            h0,
            w_proc_dst,
            w_proc_edge,
            mesh_edge_latent,
            w_proc_out,
            w_node_self,
            w_node_agg,
            w_node_out,
            cotangent,
        ],
        [block] * 9 + [square],
        [
            ((reach, width), BF),
            ((mesh_edges, reach), BF),
            ((mesh_edges, width), BF),
            ((256, width), F32),
            ((reach, width), F32),
            ((width, width), F32),
        ],
        flops=12 * mesh_edges * width * width,
    )
    from_after = lax.ppermute(s_before, "wide", down)
    from_before = lax.ppermute(s_after, "wide", up)

    chips = wide // 2
    chunk = 10 * width // devices
    half = narrow * chunk
    far = 4 if chips > 4 else 2
    near = chips // far
    small = chunk % 16 != 0
    turn = turned(narrow, chunk, 4 if small else 2)
    late_turn = turned(narrow, chunk, 4 if small else 1)
    late = 2 * width
    start = late // turn.shape[0] * turn.shape[0]
    length = (10 * width - start) // narrow
    split = (5 * width - start) // narrow
    early_shape = ((narrow, length, width), BF)
    mesh_out, partial_grad, early = call(
        functools.partial(node_gradients, (proc_scale, node_scale)),
        [h0, unit, w_node_out, cotangent, d_node, w_node_self, d_agg, agg, zeta]
        + [dst_sum, w_proc_dst, turn],
        [block, ((rows, width), F32), early_shape],
        [square] * 5,
        place={2: (split, length - split)},
        flops=24 * rows * width * width,
    )
    mesh_grad, returning, early = call(
        functools.partial(mesh_backward, (proc_scale, enc_scale), start),
        [s_own, from_after, from_before, w_proc_src, partial_grad, w_enc_out, received, h0, a0]
        + [gpe, turn],
        [((rows, width), F32), ((slots, width), BF), early_shape],
        [((256, width), BF), square, square],
        cut={6: (width, LANE)},
        place={2: (0, split)},
        alias=early,
        flops=12 * rows * width * width,
    )
    line = [[i + j * 2 * near for j in range(far)] for i in range(2 * near)]
    plane = [[i * 2 * near + j for j in range(2 * near)] for i in range(far)]
    early = lax.psum_scatter(early, "narrow", scatter_dimension=0, tiled=True)
    early = jnp.pad(early.reshape(length, width), ((start // narrow, 0), (0, 0)))
    early = lax.psum_scatter(
        early.reshape(far, near * 2 * chunk, width),
        "wide",
        scatter_dimension=0,
        tiled=True,
        axis_index_groups=line,
    )
    returned = lax.all_to_all(
        returning.reshape(devices, capacity, width),
        ("wide", "narrow"),
        split_axis=0,
        concat_axis=0,
        tiled=True,
    ).reshape(slots, width)
    spread = -(-late // (2 * late_turn.shape[0])) * late_turn.shape[0] // narrow
    late_shape = ((narrow, spread, width), BF)
    grid_grad, kept, sent = call(
        functools.partial(enc_backward, enc_scale, half),
        [slot, source, returned, enc_sg, enc_edge_latent, grid_latent, late_turn, w_enc_grid],
        [((grid_rows, width), F32), late_shape, late_shape],
        [square, square],
        scalar=core.reshape(1),
        flops=8 * edges * width * width,
    )
    came = lax.ppermute(sent, "wide", [(i, i ^ 1) for i in range(wide)])
    last = (kept.astype(F32) + came.astype(F32)).astype(BF)
    last = lax.all_to_all(last, "narrow", split_axis=0, concat_axis=0, tiled=True)
    last = jnp.sum(last.astype(F32), axis=0).astype(BF)
    parts = [
        lax.ppermute(last, "wide", [(j * 2 * near + i, i) for i in range(2 * near)])
        for j in range(1, far)
    ]
    at_first = lax.axis_index("wide") < 2 * near
    last = jnp.where(at_first, last.astype(F32), 0.0) + sum(p.astype(F32) for p in parts)
    last = last[: near * chunk].reshape(near, 1, chunk, width)
    own = (jnp.arange(2) == core)[None, :, None, None]
    both = early.reshape(near, 2, chunk, width).astype(F32) + jnp.where(own, last, 0.0)
    both = lax.all_to_all(
        both.astype(BF).reshape(2 * near, chunk, width),
        "wide",
        split_axis=0,
        concat_axis=0,
        tiled=True,
        axis_index_groups=plane,
    )
    summed = jnp.sum(both.astype(F32), axis=0).reshape(-1)
    return (mesh_out, grid_grad, summed, mesh_grad)


def solution(mesh):
    in_specs = (
        P(("wide", "narrow"), None),
        P(("wide", "narrow"), None),
        P(("wide", "narrow")),
        P(("wide", "narrow"), None),
        P(("wide", "narrow")),
        P(("wide", "narrow"), None),
        P(("wide", "narrow"), None),
        P(("wide", "narrow")),
        P(("wide", "narrow")),
        P(),
        P(),
        P(),
        P(),
        P(),
        P(),
        P(),
        P(),
        P(),
        P(),
        P(("wide", "narrow"), None),
    )
    out_specs = (
        P(("wide", "narrow"), None),
        P(("wide", "narrow"), None),
        P(("wide", "narrow")),
        P(("wide", "narrow"), None),
    )
    return jax.shard_map(
        on_device, mesh=mesh, in_specs=in_specs, out_specs=out_specs, check_vma=False
    )
```

time: 226 us -> 243 us (1.075); the launches traced: 226 us -> 239 us
  waiting for transfers between devices: 29.8 us -> 61.8 us
  blocking collectives: 117 us -> 86.7 us
  starting transfers between devices: 5.3 us -> 21.1 us
  Pallas kernels: 46.4 us -> 39.9 us
    reduce_scatter x1, waiting for transfers between devices: 0.02 us -> 46 us  [on_device(): early = lax.psum_scatter(early, 'narrow', scatter_dimension=0, tiled=True)]
    all_to_all x2 -> x1, blocking collectives: 50.3 us -> 20.6 us  [on_device(): lax.all_to_all(both.astype(BF).reshape(2 * near, chunk, width), 'wide', s...]
    all_to_all x0 -> x1, starting transfers between devices: none -> 6.87 us  [on_device(): lax.all_to_all(returning.reshape(devices, capacity, width), ('wide', 'nar...]
    pallas_call x7 -> x6, Pallas kernels: 46.4 us -> 39.9 us  [call(): pl.pallas_call(kernel, in_specs=[pl.BlockSpec(memory_space=pltpu.SMEM)] *...]
    ppermute x1, starting transfers between devices: 0.08 us -> 5.08 us  [on_device(): from_after = lax.ppermute(s_before, 'wide', down)]
    ppermute x1, starting transfers between devices: 0.08 us -> 5.05 us  [on_device(): p_after = lax.ppermute(p_src, 'wide', down)]
    ppermute x2 -> x1, waiting for transfers between devices: 6.88 us -> 2.3 us  [on_device(): came = lax.ppermute(sent, 'wide', [(i, i ^ 1) for i in range(wide)])]
    ppermute x1, waiting for transfers between devices: 5.38 us -> 1.82 us  [on_device(): from_before = lax.ppermute(s_after, 'wide', up)]
  transfers between devices with their start and end apart: 11 -> 11, of which waited for: 7 -> 7; matrix products, arithmetic and copies ran while one was open for 1% -> 3% of each run, Pallas kernels for 4% -> 5%
where the time goes in v4:
time: 243 us; the launch traced here: 239 us
  blocking collectives  86.7 us (36%)
  waiting for transfers between devices  61.8 us (25%)
  Pallas kernels  39.9 us (16%)
  starting transfers between devices  21.1 us (9%)
  between operations  14.3 us (6%)
  local copies, waits for them, and re-layouts  14 us (6%)
    all_to_all x1, blocking collectives, on_device(): lax.all_to_all(payload.reshape(devices, capacity, width + LANE), ('wide',...  51.9 us
    reduce_scatter x1, waiting for transfers between devices, on_device(): early = lax.psum_scatter(early, 'narrow', scatter_dimension=0, tiled=True)  46 us
    pallas_call x6, Pallas kernels, call(): pl.pallas_call(kernel, in_specs=[pl.BlockSpec(memory_space=pltpu.SMEM)] *...  39.9 us
    all_to_all x1, blocking collectives, on_device(): lax.all_to_all(both.astype(BF).reshape(2 * near, chunk, width), 'wide', s...  20.6 us
    all_to_all x1, blocking collectives, on_device(): lax.all_to_all(last, 'narrow', split_axis=0, concat_axis=0, tiled=True)  14.2 us
    ppermute x3, waiting for transfers between devices, on_device(): lax.ppermute(last, 'wide', [(j * 2 * near + i, i) for i in range(2 * near)])  9.58 us
    all_to_all x1, starting transfers between devices, on_device(): lax.all_to_all(returning.reshape(devices, capacity, width), ('wide', 'nar...  6.87 us
    ppermute x1, starting transfers between devices, on_device(): from_after = lax.ppermute(s_before, 'wide', down)  5.08 us
  transfers between devices with their start and end apart: 11, of which 7 were waited for; matrix products, arithmetic and copies ran while one was open for 3% of the time, Pallas kernels for 5%

profile of v4, /device:TPU:8, one launch (start us, length us, event | category | flops | bytes accessed | tf_op | source)
XLA Modules:
  0.0 239.4 jit_solution(17438476495685297584)
XLA Ops:
  7.2 0.0 reduce-scatter.3.cloned.1.call-start
  7.2 4.7 %shard_map.237 = (bf16[1024,640]{1,0:T(8,128)(2,1)}, bf16[512,512]{1,0:T(8,128)(2,1)}, s32[1,512]{1,0:T(1,128)}) custom-call(s32[1,512]{1,0:T(1,128)} %bitcast.14, s32[1,512]{1,0:T(1,128)} %bitcast.15, s32[1,512]{1,0:T(1,128)} %bitcast.16, bf16[512,512]{1,0:T(8,128)(2,1)} %refs_6_.5, bf16[512,512]{1,0:T(8,128)(2,1)} %refs_5_.7, bf16[512,512]{1,0:T(8,128)(2,1)} %refs_5_.4, ...), custom_call_target="tpu_custom_call" | custom-call | bytes 2103296 | tf_op jit(solution)/shard_map/pallas_call | solution.py:364
  11.9 2.6 %reshape.63 = bf16[256,4,640]{2,1,0:T(4,128)(2,1)S(1)} reshape(bf16[1024,640]{1,0:T(8,128)(2,1)} %get-tuple-element.29) | data formatting | bytes 2621440 | tf_op jit(solution)/shard_map/reshape | solution.py:430
  14.5 51.9 %all_to_all.20 = bf16[256,4,640]{2,1,0:T(4,128)(2,1)S(1)} all-to-all(bf16[256,4,640]{2,1,0:T(4,128)(2,1)S(1)} %reshape.63), channel_id=1, replica_groups=mesh['wide'=64,'narrow'=4] {'wide','narrow'}, dimensions={0} | all-to-all | bytes 2621440 | tf_op jit(solution)/shard_map/all_to_all | solution.py:429
  66.4 1.3 reshape.64.refs_0_.refs_6_
  67.6 3.5 %shard_map.238 = (bf16[160,512]{1,0:T(8,128)(2,1)}, bf16[160,512]{1,0:T(8,128)(2,1)}, bf16[160,512]{1,0:T(8,128)(2,1)}) custom-call(bf16[1024,640]{1,0:T(8,128)(2,1)} %reshape.64.refs_0_.refs_6_, bf16[512,512]{1,0:T(8,128)(2,1)} %refs_5_.6, bf16[160,512]{1,0:T(8,128)(2,1)} %refs_2_.2, bf16[512,512]{1,0:T(8,128)(2,1)} %refs_3_.7), custom_call_target="tpu_custom_call" | custom-call | bytes 2523136 | tf_op jit(solution)/shard_map/pallas_call | solution.py:364
  71.1 0.1 collective-permute-start
  71.2 5.1 %collective-permute-start.1 = (bf16[160,512]{1,0:T(8,128)(2,1)}, bf16[160,512]{1,0:T(8,128)(2,1)S(1)}, u32[]{:S(2)}, u32[]{:S(2)}) collective-permute-start(bf16[160,512]{1,0:T(8,128)(2,1)} %get-tuple-element.31.refs_3_), channel_id=1, source_target_pairs={{4,0},{8,4},{12,8},{16,12},{20,16},{24,20},{28,24},{32,28},{36,32}... | collective-permute-start | bytes 491528 | tf_op jit(solution)/shard_map/ppermute | solution.py:444
  76.3 0.6 reshape.65.refs_0_
  76.9 0.6 reshape.66.refs_1_
  77.5 2.0 collective-permute-done.refs_2_
  79.5 0.7 copy-done.5
  80.2 0.1 copy-done.6
  80.2 13.3 %shard_map.239 = (bf16[160,512]{1,0:T(8,128)(2,1)}, bf16[160,512]{1,0:T(8,128)(2,1)}, bf16[160,512]{1,0:T(8,128)(2,1)}, bf16[160,512]{1,0:T(8,128)(2,1)}, bf16[1...) custom-call(s32[5,256]{1,0:T(8,128)} %reshape.65.refs_0_, ...), custom_call_target="tpu_custom_call" | custom-call | flops 4026531840 | bytes 5285888 | tf_op jit(solution)/shard_map/pallas_call | solution.py:364
  93.5 5.1 %collective-permute-start.2 = (bf16[160,512]{1,0:T(8,128)(2,1)}, bf16[160,512]{1,0:T(8,128)(2,1)S(1)}, u32[]{:S(2)}, u32[]{:S(2)}) collective-permute-start(bf16[160,512]{1,0:T(8,128)(2,1)} %get-tuple-element.41), channel_id=1, source_target_pairs={{4,0},{8,4},{12,8},{16,12},{20,16},{24,20},{28,24},{32,28},{36,32}... | collective-permute-start | bytes 491528 | tf_op jit(solution)/shard_map/ppermute | solution.py:477
  98.6 6.4 %shard_map.240 = (bf16[160,512]{1,0:T(8,128)(2,1)}, f32[160,512]{1,0:T(8,128)}, bf16[4,1040,512]{2,1,0:T(8,128)(2,1)}) custom-call(bf16[160,512]{1,0:T(8,128)(2,1)} %get-tuple-element.30.refs_5_.refs_0_.refs_7_, bf16[160,512]{1,0:T(8,128)(2,1)} %get-tuple-element.32.refs_1_, bf16[512,512]{1,0:T(8,128)(2,1)} %refs_2_.3, bf16[160,512]{1,0:T(8,128)(2,1)} %refs_3_.6, ...), custom_call_target="tpu_custom_call" | custom-call | flops 1006632960 | bytes 3088384 | tf_op jit(solution)/shard_map/pallas_call | solution.py:364
  105.0 1.8 collective-permute-done.3.refs_2_
  106.9 0.6 copy-done.2
  107.5 5.5 %shard_map.241 = (f32[160,512]{1,0:T(8,128)}, bf16[1024,512]{1,0:T(8,128)(2,1)}, bf16[4,1040,512]{2,1,0:T(8,128)(2,1)}) custom-call(bf16[160,512]{1,0:T(8,128)(2,1)} %get-tuple-element.40.refs_0_, bf16[160,512]{1,0:T(8,128)(2,1)} %copy-done.1, bf16[160,512]{1,0:T(8,128)(2,1)} %copy-done.2, ...), custom_call_target="tpu_custom_call", output_to_operand_aliasing={{2}: (11, {})} | custom-call | flops 503316480 | bytes 4235264 | tf_op jit(solution)/shard_map/pallas_call | solution.py:364
  113.0 0.0 reduce-scatter.3.cloned.1.call-update
  113.0 1.2 copy-done
  114.2 1.1 reshape.68
  115.3 6.9 %all-to-all-start.1 = ((bf16[256,4,512]{2,1,0:T(4,128)(2,1)}), bf16[256,4,512]{2,1,0:T(4,128)(2,1)S(1)}, u32[]{:S(2)}, u32[]{:S(2)}) async-start(bf16[256,4,512]{2,1,0:T(4,128)(2,1)} %reshape.68), calls=%async_computation.1 | async-start | bytes 2097152 | tf_op jit(solution)/shard_map/all_to_all | solution.py:524
  122.2 0.0 reduce-scatter.5.cloned.1.call-start
  122.3 46.0 %reduce-scatter.3.cloned.1.call-done = bf16[1,1040,512]{2,1,0:T(8,128)(2,1)} async-done(((bf16[4,1040,512]{2,1,0:T(8,128)(2,1)}), bf16[1,1040,512]{2,1,0:T(8,128)(2,1)}) %reduce-scatter.3.cloned.1.call-update) | async-done | bytes 1064976 | tf_op jit(solution)/shard_map/reduce_scatter | solution.py:515
  168.3 2.4 %pad.4 = bf16[1280,512]{1,0:T(8,128)(2,1)} pad(bf16[1040,512]{1,0:T(8,128)(2,1)} %bitcast.13, bf16[]{:T(256)} %constant.26.clone.1), padding=240_0x0_0 | pad | bytes 2375682 | tf_op jit(solution)/shard_map/jit(_pad)/pad | solution.py:516
  170.7 0.0 reduce-scatter.5.cloned.1.call-update
  170.7 1.1 reshape.69.refs_3_
  171.8 6.5 %shard_map.242 = (f32[512,512]{1,0:T(8,128)}, bf16[4,160,512]{2,1,0:T(8,128)(2,1)}, bf16[4,160,512]{2,1,0:T(8,128)(2,1)}) custom-call(s32[1]{0:T(128)} %bitcast.3.refs_0_, s32[1,512]{1,0:T(1,128)} %get-tuple-element.39.refs_1_, s32[1,512]{1,0:T(1,128)} %bitcast.17, bf16[1024,512]{1,0:T(8,128)(2,1)} %reshape.69.refs_3_, ...), custom_call_target="tpu_custom_call" | custom-call | flops 1073741824 | bytes 3354624 | tf_op jit(solution)/shard_map/pallas_call | solution.py:364
  178.4 0.1 collective-permute-start.4
  178.5 2.3 collective-permute-done.4
  180.8 1.3 add_convert_fusion
  182.0 14.2 %all_to_all.21 = bf16[4,160,512]{2,1,0:T(8,128)(2,1)S(1)} all-to-all(bf16[4,160,512]{2,1,0:T(8,128)(2,1)S(1)} %add_convert_fusion), channel_id=1, replica_groups=mesh['wide'=64,'narrow'=4] {'narrow'}, dimensions={0} | all-to-all | bytes 1310720 | tf_op jit(solution)/shard_map/all_to_all | solution.py:543
  196.3 0.1 reduce_sum.21
  196.4 1.3 collective-permute-start.5
  197.7 1.3 collective-permute-start.6
  199.0 1.3 collective-permute-start.7
  200.3 0.1 broadcast_in_dim.34
  200.4 3.3 %collective-permute-done.5 = bf16[160,512]{1,0:T(8,128)(2,1)S(1)} collective-permute-done((bf16[160,512]{1,0:T(8,128)(2,1)S(1)}, bf16[160,512]{1,0:T(8,128)(2,1)S(1)}, u32[]{:S(2)}, u32[]{:S(2)}) %collective-permute-start.5) | collective-permute-done | bytes 163872 | tf_op jit(solution)/shard_map/ppermute | solution.py:546
  203.6 2.9 %collective-permute-done.6 = bf16[160,512]{1,0:T(8,128)(2,1)S(1)} collective-permute-done((bf16[160,512]{1,0:T(8,128)(2,1)S(1)}, bf16[160,512]{1,0:T(8,128)(2,1)S(1)}, u32[]{:S(2)}, u32[]{:S(2)}) %collective-permute-start.6) | collective-permute-done | bytes 163872 | tf_op jit(solution)/shard_map/ppermute | solution.py:546
  206.6 3.4 %collective-permute-done.7 = bf16[160,512]{1,0:T(8,128)(2,1)S(1)} collective-permute-done((bf16[160,512]{1,0:T(8,128)(2,1)S(1)}, bf16[160,512]{1,0:T(8,128)(2,1)S(1)}, u32[]{:S(2)}, u32[]{:S(2)}) %collective-permute-start.7) | collective-permute-done | bytes 163872 | tf_op jit(solution)/shard_map/ppermute | solution.py:546
  210.0 0.1 add_add_fusion
  210.1 0.0 reduce-scatter.5.cloned.1.call-done
  210.1 1.0 reshape.73
  211.2 0.1 fusion.1
  211.3 20.6 %all_to_all.22 = bf16[16,20,512]{2,1,0:T(8,128)(2,1)S(1)} all-to-all(bf16[16,20,512]{2,1,0:T(8,128)(2,1)S(1)} %fusion.1), channel_id=1, replica_groups={{0,4,8,12,16,20,24,28,32,36,40,44,48,52,56,60},{64,68,72,76,80,84,88,92..., dimensions={0} | all-to-all | bytes 655360 | tf_op jit(solution)/shard_map/all_to_all | solution.py:554
  231.9 0.1 convert_reduce_fusion
  231.9 0.6 reshape.72
  (17 shorter events, 0.1 us)
Async XLA Ops:
  7.2 161.1 %reduce-scatter.3.cloned.1.call-start = ((), (), s32[]{:S(2)}) async-start(), calls=%async_computation.6 | async-start | bytes 5324800 | tf_op jit(solution)/shard_map/reduce_scatter | solution.py:515
  67.6 8.7 %copy-start.3 = (s32[1280]{0:T(1024)S(1)}, s32[1280]{0:T(1024)}, u32[]{:S(2)}) copy-start(s32[1280]{0:T(1024)} %param.29) | copy-start | bytes 15364
  67.6 9.3 %copy-start.4 = (s32[1280]{0:T(1024)S(1)}, s32[1280]{0:T(1024)}, u32[]{:S(2)}) copy-start(s32[1280]{0:T(1024)} %param.30) | copy-start | bytes 15364
  71.1 8.4 %collective-permute-start = (bf16[160,512]{1,0:T(8,128)(2,1)}, bf16[160,512]{1,0:T(8,128)(2,1)S(1)}, u32[]{:S(2)}, u32[]{:S(2)}) collective-permute-start(bf16[160,512]{1,0:T(8,128)(2,1)} %get-tuple-element.31.refs_3_), channel_id=1, source_target_pairs={{0,4},{4,8},{8,12},{12,16},{16,20},{20,24},{24,28},{28,32},{32,36}... | collective-permute-start | bytes 491528 | tf_op jit(solution)/shard_map/ppermute | solution.py:443
  71.2 8.3 %collective-permute-start.1 = (bf16[160,512]{1,0:T(8,128)(2,1)}, bf16[160,512]{1,0:T(8,128)(2,1)S(1)}, u32[]{:S(2)}, u32[]{:S(2)}) collective-permute-start(bf16[160,512]{1,0:T(8,128)(2,1)} %get-tuple-element.31.refs_3_), channel_id=1, source_target_pairs={{4,0},{8,4},{12,8},{16,12},{20,16},{24,20},{28,24},{32,28},{36,32}... | collective-permute-start | bytes 491528 | tf_op jit(solution)/shard_map/ppermute | solution.py:444
  79.5 0.7 copy-start.5
  79.5 0.7 copy-start.6
  93.5 11.5 %collective-permute-start.2 = (bf16[160,512]{1,0:T(8,128)(2,1)}, bf16[160,512]{1,0:T(8,128)(2,1)S(1)}, u32[]{:S(2)}, u32[]{:S(2)}) collective-permute-start(bf16[160,512]{1,0:T(8,128)(2,1)} %get-tuple-element.41), channel_id=1, source_target_pairs={{4,0},{8,4},{12,8},{16,12},{20,16},{24,20},{28,24},{32,28},{36,32}... | collective-permute-start | bytes 491528 | tf_op jit(solution)/shard_map/ppermute | solution.py:477
  98.6 8.3 %collective-permute-start.3 = (bf16[160,512]{1,0:T(8,128)(2,1)}, bf16[160,512]{1,0:T(8,128)(2,1)S(1)}, u32[]{:S(2)}, u32[]{:S(2)}) collective-permute-start(bf16[160,512]{1,0:T(8,128)(2,1)} %get-tuple-element.42), channel_id=1, source_target_pairs={{0,4},{4,8},{8,12},{12,16},{16,20},{20,24},{24,28},{28,32},{32,36}... | collective-permute-start | bytes 491528 | tf_op jit(solution)/shard_map/ppermute | solution.py:478
  105.0 1.8 copy-start.1
  106.9 0.7 copy-start.2
  113.0 1.2 copy-start
  115.3 55.4 %all-to-all-start.1 = ((bf16[256,4,512]{2,1,0:T(4,128)(2,1)}), bf16[256,4,512]{2,1,0:T(4,128)(2,1)S(1)}, u32[]{:S(2)}, u32[]{:S(2)}) async-start(bf16[256,4,512]{2,1,0:T(4,128)(2,1)} %reshape.68), calls=%async_computation.1 | async-start | bytes 2097152 | tf_op jit(solution)/shard_map/all_to_all | solution.py:524
  122.2 87.9 %reduce-scatter.5.cloned.1.call-start = ((), (), s32[]{:S(2)}) async-start(), calls=%async_computation.7 | async-start | bytes 1638400 | tf_op jit(solution)/shard_map/reduce_scatter | solution.py:517
  178.4 2.4 %collective-permute-start.4 = (bf16[4,160,512]{2,1,0:T(8,128)(2,1)}, bf16[4,160,512]{2,1,0:T(8,128)(2,1)S(1)}, u32[]{:S(2)}, u32[]{:S(2)}) collective-permute-start(bf16[4,160,512]{2,1,0:T(8,128)(2,1)} %get-tuple-element.52), channel_id=1, source_target_pairs={{0,4},{4,0},{8,12},{12,8},{16,20},{20,16},{24,28},{28,24},{32,36},... | collective-permute-start | bytes 1966088 | tf_op jit(solution)/shard_map/ppermute | solution.py:541
  196.4 7.3 %collective-permute-start.5 = (bf16[160,512]{1,0:T(8,128)(2,1)S(1)}, bf16[160,512]{1,0:T(8,128)(2,1)S(1)}, u32[]{:S(2)}, u32[]{:S(2)}) collective-permute-start(bf16[160,512]{1,0:T(8,128)(2,1)S(1)} %reduce_sum.21), channel_id=1, source_target_pairs={{64,0},{68,4},{72,8},{76,12},{80,16},{84,20},{88,24},{92,28},{96,3... | collective-permute-start | bytes 491528 | tf_op jit(solution)/shard_map/ppermute | solution.py:546
  197.7 8.9 %collective-permute-start.6 = (bf16[160,512]{1,0:T(8,128)(2,1)S(1)}, bf16[160,512]{1,0:T(8,128)(2,1)S(1)}, u32[]{:S(2)}, u32[]{:S(2)}) collective-permute-start(bf16[160,512]{1,0:T(8,128)(2,1)S(1)} %reduce_sum.21), channel_id=1, source_target_pairs={{128,0},{132,4},{136,8},{140,12},{144,16},{148,20},{152,24},{156,2... | collective-permute-start | bytes 491528 | tf_op jit(solution)/shard_map/ppermute | solution.py:546
  199.0 11.0 %collective-permute-start.7 = (bf16[160,512]{1,0:T(8,128)(2,1)S(1)}, bf16[160,512]{1,0:T(8,128)(2,1)S(1)}, u32[]{:S(2)}, u32[]{:S(2)}) collective-permute-start(bf16[160,512]{1,0:T(8,128)(2,1)S(1)} %reduce_sum.21), channel_id=1, source_target_pairs={{192,0},{196,4},{200,8},{204,12},{208,16},{212,20},{216,24},{220,2... | collective-permute-start | bytes 491528 | tf_op jit(solution)/shard_map/ppermute | solution.py:546
Sparse Core Ops, SparseCore 0:
  113.2 55.0 reduce-scatter.2
  171.0 27.9 reduce-scatter.4

commit v5 on v4

--- a/solution.py
+++ b/solution.py
@@ -190,32 +190,6 @@
     gpe_ref.buffer[...] = (gacc[...] * proc_scale).astype(BF)
 
 
-def node_gradients(
-    scales, h0_ref, unit_ref, wno_ref, cot_ref, dnode_ref, wns_ref, dagg_ref, agg_ref, zeta_ref,
-    dst_ref, wdst_ref, turn_ref, out_ref, mg_ref, early_ref, gpd, gpo, gns, gna, gno,
-):
-    proc_scale, node_scale = scales
-    h0 = h0_ref.get()[...]
-    unit = unit_ref.get()[...]
-    out_ref.buffer[...] = (h0.astype(F32) + dot(unit, wno_ref.get()[...])).astype(BF)
-    out_ref.send()
-    cot = cot_ref.get()[...]
-    d_node = dnode_ref.get()[...]
-    dst_sum = dst_ref.get()[...]
-    mg_ref.buffer[...] = (
-        cot.astype(F32) + dot_rt(d_node, wns_ref.get()[...]) + dot_rt(dst_sum, wdst_ref.get()[...])
-    )
-    mg_ref.send()
-    gno[...] = (dot_lt(unit, cot) * node_scale).astype(BF)
-    gns[...] = (dot_lt(h0, d_node) * node_scale).astype(BF)
-    gna[...] = (dot_lt(agg_ref.get()[...], d_node) * node_scale).astype(BF)
-    gpo[...] = (dot_lt(zeta_ref.get()[...], dagg_ref.get()[...]) * proc_scale).astype(BF)
-    gpd[...] = (dot_lt(h0, dst_sum) * proc_scale).astype(BF)
-    held = [None] * 5 + [gpd, gpo, gns, gna, gno]
-    width = h0.shape[1]
-    turn_rows(held, turn_ref.get()[...], 5 * width, 10 * width, early_ref.buffer)
-
-
 def rows_of(held, start, count):
     width = next(ref for ref in held if ref is not None).shape[1]
     pieces = []
@@ -229,27 +203,39 @@
     return pieces[0] if len(pieces) == 1 else jnp.concatenate(pieces, axis=0)
 
 
-def turn_rows(held, turn, start, stop, out):
-    narrow = out.shape[0]
-    block = turn.shape[0]
-    slab = block // narrow
-    for at in range(start, stop, block):
-        value = dot(turn, rows_of(held, at, block)).astype(BF)
+def split_turned(held, turn, core, start, half, kept, sent):
+    even = core == 0
+    narrow, length, _ = kept.shape
+    slab = turn.shape[0] // narrow
+    for at in range(0, length, slab):
+        both = []
+        for c in range(2):
+            lead = range(start + 2 * at * narrow, start + 2 * (at + slab) * narrow, 2 * half)
+            rows = [rows_of(held, row + c * half, half) for row in lead]
+            rows = rows[0] if len(rows) == 1 else jnp.concatenate(rows, axis=0)
+            both.append(dot(turn, rows).astype(BF))
+        own, other = jnp.where(even, both[0], both[1]), jnp.where(even, both[1], both[0])
         for y in range(narrow):
-            out[y, pl.ds((at - start) // narrow, slab), :] = value[y * slab : (y + 1) * slab]
+            kept[y, pl.ds(at, slab), :] = own[y * slab : (y + 1) * slab]
+            sent[y, pl.ds(at, slab), :] = other[y * slab : (y + 1) * slab]
 
 
 def mesh_backward(
-    scales, start, so_ref, sb_ref, sa_ref, wsrc_ref, mg_ref, wout_ref, tag_ref, h0_ref, a0_ref,
-    gpe_ref, turn_ref, out_ref, ret_ref, early_ref, padded, geo, gps,
+    so_ref, sb_ref, sa_ref, wsrc_ref, dnode_ref, wns_ref, dst_ref, wdst_ref, cot_ref, wout_ref,
+    tag_ref, out_ref, ret_ref, total_ref, dmesh_ref, padded,
 ):
-    proc_scale, enc_scale = scales
-    rows, width = h0_ref.buffer.shape
+    rows = so_ref.buffer.shape[0]
     total = sum(ref.get()[...].astype(F32) for ref in (so_ref, sb_ref, sa_ref)).astype(BF)
-    grad = mg_ref.get()[...] + dot_rt(total, wsrc_ref.get()[...])
+    total_ref.buffer[...] = total
+    total_ref.send()
+    grad = cot_ref.get()[...].astype(F32) + dot_rt(dnode_ref.get()[...], wns_ref.get()[...])
+    grad += dot_rt(dst_ref.get()[...], wdst_ref.get()[...])
+    grad += dot_rt(total, wsrc_ref.get()[...])
     out_ref.buffer[...] = grad
     out_ref.send()
     d_mesh = grad.astype(BF)
+    dmesh_ref.buffer[...] = d_mesh
+    dmesh_ref.send()
     padded[pl.ds(rows, 256 - rows), :] = jnp.zeros((256 - rows, padded.shape[1]), BF)
     padded[pl.ds(0, rows), :] = dot_rt(d_mesh, wout_ref.get()[...]).astype(BF)
     tag = tag_ref.get()
@@ -257,17 +243,34 @@
     for at in range(0, ret_ref.buffer.shape[0], step):
         pick = same(tag[pl.ds(at, step), :].astype(F32), 256, 1)
         ret_ref.buffer[pl.ds(at, step), :] = dot(pick, padded[...]).astype(BF)
-    ret_ref.send()
-    gps[...] = (dot_lt(h0_ref.get()[...], total) * proc_scale).astype(BF)
-    geo[...] = (dot_lt(a0_ref.get()[...], d_mesh) * enc_scale).astype(BF)
-    held = [None, None, geo, gpe_ref.get(), gps] + [None] * 5
-    turn_rows(held, turn_ref.get()[...], start, 5 * width, early_ref.buffer)
+
+
+def mesh_gradients(
+    scales, start, half, core_ref, h0_ref, unit_ref, wno_ref, cot_ref, dnode_ref, dagg_ref, agg_ref,
+    zeta_ref, dst_ref, total_ref, a0_ref, dmesh_ref, gpe_ref, turn_ref,
+    out_ref, kept_ref, sent_ref, geo, gps, gpd, gpo, gns, gna, gno,
+):
+    enc_scale, proc_scale, node_scale = scales
+    h0 = h0_ref.get()[...]
+    unit = unit_ref.get()[...]
+    out_ref.buffer[...] = (h0.astype(F32) + dot(unit, wno_ref.get()[...])).astype(BF)
+    out_ref.send()
+    d_node = dnode_ref.get()[...]
+    gno[...] = (dot_lt(unit, cot_ref.get()[...]) * node_scale).astype(BF)
+    gns[...] = (dot_lt(h0, d_node) * node_scale).astype(BF)
+    gna[...] = (dot_lt(agg_ref.get()[...], d_node) * node_scale).astype(BF)
+    gpo[...] = (dot_lt(zeta_ref.get()[...], dagg_ref.get()[...]) * proc_scale).astype(BF)
+    gpd[...] = (dot_lt(h0, dst_ref.get()[...]) * proc_scale).astype(BF)
+    gps[...] = (dot_lt(h0, total_ref.get()[...]) * proc_scale).astype(BF)
+    geo[...] = (dot_lt(a0_ref.get()[...], dmesh_ref.get()[...]) * enc_scale).astype(BF)
+    held = [None, None, geo, gpe_ref.get(), gps, gpd, gpo, gns, gna, gno]
+    turn = turn_ref.get()[...]
+    split_turned(held, turn, core_ref[0], start, half, kept_ref.buffer, sent_ref.buffer)
 
 
 def enc_backward(
-    enc_scale, half, core_ref, slot_ref, src_ref, ret_ref, sg_ref, edge_ref, grid_ref, turn_ref,
-    wg_ref,
-    out_ref, kept_ref, sent_ref, gee, geg,
+    enc_scale, half, core_ref, slot_ref, src_ref, ret_ref, sg_ref, edge_ref, grid_ref, wg_ref,
+    turn_ref, out_ref, kept_ref, sent_ref, gee, geg,
 ):
     chosen = same(columns(slot_ref.get()[...]), ret_ref.buffer.shape[0])
     d_enc = (dot(chosen, ret_ref.get()[...]) * sg_ref.get()[...].astype(F32)).astype(BF)
@@ -277,21 +280,8 @@
     gee[...] = (dot_lt(edge_ref.get()[...], d_enc) * enc_scale).astype(BF)
     geg[...] = (dot_lt(grid_ref.get()[...], grid_sum) * enc_scale).astype(BF)
     held = [gee, geg] + [None] * 8
-    even = core_ref[0] == 0
     turn = turn_ref.get()[...]
-    narrow, length, _ = kept_ref.buffer.shape
-    block = turn.shape[0]
-    slab = block // narrow
-    for at in range(0, length, slab):
-        both = []
-        for c in range(2):
-            lead = range(2 * at * narrow, 2 * (at + slab) * narrow, 2 * half)
-            rows = [rows_of(held, row + c * half, half) for row in lead]
-            both.append(dot(turn, jnp.concatenate(rows, axis=0)).astype(BF))
-        own, other = jnp.where(even, both[0], both[1]), jnp.where(even, both[1], both[0])
-        for y in range(narrow):
-            kept_ref.buffer[y, pl.ds(at, slab), :] = own[y * slab : (y + 1) * slab]
-            sent_ref.buffer[y, pl.ds(at, slab), :] = other[y * slab : (y + 1) * slab]
+    split_turned(held, turn, core_ref[0], 0, half, kept_ref.buffer, sent_ref.buffer)
 
 
 def turned(narrow, chunk, groups):
@@ -330,29 +320,22 @@
         self.copy.wait()
 
 
-def call(body, ins, outs, scratch=(), scalar=None, cut=None, place=None, alias=None, flops=0):
-    cut, place = cut or {}, place or {}
-    extra, more = int(scalar is not None), int(alias is not None)
+def call(body, ins, outs, scratch=(), scalar=None, cut=None, flops=0):
+    cut = cut or {}
+    extra = int(scalar is not None)
     count, made = len(ins), len(outs)
-    held_in = [(one.shape[0], cut[i][1]) if i in cut else one.shape for i, one in enumerate(ins)]
-    held_out = [
-        (shape[0], place[i][1], shape[2]) if i in place else shape
-        for i, (shape, _) in enumerate(outs)
-    ]
+    held = [(one.shape[0], cut[i][1]) if i in cut else one.shape for i, one in enumerate(ins)]
 
     def kernel(*refs):
         lead, refs = refs[:extra], refs[extra:]
-        source, refs = refs[:count], refs[count + more :]
-        target, refs = refs[:made], refs[made:]
+        source, target, refs = refs[:count], refs[count : count + made], refs[count + made :]
         here, there, refs = refs[:count], refs[count : count + made], refs[count + made :]
         in_sem, out_sem = refs[:2]
-        got, put = [], []
+        got = []
         for i in range(count):
             part = source[i].at[:, pl.ds(*cut[i])] if i in cut else source[i]
             got.append(Inward(part, here[i], in_sem.at[i]))
-        for i in range(made):
-            part = target[i].at[:, pl.ds(*place[i]), :] if i in place else target[i]
-            put.append(Outward(there[i], part, out_sem.at[i]))
+        put = [Outward(there[i], target[i], out_sem.at[i]) for i in range(made)]
         body(*lead, *got, *put, *refs[2:])
         for one in got:
             one.get()
@@ -363,17 +346,16 @@
     moved = sum(one.size * one.dtype.itemsize for one in ins)
     return pl.pallas_call(
         kernel,
-        in_specs=[pl.BlockSpec(memory_space=pltpu.SMEM)] * extra + [hbm] * (count + more),
+        in_specs=[pl.BlockSpec(memory_space=pltpu.SMEM)] * extra + [hbm] * count,
         out_specs=[hbm] * made,
         out_shape=[jax.ShapeDtypeStruct(shape, kind) for shape, kind in outs],
-        scratch_shapes=[pltpu.VMEM(held_in[i], ins[i].dtype) for i in range(count)]
-        + [pltpu.VMEM(held_out[i], outs[i][1]) for i in range(made)]
+        scratch_shapes=[pltpu.VMEM(held[i], ins[i].dtype) for i in range(count)]
+        + [pltpu.VMEM(shape, kind) for shape, kind in outs]
         + [pltpu.SemaphoreType.DMA((count,)), pltpu.SemaphoreType.DMA((made,))]
         + [pltpu.VMEM(shape, kind) for shape, kind in scratch],
-        input_output_aliases={extra + count: next(iter(place))} if more else {},
         compiler_params=pltpu.CompilerParams(vmem_limit_bytes=60 << 20),
         cost_estimate=pl.CostEstimate(flops=flops, bytes_accessed=moved, transcendentals=0),
-    )(*([scalar] * extra), *ins, *([alias] * more))
+    )(*([scalar] * extra), *ins)
 
 
 def on_device(
@@ -477,50 +459,39 @@
     from_after = lax.ppermute(s_before, "wide", down)
     from_before = lax.ppermute(s_after, "wide", up)
 
+    mesh_grad, returning, total, d_mesh = call(
+        mesh_backward,
+        [s_own, from_after, from_before, w_proc_src, d_node, w_node_self, dst_sum, w_proc_dst]
+        + [cotangent, w_enc_out, received],
+        [((rows, width), F32), ((slots, width), BF), block, block],
+        [((256, width), BF)],
+        cut={10: (width, LANE)},
+        flops=12 * rows * width * width,
+    )
+
     chips = wide // 2
     chunk = 10 * width // devices
     half = narrow * chunk
     far = 4 if chips > 4 else 2
     near = chips // far
-    small = chunk % 16 != 0
-    turn = turned(narrow, chunk, 4 if small else 2)
-    late_turn = turned(narrow, chunk, 4 if small else 1)
+    turn = turned(narrow, chunk, 4 if chunk % 16 else 1)
     late = 2 * width
-    start = late // turn.shape[0] * turn.shape[0]
-    length = (10 * width - start) // narrow
-    split = (5 * width - start) // narrow
-    early_shape = ((narrow, length, width), BF)
-    mesh_out, partial_grad, early = call(
-        functools.partial(node_gradients, (proc_scale, node_scale)),
-        [h0, unit, w_node_out, cotangent, d_node, w_node_self, d_agg, agg, zeta]
-        + [dst_sum, w_proc_dst, turn],
-        [block, ((rows, width), F32), early_shape],
-        [square] * 5,
-        place={2: (split, length - split)},
-        flops=24 * rows * width * width,
-    )
-    mesh_grad, returning, early = call(
-        functools.partial(mesh_backward, (proc_scale, enc_scale), start),
-        [s_own, from_after, from_before, w_proc_src, partial_grad, w_enc_out, received, h0, a0]
+    start = late // (2 * turn.shape[0]) * 2 * turn.shape[0]
+    scales = (enc_scale, proc_scale, node_scale)
+    early_shape = ((narrow, (10 * width - start) // (2 * narrow), width), BF)
+    swap = [(i, i ^ 1) for i in range(wide)]
+    mesh_out, kept, sent = call(
+        functools.partial(mesh_gradients, scales, start, half),
+        [h0, unit, w_node_out, cotangent, d_node, d_agg, agg, zeta, dst_sum, total, a0, d_mesh]
         + [gpe, turn],
-        [((rows, width), F32), ((slots, width), BF), early_shape],
-        [((256, width), BF), square, square],
-        cut={6: (width, LANE)},
-        place={2: (0, split)},
-        alias=early,
-        flops=12 * rows * width * width,
-    )
-    line = [[i + j * 2 * near for j in range(far)] for i in range(2 * near)]
-    plane = [[i * 2 * near + j for j in range(2 * near)] for i in range(far)]
+        [block, early_shape, early_shape],
+        [square] * 7,
+        scalar=core.reshape(1),
+        flops=32 * rows * width * width,
+    )
+    came = lax.ppermute(sent, "wide", swap)
+    early = (kept.astype(F32) + came.astype(F32)).astype(BF)
     early = lax.psum_scatter(early, "narrow", scatter_dimension=0, tiled=True)
-    early = jnp.pad(early.reshape(length, width), ((start // narrow, 0), (0, 0)))
-    early = lax.psum_scatter(
-        early.reshape(far, near * 2 * chunk, width),
-        "wide",
-        scatter_dimension=0,
-        tiled=True,
-        axis_index_groups=line,
-    )
     returned = lax.all_to_all(
         returning.reshape(devices, capacity, width),
         ("wide", "narrow"),
@@ -528,36 +499,42 @@
         concat_axis=0,
         tiled=True,
     ).reshape(slots, width)
-    spread = -(-late // (2 * late_turn.shape[0])) * late_turn.shape[0] // narrow
+    spread = -(-late // (2 * turn.shape[0])) * turn.shape[0] // narrow
     late_shape = ((narrow, spread, width), BF)
     grid_grad, kept, sent = call(
         functools.partial(enc_backward, enc_scale, half),
-        [slot, source, returned, enc_sg, enc_edge_latent, grid_latent, late_turn, w_enc_grid],
+        [slot, source, returned, enc_sg, enc_edge_latent, grid_latent, w_enc_grid, turn],
         [((grid_rows, width), F32), late_shape, late_shape],
         [square, square],
         scalar=core.reshape(1),
         flops=8 * edges * width * width,
     )
-    came = lax.ppermute(sent, "wide", [(i, i ^ 1) for i in range(wide)])
+    came = lax.ppermute(sent, "wide", swap)
     last = (kept.astype(F32) + came.astype(F32)).astype(BF)
     last = lax.all_to_all(last, "narrow", split_axis=0, concat_axis=0, tiled=True)
-    last = jnp.sum(last.astype(F32), axis=0).astype(BF)
-    parts = [
-        lax.ppermute(last, "wide", [(j * 2 * near + i, i) for i in range(2 * near)])
-        for j in range(1, far)
-    ]
-    at_first = lax.axis_index("wide") < 2 * near
-    last = jnp.where(at_first, last.astype(F32), 0.0) + sum(p.astype(F32) for p in parts)
-    last = last[: near * chunk].reshape(near, 1, chunk, width)
-    own = (jnp.arange(2) == core)[None, :, None, None]
-    both = early.reshape(near, 2, chunk, width).astype(F32) + jnp.where(own, last, 0.0)
+    last = jnp.sum(last.astype(F32), axis=0)[: near * chunk]
+    early = jnp.pad(early[0], ((start // (2 * narrow), 0), (0, 0)))
+    early = early.reshape(far, near * chunk, width)
+    x = lax.axis_index("wide") // (2 * near)
+
+    def toward(j):
+        to = lax.rem(x + j, far)
+        part = lax.dynamic_index_in_dim(early, to, 0, keepdims=False).astype(F32)
+        return (part + jnp.where(to == 0, last, 0.0)).astype(BF)
+
+    both = toward(0).astype(F32)
+    for j in range(1, far):
+        ring = [(i, (i + j * 2 * near) % wide) for i in range(wide)]
+        both += lax.ppermute(toward(j), "wide", ring).astype(F32)
     both = lax.all_to_all(
-        both.astype(BF).reshape(2 * near, chunk, width),
+        both.astype(BF).reshape(near, chunk, width),
         "wide",
         split_axis=0,
         concat_axis=0,
         tiled=True,
-        axis_index_groups=plane,
+        axis_index_groups=[
+            [i * 2 * near + 2 * j + c for j in range(near)] for i in range(far) for c in range(2)
+        ],
     )
     summed = jnp.sum(both.astype(F32), axis=0).reshape(-1)
     return (mesh_out, grid_grad, summed, mesh_grad)

time: 243 us -> 225 us (0.926)
  waiting for transfers between devices: 61.8 us -> 38.6 us
  blocking collectives: 86.7 us -> 102 us
  starting transfers between devices: 21.1 us -> 9.51 us
  other arithmetic: 1.65 us -> 6.15 us
  local copies, waits for them, and re-layouts: 14 us -> 10.7 us
    reduce_scatter x1, waiting for transfers between devices: 46 us -> 0.02 us  [on_device(): early = lax.psum_scatter(early, 'narrow', scatter_dimension=0, tiled=True)]
    all_to_all x2, blocking collectives: 34.8 us -> 50.3 us  [the longest x1 38.1 us: on_device(): lax.all_to_all(returning.reshape(devices, capacity, width), ('wide', 'nar...]
    all_to_all x1, waiting for transfers between devices: 0.01 us -> 10 us  [on_device(): lax.all_to_all(last, 'narrow', split_axis=0, concat_axis=0, tiled=True)]
    ppermute x1, starting transfers between devices: 5.08 us -> 0.08 us  [on_device(): from_after = lax.ppermute(s_before, 'wide', down)]
    ppermute x1, starting transfers between devices: 5.05 us -> 0.08 us  [on_device(): p_after = lax.ppermute(p_src, 'wide', down)]
    convert_element_type x1 -> x3, other arithmetic: 0.13 us -> 3.92 us  [the longest x1 3.68 us: on_device(): early = (kept.astype(F32) + came.astype(F32)).astype(BF)]
    ppermute x1, waiting for transfers between devices: 1.82 us -> 5.38 us  [on_device(): from_before = lax.ppermute(s_after, 'wide', up)]
    ppermute x1, waiting for transfers between devices: 2 us -> 5.2 us  [on_device(): p_before = lax.ppermute(p_src, 'wide', up)]
  transfers between devices with their start and end apart: 11 -> 11, of which waited for: 7 -> 8; matrix products, arithmetic and copies ran while one was open for 3% -> 2% of each run, Pallas kernels for 5% -> 3%
where the time goes in v5:
time: 225 us; the launch traced here: 223 us
  blocking collectives  102 us (45%)
  Pallas kernels  41.5 us (18%)
  waiting for transfers between devices  38.6 us (17%)
  between operations  14.2 us (6%)
  local copies, waits for them, and re-layouts  10.7 us (5%)
  starting transfers between devices  9.51 us (4%)
  other arithmetic  6.15 us (3%)
    all_to_all x1, blocking collectives, on_device(): lax.all_to_all(payload.reshape(devices, capacity, width + LANE), ('wide',...  51.9 us
    pallas_call x6, Pallas kernels, call(): pl.pallas_call(kernel, in_specs=[pl.BlockSpec(memory_space=pltpu.SMEM)] *...  41.5 us
    all_to_all x1, blocking collectives, on_device(): lax.all_to_all(returning.reshape(devices, capacity, width), ('wide', 'nar...  38.1 us
    all_to_all x1, blocking collectives, on_device(): lax.all_to_all(both.astype(BF).reshape(near, chunk, width), 'wide', split...  12.2 us
    all_to_all x1, waiting for transfers between devices, on_device(): lax.all_to_all(last, 'narrow', split_axis=0, concat_axis=0, tiled=True)  10 us
    ppermute x2, waiting for transfers between devices, on_device(): came = lax.ppermute(sent, 'wide', swap)  6.93 us
    ppermute x3, waiting for transfers between devices, on_device(): both += lax.ppermute(toward(j), 'wide', ring).astype(F32)  6.9 us
    ppermute x1, waiting for transfers between devices, on_device(): from_before = lax.ppermute(s_after, 'wide', up)  5.38 us
  transfers between devices with their start and end apart: 11, of which 8 were waited for; matrix products, arithmetic and copies ran while one was open for 2% of the time, Pallas kernels for 3%

profile of v5, /device:TPU:8, one launch (start us, length us, event | category | flops | bytes accessed | tf_op | source)
XLA Modules:
  0.0 222.8 jit_solution(17405363441853253140)
XLA Ops:
  7.2 0.0 reduce-scatter.2.cloned.1.call-start
  7.2 4.7 %shard_map.228 = (bf16[1024,640]{1,0:T(8,128)(2,1)}, bf16[512,512]{1,0:T(8,128)(2,1)}, s32[1,512]{1,0:T(1,128)}) custom-call(s32[1,512]{1,0:T(1,128)} %bitcast.21, s32[1,512]{1,0:T(1,128)} %bitcast.22, s32[1,512]{1,0:T(1,128)} %bitcast.23, bf16[512,512]{1,0:T(8,128)(2,1)} %refs_6_.5, bf16[512,512]{1,0:T(8,128)(2,1)} %refs_5_.5, bf16[512,512]{1,0:T(8,128)(2,1)} %refs_5_.3, ...), custom_call_target="tpu_custom_call" | custom-call | bytes 2103296 | tf_op jit(solution)/shard_map/pallas_call | solution.py:347
  11.9 2.6 %reshape.60 = bf16[256,4,640]{2,1,0:T(4,128)(2,1)S(1)} reshape(bf16[1024,640]{1,0:T(8,128)(2,1)} %get-tuple-element.30) | data formatting | bytes 2621440 | tf_op jit(solution)/shard_map/reshape | solution.py:412
  14.5 51.9 %all_to_all.20 = bf16[256,4,640]{2,1,0:T(4,128)(2,1)S(1)} all-to-all(bf16[256,4,640]{2,1,0:T(4,128)(2,1)S(1)} %reshape.60), channel_id=1, replica_groups=mesh['wide'=64,'narrow'=4] {'wide','narrow'}, dimensions={0} | all-to-all | bytes 2621440 | tf_op jit(solution)/shard_map/all_to_all | solution.py:411
  66.4 1.2 reshape.61.refs_0_.refs_10_
  67.6 3.5 %shard_map.229 = (bf16[160,512]{1,0:T(8,128)(2,1)}, bf16[160,512]{1,0:T(8,128)(2,1)}, bf16[160,512]{1,0:T(8,128)(2,1)}) custom-call(bf16[1024,640]{1,0:T(8,128)(2,1)} %reshape.61.refs_0_.refs_10_, bf16[512,512]{1,0:T(8,128)(2,1)} %refs_9_.3, bf16[160,512]{1,0:T(8,128)(2,1)} %refs_2_.1, bf16[512,512]{1,0:T(8,128)(2,1)} %refs_3_.6), custom_call_target="tpu_custom_call" | custom-call | bytes 2523136 | tf_op jit(solution)/shard_map/pallas_call | solution.py:347
  71.1 0.1 collective-permute-start.1
  71.2 0.5 collective-permute-start
  71.7 0.6 reshape.62.refs_0_
  72.3 0.6 reshape.63.refs_1_
  72.9 1.4 collective-permute-done.1.refs_4_
  74.3 5.2 %collective-permute-done.refs_2_ = bf16[160,512]{1,0:T(8,128)(2,1)S(1)} collective-permute-done((bf16[160,512]{1,0:T(8,128)(2,1)}, bf16[160,512]{1,0:T(8,128)(2,1)S(1)}, u32[]{:S(2)}, u32[]{:S(2)}) %collective-permute-start) | collective-permute-done | bytes 163872 | tf_op jit(solution)/shard_map/ppermute | solution.py:425
  79.6 0.7 copy-done.6
  80.2 13.3 %shard_map.230 = (bf16[160,512]{1,0:T(8,128)(2,1)}, bf16[160,512]{1,0:T(8,128)(2,1)}, bf16[160,512]{1,0:T(8,128)(2,1)}, bf16[160,512]{1,0:T(8,128)(2,1)}, bf16[1...) custom-call(s32[5,256]{1,0:T(8,128)} %reshape.62.refs_0_, ...), custom_call_target="tpu_custom_call" | custom-call | flops 4026531840 | bytes 5285888 | tf_op jit(solution)/shard_map/pallas_call | solution.py:347
  93.5 0.1 collective-permute-start.2
  93.6 0.5 collective-permute-start.3
  94.1 2.6 %collective-permute-done.2.refs_1_ = bf16[160,512]{1,0:T(8,128)(2,1)S(1)} collective-permute-done((bf16[160,512]{1,0:T(8,128)(2,1)}, bf16[160,512]{1,0:T(8,128)(2,1)S(1)}, u32[]{:S(2)}, u32[]{:S(2)}) %collective-permute-start.2) | collective-permute-done | bytes 163872 | tf_op jit(solution)/shard_map/ppermute | solution.py:459
  96.7 5.4 %collective-permute-done.3.refs_2_ = bf16[160,512]{1,0:T(8,128)(2,1)S(1)} collective-permute-done((bf16[160,512]{1,0:T(8,128)(2,1)}, bf16[160,512]{1,0:T(8,128)(2,1)S(1)}, u32[]{:S(2)}, u32[]{:S(2)}) %collective-permute-start.3) | collective-permute-done | bytes 163872 | tf_op jit(solution)/shard_map/ppermute | solution.py:460
  102.1 0.6 copy-done.2
  102.8 4.4 %shard_map.231 = (f32[160,512]{1,0:T(8,128)}, bf16[1024,512]{1,0:T(8,128)(2,1)}, bf16[160,512]{1,0:T(8,128)(2,1)}, bf16[160,512]{1,0:T(8,128)(2,1)}) custom-call(bf16[160,512]{1,0:T(8,128)(2,1)} %get-tuple-element.39.refs_0_, bf16[160,512]{1,0:T(8,128)(2,1)} %copy-done.1, bf16[160,512]{1,0:T(8,128)(2,1)} %copy-done.2, bf16[512,512]{1,0:T(8,128)(2,1)} %refs_3_.6, ...), custom_call_target="tpu_custom_call" | custom-call | flops 503316480 | bytes 4390912 | tf_op jit(solution)/shard_map/pallas_call | solution.py:347
  107.2 9.1 %shard_map.232 = (bf16[160,512]{1,0:T(8,128)(2,1)}, bf16[4,560,512]{2,1,0:T(8,128)(2,1)}, bf16[4,560,512]{2,1,0:T(8,128)(2,1)}) custom-call(s32[1]{0:T(128)} %bitcast.refs_0_, bf16[160,512]{1,0:T(8,128)(2,1)} %get-tuple-element.31.refs_5_.refs_1_, bf16[160,512]{1,0:T(8,128)(2,1)} %get-tuple-element.33.refs_2_, bf16[512,512]{1,0:T(8,128)(2,1)} %refs_3_.7, ...), custom_call_target="tpu_custom_call" | custom-call | flops 1342177280 | bytes 3055616 | tf_op jit(solution)/shard_map/pallas_call | solution.py:347
  116.3 0.1 collective-permute-start.4
  116.4 4.6 %collective-permute-done.4 = bf16[4,560,512]{2,1,0:T(8,128)(2,1)S(1)} collective-permute-done((bf16[4,560,512]{2,1,0:T(8,128)(2,1)}, bf16[4,560,512]{2,1,0:T(8,128)(2,1)S(1)}, u32[]{:S(2)}, u32[]{:S(2)}) %collective-permute-start.4) | collective-permute-done | bytes 2293792 | tf_op jit(solution)/shard_map/ppermute | solution.py:492
  121.0 3.7 %add_convert_fusion = bf16[4,560,512]{2,1,0:T(8,128)(2,1)} fusion(bf16[4,560,512]{2,1,0:T(8,128)(2,1)S(1)} %collective-permute-done.4, bf16[4,560,512]{2,1,0:T(8,128)(2,1)} %get-tuple-element.51), kind=kLoop, calls=%fused_computation | loop fusion | flops 4587520 | bytes 6881280 | tf_op jit(solution)/shard_map/convert_element_type | solution.py:493
  124.7 0.0 reduce-scatter.2.cloned.1.call-update
  124.7 1.2 copy-done
  125.9 0.3 reshape.64
  126.2 38.1 %all_to_all.21 = bf16[256,4,512]{2,1,0:T(4,128)(2,1)S(1)} all-to-all(bf16[256,4,512]{2,1,0:T(4,128)(2,1)S(1)} %reshape.64), channel_id=1, replica_groups=mesh['wide'=64,'narrow'=4] {'wide','narrow'}, dimensions={0} | all-to-all | bytes 2097152 | tf_op jit(solution)/shard_map/all_to_all | solution.py:495
  164.3 1.1 reshape.65.refs_3_
  165.4 6.6 %shard_map.233 = (f32[512,512]{1,0:T(8,128)}, bf16[4,160,512]{2,1,0:T(8,128)(2,1)}, bf16[4,160,512]{2,1,0:T(8,128)(2,1)}) custom-call(s32[1]{0:T(128)} %bitcast.refs_0_, s32[1,512]{1,0:T(1,128)} %get-tuple-element.47.refs_1_, s32[1,512]{1,0:T(1,128)} %bitcast.24, bf16[1024,512]{1,0:T(8,128)(2,1)} %reshape.65.refs_3_, ...), custom_call_target="tpu_custom_call" | custom-call | flops 1073741824 | bytes 3354624 | tf_op jit(solution)/shard_map/pallas_call | solution.py:347
  172.0 0.1 collective-permute-start.5
  172.1 2.3 %collective-permute-done.5 = bf16[4,160,512]{2,1,0:T(8,128)(2,1)S(1)} collective-permute-done((bf16[4,160,512]{2,1,0:T(8,128)(2,1)}, bf16[4,160,512]{2,1,0:T(8,128)(2,1)S(1)}, u32[]{:S(2)}, u32[]{:S(2)}) %collective-permute-start.5) | collective-permute-done | bytes 655392 | tf_op jit(solution)/shard_map/ppermute | solution.py:512
  174.4 2.1 add_convert_fusion.1
  176.5 4.8 %all-to-all-start.2 = ((bf16[4,160,512]{2,1,0:T(8,128)(2,1)}), bf16[4,160,512]{2,1,0:T(8,128)(2,1)S(1)}, u32[]{:S(2)}, u32[]{:S(2)}) async-start(bf16[4,160,512]{2,1,0:T(8,128)(2,1)} %add_convert_fusion.1), calls=%async_computation.3 | async-start | bytes 1310720 | tf_op jit(solution)/shard_map/all_to_all | solution.py:514
  181.3 10.0 %all-to-all-done.2 = bf16[4,160,512]{2,1,0:T(8,128)(2,1)S(1)} async-done(((bf16[4,160,512]{2,1,0:T(8,128)(2,1)}), bf16[4,160,512]{2,1,0:T(8,128)(2,1)S(1)}, u32[]{:S(2)}, u32[]{:S(2)}) %all-to-all-start.2) | async-done | bytes 655392 | tf_op jit(solution)/shard_map/all_to_all | solution.py:514
  191.3 0.1 convert_reduce_fusion
  191.4 0.0 reduce-scatter.2.cloned.1.call-done
  191.5 1.1 pad.4
  192.6 0.1 fusion.2
  192.7 0.1 collective-permute-start.6
  192.8 3.2 %collective-permute-start.8 = (bf16[160,512]{1,0:T(8,128)(2,1)S(1)}, bf16[160,512]{1,0:T(8,128)(2,1)S(1)}, u32[]{:S(2)}, u32[]{:S(2)}) collective-permute-start(bf16[160,512]{1,0:T(8,128)(2,1)S(1)} %get-tuple-element.57), channel_id=1, source_target_pairs={{0,192},{4,196},{8,200},{12,204},{16,208},{20,212},{24,216},{28,22... | collective-permute-start | bytes 491528 | tf_op jit(solution)/shard_map/ppermute | solution.py:528
  196.0 0.0 collective-permute-start.7
  196.0 6.9 %collective-permute-done.6 = bf16[160,512]{1,0:T(8,128)(2,1)S(1)} collective-permute-done((bf16[160,512]{1,0:T(8,128)(2,1)S(1)}, bf16[160,512]{1,0:T(8,128)(2,1)S(1)}, u32[]{:S(2)}, u32[]{:S(2)}) %collective-permute-start.6) | collective-permute-done | bytes 163872 | tf_op jit(solution)/shard_map/ppermute | solution.py:528
  202.9 0.0 collective-permute-done.8
  202.9 0.0 collective-permute-done.7
  202.9 0.1 add_convert_fusion.2
  203.1 12.2 %all_to_all.22 = bf16[8,20,512]{2,1,0:T(8,128)(2,1)S(1)} all-to-all(bf16[8,20,512]{2,1,0:T(8,128)(2,1)S(1)} %reshape.67), channel_id=1, replica_groups={{0,8,16,24,32,40,48,56},{4,12,20,28,36,44,52,60},{64,72,80,88,96,104,11..., dimensions={0} | all-to-all | bytes 327680 | tf_op jit(solution)/shard_map/all_to_all | solution.py:529
  215.3 0.6 reshape.68
  (13 shorter events, 0.1 us)
Async XLA Ops:
  7.2 184.3 %reduce-scatter.2.cloned.1.call-start = ((), (), s32[]{:S(2)}) async-start(), calls=%async_computation.5 | async-start | bytes 2867200 | tf_op jit(solution)/shard_map/reduce_scatter | solution.py:494
  66.4 5.3 %copy-start.3 = (s32[1280]{0:T(1024)S(1)}, s32[1280]{0:T(1024)}, u32[]{:S(2)}) copy-start(s32[1280]{0:T(1024)} %param.28) | copy-start | bytes 15364
  66.4 5.9 %copy-start.4 = (s32[1280]{0:T(1024)S(1)}, s32[1280]{0:T(1024)}, u32[]{:S(2)}) copy-start(s32[1280]{0:T(1024)} %param.29) | copy-start | bytes 15364
  71.1 3.2 %collective-permute-start.1 = (bf16[160,512]{1,0:T(8,128)(2,1)}, bf16[160,512]{1,0:T(8,128)(2,1)S(1)}, u32[]{:S(2)}, u32[]{:S(2)}) collective-permute-start(bf16[160,512]{1,0:T(8,128)(2,1)} %get-tuple-element.32.refs_3_), channel_id=1, source_target_pairs={{4,0},{8,4},{12,8},{16,12},{20,16},{24,20},{28,24},{32,28},{36,32}... | collective-permute-start | bytes 491528 | tf_op jit(solution)/shard_map/ppermute | solution.py:426
  71.2 8.4 %collective-permute-start = (bf16[160,512]{1,0:T(8,128)(2,1)}, bf16[160,512]{1,0:T(8,128)(2,1)S(1)}, u32[]{:S(2)}, u32[]{:S(2)}) collective-permute-start(bf16[160,512]{1,0:T(8,128)(2,1)} %get-tuple-element.32.refs_3_), channel_id=1, source_target_pairs={{0,4},{4,8},{8,12},{12,16},{16,20},{20,24},{24,28},{28,32},{32,36}... | collective-permute-start | bytes 491528 | tf_op jit(solution)/shard_map/ppermute | solution.py:425
  74.3 5.2 %copy-start.5 = (bf16[160,512]{1,0:T(8,128)(2,1)}, bf16[160,512]{1,0:T(8,128)(2,1)S(1)}, u32[]{:S(2)}) copy-start(bf16[160,512]{1,0:T(8,128)(2,1)S(1)} %collective-permute-done.1.refs_4_) | copy-start | bytes 491524
  79.6 0.7 copy-start.6
  93.5 3.2 %collective-permute-start.2 = (bf16[160,512]{1,0:T(8,128)(2,1)}, bf16[160,512]{1,0:T(8,128)(2,1)S(1)}, u32[]{:S(2)}, u32[]{:S(2)}) collective-permute-start(bf16[160,512]{1,0:T(8,128)(2,1)} %get-tuple-element.40), channel_id=1, source_target_pairs={{4,0},{8,4},{12,8},{16,12},{20,16},{24,20},{28,24},{32,28},{36,32}... | collective-permute-start | bytes 491528 | tf_op jit(solution)/shard_map/ppermute | solution.py:459
  93.6 8.5 %collective-permute-start.3 = (bf16[160,512]{1,0:T(8,128)(2,1)}, bf16[160,512]{1,0:T(8,128)(2,1)S(1)}, u32[]{:S(2)}, u32[]{:S(2)}) collective-permute-start(bf16[160,512]{1,0:T(8,128)(2,1)} %get-tuple-element.41), channel_id=1, source_target_pairs={{0,4},{4,8},{8,12},{12,16},{16,20},{20,24},{24,28},{28,32},{32,36}... | collective-permute-start | bytes 491528 | tf_op jit(solution)/shard_map/ppermute | solution.py:460
  96.7 5.4 %copy-start.1 = (bf16[160,512]{1,0:T(8,128)(2,1)}, bf16[160,512]{1,0:T(8,128)(2,1)S(1)}, u32[]{:S(2)}) copy-start(bf16[160,512]{1,0:T(8,128)(2,1)S(1)} %collective-permute-done.2.refs_1_) | copy-start | bytes 491524
  102.1 0.7 copy-start.2
  116.3 4.7 %collective-permute-start.4 = (bf16[4,560,512]{2,1,0:T(8,128)(2,1)}, bf16[4,560,512]{2,1,0:T(8,128)(2,1)S(1)}, u32[]{:S(2)}, u32[]{:S(2)}) collective-permute-start(bf16[4,560,512]{2,1,0:T(8,128)(2,1)} %get-tuple-element.52), channel_id=1, source_target_pairs={{0,4},{4,0},{8,12},{12,8},{16,20},{20,16},{24,28},{28,24},{32,36},... | collective-permute-start | bytes 6881288 | tf_op jit(solution)/shard_map/ppermute | solution.py:492
  124.7 1.2 copy-start
  172.0 2.4 %collective-permute-start.5 = (bf16[4,160,512]{2,1,0:T(8,128)(2,1)}, bf16[4,160,512]{2,1,0:T(8,128)(2,1)S(1)}, u32[]{:S(2)}, u32[]{:S(2)}) collective-permute-start(bf16[4,160,512]{2,1,0:T(8,128)(2,1)} %get-tuple-element.54), channel_id=1, source_target_pairs={{0,4},{4,0},{8,12},{12,8},{16,20},{20,16},{24,28},{28,24},{32,36},... | collective-permute-start | bytes 1966088 | tf_op jit(solution)/shard_map/ppermute | solution.py:512
  176.5 14.8 %all-to-all-start.2 = ((bf16[4,160,512]{2,1,0:T(8,128)(2,1)}), bf16[4,160,512]{2,1,0:T(8,128)(2,1)S(1)}, u32[]{:S(2)}, u32[]{:S(2)}) async-start(bf16[4,160,512]{2,1,0:T(8,128)(2,1)} %add_convert_fusion.1), calls=%async_computation.3 | async-start | bytes 1310720 | tf_op jit(solution)/shard_map/all_to_all | solution.py:514
  192.7 10.2 %collective-permute-start.6 = (bf16[160,512]{1,0:T(8,128)(2,1)S(1)}, bf16[160,512]{1,0:T(8,128)(2,1)S(1)}, u32[]{:S(2)}, u32[]{:S(2)}) collective-permute-start(bf16[160,512]{1,0:T(8,128)(2,1)S(1)} %get-tuple-element.56), channel_id=1, source_target_pairs={{0,64},{4,68},{8,72},{12,76},{16,80},{20,84},{24,88},{28,92},{32,9... | collective-permute-start | bytes 491528 | tf_op jit(solution)/shard_map/ppermute | solution.py:528
  192.8 10.1 %collective-permute-start.8 = (bf16[160,512]{1,0:T(8,128)(2,1)S(1)}, bf16[160,512]{1,0:T(8,128)(2,1)S(1)}, u32[]{:S(2)}, u32[]{:S(2)}) collective-permute-start(bf16[160,512]{1,0:T(8,128)(2,1)S(1)} %get-tuple-element.57), channel_id=1, source_target_pairs={{0,192},{4,196},{8,200},{12,204},{16,208},{20,212},{24,216},{28,22... | collective-permute-start | bytes 491528 | tf_op jit(solution)/shard_map/ppermute | solution.py:528
  196.0 6.9 %collective-permute-start.7 = (bf16[160,512]{1,0:T(8,128)(2,1)S(1)}, bf16[160,512]{1,0:T(8,128)(2,1)S(1)}, u32[]{:S(2)}, u32[]{:S(2)}) collective-permute-start(bf16[160,512]{1,0:T(8,128)(2,1)S(1)} %get-tuple-element.58), channel_id=1, source_target_pairs={{0,128},{4,132},{8,136},{12,140},{16,144},{20,148},{24,152},{28,15... | collective-permute-start | bytes 491528 | tf_op jit(solution)/shard_map/ppermute | solution.py:528
Sparse Core Ops, SparseCore 0:
  124.9 35.7 reduce-scatter.1

commit v6 on v5

--- a/solution.py
+++ b/solution.py
@@ -220,22 +220,47 @@
             sent[y, pl.ds(at, slab), :] = other[y * slab : (y + 1) * slab]
 
 
+def turn_cores(held, turn, start, half, out):
+    narrow = out.buffer.shape[0]
+    slab = turn.shape[0] // narrow
+    span = 2 * turn.shape[0]
+    width = out.buffer.shape[3]
+    first = start // span * span
+    skip = (start - first) // (2 * narrow)
+    leads = [*range(first + span, 10 * width, span), first]
+    for k, lead in enumerate(leads):
+        low = skip if lead == first else 0
+        for c in range(2):
+            rows = [rows_of(held, row + c * half, half) for row in range(lead, lead + span, 2 * half)]
+            rows = rows[0] if len(rows) == 1 else jnp.concatenate(rows, axis=0)
+            value = dot(turn, rows)
+            for y in range(narrow):
+                piece = value[y * slab + low : (y + 1) * slab]
+                out.buffer[y, c, pl.ds(k * slab, slab - low), :] = piece.astype(BF)
+    fill = out.buffer.shape[2] - len(leads) * slab + skip
+    if fill:
+        at = pl.ds(len(leads) * slab - skip, fill)
+        out.buffer[:, :, at, :] = jnp.zeros((narrow, 2, fill, width), BF)
+
+
 def mesh_backward(
-    so_ref, sb_ref, sa_ref, wsrc_ref, dnode_ref, wns_ref, dst_ref, wdst_ref, cot_ref, wout_ref,
-    tag_ref, out_ref, ret_ref, total_ref, dmesh_ref, padded,
+    scales, start, half, so_ref, sb_ref, sa_ref, wsrc_ref, dnode_ref, wns_ref, dst_ref, wdst_ref,
+    cot_ref, wout_ref, tag_ref, h0_ref, a0_ref, agg_ref, dagg_ref, zeta_ref, unit_ref, wno_ref,
+    gpe_ref, turn_ref, out_ref, grad_ref, ret_ref, early_ref,
+    padded, geo, gps, gpd, gpo, gns, gna, gno,
 ):
+    enc_scale, proc_scale, node_scale = scales
     rows = so_ref.buffer.shape[0]
     total = sum(ref.get()[...].astype(F32) for ref in (so_ref, sb_ref, sa_ref)).astype(BF)
-    total_ref.buffer[...] = total
-    total_ref.send()
-    grad = cot_ref.get()[...].astype(F32) + dot_rt(dnode_ref.get()[...], wns_ref.get()[...])
-    grad += dot_rt(dst_ref.get()[...], wdst_ref.get()[...])
+    d_node = dnode_ref.get()[...]
+    dst_sum = dst_ref.get()[...]
+    cot = cot_ref.get()[...]
+    grad = cot.astype(F32) + dot_rt(d_node, wns_ref.get()[...])
+    grad += dot_rt(dst_sum, wdst_ref.get()[...])
     grad += dot_rt(total, wsrc_ref.get()[...])
-    out_ref.buffer[...] = grad
-    out_ref.send()
+    grad_ref.buffer[...] = grad
+    grad_ref.send()
     d_mesh = grad.astype(BF)
-    dmesh_ref.buffer[...] = d_mesh
-    dmesh_ref.send()
     padded[pl.ds(rows, 256 - rows), :] = jnp.zeros((256 - rows, padded.shape[1]), BF)
     padded[pl.ds(0, rows), :] = dot_rt(d_mesh, wout_ref.get()[...]).astype(BF)
     tag = tag_ref.get()
@@ -243,29 +268,20 @@
     for at in range(0, ret_ref.buffer.shape[0], step):
         pick = same(tag[pl.ds(at, step), :].astype(F32), 256, 1)
         ret_ref.buffer[pl.ds(at, step), :] = dot(pick, padded[...]).astype(BF)
-
-
-def mesh_gradients(
-    scales, start, half, core_ref, h0_ref, unit_ref, wno_ref, cot_ref, dnode_ref, dagg_ref, agg_ref,
-    zeta_ref, dst_ref, total_ref, a0_ref, dmesh_ref, gpe_ref, turn_ref,
-    out_ref, kept_ref, sent_ref, geo, gps, gpd, gpo, gns, gna, gno,
-):
-    enc_scale, proc_scale, node_scale = scales
+    ret_ref.send()
     h0 = h0_ref.get()[...]
+    gps[...] = (dot_lt(h0, total) * proc_scale).astype(BF)
+    geo[...] = (dot_lt(a0_ref.get()[...], d_mesh) * enc_scale).astype(BF)
+    gns[...] = (dot_lt(h0, d_node) * node_scale).astype(BF)
+    gna[...] = (dot_lt(agg_ref.get()[...], d_node) * node_scale).astype(BF)
+    gpd[...] = (dot_lt(h0, dst_sum) * proc_scale).astype(BF)
+    gpo[...] = (dot_lt(zeta_ref.get()[...], dagg_ref.get()[...]) * proc_scale).astype(BF)
     unit = unit_ref.get()[...]
+    gno[...] = (dot_lt(unit, cot) * node_scale).astype(BF)
     out_ref.buffer[...] = (h0.astype(F32) + dot(unit, wno_ref.get()[...])).astype(BF)
     out_ref.send()
-    d_node = dnode_ref.get()[...]
-    gno[...] = (dot_lt(unit, cot_ref.get()[...]) * node_scale).astype(BF)
-    gns[...] = (dot_lt(h0, d_node) * node_scale).astype(BF)
-    gna[...] = (dot_lt(agg_ref.get()[...], d_node) * node_scale).astype(BF)
-    gpo[...] = (dot_lt(zeta_ref.get()[...], dagg_ref.get()[...]) * proc_scale).astype(BF)
-    gpd[...] = (dot_lt(h0, dst_ref.get()[...]) * proc_scale).astype(BF)
-    gps[...] = (dot_lt(h0, total_ref.get()[...]) * proc_scale).astype(BF)
-    geo[...] = (dot_lt(a0_ref.get()[...], dmesh_ref.get()[...]) * enc_scale).astype(BF)
     held = [None, None, geo, gpe_ref.get(), gps, gpd, gpo, gns, gna, gno]
-    turn = turn_ref.get()[...]
-    split_turned(held, turn, core_ref[0], start, half, kept_ref.buffer, sent_ref.buffer)
+    turn_cores(held, turn_ref.get()[...], start, half, early_ref)
 
 
 def enc_backward(
@@ -459,16 +475,6 @@
     from_after = lax.ppermute(s_before, "wide", down)
     from_before = lax.ppermute(s_after, "wide", up)
 
-    mesh_grad, returning, total, d_mesh = call(
-        mesh_backward,
-        [s_own, from_after, from_before, w_proc_src, d_node, w_node_self, dst_sum, w_proc_dst]
-        + [cotangent, w_enc_out, received],
-        [((rows, width), F32), ((slots, width), BF), block, block],
-        [((256, width), BF)],
-        cut={10: (width, LANE)},
-        flops=12 * rows * width * width,
-    )
-
     chips = wide // 2
     chunk = 10 * width // devices
     half = narrow * chunk
@@ -476,22 +482,21 @@
     near = chips // far
     turn = turned(narrow, chunk, 4 if chunk % 16 else 1)
     late = 2 * width
-    start = late // (2 * turn.shape[0]) * 2 * turn.shape[0]
+    start = late // (2 * half) * 2 * half
     scales = (enc_scale, proc_scale, node_scale)
-    early_shape = ((narrow, (10 * width - start) // (2 * narrow), width), BF)
+    count = (10 * width - start) // (2 * narrow)
+    early_shape = ((narrow, 2, -(-count // 16) * 16, width), BF)
     swap = [(i, i ^ 1) for i in range(wide)]
-    mesh_out, kept, sent = call(
-        functools.partial(mesh_gradients, scales, start, half),
-        [h0, unit, w_node_out, cotangent, d_node, d_agg, agg, zeta, dst_sum, total, a0, d_mesh]
-        + [gpe, turn],
-        [block, early_shape, early_shape],
-        [square] * 7,
-        scalar=core.reshape(1),
-        flops=32 * rows * width * width,
-    )
-    came = lax.ppermute(sent, "wide", swap)
-    early = (kept.astype(F32) + came.astype(F32)).astype(BF)
-    early = lax.psum_scatter(early, "narrow", scatter_dimension=0, tiled=True)
+    mesh_out, mesh_grad, returning, early = call(
+        functools.partial(mesh_backward, scales, start, half),
+        [s_own, from_after, from_before, w_proc_src, d_node, w_node_self, dst_sum, w_proc_dst]
+        + [cotangent, w_enc_out, received, h0, a0, agg, d_agg, zeta, unit, w_node_out, gpe, turn],
+        [block, ((rows, width), F32), ((slots, width), BF), early_shape],
+        [((256, width), BF)] + [square] * 7,
+        cut={10: (width, LANE)},
+        flops=44 * rows * width * width,
+    )
+    early = lax.psum_scatter(early, "narrow", scatter_dimension=0, tiled=True)[0]
     returned = lax.all_to_all(
         returning.reshape(devices, capacity, width),
         ("wide", "narrow"),
@@ -511,21 +516,27 @@
     )
     came = lax.ppermute(sent, "wide", swap)
     last = (kept.astype(F32) + came.astype(F32)).astype(BF)
+    early, last = lax.optimization_barrier((early, last))
+    sent = lax.dynamic_index_in_dim(early, 1 - core, 0, keepdims=False)
+    came = lax.ppermute(sent, "wide", swap)
     last = lax.all_to_all(last, "narrow", split_axis=0, concat_axis=0, tiled=True)
     last = jnp.sum(last.astype(F32), axis=0)[: near * chunk]
-    early = jnp.pad(early[0], ((start // (2 * narrow), 0), (0, 0)))
-    early = early.reshape(far, near * chunk, width)
+    early = lax.dynamic_index_in_dim(early, core, 0, keepdims=False).astype(F32)
+    early = (early + came.astype(F32))[:count]
+    rest = (10 * width - near * far * 2 * half // far) // (2 * narrow)
+    last += jnp.pad(early[rest:], ((near * chunk - (count - rest), 0), (0, 0)))
+    both = jnp.concatenate([last, early[:rest]], axis=0).astype(BF)
+    both = both.reshape(far, near * chunk, width)
     x = lax.axis_index("wide") // (2 * near)
 
     def toward(j):
-        to = lax.rem(x + j, far)
-        part = lax.dynamic_index_in_dim(early, to, 0, keepdims=False).astype(F32)
-        return (part + jnp.where(to == 0, last, 0.0)).astype(BF)
-
-    both = toward(0).astype(F32)
+        return lax.dynamic_index_in_dim(both, lax.rem(x + j, far), 0, keepdims=False)
+
+    total = toward(0).astype(F32)
     for j in range(1, far):
         ring = [(i, (i + j * 2 * near) % wide) for i in range(wide)]
-        both += lax.ppermute(toward(j), "wide", ring).astype(F32)
+        total += lax.ppermute(toward(j), "wide", ring).astype(F32)
+    both = total
     both = lax.all_to_all(
         both.astype(BF).reshape(near, chunk, width),
         "wide",

time: 225 us -> 223 us (level)
  blocking collectives: 102 us -> 68.5 us
  waiting for transfers between devices: 38.6 us -> 59.3 us
  starting transfers between devices: 9.51 us -> 27.9 us
  other arithmetic: 6.15 us -> 2.54 us
  Pallas kernels: 41.5 us -> 38.4 us
    all_to_all x1 -> x0, blocking collectives: 38.1 us -> none  [on_device(): lax.all_to_all(returning.reshape(devices, capacity, width), ('wide', 'nar...]
    all_to_all x0 -> x1, waiting for transfers between devices: none -> 32 us  [on_device(): lax.all_to_all(returning.reshape(devices, capacity, width), ('wide', 'nar...]
    all_to_all x0 -> x1, starting transfers between devices: none -> 6.49 us  [on_device(): lax.all_to_all(returning.reshape(devices, capacity, width), ('wide', 'nar...]
    ppermute x1, starting transfers between devices: 0.08 us -> 5.1 us  [on_device(): from_after = lax.ppermute(s_before, 'wide', down)]
    ppermute x1, starting transfers between devices: 0.08 us -> 5.05 us  [on_device(): p_after = lax.ppermute(p_src, 'wide', down)]
    ppermute x2, waiting for transfers between devices: 6.93 us -> 2.29 us  [on_device(): came = lax.ppermute(sent, 'wide', swap)]
    all_to_all x1, blocking collectives: 12.2 us -> 16.6 us  [on_device(): lax.all_to_all(both.astype(BF).reshape(near, chunk, width), 'wide', split...]
    convert_element_type x2 -> x0, other arithmetic: 3.8 us -> none  [the longest x1 3.68 us: on_device(): early = (kept.astype(F32) + came.astype(F32)).astype(BF)]
  transfers between devices with their start and end apart: 11 -> 12, of which waited for: 8 -> 8; matrix products, arithmetic and copies ran while one was open for 2% -> 3% of each run, Pallas kernels for 3% -> 3%
where the time goes in v6:
time: 223 us; the launch traced here: 222 us
  blocking collectives  68.5 us (31%)
  waiting for transfers between devices  59.3 us (27%)
  Pallas kernels  38.4 us (17%)
  starting transfers between devices  27.9 us (13%)
  between operations  14.3 us (6%)
  local copies, waits for them, and re-layouts  10.7 us (5%)
  other arithmetic  2.54 us (1%)
    all_to_all x1, blocking collectives, on_device(): lax.all_to_all(payload.reshape(devices, capacity, width + LANE), ('wide',...  51.9 us
    pallas_call x5, Pallas kernels, call(): pl.pallas_call(kernel, in_specs=[pl.BlockSpec(memory_space=pltpu.SMEM)] *...  38.4 us
    all_to_all x1, waiting for transfers between devices, on_device(): lax.all_to_all(returning.reshape(devices, capacity, width), ('wide', 'nar...  32 us
    all_to_all x1, blocking collectives, on_device(): lax.all_to_all(both.astype(BF).reshape(near, chunk, width), 'wide', split...  16.6 us
    all_to_all x1, waiting for transfers between devices, on_device(): lax.all_to_all(last, 'narrow', split_axis=0, concat_axis=0, tiled=True)  9.56 us
    all_to_all x1, starting transfers between devices, on_device(): lax.all_to_all(returning.reshape(devices, capacity, width), ('wide', 'nar...  6.49 us
    ppermute x3, starting transfers between devices, on_device(): total += lax.ppermute(toward(j), 'wide', ring).astype(F32)  5.68 us
    all_to_all x1, starting transfers between devices, on_device(): lax.all_to_all(last, 'narrow', split_axis=0, concat_axis=0, tiled=True)  5.31 us
  transfers between devices with their start and end apart: 12, of which 8 were waited for; matrix products, arithmetic and copies ran while one was open for 3% of the time, Pallas kernels for 3%

profile of v6, /device:TPU:8, one launch (start us, length us, event | category | flops | bytes accessed | tf_op | source)
XLA Modules:
  0.0 221.6 jit_solution(16119438110784367055)
XLA Ops:
  7.2 0.0 reduce-scatter.2.cloned.1.call-start
  7.2 4.7 %shard_map.228 = (bf16[1024,640]{1,0:T(8,128)(2,1)}, bf16[512,512]{1,0:T(8,128)(2,1)}, s32[1,512]{1,0:T(1,128)}) custom-call(s32[1,512]{1,0:T(1,128)} %bitcast.24, s32[1,512]{1,0:T(1,128)} %bitcast.25, s32[1,512]{1,0:T(1,128)} %bitcast.26, bf16[512,512]{1,0:T(8,128)(2,1)} %refs_6_.5, bf16[512,512]{1,0:T(8,128)(2,1)} %refs_5_.5, bf16[512,512]{1,0:T(8,128)(2,1)} %refs_5_.3, ...), custom_call_target="tpu_custom_call" | custom-call | bytes 2103296 | tf_op jit(solution)/shard_map/pallas_call | solution.py:363
  11.9 2.6 %reshape.56 = bf16[256,4,640]{2,1,0:T(4,128)(2,1)S(1)} reshape(bf16[1024,640]{1,0:T(8,128)(2,1)} %get-tuple-element.29) | data formatting | bytes 2621440 | tf_op jit(solution)/shard_map/reshape | solution.py:428
  14.5 51.9 %all_to_all.20 = bf16[256,4,640]{2,1,0:T(4,128)(2,1)S(1)} all-to-all(bf16[256,4,640]{2,1,0:T(4,128)(2,1)S(1)} %reshape.56), channel_id=1, replica_groups=mesh['wide'=64,'narrow'=4] {'wide','narrow'}, dimensions={0} | all-to-all | bytes 2621440 | tf_op jit(solution)/shard_map/all_to_all | solution.py:427
  66.4 1.2 reshape.57.refs_0_.refs_10_
  67.7 3.5 %shard_map.229 = (bf16[160,512]{1,0:T(8,128)(2,1)}, bf16[160,512]{1,0:T(8,128)(2,1)}, bf16[160,512]{1,0:T(8,128)(2,1)}) custom-call(bf16[1024,640]{1,0:T(8,128)(2,1)} %reshape.57.refs_0_.refs_10_, bf16[512,512]{1,0:T(8,128)(2,1)} %refs_9_.3, bf16[160,512]{1,0:T(8,128)(2,1)} %refs_2_.1, bf16[512,512]{1,0:T(8,128)(2,1)} %refs_3_.5), custom_call_target="tpu_custom_call" | custom-call | bytes 2523136 | tf_op jit(solution)/shard_map/pallas_call | solution.py:363
  71.2 0.1 collective-permute-start
  71.3 5.1 %collective-permute-start.1 = (bf16[160,512]{1,0:T(8,128)(2,1)}, bf16[160,512]{1,0:T(8,128)(2,1)S(1)}, u32[]{:S(2)}, u32[]{:S(2)}) collective-permute-start(bf16[160,512]{1,0:T(8,128)(2,1)} %get-tuple-element.30.refs_3_), channel_id=1, source_target_pairs={{4,0},{8,4},{12,8},{16,12},{20,16},{24,20},{28,24},{32,28},{36,32}... | collective-permute-start | bytes 491528 | tf_op jit(solution)/shard_map/ppermute | solution.py:442
  76.3 0.6 reshape.51.refs_0_
  76.9 0.6 reshape.52.refs_1_
  77.5 2.0 collective-permute-done.refs_2_
  79.5 0.0 collective-permute-done.1.refs_4_
  79.5 0.7 copy-done.6
  80.2 0.1 copy-done.7
  80.2 13.3 %shard_map.230 = (bf16[160,512]{1,0:T(8,128)(2,1)}, bf16[160,512]{1,0:T(8,128)(2,1)}, bf16[160,512]{1,0:T(8,128)(2,1)}, bf16[160,512]{1,0:T(8,128)(2,1)}, bf16[1...) custom-call(s32[5,256]{1,0:T(8,128)} %reshape.51.refs_0_, ...), custom_call_target="tpu_custom_call" | custom-call | flops 4026531840 | bytes 5285888 | tf_op jit(solution)/shard_map/pallas_call | solution.py:363
  93.5 5.1 %collective-permute-start.2 = (bf16[160,512]{1,0:T(8,128)(2,1)}, bf16[160,512]{1,0:T(8,128)(2,1)S(1)}, u32[]{:S(2)}, u32[]{:S(2)}) collective-permute-start(bf16[160,512]{1,0:T(8,128)(2,1)} %get-tuple-element.33), channel_id=1, source_target_pairs={{4,0},{8,4},{12,8},{16,12},{20,16},{24,20},{28,24},{32,28},{36,32}... | collective-permute-start | bytes 491528 | tf_op jit(solution)/shard_map/ppermute | solution.py:475
  98.6 0.0 collective-permute-start.3
  98.6 3.1 %collective-permute-done.2.refs_1_ = bf16[160,512]{1,0:T(8,128)(2,1)S(1)} collective-permute-done((bf16[160,512]{1,0:T(8,128)(2,1)}, bf16[160,512]{1,0:T(8,128)(2,1)S(1)}, u32[]{:S(2)}, u32[]{:S(2)}) %collective-permute-start.2) | collective-permute-done | bytes 163872 | tf_op jit(solution)/shard_map/ppermute | solution.py:475
  101.8 5.1 %collective-permute-done.3.refs_2_ = bf16[160,512]{1,0:T(8,128)(2,1)S(1)} collective-permute-done((bf16[160,512]{1,0:T(8,128)(2,1)}, bf16[160,512]{1,0:T(8,128)(2,1)S(1)}, u32[]{:S(2)}, u32[]{:S(2)}) %collective-permute-start.3) | collective-permute-done | bytes 163872 | tf_op jit(solution)/shard_map/ppermute | solution.py:476
  106.9 0.7 copy-done.5
  107.6 10.3 %shard_map.231 = (bf16[160,512]{1,0:T(8,128)(2,1)}, f32[160,512]{1,0:T(8,128)}, bf16[1024,512]{1,0:T(8,128)(2,1)}, bf16[4,2,528,512]{3,2,1,0:T(8,128)(2,1)}) custom-call(bf16[160,512]{1,0:T(8,128)(2,1)} %get-tuple-element.32.refs_0_, bf16[160,512]{1,0:T(8,128)(2,1)} %copy-done.4, bf16[160,512]{1,0:T(8,128)(2,1)} %copy-done.5, bf16[512,512]{1,0:T(8,128)(2,1)} %refs_3_.5, ...), custom_call_target="tpu_custom_call" | custom-call | flops 1845493760 | bytes 6627328 | tf_op jit(solution)/shard_map/pallas_call | solution.py:363
  117.9 0.0 copy-start.1
  117.9 0.0 reduce-scatter.2.cloned.1.call-update
  117.9 1.2 copy-done.1
  119.1 1.1 reshape.59
  120.2 6.5 %all-to-all-start.1 = ((bf16[256,4,512]{2,1,0:T(4,128)(2,1)}), bf16[256,4,512]{2,1,0:T(4,128)(2,1)S(1)}, u32[]{:S(2)}, u32[]{:S(2)}) async-start(bf16[256,4,512]{2,1,0:T(4,128)(2,1)} %reshape.59), calls=%async_computation.1 | async-start | bytes 2097152 | tf_op jit(solution)/shard_map/all_to_all | solution.py:500
  126.7 32.0 %all-to-all-done.1 = bf16[256,4,512]{2,1,0:T(4,128)(2,1)S(1)} async-done(((bf16[256,4,512]{2,1,0:T(4,128)(2,1)}), bf16[256,4,512]{2,1,0:T(4,128)(2,1)S(1)}, u32[]{:S(2)}, u32[]{:S(2)}) %all-to-all-start.1) | async-done | bytes 1048608 | tf_op jit(solution)/shard_map/all_to_all | solution.py:500
  158.7 1.1 reshape.60.refs_3_
  159.9 6.6 %shard_map.232 = (f32[512,512]{1,0:T(8,128)}, bf16[4,160,512]{2,1,0:T(8,128)(2,1)}, bf16[4,160,512]{2,1,0:T(8,128)(2,1)}) custom-call(s32[1]{0:T(128)} %bitcast.3.refs_0_, s32[1,512]{1,0:T(1,128)} %get-tuple-element.44.refs_1_, s32[1,512]{1,0:T(1,128)} %bitcast.27, bf16[1024,512]{1,0:T(8,128)(2,1)} %reshape.60.refs_3_, ...), custom_call_target="tpu_custom_call" | custom-call | flops 1073741824 | bytes 3354624 | tf_op jit(solution)/shard_map/pallas_call | solution.py:363
  166.5 0.1 collective-permute-start.4
  166.6 2.3 %collective-permute-done.4 = bf16[4,160,512]{2,1,0:T(8,128)(2,1)S(1)} collective-permute-done((bf16[4,160,512]{2,1,0:T(8,128)(2,1)}, bf16[4,160,512]{2,1,0:T(8,128)(2,1)S(1)}, u32[]{:S(2)}, u32[]{:S(2)}) %collective-permute-start.4) | collective-permute-done | bytes 655392 | tf_op jit(solution)/shard_map/ppermute | solution.py:517
  168.9 2.1 add_convert_fusion
  171.0 5.3 %all-to-all-start.2 = ((bf16[4,160,512]{2,1,0:T(8,128)(2,1)}), bf16[4,160,512]{2,1,0:T(8,128)(2,1)S(1)}, u32[]{:S(2)}, u32[]{:S(2)}) async-start(bf16[4,160,512]{2,1,0:T(8,128)(2,1)} %add_convert_fusion), calls=%async_computation.3 | async-start | bytes 1310720 | tf_op jit(solution)/shard_map/all_to_all | solution.py:522
  176.3 0.1 collective-permute-start.5
  176.5 9.6 %all-to-all-done.2 = bf16[4,160,512]{2,1,0:T(8,128)(2,1)S(1)} async-done(((bf16[4,160,512]{2,1,0:T(8,128)(2,1)}), bf16[4,160,512]{2,1,0:T(8,128)(2,1)S(1)}, u32[]{:S(2)}, u32[]{:S(2)}) %all-to-all-start.2) | async-done | bytes 655392 | tf_op jit(solution)/shard_map/all_to_all | solution.py:522
  186.1 0.1 convert_reduce_fusion
  186.1 0.0 collective-permute-done.5
  186.2 0.2 convert_add_fusion
  186.3 0.1 slice.15
  186.6 1.6 collective-permute-start.6
  188.1 2.7 %collective-permute-start.7 = (bf16[160,512]{1,0:T(8,128)(2,1)S(1)}, bf16[160,512]{1,0:T(8,128)(2,1)S(1)}, u32[]{:S(2)}, u32[]{:S(2)}) collective-permute-start(bf16[160,512]{1,0:T(8,128)(2,1)S(1)} %get-tuple-element.56), channel_id=1, source_target_pairs={{0,128},{4,132},{8,136},{12,140},{16,144},{20,148},{24,152},{28,15... | collective-permute-start | bytes 491528 | tf_op jit(solution)/shard_map/ppermute | solution.py:538
  190.8 1.5 collective-permute-start.8
  192.2 2.2 collective-permute-done.6
  194.4 3.0 %collective-permute-done.7 = bf16[160,512]{1,0:T(8,128)(2,1)S(1)} collective-permute-done((bf16[160,512]{1,0:T(8,128)(2,1)S(1)}, bf16[160,512]{1,0:T(8,128)(2,1)S(1)}, u32[]{:S(2)}, u32[]{:S(2)}) %collective-permute-start.7) | collective-permute-done | bytes 163872 | tf_op jit(solution)/shard_map/ppermute | solution.py:538
  197.4 0.0 collective-permute-done.8
  197.4 0.1 fusion.2
  197.6 16.6 %all_to_all.21 = bf16[8,20,512]{2,1,0:T(8,128)(2,1)S(1)} all-to-all(bf16[8,20,512]{2,1,0:T(8,128)(2,1)S(1)} %reshape.61), channel_id=1, replica_groups={{0,8,16,24,32,40,48,56},{4,12,20,28,36,44,52,60},{64,72,80,88,96,104,11..., dimensions={0} | all-to-all | bytes 327680 | tf_op jit(solution)/shard_map/all_to_all | solution.py:540
  214.2 0.6 reshape.62
  (19 shorter events, 0.3 us)
Async XLA Ops:
  7.2 163.8 %reduce-scatter.2.cloned.1.call-start = ((), (), s32[]{:S(2)}) async-start(), calls=%async_computation.5 | async-start | bytes 5406720 | tf_op jit(solution)/shard_map/reduce_scatter | solution.py:499
  67.7 8.6 %copy-start.2 = (s32[1280]{0:T(1024)S(1)}, s32[1280]{0:T(1024)}, u32[]{:S(2)}) copy-start(s32[1280]{0:T(1024)} %param.28) | copy-start | bytes 15364
  67.7 9.2 %copy-start.3 = (s32[1280]{0:T(1024)S(1)}, s32[1280]{0:T(1024)}, u32[]{:S(2)}) copy-start(s32[1280]{0:T(1024)} %param.29) | copy-start | bytes 15364
  71.2 8.4 %collective-permute-start = (bf16[160,512]{1,0:T(8,128)(2,1)}, bf16[160,512]{1,0:T(8,128)(2,1)S(1)}, u32[]{:S(2)}, u32[]{:S(2)}) collective-permute-start(bf16[160,512]{1,0:T(8,128)(2,1)} %get-tuple-element.30.refs_3_), channel_id=1, source_target_pairs={{0,4},{4,8},{8,12},{12,16},{16,20},{20,24},{24,28},{28,32},{32,36}... | collective-permute-start | bytes 491528 | tf_op jit(solution)/shard_map/ppermute | solution.py:441
  71.3 8.3 %collective-permute-start.1 = (bf16[160,512]{1,0:T(8,128)(2,1)}, bf16[160,512]{1,0:T(8,128)(2,1)S(1)}, u32[]{:S(2)}, u32[]{:S(2)}) collective-permute-start(bf16[160,512]{1,0:T(8,128)(2,1)} %get-tuple-element.30.refs_3_), channel_id=1, source_target_pairs={{4,0},{8,4},{12,8},{16,12},{20,16},{24,20},{28,24},{32,28},{36,32}... | collective-permute-start | bytes 491528 | tf_op jit(solution)/shard_map/ppermute | solution.py:442
  79.5 0.7 copy-start.6
  79.5 0.7 copy-start.7
  93.5 8.3 %collective-permute-start.2 = (bf16[160,512]{1,0:T(8,128)(2,1)}, bf16[160,512]{1,0:T(8,128)(2,1)S(1)}, u32[]{:S(2)}, u32[]{:S(2)}) collective-permute-start(bf16[160,512]{1,0:T(8,128)(2,1)} %get-tuple-element.33), channel_id=1, source_target_pairs={{4,0},{8,4},{12,8},{16,12},{20,16},{24,20},{28,24},{32,28},{36,32}... | collective-permute-start | bytes 491528 | tf_op jit(solution)/shard_map/ppermute | solution.py:475
  98.6 8.3 %collective-permute-start.3 = (bf16[160,512]{1,0:T(8,128)(2,1)}, bf16[160,512]{1,0:T(8,128)(2,1)S(1)}, u32[]{:S(2)}, u32[]{:S(2)}) collective-permute-start(bf16[160,512]{1,0:T(8,128)(2,1)} %get-tuple-element.34), channel_id=1, source_target_pairs={{0,4},{4,8},{8,12},{12,16},{16,20},{20,24},{24,28},{28,32},{32,36}... | collective-permute-start | bytes 491528 | tf_op jit(solution)/shard_map/ppermute | solution.py:476
  101.8 5.1 %copy-start.4 = (bf16[160,512]{1,0:T(8,128)(2,1)}, bf16[160,512]{1,0:T(8,128)(2,1)S(1)}, u32[]{:S(2)}) copy-start(bf16[160,512]{1,0:T(8,128)(2,1)S(1)} %collective-permute-done.2.refs_1_) | copy-start | bytes 491524
  106.9 0.7 copy-start.5
  117.9 1.2 copy-start.1
  120.2 38.5 %all-to-all-start.1 = ((bf16[256,4,512]{2,1,0:T(4,128)(2,1)}), bf16[256,4,512]{2,1,0:T(4,128)(2,1)S(1)}, u32[]{:S(2)}, u32[]{:S(2)}) async-start(bf16[256,4,512]{2,1,0:T(4,128)(2,1)} %reshape.59), calls=%async_computation.1 | async-start | bytes 2097152 | tf_op jit(solution)/shard_map/all_to_all | solution.py:500
  166.5 2.4 %collective-permute-start.4 = (bf16[4,160,512]{2,1,0:T(8,128)(2,1)}, bf16[4,160,512]{2,1,0:T(8,128)(2,1)S(1)}, u32[]{:S(2)}, u32[]{:S(2)}) collective-permute-start(bf16[4,160,512]{2,1,0:T(8,128)(2,1)} %get-tuple-element.50), channel_id=1, source_target_pairs={{0,4},{4,0},{8,12},{12,8},{16,20},{20,16},{24,28},{28,24},{32,36},... | collective-permute-start | bytes 1966088 | tf_op jit(solution)/shard_map/ppermute | solution.py:517
  171.0 5.3 %copy-start = (bf16[1,2,528,512]{3,2,1,0:T(8,128)(2,1)S(1)}, bf16[1,2,528,512]{3,2,1,0:T(8,128)(2,1)}, u32[]{:S(2)}) copy-start(bf16[1,2,528,512]{3,2,1,0:T(8,128)(2,1)} %reduce-scatter.2.cloned.1.call-done) | copy-start | bytes 3244036
  171.0 15.1 %all-to-all-start.2 = ((bf16[4,160,512]{2,1,0:T(8,128)(2,1)}), bf16[4,160,512]{2,1,0:T(8,128)(2,1)S(1)}, u32[]{:S(2)}, u32[]{:S(2)}) async-start(bf16[4,160,512]{2,1,0:T(8,128)(2,1)} %add_convert_fusion), calls=%async_computation.3 | async-start | bytes 1310720 | tf_op jit(solution)/shard_map/all_to_all | solution.py:522
  176.3 9.8 %collective-permute-start.5 = (bf16[528,512]{1,0:T(8,128)(2,1)S(1)}, bf16[528,512]{1,0:T(8,128)(2,1)S(1)}, u32[]{:S(2)}, u32[]{:S(2)}) collective-permute-start(bf16[528,512]{1,0:T(8,128)(2,1)S(1)} %dynamic-slice_bitcast_fusion), channel_id=1, source_target_pairs={{0,4},{4,0},{8,12},{12,8},{16,20},{20,16},{24,28},{28,24},{32,36},... | collective-permute-start | bytes 1622024 | tf_op jit(solution)/shard_map/ppermute | solution.py:521
  186.6 7.9 %collective-permute-start.6 = (bf16[160,512]{1,0:T(8,128)(2,1)S(1)}, bf16[160,512]{1,0:T(8,128)(2,1)S(1)}, u32[]{:S(2)}, u32[]{:S(2)}) collective-permute-start(bf16[160,512]{1,0:T(8,128)(2,1)S(1)} %get-tuple-element.54), channel_id=1, source_target_pairs={{0,64},{4,68},{8,72},{12,76},{16,80},{20,84},{24,88},{28,92},{32,9... | collective-permute-start | bytes 491528 | tf_op jit(solution)/shard_map/ppermute | solution.py:538
  188.1 9.3 %collective-permute-start.7 = (bf16[160,512]{1,0:T(8,128)(2,1)S(1)}, bf16[160,512]{1,0:T(8,128)(2,1)S(1)}, u32[]{:S(2)}, u32[]{:S(2)}) collective-permute-start(bf16[160,512]{1,0:T(8,128)(2,1)S(1)} %get-tuple-element.56), channel_id=1, source_target_pairs={{0,128},{4,132},{8,136},{12,140},{16,144},{20,148},{24,152},{28,15... | collective-permute-start | bytes 491528 | tf_op jit(solution)/shard_map/ppermute | solution.py:538
  190.8 6.6 %collective-permute-start.8 = (bf16[160,512]{1,0:T(8,128)(2,1)S(1)}, bf16[160,512]{1,0:T(8,128)(2,1)S(1)}, u32[]{:S(2)}, u32[]{:S(2)}) collective-permute-start(bf16[160,512]{1,0:T(8,128)(2,1)S(1)} %get-tuple-element.55), channel_id=1, source_target_pairs={{0,192},{4,196},{8,200},{12,204},{16,208},{20,212},{24,216},{28,22... | collective-permute-start | bytes 491528 | tf_op jit(solution)/shard_map/ppermute | solution.py:538
Sparse Core Ops, SparseCore 0:
  118.1 52.8 reduce-scatter.1

commit v7 on v6

--- a/solution.py
+++ b/solution.py
@@ -12,6 +12,7 @@
 F32 = jnp.float32
 I32 = jnp.int32
 LANE = 128
+STEP = 640
 
 
 def dot(left, right):
@@ -51,7 +52,7 @@
     capacity, tdev_ref, trow_ref, src_ref, grid_ref, edge_ref, we_ref, wg_ref, out_ref, sg_ref, slot_ref
 ):
     edges, width = edge_ref.buffer.shape
-    slots = out_ref.buffer.shape[0]
+    slots = out_ref.buffer.shape[0] * capacity
     tdev = tdev_ref.get()[...]
     member = same_t(tdev, slots // capacity)
     before = lax.broadcasted_iota(I32, (edges, edges), 0) < lax.broadcasted_iota(
@@ -73,14 +74,15 @@
     step = 256
     for at in range(0, slots, step):
         place = same_t(slot, step, at)
-        out_ref.buffer[pl.ds(at, step), :] = dot(place, payload).astype(BF)
+        value = dot(place, payload).reshape(step // capacity, capacity, payload.shape[1])
+        out_ref.buffer[pl.ds(at // capacity, step // capacity)] = value.astype(BF)
 
 
 def mesh_forward(recv_ref, wout_ref, static_ref, wsrc_ref, h0_ref, a0_ref, psrc_ref):
     rows, width = static_ref.buffer.shape
-    recv = recv_ref.get()
-    pick = same(recv[:, width:].astype(F32), 256, 1)
-    a0 = dot_lt(pick, recv[:, :width])[:rows].astype(BF)
+    recv = recv_ref.get()[...].astype(F32).reshape(-1, recv_ref.buffer.shape[2])
+    pick = same(recv[:, width:], 256, 1)
+    a0 = dot_lt(pick, recv[:, :width].astype(BF))[:rows].astype(BF)
     a0_ref.buffer[...] = a0
     a0_ref.send()
     h0 = (static_ref.get()[...].astype(F32) + dot(a0, wout_ref.get()[...])).astype(BF)
@@ -91,11 +93,12 @@
 
 def processor(
     proc_scale,
+    core_ref,
     msrc_ref,
     mtgt_ref,
-    pb_ref,
+    mate_ref,
     po_ref,
-    pa_ref,
+    other_ref,
     h0_ref,
     wdst_ref,
     we_ref,
@@ -105,9 +108,9 @@
     wna_ref,
     wno_ref,
     cot_ref,
-    sb_ref,
+    smate_ref,
     so_ref,
-    sa_ref,
+    sother_ref,
     dst_ref,
     unit_ref,
     dnode_ref,
@@ -126,14 +129,15 @@
     rows = h0_ref.buffer.shape[0]
     reach = table.shape[0]
     first = reach - 256
-    step = 256
-    steps = edges // step
+    steps, step = msrc_ref.buffer.shape
     h0 = h0_ref.get()[...]
     table[pl.ds(3 * rows, reach - 3 * rows), :] = jnp.zeros((reach - 3 * rows, width), BF)
     table[pl.ds(first, rows), :] = dot(h0, wdst_ref.get()[...]).astype(BF)
-    table[pl.ds(0, rows), :] = pb_ref.get()[...]
+    even = core_ref[0] == 0
+    mate, other = mate_ref.get()[...], other_ref.get()[...]
+    table[pl.ds(0, rows), :] = jnp.where(even, other, mate)
     table[pl.ds(rows, rows), :] = po_ref.get()[...]
-    table[pl.ds(2 * rows, rows), :] = pa_ref.get()[...]
+    table[pl.ds(2 * rows, rows), :] = jnp.where(even, mate, other)
     zsum[...] = jnp.zeros_like(zsum)
     for ref in (msrc_ref, mtgt_ref, we_ref, mel_ref):
         ref.get()
@@ -184,8 +188,15 @@
         return carry
 
     lax.fori_loop(0, steps, behind, 0)
-    for ref, at in ((sa_ref, 2 * rows), (sb_ref, 0), (so_ref, rows), (dst_ref, first)):
-        ref.buffer[...] = back[pl.ds(at, rows), :].astype(BF)
+    lower = back[pl.ds(0, rows), :].astype(BF)
+    upper = back[pl.ds(2 * rows, rows), :].astype(BF)
+    for ref, value in (
+        (sother_ref, jnp.where(even, lower, upper)),
+        (smate_ref, jnp.where(even, upper, lower)),
+        (so_ref, back[pl.ds(rows, rows), :].astype(BF)),
+        (dst_ref, back[pl.ds(first, rows), :].astype(BF)),
+    ):
+        ref.buffer[...] = value
         ref.send()
     gpe_ref.buffer[...] = (gacc[...] * proc_scale).astype(BF)
 
@@ -264,10 +275,12 @@
     padded[pl.ds(rows, 256 - rows), :] = jnp.zeros((256 - rows, padded.shape[1]), BF)
     padded[pl.ds(0, rows), :] = dot_rt(d_mesh, wout_ref.get()[...]).astype(BF)
     tag = tag_ref.get()
-    step = 256
-    for at in range(0, ret_ref.buffer.shape[0], step):
-        pick = same(tag[pl.ds(at, step), :].astype(F32), 256, 1)
-        ret_ref.buffer[pl.ds(at, step), :] = dot(pick, padded[...]).astype(BF)
+    devices, capacity, width = ret_ref.buffer.shape
+    step = 256 // capacity
+    for at in range(0, devices, step):
+        pick = same(tag[pl.ds(at, step)].astype(F32).reshape(-1, LANE), 256, 1)
+        value = dot(pick, padded[...]).reshape(step, capacity, width)
+        ret_ref.buffer[pl.ds(at, step)] = value.astype(BF)
     ret_ref.send()
     h0 = h0_ref.get()[...]
     gps[...] = (dot_lt(h0, total) * proc_scale).astype(BF)
@@ -288,8 +301,9 @@
     enc_scale, half, core_ref, slot_ref, src_ref, ret_ref, sg_ref, edge_ref, grid_ref, wg_ref,
     turn_ref, out_ref, kept_ref, sent_ref, gee, geg,
 ):
-    chosen = same(columns(slot_ref.get()[...]), ret_ref.buffer.shape[0])
-    d_enc = (dot(chosen, ret_ref.get()[...]) * sg_ref.get()[...].astype(F32)).astype(BF)
+    returned = ret_ref.get()[...].astype(F32).reshape(-1, ret_ref.buffer.shape[2]).astype(BF)
+    chosen = same(columns(slot_ref.get()[...]), returned.shape[0])
+    d_enc = (dot(chosen, returned) * sg_ref.get()[...].astype(F32)).astype(BF)
     grid_sum = dot(same_t(src_ref.get()[...], grid_ref.buffer.shape[0]), d_enc).astype(BF)
     out_ref.buffer[...] = dot_rt(grid_sum, wg_ref.get()[...])
     out_ref.send()
@@ -340,7 +354,7 @@
     cut = cut or {}
     extra = int(scalar is not None)
     count, made = len(ins), len(outs)
-    held = [(one.shape[0], cut[i][1]) if i in cut else one.shape for i, one in enumerate(ins)]
+    held = [(*one.shape[:-1], cut[i][1]) if i in cut else one.shape for i, one in enumerate(ins)]
 
     def kernel(*refs):
         lead, refs = refs[:extra], refs[extra:]
@@ -349,7 +363,7 @@
         in_sem, out_sem = refs[:2]
         got = []
         for i in range(count):
-            part = source[i].at[:, pl.ds(*cut[i])] if i in cut else source[i]
+            part = source[i].at[:, :, pl.ds(*cut[i])] if i in cut else source[i]
             got.append(Inward(part, here[i], in_sem.at[i]))
         put = [Outward(there[i], target[i], out_sem.at[i]) for i in range(made)]
         body(*lead, *got, *put, *refs[2:])
@@ -422,35 +436,32 @@
             w_enc_edge,
             w_enc_grid,
         ],
-        [((slots, width + LANE), BF), ((edges, width), BF), ((1, edges), I32)],
+        [((devices, capacity, width + LANE), BF), ((edges, width), BF), ((1, edges), I32)],
     )
     received = lax.all_to_all(
-        payload.reshape(devices, capacity, width + LANE),
-        ("wide", "narrow"),
-        split_axis=0,
-        concat_axis=0,
-        tiled=True,
-    ).reshape(slots, width + LANE)
+        payload, ("wide", "narrow"), split_axis=0, concat_axis=0, tiled=True
+    )
     h0, a0, p_src = call(
         mesh_forward,
         [received, w_enc_out, mesh_static, w_proc_src],
         [((rows, width), BF)] * 3,
     )
-    up = [(i, (i + 1) % wide) for i in range(wide)]
-    down = [(j, i) for i, j in up]
-    p_before = lax.ppermute(p_src, "wide", up)
-    p_after = lax.ppermute(p_src, "wide", down)
+    swap = [(i, i ^ 1) for i in range(wide)]
+    cross = [(i, (i + (1 if i % 2 else -1)) % wide) for i in range(wide)]
+    p_other = lax.ppermute(p_src, "wide", cross)
+    p_mate = lax.ppermute(p_src, "wide", swap)
+    where = core.reshape(1)
     square = ((width, width), BF)
     block = ((rows, width), BF)
     reach = -(-3 * rows // LANE) * LANE + 256
-    s_before, s_own, s_after, dst_sum, unit, d_node, d_agg, agg, zeta, gpe = call(
+    s_mate, s_own, s_other, dst_sum, unit, d_node, d_agg, agg, zeta, gpe = call(
         functools.partial(processor, proc_scale),
         [
-            mesh_source.reshape(-1, 256),
-            mesh_target.reshape(-1, 256),
-            p_before,
+            mesh_source.reshape(-1, STEP),
+            mesh_target.reshape(-1, STEP),
+            p_mate,
             p_src,
-            p_after,
+            p_other,
             h0,
             w_proc_dst,
             w_proc_edge,
@@ -470,10 +481,11 @@
             ((reach, width), F32),
             ((width, width), F32),
         ],
+        scalar=where,
         flops=12 * mesh_edges * width * width,
     )
-    from_after = lax.ppermute(s_before, "wide", down)
-    from_before = lax.ppermute(s_after, "wide", up)
+    from_other = lax.ppermute(s_other, "wide", cross)
+    from_mate = lax.ppermute(s_mate, "wide", swap)
 
     chips = wide // 2
     chunk = 10 * width // devices
@@ -486,24 +498,19 @@
     scales = (enc_scale, proc_scale, node_scale)
     count = (10 * width - start) // (2 * narrow)
     early_shape = ((narrow, 2, -(-count // 16) * 16, width), BF)
-    swap = [(i, i ^ 1) for i in range(wide)]
     mesh_out, mesh_grad, returning, early = call(
         functools.partial(mesh_backward, scales, start, half),
-        [s_own, from_after, from_before, w_proc_src, d_node, w_node_self, dst_sum, w_proc_dst]
+        [s_own, from_mate, from_other, w_proc_src, d_node, w_node_self, dst_sum, w_proc_dst]
         + [cotangent, w_enc_out, received, h0, a0, agg, d_agg, zeta, unit, w_node_out, gpe, turn],
-        [block, ((rows, width), F32), ((slots, width), BF), early_shape],
+        [block, ((rows, width), F32), ((devices, capacity, width), BF), early_shape],
         [((256, width), BF)] + [square] * 7,
         cut={10: (width, LANE)},
         flops=44 * rows * width * width,
     )
     early = lax.psum_scatter(early, "narrow", scatter_dimension=0, tiled=True)[0]
     returned = lax.all_to_all(
-        returning.reshape(devices, capacity, width),
-        ("wide", "narrow"),
-        split_axis=0,
-        concat_axis=0,
-        tiled=True,
-    ).reshape(slots, width)
+        returning, ("wide", "narrow"), split_axis=0, concat_axis=0, tiled=True
+    )
     spread = -(-late // (2 * turn.shape[0])) * turn.shape[0] // narrow
     late_shape = ((narrow, spread, width), BF)
     grid_grad, kept, sent = call(
@@ -511,16 +518,16 @@
         [slot, source, returned, enc_sg, enc_edge_latent, grid_latent, w_enc_grid, turn],
         [((grid_rows, width), F32), late_shape, late_shape],
         [square, square],
-        scalar=core.reshape(1),
+        scalar=where,
         flops=8 * edges * width * width,
     )
     came = lax.ppermute(sent, "wide", swap)
     last = (kept.astype(F32) + came.astype(F32)).astype(BF)
+    last = lax.all_to_all(last, "narrow", split_axis=0, concat_axis=0, tiled=True)
+    last = jnp.sum(last.astype(F32), axis=0)[: near * chunk]
     early, last = lax.optimization_barrier((early, last))
     sent = lax.dynamic_index_in_dim(early, 1 - core, 0, keepdims=False)
     came = lax.ppermute(sent, "wide", swap)
-    last = lax.all_to_all(last, "narrow", split_axis=0, concat_axis=0, tiled=True)
-    last = jnp.sum(last.astype(F32), axis=0)[: near * chunk]
     early = lax.dynamic_index_in_dim(early, core, 0, keepdims=False).astype(F32)
     early = (early + came.astype(F32))[:count]
     rest = (10 * width - near * far * 2 * half // far) // (2 * narrow)

time: 223 us -> 211 us (0.946)
  blocking collectives: 68.5 us -> 103 us
  waiting for transfers between devices: 59.3 us -> 37.6 us
  starting transfers between devices: 27.9 us -> 9.06 us
  local copies, waits for them, and re-layouts: 10.7 us -> 5.68 us
    all_to_all x1 -> x2, blocking collectives: 51.9 us -> 91.1 us  [the longest x1 52.2 us: on_device(): lax.all_to_all(payload, ('wide', 'narrow'), split_axis=0, concat_axis=0,...]
    all_to_all x1 -> x0, waiting for transfers between devices: 32 us -> none  [on_device(): lax.all_to_all(returning.reshape(devices, capacity, width), ('wide', 'nar...]
    ppermute x4, starting transfers between devices: 10.2 us -> 0.55 us  [the longest x1 0.27 us: on_device(): from_other = lax.ppermute(s_other, 'wide', cross)]
    all_to_all x1 -> x0, starting transfers between devices: 6.49 us -> none  [on_device(): lax.all_to_all(returning.reshape(devices, capacity, width), ('wide', 'nar...]
    reshape x6 -> x2, local copies, waits for them, and re-layouts: 7.25 us -> 1.2 us  [the longest x1 0.6 us: on_device(): mesh_source.reshape(-1, STEP)]
    ppermute x4, waiting for transfers between devices: 10.3 us -> 15.3 us  [the longest x1 6.95 us: on_device(): from_other = lax.ppermute(s_other, 'wide', cross)]
    all_to_all x1, blocking collectives: 16.6 us -> 12.4 us  [on_device(): lax.all_to_all(both.astype(BF).reshape(near, chunk, width), 'wide', split...]
    ppermute x3, waiting for transfers between devices: 5.17 us -> 8.07 us  [on_device(): total += lax.ppermute(toward(j), 'wide', ring).astype(F32)]
  transfers between devices with their start and end apart: 12 -> 11, of which waited for: 8 -> 9; matrix products, arithmetic and copies ran while one was open for 3% -> 2% of each run, Pallas kernels for 3% -> 3%
where the time goes in v7:
time: 211 us; the launch traced here: 210 us
  blocking collectives  103 us (49%)
  waiting for transfers between devices  37.6 us (18%)
  Pallas kernels  37.1 us (18%)
  between operations  14.3 us (7%)
  starting transfers between devices  9.06 us (4%)
  local copies, waits for them, and re-layouts  5.68 us (3%)
  other arithmetic  2.59 us (1%)
    all_to_all x1, blocking collectives, on_device(): lax.all_to_all(payload, ('wide', 'narrow'), split_axis=0, concat_axis=0,...  52.2 us
    all_to_all x1, blocking collectives, on_device(): lax.all_to_all(returning, ('wide', 'narrow'), split_axis=0, concat_axis=0...  38.9 us
    pallas_call x5, Pallas kernels, call(): pl.pallas_call(kernel, in_specs=[pl.BlockSpec(memory_space=pltpu.SMEM)] *...  37.1 us
    all_to_all x1, blocking collectives, on_device(): lax.all_to_all(both.astype(BF).reshape(near, chunk, width), 'wide', split...  12.4 us
    all_to_all x1, waiting for transfers between devices, on_device(): lax.all_to_all(last, 'narrow', split_axis=0, concat_axis=0, tiled=True)  10 us
    ppermute x3, waiting for transfers between devices, on_device(): total += lax.ppermute(toward(j), 'wide', ring).astype(F32)  8.07 us
    ppermute x1, waiting for transfers between devices, on_device(): from_other = lax.ppermute(s_other, 'wide', cross)  6.95 us
    ppermute x1, waiting for transfers between devices, on_device(): p_other = lax.ppermute(p_src, 'wide', cross)  6.77 us
  transfers between devices with their start and end apart: 11, of which 9 were waited for; matrix products, arithmetic and copies ran while one was open for 2% of the time, Pallas kernels for 3%

profile of v7, /device:TPU:8, one launch (start us, length us, event | category | flops | bytes accessed | tf_op | source)
XLA Modules:
  0.0 209.8 jit_solution(11225283739932173182)
XLA Ops:
  7.2 0.0 reduce-scatter.2.cloned.1.call-start
  7.2 4.8 %shard_map.228 = (bf16[256,4,640]{2,1,0:T(4,128)(2,1)}, bf16[512,512]{1,0:T(8,128)(2,1)}, s32[1,512]{1,0:T(1,128)}) custom-call(s32[1,512]{1,0:T(1,128)} %bitcast.24, s32[1,512]{1,0:T(1,128)} %bitcast.25, s32[1,512]{1,0:T(1,128)} %bitcast.26, bf16[512,512]{1,0:T(8,128)(2,1)} %refs_6_.3, bf16[512,512]{1,0:T(8,128)(2,1)} %refs_5_.5, bf16[512,512]{1,0:T(8,128)(2,1)} %refs_5_.3, ...), custom_call_target="tpu_custom_call" | custom-call | bytes 2103296 | tf_op jit(solution)/shard_map/pallas_call | solution.py:377
  12.0 52.2 %all_to_all.20.refs_0_.refs_10_ = bf16[256,4,640]{2,1,0:T(4,128)(2,1)} all-to-all(bf16[256,4,640]{2,1,0:T(4,128)(2,1)} %get-tuple-element.29), channel_id=1, replica_groups=mesh['wide'=64,'narrow'=4] {'wide','narrow'}, dimensions={0} | all-to-all | bytes 2621440 | tf_op jit(solution)/shard_map/all_to_all | solution.py:441
  64.2 3.5 %shard_map.229 = (bf16[160,512]{1,0:T(8,128)(2,1)}, bf16[160,512]{1,0:T(8,128)(2,1)}, bf16[160,512]{1,0:T(8,128)(2,1)}) custom-call(bf16[256,4,640]{2,1,0:T(4,128)(2,1)} %all_to_all.20.refs_0_.refs_10_, bf16[512,512]{1,0:T(8,128)(2,1)} %refs_9_.3, bf16[160,512]{1,0:T(8,128)(2,1)} %refs_2_.1, bf16[512,512]{1,0:T(8,128)(2,1)} %refs_3_.5), custom_call_target="tpu_custom_call" | custom-call | bytes 2523136 | tf_op jit(solution)/shard_map/pallas_call | solution.py:377
  67.8 0.1 collective-permute-start
  67.9 0.1 collective-permute-start.1
  68.0 0.0 copy-done.2
  68.0 0.6 reshape.40.refs_1_
  68.6 0.0 copy-done.3
  68.6 0.6 reshape.41.refs_2_
  69.2 0.3 collective-permute-done.refs_3_
  69.5 6.8 %collective-permute-done.1.refs_5_ = bf16[160,512]{1,0:T(8,128)(2,1)S(1)} collective-permute-done((bf16[160,512]{1,0:T(8,128)(2,1)}, bf16[160,512]{1,0:T(8,128)(2,1)S(1)}, u32[]{:S(2)}, u32[]{:S(2)}) %collective-permute-start.1) | collective-permute-done | bytes 163872 | tf_op jit(solution)/shard_map/ppermute | solution.py:451
  76.2 0.0 copy-done.4
  76.2 0.7 copy-done.5
  76.9 11.5 %shard_map.230 = (bf16[160,512]{1,0:T(8,128)(2,1)}, bf16[160,512]{1,0:T(8,128)(2,1)}, bf16[160,512]{1,0:T(8,128)(2,1)}, bf16[160,512]{1,0:T(8,128)(2,1)}, bf16[1...) custom-call(s32[1]{0:T(128)} %bitcast.refs_0_, ...), custom_call_target="tpu_custom_call" | custom-call | flops 4026531840 | bytes 5285888 | tf_op jit(solution)/shard_map/pallas_call | solution.py:377
  88.4 0.1 collective-permute-start.2
  88.5 0.3 collective-permute-start.3
  88.8 1.3 collective-permute-done.2.refs_1_
  90.1 6.9 %collective-permute-done.3.refs_2_ = bf16[160,512]{1,0:T(8,128)(2,1)S(1)} collective-permute-done((bf16[160,512]{1,0:T(8,128)(2,1)}, bf16[160,512]{1,0:T(8,128)(2,1)S(1)}, u32[]{:S(2)}, u32[]{:S(2)}) %collective-permute-start.3) | collective-permute-done | bytes 163872 | tf_op jit(solution)/shard_map/ppermute | solution.py:487
  97.1 0.7 copy-done.7
  97.7 10.4 %shard_map.231 = (bf16[160,512]{1,0:T(8,128)(2,1)}, f32[160,512]{1,0:T(8,128)}, bf16[256,4,512]{2,1,0:T(4,128)(2,1)}, bf16[4,2,528,512]{3,2,1,0:T(8,128)(2,1)}) custom-call(bf16[160,512]{1,0:T(8,128)(2,1)} %get-tuple-element.32.refs_0_, bf16[160,512]{1,0:T(8,128)(2,1)} %copy-done.6, bf16[160,512]{1,0:T(8,128)(2,1)} %copy-done.7, bf16[512,512]{1,0:T(8,128)(2,1)} %refs_3_.5, ...), custom_call_target="tpu_custom_call" | custom-call | flops 1845493760 | bytes 6627328 | tf_op jit(solution)/shard_map/pallas_call | solution.py:377
  108.1 0.0 copy-start.1
  108.1 0.0 reduce-scatter.2.cloned.1.call-update
  108.1 1.2 copy-done.1
  109.3 38.9 %all_to_all.21.refs_3_ = bf16[256,4,512]{2,1,0:T(4,128)(2,1)} all-to-all(bf16[256,4,512]{2,1,0:T(4,128)(2,1)S(1)} %copy-done.1), channel_id=1, replica_groups=mesh['wide'=64,'narrow'=4] {'wide','narrow'}, dimensions={0} | all-to-all | bytes 2097152 | tf_op jit(solution)/shard_map/all_to_all | solution.py:511
  148.2 6.9 %shard_map.232 = (f32[512,512]{1,0:T(8,128)}, bf16[4,160,512]{2,1,0:T(8,128)(2,1)}, bf16[4,160,512]{2,1,0:T(8,128)(2,1)}) custom-call(s32[1]{0:T(128)} %bitcast.refs_0_, s32[1,512]{1,0:T(1,128)} %get-tuple-element.44.refs_1_, s32[1,512]{1,0:T(1,128)} %bitcast.27, bf16[256,4,512]{2,1,0:T(4,128)(2,1)} %all_to_all.21.refs_3_, ...), custom_call_target="tpu_custom_call" | custom-call | flops 1073741824 | bytes 3354624 | tf_op jit(solution)/shard_map/pallas_call | solution.py:377
  155.1 0.1 collective-permute-start.4
  155.2 2.3 %collective-permute-done.4 = bf16[4,160,512]{2,1,0:T(8,128)(2,1)S(1)} collective-permute-done((bf16[4,160,512]{2,1,0:T(8,128)(2,1)}, bf16[4,160,512]{2,1,0:T(8,128)(2,1)S(1)}, u32[]{:S(2)}, u32[]{:S(2)}) %collective-permute-start.4) | collective-permute-done | bytes 655392 | tf_op jit(solution)/shard_map/ppermute | solution.py:524
  157.5 2.1 %add_convert_fusion = bf16[4,160,512]{2,1,0:T(8,128)(2,1)} fusion(bf16[4,160,512]{2,1,0:T(8,128)(2,1)S(1)} %collective-permute-done.4, bf16[4,160,512]{2,1,0:T(8,128)(2,1)} %get-tuple-element.49), kind=kLoop, calls=%fused_computation.1 | loop fusion | flops 1310720 | bytes 1966080 | tf_op jit(solution)/shard_map/convert_element_type | solution.py:525
  159.6 4.7 %all-to-all-start.2 = ((bf16[4,160,512]{2,1,0:T(8,128)(2,1)}), bf16[4,160,512]{2,1,0:T(8,128)(2,1)S(1)}, u32[]{:S(2)}, u32[]{:S(2)}) async-start(bf16[4,160,512]{2,1,0:T(8,128)(2,1)} %add_convert_fusion), calls=%async_computation.3 | async-start | bytes 1310720 | tf_op jit(solution)/shard_map/all_to_all | solution.py:526
  164.3 10.0 %all-to-all-done.2 = bf16[4,160,512]{2,1,0:T(8,128)(2,1)S(1)} async-done(((bf16[4,160,512]{2,1,0:T(8,128)(2,1)}), bf16[4,160,512]{2,1,0:T(8,128)(2,1)S(1)}, u32[]{:S(2)}, u32[]{:S(2)}) %all-to-all-start.2) | async-done | bytes 655392 | tf_op jit(solution)/shard_map/all_to_all | solution.py:526
  174.4 0.1 convert_reduce_fusion
  174.5 0.0 reduce-scatter.2.cloned.1.call-done
  174.5 1.2 dynamic-slice_bitcast_fusion
  175.7 0.1 collective-permute-start.5
  175.8 1.9 collective-permute-done.5
  177.7 0.0 copy-done
  177.7 0.2 convert_add_fusion
  177.9 0.1 slice.15
  178.1 0.1 collective-permute-start.6
  178.2 2.3 %collective-permute-start.7 = (bf16[160,512]{1,0:T(8,128)(2,1)S(1)}, bf16[160,512]{1,0:T(8,128)(2,1)S(1)}, u32[]{:S(2)}, u32[]{:S(2)}) collective-permute-start(bf16[160,512]{1,0:T(8,128)(2,1)S(1)} %get-tuple-element.56), channel_id=1, source_target_pairs={{0,128},{4,132},{8,136},{12,140},{16,144},{20,148},{24,152},{28,15... | collective-permute-start | bytes 491528 | tf_op jit(solution)/shard_map/ppermute | solution.py:545
  180.5 1.2 collective-permute-start.8
  181.7 7.5 %collective-permute-done.6 = bf16[160,512]{1,0:T(8,128)(2,1)S(1)} collective-permute-done((bf16[160,512]{1,0:T(8,128)(2,1)S(1)}, bf16[160,512]{1,0:T(8,128)(2,1)S(1)}, u32[]{:S(2)}, u32[]{:S(2)}) %collective-permute-start.6) | collective-permute-done | bytes 163872 | tf_op jit(solution)/shard_map/ppermute | solution.py:545
  189.2 0.0 collective-permute-done.7
  189.2 0.6 collective-permute-done.8
  189.8 0.1 fusion.2
  189.9 12.4 %all_to_all.22 = bf16[8,20,512]{2,1,0:T(8,128)(2,1)S(1)} all-to-all(bf16[8,20,512]{2,1,0:T(8,128)(2,1)S(1)} %reshape.45), channel_id=1, replica_groups={{0,8,16,24,32,40,48,56},{4,12,20,28,36,44,52,60},{64,72,80,88,96,104,11..., dimensions={0} | all-to-all | bytes 327680 | tf_op jit(solution)/shard_map/all_to_all | solution.py:547
  202.3 0.6 reshape.46
  (14 shorter events, 0.2 us)
Async XLA Ops:
  7.2 167.3 %reduce-scatter.2.cloned.1.call-start = ((), (), s32[]{:S(2)}) async-start(), calls=%async_computation.5 | async-start | bytes 5406720 | tf_op jit(solution)/shard_map/reduce_scatter | solution.py:510
  64.2 3.8 %copy-start.2 = (s32[1280]{0:T(1024)S(1)}, s32[1280]{0:T(1024)}, u32[]{:S(2)}) copy-start(s32[1280]{0:T(1024)} %param.28) | copy-start | bytes 15364
  64.2 4.4 %copy-start.3 = (s32[1280]{0:T(1024)S(1)}, s32[1280]{0:T(1024)}, u32[]{:S(2)}) copy-start(s32[1280]{0:T(1024)} %param.29) | copy-start | bytes 15364
  67.8 1.7 collective-permute-start
  67.9 8.4 %collective-permute-start.1 = (bf16[160,512]{1,0:T(8,128)(2,1)}, bf16[160,512]{1,0:T(8,128)(2,1)S(1)}, u32[]{:S(2)}, u32[]{:S(2)}) collective-permute-start(bf16[160,512]{1,0:T(8,128)(2,1)} %get-tuple-element.30.refs_4_), channel_id=1, source_target_pairs={{0,252},{4,8},{8,4},{12,16},{16,12},{20,24},{24,20},{28,32},{32,28... | collective-permute-start | bytes 491528 | tf_op jit(solution)/shard_map/ppermute | solution.py:451
  69.5 6.8 %copy-start.4 = (bf16[160,512]{1,0:T(8,128)(2,1)}, bf16[160,512]{1,0:T(8,128)(2,1)S(1)}, u32[]{:S(2)}) copy-start(bf16[160,512]{1,0:T(8,128)(2,1)S(1)} %collective-permute-done.refs_3_) | copy-start | bytes 491524
  76.2 0.7 copy-start.5
  88.4 1.7 collective-permute-start.2
  88.5 8.5 %collective-permute-start.3 = (bf16[160,512]{1,0:T(8,128)(2,1)}, bf16[160,512]{1,0:T(8,128)(2,1)S(1)}, u32[]{:S(2)}, u32[]{:S(2)}) collective-permute-start(bf16[160,512]{1,0:T(8,128)(2,1)} %get-tuple-element.34), channel_id=1, source_target_pairs={{0,252},{4,8},{8,4},{12,16},{16,12},{20,24},{24,20},{28,32},{32,28... | collective-permute-start | bytes 491528 | tf_op jit(solution)/shard_map/ppermute | solution.py:487
  90.1 7.0 %copy-start.6 = (bf16[160,512]{1,0:T(8,128)(2,1)}, bf16[160,512]{1,0:T(8,128)(2,1)S(1)}, u32[]{:S(2)}) copy-start(bf16[160,512]{1,0:T(8,128)(2,1)S(1)} %collective-permute-done.2.refs_1_) | copy-start | bytes 491524
  97.0 0.7 copy-start.7
  108.1 1.2 copy-start.1
  155.1 2.4 %collective-permute-start.4 = (bf16[4,160,512]{2,1,0:T(8,128)(2,1)}, bf16[4,160,512]{2,1,0:T(8,128)(2,1)S(1)}, u32[]{:S(2)}, u32[]{:S(2)}) collective-permute-start(bf16[4,160,512]{2,1,0:T(8,128)(2,1)} %get-tuple-element.50), channel_id=1, source_target_pairs={{0,4},{4,0},{8,12},{12,8},{16,20},{20,16},{24,28},{28,24},{32,36},... | collective-permute-start | bytes 1966088 | tf_op jit(solution)/shard_map/ppermute | solution.py:524
  159.6 14.7 %all-to-all-start.2 = ((bf16[4,160,512]{2,1,0:T(8,128)(2,1)}), bf16[4,160,512]{2,1,0:T(8,128)(2,1)S(1)}, u32[]{:S(2)}, u32[]{:S(2)}) async-start(bf16[4,160,512]{2,1,0:T(8,128)(2,1)} %add_convert_fusion), calls=%async_computation.3 | async-start | bytes 1310720 | tf_op jit(solution)/shard_map/all_to_all | solution.py:526
  174.5 3.2 %copy-start = (bf16[1,2,528,512]{3,2,1,0:T(8,128)(2,1)S(1)}, bf16[1,2,528,512]{3,2,1,0:T(8,128)(2,1)}, u32[]{:S(2)}) copy-start(bf16[1,2,528,512]{3,2,1,0:T(8,128)(2,1)} %reduce-scatter.2.cloned.1.call-done) | copy-start | bytes 3244036
  175.7 2.0 collective-permute-start.5
  178.1 11.0 %collective-permute-start.6 = (bf16[160,512]{1,0:T(8,128)(2,1)S(1)}, bf16[160,512]{1,0:T(8,128)(2,1)S(1)}, u32[]{:S(2)}, u32[]{:S(2)}) collective-permute-start(bf16[160,512]{1,0:T(8,128)(2,1)S(1)} %get-tuple-element.54), channel_id=1, source_target_pairs={{0,64},{4,68},{8,72},{12,76},{16,80},{20,84},{24,88},{28,92},{32,9... | collective-permute-start | bytes 491528 | tf_op jit(solution)/shard_map/ppermute | solution.py:545
  178.2 11.0 %collective-permute-start.7 = (bf16[160,512]{1,0:T(8,128)(2,1)S(1)}, bf16[160,512]{1,0:T(8,128)(2,1)S(1)}, u32[]{:S(2)}, u32[]{:S(2)}) collective-permute-start(bf16[160,512]{1,0:T(8,128)(2,1)S(1)} %get-tuple-element.56), channel_id=1, source_target_pairs={{0,128},{4,132},{8,136},{12,140},{16,144},{20,148},{24,152},{28,15... | collective-permute-start | bytes 491528 | tf_op jit(solution)/shard_map/ppermute | solution.py:545
  180.5 9.3 %collective-permute-start.8 = (bf16[160,512]{1,0:T(8,128)(2,1)S(1)}, bf16[160,512]{1,0:T(8,128)(2,1)S(1)}, u32[]{:S(2)}, u32[]{:S(2)}) collective-permute-start(bf16[160,512]{1,0:T(8,128)(2,1)S(1)} %get-tuple-element.55), channel_id=1, source_target_pairs={{0,192},{4,196},{8,200},{12,204},{16,208},{20,212},{24,216},{28,22... | collective-permute-start | bytes 491528 | tf_op jit(solution)/shard_map/ppermute | solution.py:545
Sparse Core Ops, SparseCore 0:
  108.3 52.8 reduce-scatter.1

commit v8 on v7

--- a/solution.py
+++ b/solution.py
@@ -143,7 +143,7 @@
         ref.get()
 
     def ahead(i, carry):
-        at = pl.multiple_of(i * step, step)
+        at = i * step
         src = columns(msrc_ref.buffer[pl.ds(i, 1), :])
         tgt = columns(mtgt_ref.buffer[pl.ds(i, 1), :] + first)
         src = jnp.concatenate([src] * (reach // LANE), axis=1)
@@ -157,7 +157,8 @@
         zsum[...] += dot_lt(chosen[:, first:], act.astype(BF))
         return carry
 
-    lax.fori_loop(0, steps, ahead, 0)
+    for i in range(steps):
+        ahead(i, 0)
     zeta = zsum[pl.ds(0, rows), :].astype(BF)
     cot = cot_ref.get()[...]
     agg = dot(zeta, wpo_ref.get()[...]).astype(BF)
@@ -179,7 +180,7 @@
     gacc[...] = jnp.zeros_like(gacc)
 
     def behind(i, carry):
-        at = pl.multiple_of(i * step, step)
+        at = i * step
         chosen = hot[pl.ds(at, step), :]
         d_edge = dot(chosen[:, first:], table[pl.ds(first, 256), :])
         d_proc = (d_edge * sg[pl.ds(at, step), :].astype(F32)).astype(BF)
@@ -187,7 +188,8 @@
         gacc[...] += dot_lt(mel_ref.buffer[pl.ds(at, step), :], d_proc)
         return carry
 
-    lax.fori_loop(0, steps, behind, 0)
+    for i in range(steps):
+        behind(i, 0)
     lower = back[pl.ds(0, rows), :].astype(BF)
     upper = back[pl.ds(2 * rows, rows), :].astype(BF)
     for ref, value in (
@@ -239,6 +241,7 @@
     first = start // span * span
     skip = (start - first) // (2 * narrow)
     leads = [*range(first + span, 10 * width, span), first]
+    length = out.buffer.shape[2]
     for k, lead in enumerate(leads):
         low = skip if lead == first else 0
         for c in range(2):
@@ -248,30 +251,32 @@
             for y in range(narrow):
                 piece = value[y * slab + low : (y + 1) * slab]
                 out.buffer[y, c, pl.ds(k * slab, slab - low), :] = piece.astype(BF)
-    fill = out.buffer.shape[2] - len(leads) * slab + skip
+        if lead != first:
+            out.send_rows(pl.ds(k * slab, slab))
+    last = (len(leads) - 1) * slab
+    fill = length - last - slab + skip
     if fill:
-        at = pl.ds(len(leads) * slab - skip, fill)
+        at = pl.ds(length - fill, fill)
         out.buffer[:, :, at, :] = jnp.zeros((narrow, 2, fill, width), BF)
+    out.send_rows(pl.ds(last, length - last))
 
 
 def mesh_backward(
-    scales, start, half, so_ref, sb_ref, sa_ref, wsrc_ref, dnode_ref, wns_ref, dst_ref, wdst_ref,
-    cot_ref, wout_ref, tag_ref, h0_ref, a0_ref, agg_ref, dagg_ref, zeta_ref, unit_ref, wno_ref,
-    gpe_ref, turn_ref, out_ref, grad_ref, ret_ref, early_ref,
-    padded, geo, gps, gpd, gpo, gns, gna, gno,
+    so_ref, sb_ref, sa_ref, wsrc_ref, dnode_ref, wns_ref, dst_ref, wdst_ref, cot_ref, wout_ref,
+    tag_ref, grad_ref, ret_ref, total_ref, dmesh_ref, padded,
 ):
-    enc_scale, proc_scale, node_scale = scales
     rows = so_ref.buffer.shape[0]
     total = sum(ref.get()[...].astype(F32) for ref in (so_ref, sb_ref, sa_ref)).astype(BF)
-    d_node = dnode_ref.get()[...]
-    dst_sum = dst_ref.get()[...]
-    cot = cot_ref.get()[...]
-    grad = cot.astype(F32) + dot_rt(d_node, wns_ref.get()[...])
-    grad += dot_rt(dst_sum, wdst_ref.get()[...])
-    grad += dot_rt(total, wsrc_ref.get()[...])
+    total_ref.buffer[...] = total
+    total_ref.send()
+    grad = dot_rt(total, wsrc_ref.get()[...]) + dot_rt(dnode_ref.get()[...], wns_ref.get()[...])
+    grad += dot_rt(dst_ref.get()[...], wdst_ref.get()[...])
+    grad += cot_ref.get()[...].astype(F32)
     grad_ref.buffer[...] = grad
     grad_ref.send()
     d_mesh = grad.astype(BF)
+    dmesh_ref.buffer[...] = d_mesh
+    dmesh_ref.send()
     padded[pl.ds(rows, 256 - rows), :] = jnp.zeros((256 - rows, padded.shape[1]), BF)
     padded[pl.ds(0, rows), :] = dot_rt(d_mesh, wout_ref.get()[...]).astype(BF)
     tag = tag_ref.get()
@@ -281,16 +286,24 @@
         pick = same(tag[pl.ds(at, step)].astype(F32).reshape(-1, LANE), 256, 1)
         value = dot(pick, padded[...]).reshape(step, capacity, width)
         ret_ref.buffer[pl.ds(at, step)] = value.astype(BF)
-    ret_ref.send()
+
+
+def mesh_gradients(
+    scales, start, half, h0_ref, total_ref, a0_ref, dmesh_ref, dnode_ref, agg_ref, dst_ref,
+    zeta_ref, dagg_ref, unit_ref, cot_ref, wno_ref, gpe_ref, turn_ref, out_ref, early_ref,
+    geo, gps, gpd, gpo, gns, gna, gno,
+):
+    enc_scale, proc_scale, node_scale = scales
     h0 = h0_ref.get()[...]
-    gps[...] = (dot_lt(h0, total) * proc_scale).astype(BF)
-    geo[...] = (dot_lt(a0_ref.get()[...], d_mesh) * enc_scale).astype(BF)
+    d_node = dnode_ref.get()[...]
+    gps[...] = (dot_lt(h0, total_ref.get()[...]) * proc_scale).astype(BF)
+    geo[...] = (dot_lt(a0_ref.get()[...], dmesh_ref.get()[...]) * enc_scale).astype(BF)
     gns[...] = (dot_lt(h0, d_node) * node_scale).astype(BF)
     gna[...] = (dot_lt(agg_ref.get()[...], d_node) * node_scale).astype(BF)
-    gpd[...] = (dot_lt(h0, dst_sum) * proc_scale).astype(BF)
+    gpd[...] = (dot_lt(h0, dst_ref.get()[...]) * proc_scale).astype(BF)
     gpo[...] = (dot_lt(zeta_ref.get()[...], dagg_ref.get()[...]) * proc_scale).astype(BF)
     unit = unit_ref.get()[...]
-    gno[...] = (dot_lt(unit, cot) * node_scale).astype(BF)
+    gno[...] = (dot_lt(unit, cot_ref.get()[...]) * node_scale).astype(BF)
     out_ref.buffer[...] = (h0.astype(F32) + dot(unit, wno_ref.get()[...])).astype(BF)
     out_ref.send()
     held = [None, None, geo, gpe_ref.get(), gps, gpd, gpo, gns, gna, gno]
@@ -335,19 +348,26 @@
 
 
 class Outward:
-    def __init__(self, buffer, target, sem):
-        self.copy = pltpu.make_async_copy(buffer, target, sem)
-        self.buffer = buffer
-        self.started = False
+    def __init__(self, buffer, target, sem, spare):
+        self.buffer, self.target, self.sem, self.spare = buffer, target, sem, spare
+        self.parts = []
+
+    def send_rows(self, at):
+        part = pltpu.make_async_copy(
+            self.buffer.at[:, :, at], self.target.at[:, :, at], self.spare.at[len(self.parts)]
+        )
+        part.start()
+        self.parts.append(part)
 
     def send(self):
-        self.copy.start()
-        self.started = True
+        self.parts.append(pltpu.make_async_copy(self.buffer, self.target, self.sem))
+        self.parts[0].start()
 
     def finish(self):
-        if not self.started:
+        if not self.parts:
             self.send()
-        self.copy.wait()
+        for part in self.parts:
+            part.wait()
 
 
 def call(body, ins, outs, scratch=(), scalar=None, cut=None, flops=0):
@@ -365,8 +385,8 @@
         for i in range(count):
             part = source[i].at[:, :, pl.ds(*cut[i])] if i in cut else source[i]
             got.append(Inward(part, here[i], in_sem.at[i]))
-        put = [Outward(there[i], target[i], out_sem.at[i]) for i in range(made)]
-        body(*lead, *got, *put, *refs[2:])
+        put = [Outward(there[i], target[i], out_sem.at[i], refs[2]) for i in range(made)]
+        body(*lead, *got, *put, *refs[3:])
         for one in got:
             one.get()
         for one in put:
@@ -381,7 +401,7 @@
         out_shape=[jax.ShapeDtypeStruct(shape, kind) for shape, kind in outs],
         scratch_shapes=[pltpu.VMEM(held[i], ins[i].dtype) for i in range(count)]
         + [pltpu.VMEM(shape, kind) for shape, kind in outs]
-        + [pltpu.SemaphoreType.DMA((count,)), pltpu.SemaphoreType.DMA((made,))]
+        + [pltpu.SemaphoreType.DMA((n,)) for n in (count, made, 8)]
         + [pltpu.VMEM(shape, kind) for shape, kind in scratch],
         compiler_params=pltpu.CompilerParams(vmem_limit_bytes=60 << 20),
         cost_estimate=pl.CostEstimate(flops=flops, bytes_accessed=moved, transcendentals=0),
@@ -498,14 +518,22 @@
     scales = (enc_scale, proc_scale, node_scale)
     count = (10 * width - start) // (2 * narrow)
     early_shape = ((narrow, 2, -(-count // 16) * 16, width), BF)
-    mesh_out, mesh_grad, returning, early = call(
-        functools.partial(mesh_backward, scales, start, half),
+    mesh_grad, returning, total, d_mesh = call(
+        mesh_backward,
         [s_own, from_mate, from_other, w_proc_src, d_node, w_node_self, dst_sum, w_proc_dst]
-        + [cotangent, w_enc_out, received, h0, a0, agg, d_agg, zeta, unit, w_node_out, gpe, turn],
-        [block, ((rows, width), F32), ((devices, capacity, width), BF), early_shape],
-        [((256, width), BF)] + [square] * 7,
+        + [cotangent, w_enc_out, received],
+        [((rows, width), F32), ((devices, capacity, width), BF), block, block],
+        [((256, width), BF)],
         cut={10: (width, LANE)},
-        flops=44 * rows * width * width,
+        flops=12 * rows * width * width,
+    )
+    mesh_out, early = call(
+        functools.partial(mesh_gradients, scales, start, half),
+        [h0, total, a0, d_mesh, d_node, agg, dst_sum, zeta, d_agg, unit, cotangent, w_node_out]
+        + [gpe, turn],
+        [block, early_shape],
+        [square] * 7,
+        flops=32 * rows * width * width,
     )
     early = lax.psum_scatter(early, "narrow", scatter_dimension=0, tiled=True)[0]
     returned = lax.all_to_all(
@@ -519,7 +547,7 @@
         [((grid_rows, width), F32), late_shape, late_shape],
         [square, square],
         scalar=where,
-        flops=8 * edges * width * width,
+        flops=1200 * edges * width * width,
     )
     came = lax.ppermute(sent, "wide", swap)
     last = (kept.astype(F32) + came.astype(F32)).astype(BF)

time: 211 us -> 217 us (1.028)
  blocking collectives: 103 us -> 67.6 us
  waiting for transfers between devices: 37.6 us -> 69.4 us
  starting transfers between devices: 9.06 us -> 17.4 us
    all_to_all x1 -> x0, blocking collectives: 38.9 us -> none  [on_device(): lax.all_to_all(returning, ('wide', 'narrow'), split_axis=0, concat_axis=0...]
    all_to_all x0 -> x1, waiting for transfers between devices: none -> 24.8 us  [on_device(): lax.all_to_all(returning, ('wide', 'narrow'), split_axis=0, concat_axis=0...]
    all_to_all x1, waiting for transfers between devices: 10 us -> 17.6 us  [on_device(): lax.all_to_all(last, 'narrow', split_axis=0, concat_axis=0, tiled=True)]
    all_to_all x0 -> x1, starting transfers between devices: none -> 6.51 us  [on_device(): lax.all_to_all(returning, ('wide', 'narrow'), split_axis=0, concat_axis=0...]
    all_to_all x1, blocking collectives: 12.4 us -> 15.4 us  [on_device(): lax.all_to_all(both.astype(BF).reshape(near, chunk, width), 'wide', split...]
    pallas_call x5 -> x6, Pallas kernels: 37.1 us -> 38.1 us  [call(): pl.pallas_call(kernel, in_specs=[pl.BlockSpec(memory_space=pltpu.SMEM)] *...]
  transfers between devices with their start and end apart: 11 -> 12, of which waited for: 9 -> 12; matrix products, arithmetic and copies ran while one was open for 2% -> 2% of each run, Pallas kernels for 3% -> 7%
where the time goes in v8:
time: 217 us; the launch traced here: 215 us
  waiting for transfers between devices  69.4 us (32%)
  blocking collectives  67.6 us (31%)
  Pallas kernels  38.1 us (18%)
  starting transfers between devices  17.4 us (8%)
  between operations  14.2 us (7%)
  local copies, waits for them, and re-layouts  5.47 us (3%)
  other arithmetic  2.56 us (1%)
    all_to_all x1, blocking collectives, on_device(): lax.all_to_all(payload, ('wide', 'narrow'), split_axis=0, concat_axis=0,...  52.2 us
    pallas_call x6, Pallas kernels, call(): pl.pallas_call(kernel, in_specs=[pl.BlockSpec(memory_space=pltpu.SMEM)] *...  38.1 us
    all_to_all x1, waiting for transfers between devices, on_device(): lax.all_to_all(returning, ('wide', 'narrow'), split_axis=0, concat_axis=0...  24.8 us
    all_to_all x1, waiting for transfers between devices, on_device(): lax.all_to_all(last, 'narrow', split_axis=0, concat_axis=0, tiled=True)  17.6 us
    all_to_all x1, blocking collectives, on_device(): lax.all_to_all(both.astype(BF).reshape(near, chunk, width), 'wide', split...  15.4 us
    ppermute x1, waiting for transfers between devices, on_device(): from_other = lax.ppermute(s_other, 'wide', cross)  6.95 us
    ppermute x1, waiting for transfers between devices, on_device(): p_other = lax.ppermute(p_src, 'wide', cross)  6.77 us
    all_to_all x1, starting transfers between devices, on_device(): lax.all_to_all(returning, ('wide', 'narrow'), split_axis=0, concat_axis=0...  6.51 us
  transfers between devices with their start and end apart: 12, of which 12 were waited for; matrix products, arithmetic and copies ran while one was open for 2% of the time, Pallas kernels for 7%

profile of v8, /device:TPU:8, one launch (start us, length us, event | category | flops | bytes accessed | tf_op | source)
XLA Modules:
  0.0 214.7 jit_solution(4339289443396008609)
XLA Ops:
  7.2 4.8 %shard_map.228 = (bf16[256,4,640]{2,1,0:T(4,128)(2,1)}, bf16[512,512]{1,0:T(8,128)(2,1)}, s32[1,512]{1,0:T(1,128)}) custom-call(s32[1,512]{1,0:T(1,128)} %bitcast.24, s32[1,512]{1,0:T(1,128)} %bitcast.25, s32[1,512]{1,0:T(1,128)} %bitcast.26, bf16[512,512]{1,0:T(8,128)(2,1)} %refs_6_.3, bf16[512,512]{1,0:T(8,128)(2,1)} %refs_5_.5, bf16[512,512]{1,0:T(8,128)(2,1)} %refs_5_.3, ...), custom_call_target="tpu_custom_call" | custom-call | bytes 2103296 | tf_op jit(solution)/shard_map/pallas_call | solution.py:397
  12.0 52.2 %all_to_all.20.refs_0_.refs_10_ = bf16[256,4,640]{2,1,0:T(4,128)(2,1)} all-to-all(bf16[256,4,640]{2,1,0:T(4,128)(2,1)} %get-tuple-element.31), channel_id=1, replica_groups=mesh['wide'=64,'narrow'=4] {'wide','narrow'}, dimensions={0} | all-to-all | bytes 2621440 | tf_op jit(solution)/shard_map/all_to_all | solution.py:461
  64.2 3.6 %shard_map.229 = (bf16[160,512]{1,0:T(8,128)(2,1)}, bf16[160,512]{1,0:T(8,128)(2,1)}, bf16[160,512]{1,0:T(8,128)(2,1)}) custom-call(bf16[256,4,640]{2,1,0:T(4,128)(2,1)} %all_to_all.20.refs_0_.refs_10_, bf16[512,512]{1,0:T(8,128)(2,1)} %refs_9_.3, bf16[160,512]{1,0:T(8,128)(2,1)} %refs_2_.1, bf16[512,512]{1,0:T(8,128)(2,1)} %refs_3_.5), custom_call_target="tpu_custom_call" | custom-call | bytes 2523136 | tf_op jit(solution)/shard_map/pallas_call | solution.py:397
  67.8 0.1 collective-permute-start
  67.9 0.1 collective-permute-start.1
  68.0 0.0 copy-done.4
  68.1 0.6 reshape.43.refs_1_
  68.7 0.0 copy-done.5
  68.7 0.6 reshape.44.refs_2_
  69.3 0.3 collective-permute-done.refs_3_
  69.5 6.8 %collective-permute-done.1.refs_5_ = bf16[160,512]{1,0:T(8,128)(2,1)S(1)} collective-permute-done((bf16[160,512]{1,0:T(8,128)(2,1)}, bf16[160,512]{1,0:T(8,128)(2,1)S(1)}, u32[]{:S(2)}, u32[]{:S(2)}) %collective-permute-start.1) | collective-permute-done | bytes 163872 | tf_op jit(solution)/shard_map/ppermute | solution.py:471
  76.3 0.0 copy-done.6
  76.3 0.7 copy-done.7
  77.0 11.2 %shard_map.230 = (bf16[160,512]{1,0:T(8,128)(2,1)}, bf16[160,512]{1,0:T(8,128)(2,1)}, bf16[160,512]{1,0:T(8,128)(2,1)}, bf16[160,512]{1,0:T(8,128)(2,1)}, bf16[1...) custom-call(s32[1]{0:T(128)} %bitcast.3.refs_0_, ...), custom_call_target="tpu_custom_call" | custom-call | flops 4026531840 | bytes 5285888 | tf_op jit(solution)/shard_map/pallas_call | solution.py:397
  88.2 0.1 collective-permute-start.2
  88.3 0.3 collective-permute-start.3
  88.6 1.3 collective-permute-done.2.refs_1_
  89.9 6.9 %collective-permute-done.3.refs_2_ = bf16[160,512]{1,0:T(8,128)(2,1)S(1)} collective-permute-done((bf16[160,512]{1,0:T(8,128)(2,1)}, bf16[160,512]{1,0:T(8,128)(2,1)S(1)}, u32[]{:S(2)}, u32[]{:S(2)}) %collective-permute-start.3) | collective-permute-done | bytes 163872 | tf_op jit(solution)/shard_map/ppermute | solution.py:507
  96.9 0.6 copy-done.3
  97.5 4.3 %shard_map.231 = (f32[160,512]{1,0:T(8,128)}, bf16[256,4,512]{2,1,0:T(4,128)(2,1)}, bf16[160,512]{1,0:T(8,128)(2,1)}, bf16[160,512]{1,0:T(8,128)(2,1)}) custom-call(bf16[160,512]{1,0:T(8,128)(2,1)} %get-tuple-element.34.refs_0_, bf16[160,512]{1,0:T(8,128)(2,1)} %copy-done.2, bf16[160,512]{1,0:T(8,128)(2,1)} %copy-done.3, bf16[512,512]{1,0:T(8,128)(2,1)} %refs_3_.5, ...), custom_call_target="tpu_custom_call" | custom-call | flops 503316480 | bytes 4390912 | tf_op jit(solution)/shard_map/pallas_call | solution.py:397
  101.8 6.5 %all-to-all-start.1 = ((bf16[256,4,512]{2,1,0:T(4,128)(2,1)}), bf16[256,4,512]{2,1,0:T(4,128)(2,1)S(1)}, u32[]{:S(2)}, u32[]{:S(2)}) async-start(bf16[256,4,512]{2,1,0:T(4,128)(2,1)} %get-tuple-element.49), calls=%async_computation.1 | async-start | bytes 2097152 | tf_op jit(solution)/shard_map/all_to_all | solution.py:539
  108.3 0.0 reduce-scatter.2.cloned.1.call-start
  108.4 7.2 %shard_map.232 = (bf16[160,512]{1,0:T(8,128)(2,1)}, bf16[4,2,528,512]{3,2,1,0:T(8,128)(2,1)}) custom-call(bf16[160,512]{1,0:T(8,128)(2,1)} %get-tuple-element.32.refs_6_.refs_0_, bf16[160,512]{1,0:T(8,128)(2,1)} %get-tuple-element.39.refs_1_, bf16[160,512]{1,0:T(8,128)(2,1)} %get-tuple-element.40.refs_2_, bf16[160,512]{1,0:T(8,128)(2,1)} %get-tuple-element.41.refs_3_, ...), custom_call_target="tpu_custom_call" | custom-call | flops 1342177280 | bytes 3055616 | tf_op jit(solution)/shard_map/pallas_call | solution.py:397
  115.6 0.0 reduce-scatter.2.cloned.1.call-update
  115.6 24.8 %all-to-all-done.1.refs_3_ = bf16[256,4,512]{2,1,0:T(4,128)(2,1)S(1)} async-done(((bf16[256,4,512]{2,1,0:T(4,128)(2,1)}), bf16[256,4,512]{2,1,0:T(4,128)(2,1)S(1)}, u32[]{:S(2)}, u32[]{:S(2)}) %all-to-all-start.1) | async-done | bytes 1048608 | tf_op jit(solution)/shard_map/all_to_all | solution.py:539
  140.4 1.0 copy-done.1
  141.4 6.9 %shard_map.233 = (f32[512,512]{1,0:T(8,128)}, bf16[4,160,512]{2,1,0:T(8,128)(2,1)}, bf16[4,160,512]{2,1,0:T(8,128)(2,1)}) custom-call(s32[1]{0:T(128)} %bitcast.3.refs_0_, s32[1,512]{1,0:T(1,128)} %get-tuple-element.48.refs_1_, s32[1,512]{1,0:T(1,128)} %bitcast.27, bf16[256,4,512]{2,1,0:T(4,128)(2,1)} %copy-done.1, ...), custom_call_target="tpu_custom_call" | custom-call | flops 161061273600 | bytes 3354624 | tf_op jit(solution)/shard_map/pallas_call | solution.py:397
  148.3 0.1 collective-permute-start.4
  148.4 2.3 %collective-permute-done.4 = bf16[4,160,512]{2,1,0:T(8,128)(2,1)S(1)} collective-permute-done((bf16[4,160,512]{2,1,0:T(8,128)(2,1)}, bf16[4,160,512]{2,1,0:T(8,128)(2,1)S(1)}, u32[]{:S(2)}, u32[]{:S(2)}) %collective-permute-start.4) | collective-permute-done | bytes 655392 | tf_op jit(solution)/shard_map/ppermute | solution.py:552
  150.7 2.1 add_convert_fusion
  152.8 4.7 %all-to-all-start.2 = ((bf16[4,160,512]{2,1,0:T(8,128)(2,1)}), bf16[4,160,512]{2,1,0:T(8,128)(2,1)S(1)}, u32[]{:S(2)}, u32[]{:S(2)}) async-start(bf16[4,160,512]{2,1,0:T(8,128)(2,1)} %add_convert_fusion), calls=%async_computation.3 | async-start | bytes 1310720 | tf_op jit(solution)/shard_map/all_to_all | solution.py:554
  157.5 17.6 %all-to-all-done.2 = bf16[4,160,512]{2,1,0:T(8,128)(2,1)S(1)} async-done(((bf16[4,160,512]{2,1,0:T(8,128)(2,1)}), bf16[4,160,512]{2,1,0:T(8,128)(2,1)S(1)}, u32[]{:S(2)}, u32[]{:S(2)}) %all-to-all-start.2) | async-done | bytes 655392 | tf_op jit(solution)/shard_map/all_to_all | solution.py:554
  175.2 0.1 convert_reduce_fusion
  175.3 1.2 reduce-scatter.2.cloned.1.call-done
  176.5 1.2 dynamic-slice_bitcast_fusion
  177.6 0.2 collective-permute-start.5
  177.9 1.8 collective-permute-done.5
  179.7 0.2 convert_add_fusion
  179.9 0.1 slice.15
  180.1 1.2 collective-permute-start.6
  181.3 2.6 %collective-permute-start.7 = (bf16[160,512]{1,0:T(8,128)(2,1)S(1)}, bf16[160,512]{1,0:T(8,128)(2,1)S(1)}, u32[]{:S(2)}, u32[]{:S(2)}) collective-permute-start(bf16[160,512]{1,0:T(8,128)(2,1)S(1)} %get-tuple-element.60), channel_id=1, source_target_pairs={{0,128},{4,132},{8,136},{12,140},{16,144},{20,148},{24,152},{28,15... | collective-permute-start | bytes 491528 | tf_op jit(solution)/shard_map/ppermute | solution.py:573
  183.8 1.5 collective-permute-start.8
  185.3 2.6 %collective-permute-done.6 = bf16[160,512]{1,0:T(8,128)(2,1)S(1)} collective-permute-done((bf16[160,512]{1,0:T(8,128)(2,1)S(1)}, bf16[160,512]{1,0:T(8,128)(2,1)S(1)}, u32[]{:S(2)}, u32[]{:S(2)}) %collective-permute-start.6) | collective-permute-done | bytes 163872 | tf_op jit(solution)/shard_map/ppermute | solution.py:573
  187.9 3.6 %collective-permute-done.7 = bf16[160,512]{1,0:T(8,128)(2,1)S(1)} collective-permute-done((bf16[160,512]{1,0:T(8,128)(2,1)S(1)}, bf16[160,512]{1,0:T(8,128)(2,1)S(1)}, u32[]{:S(2)}, u32[]{:S(2)}) %collective-permute-start.7) | collective-permute-done | bytes 163872 | tf_op jit(solution)/shard_map/ppermute | solution.py:573
  191.6 0.1 collective-permute-done.8
  191.7 0.1 fusion.2
  191.8 15.4 %all_to_all.21 = bf16[8,20,512]{2,1,0:T(8,128)(2,1)S(1)} all-to-all(bf16[8,20,512]{2,1,0:T(8,128)(2,1)S(1)} %reshape.45), channel_id=1, replica_groups={{0,8,16,24,32,40,48,56},{4,12,20,28,36,44,52,60},{64,72,80,88,96,104,11..., dimensions={0} | all-to-all | bytes 327680 | tf_op jit(solution)/shard_map/all_to_all | solution.py:575
  207.2 0.6 reshape.46
  (16 shorter events, 0.2 us)
Async XLA Ops:
  64.2 3.8 %copy-start.4 = (s32[1280]{0:T(1024)S(1)}, s32[1280]{0:T(1024)}, u32[]{:S(2)}) copy-start(s32[1280]{0:T(1024)} %param.28) | copy-start | bytes 15364
  64.2 4.5 %copy-start.5 = (s32[1280]{0:T(1024)S(1)}, s32[1280]{0:T(1024)}, u32[]{:S(2)}) copy-start(s32[1280]{0:T(1024)} %param.29) | copy-start | bytes 15364
  67.8 1.7 collective-permute-start
  67.9 8.4 %collective-permute-start.1 = (bf16[160,512]{1,0:T(8,128)(2,1)}, bf16[160,512]{1,0:T(8,128)(2,1)S(1)}, u32[]{:S(2)}, u32[]{:S(2)}) collective-permute-start(bf16[160,512]{1,0:T(8,128)(2,1)} %get-tuple-element.33.refs_4_), channel_id=1, source_target_pairs={{0,252},{4,8},{8,4},{12,16},{16,12},{20,24},{24,20},{28,32},{32,28... | collective-permute-start | bytes 491528 | tf_op jit(solution)/shard_map/ppermute | solution.py:471
  69.5 6.8 %copy-start.6 = (bf16[160,512]{1,0:T(8,128)(2,1)}, bf16[160,512]{1,0:T(8,128)(2,1)S(1)}, u32[]{:S(2)}) copy-start(bf16[160,512]{1,0:T(8,128)(2,1)S(1)} %collective-permute-done.refs_3_) | copy-start | bytes 491524
  76.3 0.7 copy-start.7
  88.2 1.7 collective-permute-start.2
  88.3 8.5 %collective-permute-start.3 = (bf16[160,512]{1,0:T(8,128)(2,1)}, bf16[160,512]{1,0:T(8,128)(2,1)S(1)}, u32[]{:S(2)}, u32[]{:S(2)}) collective-permute-start(bf16[160,512]{1,0:T(8,128)(2,1)} %get-tuple-element.36), channel_id=1, source_target_pairs={{0,252},{4,8},{8,4},{12,16},{16,12},{20,24},{24,20},{28,32},{32,28... | collective-permute-start | bytes 491528 | tf_op jit(solution)/shard_map/ppermute | solution.py:507
  89.9 7.0 %copy-start.2 = (bf16[160,512]{1,0:T(8,128)(2,1)}, bf16[160,512]{1,0:T(8,128)(2,1)S(1)}, u32[]{:S(2)}) copy-start(bf16[160,512]{1,0:T(8,128)(2,1)S(1)} %collective-permute-done.2.refs_1_) | copy-start | bytes 491524
  96.9 0.7 copy-start.3
  101.8 38.6 %all-to-all-start.1 = ((bf16[256,4,512]{2,1,0:T(4,128)(2,1)}), bf16[256,4,512]{2,1,0:T(4,128)(2,1)S(1)}, u32[]{:S(2)}, u32[]{:S(2)}) async-start(bf16[256,4,512]{2,1,0:T(4,128)(2,1)} %get-tuple-element.49), calls=%async_computation.1 | async-start | bytes 2097152 | tf_op jit(solution)/shard_map/all_to_all | solution.py:539
  108.3 68.1 %reduce-scatter.2.cloned.1.call-start = ((), (), s32[]{:S(2)}) async-start(), calls=%async_computation.5 | async-start | bytes 5406720 | tf_op jit(solution)/shard_map/reduce_scatter | solution.py:538
  140.4 1.0 copy-start.1
  148.3 2.4 %collective-permute-start.4 = (bf16[4,160,512]{2,1,0:T(8,128)(2,1)}, bf16[4,160,512]{2,1,0:T(8,128)(2,1)S(1)}, u32[]{:S(2)}, u32[]{:S(2)}) collective-permute-start(bf16[4,160,512]{2,1,0:T(8,128)(2,1)} %get-tuple-element.54), channel_id=1, source_target_pairs={{0,4},{4,0},{8,12},{12,8},{16,20},{20,16},{24,28},{28,24},{32,36},... | collective-permute-start | bytes 1966088 | tf_op jit(solution)/shard_map/ppermute | solution.py:552
  152.8 22.4 %all-to-all-start.2 = ((bf16[4,160,512]{2,1,0:T(8,128)(2,1)}), bf16[4,160,512]{2,1,0:T(8,128)(2,1)S(1)}, u32[]{:S(2)}, u32[]{:S(2)}) async-start(bf16[4,160,512]{2,1,0:T(8,128)(2,1)} %add_convert_fusion), calls=%async_computation.3 | async-start | bytes 1310720 | tf_op jit(solution)/shard_map/all_to_all | solution.py:554
  176.5 3.2 %copy-start = (bf16[1,2,528,512]{3,2,1,0:T(8,128)(2,1)S(1)}, bf16[1,2,528,512]{3,2,1,0:T(8,128)(2,1)}, u32[]{:S(2)}) copy-start(bf16[1,2,528,512]{3,2,1,0:T(8,128)(2,1)} %reduce-scatter.2.cloned.1.call-done) | copy-start | bytes 3244036
  177.6 2.0 collective-permute-start.5
  180.1 7.9 %collective-permute-start.6 = (bf16[160,512]{1,0:T(8,128)(2,1)S(1)}, bf16[160,512]{1,0:T(8,128)(2,1)S(1)}, u32[]{:S(2)}, u32[]{:S(2)}) collective-permute-start(bf16[160,512]{1,0:T(8,128)(2,1)S(1)} %get-tuple-element.58), channel_id=1, source_target_pairs={{0,64},{4,68},{8,72},{12,76},{16,80},{20,84},{24,88},{28,92},{32,9... | collective-permute-start | bytes 491528 | tf_op jit(solution)/shard_map/ppermute | solution.py:573
  181.3 10.3 %collective-permute-start.7 = (bf16[160,512]{1,0:T(8,128)(2,1)S(1)}, bf16[160,512]{1,0:T(8,128)(2,1)S(1)}, u32[]{:S(2)}, u32[]{:S(2)}) collective-permute-start(bf16[160,512]{1,0:T(8,128)(2,1)S(1)} %get-tuple-element.60), channel_id=1, source_target_pairs={{0,128},{4,132},{8,136},{12,140},{16,144},{20,148},{24,152},{28,15... | collective-permute-start | bytes 491528 | tf_op jit(solution)/shard_map/ppermute | solution.py:573
  183.8 7.9 %collective-permute-start.8 = (bf16[160,512]{1,0:T(8,128)(2,1)S(1)}, bf16[160,512]{1,0:T(8,128)(2,1)S(1)}, u32[]{:S(2)}, u32[]{:S(2)}) collective-permute-start(bf16[160,512]{1,0:T(8,128)(2,1)S(1)} %get-tuple-element.59), channel_id=1, source_target_pairs={{0,192},{4,196},{8,200},{12,204},{16,208},{20,212},{24,216},{28,22... | collective-permute-start | bytes 491528 | tf_op jit(solution)/shard_map/ppermute | solution.py:573
Sparse Core Ops, SparseCore 0:
  115.7 60.6 reduce-scatter.1

commit v9 on v8

--- a/solution.py
+++ b/solution.py
@@ -218,7 +218,8 @@
 
 def split_turned(held, turn, core, start, half, kept, sent):
     even = core == 0
-    narrow, length, _ = kept.shape
+    narrow, length, _ = kept.buffer.shape
+    share = narrow // len(sent)
     slab = turn.shape[0] // narrow
     for at in range(0, length, slab):
         both = []
@@ -229,36 +230,10 @@
             both.append(dot(turn, rows).astype(BF))
         own, other = jnp.where(even, both[0], both[1]), jnp.where(even, both[1], both[0])
         for y in range(narrow):
-            kept[y, pl.ds(at, slab), :] = own[y * slab : (y + 1) * slab]
-            sent[y, pl.ds(at, slab), :] = other[y * slab : (y + 1) * slab]
-
-
-def turn_cores(held, turn, start, half, out):
-    narrow = out.buffer.shape[0]
-    slab = turn.shape[0] // narrow
-    span = 2 * turn.shape[0]
-    width = out.buffer.shape[3]
-    first = start // span * span
-    skip = (start - first) // (2 * narrow)
-    leads = [*range(first + span, 10 * width, span), first]
-    length = out.buffer.shape[2]
-    for k, lead in enumerate(leads):
-        low = skip if lead == first else 0
-        for c in range(2):
-            rows = [rows_of(held, row + c * half, half) for row in range(lead, lead + span, 2 * half)]
-            rows = rows[0] if len(rows) == 1 else jnp.concatenate(rows, axis=0)
-            value = dot(turn, rows)
-            for y in range(narrow):
-                piece = value[y * slab + low : (y + 1) * slab]
-                out.buffer[y, c, pl.ds(k * slab, slab - low), :] = piece.astype(BF)
-        if lead != first:
-            out.send_rows(pl.ds(k * slab, slab))
-    last = (len(leads) - 1) * slab
-    fill = length - last - slab + skip
-    if fill:
-        at = pl.ds(length - fill, fill)
-        out.buffer[:, :, at, :] = jnp.zeros((narrow, 2, fill, width), BF)
-    out.send_rows(pl.ds(last, length - last))
+            kept.buffer[y, pl.ds(at, slab), :] = own[y * slab : (y + 1) * slab]
+            sent[y // share].buffer[y % share, pl.ds(at, slab), :] = other[y * slab : (y + 1) * slab]
+        for one in (kept, *sent):
+            one.send_rows(pl.ds(at, slab))
 
 
 def mesh_backward(
@@ -289,10 +264,10 @@
 
 
 def mesh_gradients(
-    scales, start, half, h0_ref, total_ref, a0_ref, dmesh_ref, dnode_ref, agg_ref, dst_ref,
-    zeta_ref, dagg_ref, unit_ref, cot_ref, wno_ref, gpe_ref, turn_ref, out_ref, early_ref,
-    geo, gps, gpd, gpo, gns, gna, gno,
+    scales, start, half, core_ref, h0_ref, total_ref, a0_ref, dmesh_ref, dnode_ref, agg_ref, dst_ref,
+    zeta_ref, dagg_ref, unit_ref, cot_ref, wno_ref, gpe_ref, turn_ref, out_ref, kept_ref, *refs,
 ):
+    sent, (geo, gps, gpd, gpo, gns, gna, gno) = refs[:-7], refs[-7:]
     enc_scale, proc_scale, node_scale = scales
     h0 = h0_ref.get()[...]
     d_node = dnode_ref.get()[...]
@@ -307,7 +282,7 @@
     out_ref.buffer[...] = (h0.astype(F32) + dot(unit, wno_ref.get()[...])).astype(BF)
     out_ref.send()
     held = [None, None, geo, gpe_ref.get(), gps, gpd, gpo, gns, gna, gno]
-    turn_cores(held, turn_ref.get()[...], start, half, early_ref)
+    split_turned(held, turn_ref.get()[...], core_ref[0], start, half, kept_ref, sent)
 
 
 def enc_backward(
@@ -324,7 +299,7 @@
     geg[...] = (dot_lt(grid_ref.get()[...], grid_sum) * enc_scale).astype(BF)
     held = [gee, geg] + [None] * 8
     turn = turn_ref.get()[...]
-    split_turned(held, turn, core_ref[0], 0, half, kept_ref.buffer, sent_ref.buffer)
+    split_turned(held, turn, core_ref[0], 0, half, kept_ref, [sent_ref])
 
 
 def turned(narrow, chunk, groups):
@@ -348,13 +323,13 @@
 
 
 class Outward:
-    def __init__(self, buffer, target, sem, spare):
+    def __init__(self, buffer, target, sem, spare, first):
         self.buffer, self.target, self.sem, self.spare = buffer, target, sem, spare
-        self.parts = []
+        self.parts, self.first = [], first
 
     def send_rows(self, at):
         part = pltpu.make_async_copy(
-            self.buffer.at[:, :, at], self.target.at[:, :, at], self.spare.at[len(self.parts)]
+            self.buffer.at[:, at], self.target.at[:, at], self.spare.at[self.first + len(self.parts)]
         )
         part.start()
         self.parts.append(part)
@@ -385,7 +360,7 @@
         for i in range(count):
             part = source[i].at[:, :, pl.ds(*cut[i])] if i in cut else source[i]
             got.append(Inward(part, here[i], in_sem.at[i]))
-        put = [Outward(there[i], target[i], out_sem.at[i], refs[2]) for i in range(made)]
+        put = [Outward(there[i], target[i], out_sem.at[i], refs[2], 8 * i) for i in range(made)]
         body(*lead, *got, *put, *refs[3:])
         for one in got:
             one.get()
@@ -401,7 +376,7 @@
         out_shape=[jax.ShapeDtypeStruct(shape, kind) for shape, kind in outs],
         scratch_shapes=[pltpu.VMEM(held[i], ins[i].dtype) for i in range(count)]
         + [pltpu.VMEM(shape, kind) for shape, kind in outs]
-        + [pltpu.SemaphoreType.DMA((n,)) for n in (count, made, 8)]
+        + [pltpu.SemaphoreType.DMA((n,)) for n in (count, made, 8 * made)]
         + [pltpu.VMEM(shape, kind) for shape, kind in scratch],
         compiler_params=pltpu.CompilerParams(vmem_limit_bytes=60 << 20),
         cost_estimate=pl.CostEstimate(flops=flops, bytes_accessed=moved, transcendentals=0),
@@ -514,10 +489,13 @@
     near = chips // far
     turn = turned(narrow, chunk, 4 if chunk % 16 else 1)
     late = 2 * width
-    start = late // (2 * half) * 2 * half
+    span = 2 * turn.shape[0]
+    start = late // span * span
     scales = (enc_scale, proc_scale, node_scale)
     count = (10 * width - start) // (2 * narrow)
-    early_shape = ((narrow, 2, -(-count // 16) * 16, width), BF)
+    early_shape = ((narrow, count, width), BF)
+    pieces = min(2, narrow)
+    sent_shape = ((narrow // pieces, count, width), BF)
     mesh_grad, returning, total, d_mesh = call(
         mesh_backward,
         [s_own, from_mate, from_other, w_proc_src, d_node, w_node_self, dst_sum, w_proc_dst]
@@ -527,14 +505,17 @@
         cut={10: (width, LANE)},
         flops=12 * rows * width * width,
     )
-    mesh_out, early = call(
+    mesh_out, kept, *sent = call(
         functools.partial(mesh_gradients, scales, start, half),
         [h0, total, a0, d_mesh, d_node, agg, dst_sum, zeta, d_agg, unit, cotangent, w_node_out]
         + [gpe, turn],
-        [block, early_shape],
+        [block, early_shape] + [sent_shape] * pieces,
         [square] * 7,
+        scalar=where,
         flops=32 * rows * width * width,
     )
+    came = jnp.concatenate([lax.ppermute(one, "wide", swap) for one in sent], axis=0)
+    early = (kept.astype(F32) + came.astype(F32)).astype(BF)
     early = lax.psum_scatter(early, "narrow", scatter_dimension=0, tiled=True)[0]
     returned = lax.all_to_all(
         returning, ("wide", "narrow"), split_axis=0, concat_axis=0, tiled=True
@@ -554,14 +535,9 @@
     last = lax.all_to_all(last, "narrow", split_axis=0, concat_axis=0, tiled=True)
     last = jnp.sum(last.astype(F32), axis=0)[: near * chunk]
     early, last = lax.optimization_barrier((early, last))
-    sent = lax.dynamic_index_in_dim(early, 1 - core, 0, keepdims=False)
-    came = lax.ppermute(sent, "wide", swap)
-    early = lax.dynamic_index_in_dim(early, core, 0, keepdims=False).astype(F32)
-    early = (early + came.astype(F32))[:count]
-    rest = (10 * width - near * far * 2 * half // far) // (2 * narrow)
-    last += jnp.pad(early[rest:], ((near * chunk - (count - rest), 0), (0, 0)))
-    both = jnp.concatenate([last, early[:rest]], axis=0).astype(BF)
-    both = both.reshape(far, near * chunk, width)
+    early = jnp.pad(early, ((start // (2 * narrow), 0), (0, 0))).astype(F32)
+    early += jnp.pad(last, ((0, early.shape[0] - last.shape[0]), (0, 0)))
+    both = early.astype(BF).reshape(far, near * chunk, width)
     x = lax.axis_index("wide") // (2 * near)
 
     def toward(j):

time: 217 us -> 206 us (0.949)
  waiting for transfers between devices: 69.4 us -> 54 us
  other arithmetic: 2.56 us -> 7.21 us
    all_to_all x1, waiting for transfers between devices: 24.8 us -> 15.9 us  [on_device(): lax.all_to_all(returning, ('wide', 'narrow'), split_axis=0, concat_axis=0...]
    all_to_all x1, waiting for transfers between devices: 17.6 us -> 10 us  [on_device(): lax.all_to_all(last, 'narrow', split_axis=0, concat_axis=0, tiled=True)]
    convert_element_type x0 -> x2, other arithmetic: none -> 4.86 us  [the longest x1 3.74 us: on_device(): early = (kept.astype(F32) + came.astype(F32)).astype(BF)]
    ppermute x0 -> x2, waiting for transfers between devices: none -> 4.14 us  [on_device(): lax.ppermute(one, 'wide', swap)]
  transfers between devices with their start and end apart: 12 -> 13, of which waited for: 12 -> 12; matrix products, arithmetic and copies ran while one was open for 2% -> 4% of each run, Pallas kernels for 7% -> 7%
where the time goes in v9:
time: 206 us; the launch traced here: 204 us
  blocking collectives  68.6 us (33%)
  waiting for transfers between devices  54 us (26%)
  Pallas kernels  38.9 us (19%)
  starting transfers between devices  17.1 us (8%)
  between operations  14.2 us (7%)
  other arithmetic  7.21 us (4%)
  local copies, waits for them, and re-layouts  4.25 us (2%)
    all_to_all x1, blocking collectives, on_device(): lax.all_to_all(payload, ('wide', 'narrow'), split_axis=0, concat_axis=0,...  52.2 us
    pallas_call x6, Pallas kernels, call(): pl.pallas_call(kernel, in_specs=[pl.BlockSpec(memory_space=pltpu.SMEM)] *...  38.9 us
    all_to_all x1, blocking collectives, on_device(): lax.all_to_all(both.astype(BF).reshape(near, chunk, width), 'wide', split...  16.4 us
    all_to_all x1, waiting for transfers between devices, on_device(): lax.all_to_all(returning, ('wide', 'narrow'), split_axis=0, concat_axis=0...  15.9 us
    all_to_all x1, waiting for transfers between devices, on_device(): lax.all_to_all(last, 'narrow', split_axis=0, concat_axis=0, tiled=True)  10 us
    ppermute x1, waiting for transfers between devices, on_device(): from_other = lax.ppermute(s_other, 'wide', cross)  6.95 us
    ppermute x1, waiting for transfers between devices, on_device(): p_other = lax.ppermute(p_src, 'wide', cross)  6.77 us
    all_to_all x1, starting transfers between devices, on_device(): lax.all_to_all(returning, ('wide', 'narrow'), split_axis=0, concat_axis=0...  6.47 us
  transfers between devices with their start and end apart: 13, of which 12 were waited for; matrix products, arithmetic and copies ran while one was open for 4% of the time, Pallas kernels for 7%

profile of v9, /device:TPU:8, one launch (start us, length us, event | category | flops | bytes accessed | tf_op | source)
XLA Modules:
  0.0 204.2 jit_solution(717187144844438200)
XLA Ops:
  7.2 5.0 %shard_map.228 = (bf16[256,4,640]{2,1,0:T(4,128)(2,1)}, bf16[512,512]{1,0:T(8,128)(2,1)}, s32[1,512]{1,0:T(1,128)}) custom-call(s32[1,512]{1,0:T(1,128)} %bitcast.18, s32[1,512]{1,0:T(1,128)} %bitcast.19, s32[1,512]{1,0:T(1,128)} %bitcast.20, bf16[512,512]{1,0:T(8,128)(2,1)} %refs_6_.3, bf16[512,512]{1,0:T(8,128)(2,1)} %refs_5_.5, bf16[512,512]{1,0:T(8,128)(2,1)} %refs_5_.3, ...), custom_call_target="tpu_custom_call" | custom-call | bytes 2103296 | tf_op jit(solution)/shard_map/pallas_call | solution.py:372
  12.1 52.2 %all_to_all.20.refs_0_.refs_10_ = bf16[256,4,640]{2,1,0:T(4,128)(2,1)} all-to-all(bf16[256,4,640]{2,1,0:T(4,128)(2,1)} %get-tuple-element.33), channel_id=1, replica_groups=mesh['wide'=64,'narrow'=4] {'wide','narrow'}, dimensions={0} | all-to-all | bytes 2621440 | tf_op jit(solution)/shard_map/all_to_all | solution.py:436
  64.4 3.8 %shard_map.229 = (bf16[160,512]{1,0:T(8,128)(2,1)}, bf16[160,512]{1,0:T(8,128)(2,1)}, bf16[160,512]{1,0:T(8,128)(2,1)}) custom-call(bf16[256,4,640]{2,1,0:T(4,128)(2,1)} %all_to_all.20.refs_0_.refs_10_, bf16[512,512]{1,0:T(8,128)(2,1)} %refs_9_.3, bf16[160,512]{1,0:T(8,128)(2,1)} %refs_2_.1, bf16[512,512]{1,0:T(8,128)(2,1)} %refs_3_.5), custom_call_target="tpu_custom_call" | custom-call | bytes 2523136 | tf_op jit(solution)/shard_map/pallas_call | solution.py:372
  68.1 0.1 collective-permute-start
  68.2 0.1 collective-permute-start.1
  68.3 0.0 copy-done.3
  68.3 0.6 reshape.41.refs_1_
  69.0 0.0 copy-done.4
  69.0 0.6 reshape.42.refs_2_
  69.5 0.3 collective-permute-done.refs_3_
  69.8 6.8 %collective-permute-done.1.refs_5_ = bf16[160,512]{1,0:T(8,128)(2,1)S(1)} collective-permute-done((bf16[160,512]{1,0:T(8,128)(2,1)}, bf16[160,512]{1,0:T(8,128)(2,1)S(1)}, u32[]{:S(2)}, u32[]{:S(2)}) %collective-permute-start.1) | collective-permute-done | bytes 163872 | tf_op jit(solution)/shard_map/ppermute | solution.py:446
  76.6 0.7 copy-done.6
  77.3 11.9 %shard_map.230 = (bf16[160,512]{1,0:T(8,128)(2,1)}, bf16[160,512]{1,0:T(8,128)(2,1)}, bf16[160,512]{1,0:T(8,128)(2,1)}, bf16[160,512]{1,0:T(8,128)(2,1)}, bf16[1...) custom-call(s32[1]{0:T(128)} %bitcast.refs_0_, ...), custom_call_target="tpu_custom_call" | custom-call | flops 4026531840 | bytes 5285888 | tf_op jit(solution)/shard_map/pallas_call | solution.py:372
  89.1 0.1 collective-permute-start.2
  89.2 0.3 collective-permute-start.3
  89.5 1.3 collective-permute-done.2.refs_1_
  90.8 6.9 %collective-permute-done.3.refs_2_ = bf16[160,512]{1,0:T(8,128)(2,1)S(1)} collective-permute-done((bf16[160,512]{1,0:T(8,128)(2,1)}, bf16[160,512]{1,0:T(8,128)(2,1)S(1)}, u32[]{:S(2)}, u32[]{:S(2)}) %collective-permute-start.3) | collective-permute-done | bytes 163872 | tf_op jit(solution)/shard_map/ppermute | solution.py:482
  97.8 0.7 copy-done.2
  98.4 4.5 %shard_map.231 = (f32[160,512]{1,0:T(8,128)}, bf16[256,4,512]{2,1,0:T(4,128)(2,1)}, bf16[160,512]{1,0:T(8,128)(2,1)}, bf16[160,512]{1,0:T(8,128)(2,1)}) custom-call(bf16[160,512]{1,0:T(8,128)(2,1)} %get-tuple-element.36.refs_0_, bf16[160,512]{1,0:T(8,128)(2,1)} %copy-done.1, bf16[160,512]{1,0:T(8,128)(2,1)} %copy-done.2, bf16[512,512]{1,0:T(8,128)(2,1)} %refs_3_.5, ...), custom_call_target="tpu_custom_call" | custom-call | flops 503316480 | bytes 4390912 | tf_op jit(solution)/shard_map/pallas_call | solution.py:372
  103.0 6.5 %all-to-all-start.1 = ((bf16[256,4,512]{2,1,0:T(4,128)(2,1)}), bf16[256,4,512]{2,1,0:T(4,128)(2,1)S(1)}, u32[]{:S(2)}, u32[]{:S(2)}) async-start(bf16[256,4,512]{2,1,0:T(4,128)(2,1)} %get-tuple-element.51), calls=%async_computation.1 | async-start | bytes 2097152 | tf_op jit(solution)/shard_map/all_to_all | solution.py:520
  109.4 0.0 reduce-scatter.2.cloned.1.call-start
  109.5 7.5 %shard_map.232 = (bf16[160,512]{1,0:T(8,128)(2,1)}, bf16[4,560,512]{2,1,0:T(8,128)(2,1)}, bf16[2,560,512]{2,1,0:T(8,128)(2,1)}, bf16[2,560,512]{2,1,0:T(8,128)(2,1)}) custom-call(s32[1]{0:T(128)} %bitcast.refs_0_, bf16[160,512]{1,0:T(8,128)(2,1)} %get-tuple-element.34.refs_6_.refs_1_, bf16[160,512]{1,0:T(8,128)(2,1)} %get-tuple-element.41.refs_2_, ...), custom_call_target="tpu_custom_call" | custom-call | flops 1342177280 | bytes 3055616 | tf_op jit(solution)/shard_map/pallas_call | solution.py:372
  117.0 0.2 collective-permute-start.4
  117.3 0.4 collective-permute-start.5
  117.6 2.5 %collective-permute-done.4 = bf16[2,560,512]{2,1,0:T(8,128)(2,1)S(1)} collective-permute-done((bf16[2,560,512]{2,1,0:T(8,128)(2,1)}, bf16[2,560,512]{2,1,0:T(8,128)(2,1)S(1)}, u32[]{:S(2)}, u32[]{:S(2)}) %collective-permute-start.4) | collective-permute-done | bytes 1146912 | tf_op jit(solution)/shard_map/ppermute | solution.py:517
  120.1 1.6 collective-permute-done.5
  121.8 3.7 %add_convert_fusion = bf16[4,560,512]{2,1,0:T(8,128)(2,1)} fusion(bf16[4,560,512]{2,1,0:T(8,128)(2,1)} %get-tuple-element.54, bf16[2,560,512]{2,1,0:T(8,128)(2,1)S(1)} %collective-permute-done.5, bf16[2,560,512]{2,1,0:T(8,128)(2,1)S(1)} %collective-permute-done.4), kind=kLoop, calls=%fused_computation | loop fusion | flops 5734400 | bytes 6881280 | tf_op jit(solution)/shard_map/convert_element_type | solution.py:518
  125.5 0.0 reduce-scatter.2.cloned.1.call-update
  125.5 15.9 %all-to-all-done.1.refs_3_ = bf16[256,4,512]{2,1,0:T(4,128)(2,1)S(1)} async-done(((bf16[256,4,512]{2,1,0:T(4,128)(2,1)}), bf16[256,4,512]{2,1,0:T(4,128)(2,1)S(1)}, u32[]{:S(2)}, u32[]{:S(2)}) %all-to-all-start.1) | async-done | bytes 1048608 | tf_op jit(solution)/shard_map/all_to_all | solution.py:520
  141.5 1.0 copy-done
  142.5 6.2 %shard_map.233 = (f32[512,512]{1,0:T(8,128)}, bf16[4,160,512]{2,1,0:T(8,128)(2,1)}, bf16[4,160,512]{2,1,0:T(8,128)(2,1)}) custom-call(s32[1]{0:T(128)} %bitcast.refs_0_, s32[1,512]{1,0:T(1,128)} %get-tuple-element.50.refs_1_, s32[1,512]{1,0:T(1,128)} %bitcast.21, bf16[256,4,512]{2,1,0:T(4,128)(2,1)} %copy-done, bf16[512,512]{1,0:T(8,128)(2,1)} %get-tuple-element.52.refs_4_, ...), custom_call_target="tpu_custom_call" | custom-call | flops 161061273600 | bytes 3354624 | tf_op jit(solution)/shard_map/pallas_call | solution.py:372
  148.7 0.1 collective-permute-start.6
  148.8 2.3 %collective-permute-done.6 = bf16[4,160,512]{2,1,0:T(8,128)(2,1)S(1)} collective-permute-done((bf16[4,160,512]{2,1,0:T(8,128)(2,1)}, bf16[4,160,512]{2,1,0:T(8,128)(2,1)S(1)}, u32[]{:S(2)}, u32[]{:S(2)}) %collective-permute-start.6) | collective-permute-done | bytes 655392 | tf_op jit(solution)/shard_map/ppermute | solution.py:533
  151.1 2.1 %add_convert_fusion.2 = bf16[4,160,512]{2,1,0:T(8,128)(2,1)} fusion(bf16[4,160,512]{2,1,0:T(8,128)(2,1)S(1)} %collective-permute-done.6, bf16[4,160,512]{2,1,0:T(8,128)(2,1)} %get-tuple-element.57), kind=kLoop, calls=%fused_computation.3 | loop fusion | flops 1310720 | bytes 1966080 | tf_op jit(solution)/shard_map/convert_element_type | solution.py:534
  153.3 4.8 %all-to-all-start.2 = ((bf16[4,160,512]{2,1,0:T(8,128)(2,1)}), bf16[4,160,512]{2,1,0:T(8,128)(2,1)S(1)}, u32[]{:S(2)}, u32[]{:S(2)}) async-start(bf16[4,160,512]{2,1,0:T(8,128)(2,1)} %add_convert_fusion.2), calls=%async_computation.3 | async-start | bytes 1310720 | tf_op jit(solution)/shard_map/all_to_all | solution.py:535
  158.1 10.0 %all-to-all-done.2 = bf16[4,160,512]{2,1,0:T(8,128)(2,1)S(1)} async-done(((bf16[4,160,512]{2,1,0:T(8,128)(2,1)}), bf16[4,160,512]{2,1,0:T(8,128)(2,1)S(1)}, u32[]{:S(2)}, u32[]{:S(2)}) %all-to-all-start.2) | async-done | bytes 655392 | tf_op jit(solution)/shard_map/all_to_all | solution.py:535
  168.1 0.1 convert_reduce_fusion
  168.2 0.0 reduce-scatter.2.cloned.1.call-done
  168.2 1.1 add_convert_fusion.1
  169.4 0.4 collective-permute-start.7
  169.7 2.7 %collective-permute-start.8 = (bf16[160,512]{1,0:T(8,128)(2,1)S(1)}, bf16[160,512]{1,0:T(8,128)(2,1)S(1)}, u32[]{:S(2)}, u32[]{:S(2)}) collective-permute-start(bf16[160,512]{1,0:T(8,128)(2,1)S(1)} %get-tuple-element.64), channel_id=1, source_target_pairs={{0,128},{4,132},{8,136},{12,140},{16,144},{20,148},{24,152},{28,15... | collective-permute-start | bytes 491528 | tf_op jit(solution)/shard_map/ppermute | solution.py:549
  172.4 1.5 collective-permute-start.9
  173.9 3.0 %collective-permute-done.7 = bf16[160,512]{1,0:T(8,128)(2,1)S(1)} collective-permute-done((bf16[160,512]{1,0:T(8,128)(2,1)S(1)}, bf16[160,512]{1,0:T(8,128)(2,1)S(1)}, u32[]{:S(2)}, u32[]{:S(2)}) %collective-permute-start.7) | collective-permute-done | bytes 163872 | tf_op jit(solution)/shard_map/ppermute | solution.py:549
  176.9 3.0 %collective-permute-done.8 = bf16[160,512]{1,0:T(8,128)(2,1)S(1)} collective-permute-done((bf16[160,512]{1,0:T(8,128)(2,1)S(1)}, bf16[160,512]{1,0:T(8,128)(2,1)S(1)}, u32[]{:S(2)}, u32[]{:S(2)}) %collective-permute-start.8) | collective-permute-done | bytes 163872 | tf_op jit(solution)/shard_map/ppermute | solution.py:549
  179.9 0.3 collective-permute-done.9
  180.2 0.1 fusion.2
  180.3 16.4 %all_to_all.21 = bf16[8,20,512]{2,1,0:T(8,128)(2,1)S(1)} all-to-all(bf16[8,20,512]{2,1,0:T(8,128)(2,1)S(1)} %reshape.44), channel_id=1, replica_groups={{0,8,16,24,32,40,48,56},{4,12,20,28,36,44,52,60},{64,72,80,88,96,104,11..., dimensions={0} | all-to-all | bytes 327680 | tf_op jit(solution)/shard_map/all_to_all | solution.py:551
  196.7 0.6 reshape.45
  (12 shorter events, 0.1 us)
Async XLA Ops:
  64.3 4.0 %copy-start.3 = (s32[1280]{0:T(1024)S(1)}, s32[1280]{0:T(1024)}, u32[]{:S(2)}) copy-start(s32[1280]{0:T(1024)} %param.28) | copy-start | bytes 15364
  64.3 4.6 %copy-start.4 = (s32[1280]{0:T(1024)S(1)}, s32[1280]{0:T(1024)}, u32[]{:S(2)}) copy-start(s32[1280]{0:T(1024)} %param.29) | copy-start | bytes 15364
  68.1 1.7 collective-permute-start
  68.2 8.4 %collective-permute-start.1 = (bf16[160,512]{1,0:T(8,128)(2,1)}, bf16[160,512]{1,0:T(8,128)(2,1)S(1)}, u32[]{:S(2)}, u32[]{:S(2)}) collective-permute-start(bf16[160,512]{1,0:T(8,128)(2,1)} %get-tuple-element.35.refs_4_), channel_id=1, source_target_pairs={{0,252},{4,8},{8,4},{12,16},{16,12},{20,24},{24,20},{28,32},{32,28... | collective-permute-start | bytes 491528 | tf_op jit(solution)/shard_map/ppermute | solution.py:446
  69.8 6.8 %copy-start.5 = (bf16[160,512]{1,0:T(8,128)(2,1)}, bf16[160,512]{1,0:T(8,128)(2,1)S(1)}, u32[]{:S(2)}) copy-start(bf16[160,512]{1,0:T(8,128)(2,1)S(1)} %collective-permute-done.refs_3_) | copy-start | bytes 491524
  76.6 0.7 copy-start.6
  89.1 1.7 collective-permute-start.2
  89.2 8.5 %collective-permute-start.3 = (bf16[160,512]{1,0:T(8,128)(2,1)}, bf16[160,512]{1,0:T(8,128)(2,1)S(1)}, u32[]{:S(2)}, u32[]{:S(2)}) collective-permute-start(bf16[160,512]{1,0:T(8,128)(2,1)} %get-tuple-element.38), channel_id=1, source_target_pairs={{0,252},{4,8},{8,4},{12,16},{16,12},{20,24},{24,20},{28,32},{32,28... | collective-permute-start | bytes 491528 | tf_op jit(solution)/shard_map/ppermute | solution.py:482
  90.8 7.0 %copy-start.1 = (bf16[160,512]{1,0:T(8,128)(2,1)}, bf16[160,512]{1,0:T(8,128)(2,1)S(1)}, u32[]{:S(2)}) copy-start(bf16[160,512]{1,0:T(8,128)(2,1)S(1)} %collective-permute-done.2.refs_1_) | copy-start | bytes 491524
  97.8 0.7 copy-start.2
  103.0 38.5 %all-to-all-start.1 = ((bf16[256,4,512]{2,1,0:T(4,128)(2,1)}), bf16[256,4,512]{2,1,0:T(4,128)(2,1)S(1)}, u32[]{:S(2)}, u32[]{:S(2)}) async-start(bf16[256,4,512]{2,1,0:T(4,128)(2,1)} %get-tuple-element.51), calls=%async_computation.1 | async-start | bytes 2097152 | tf_op jit(solution)/shard_map/all_to_all | solution.py:520
  109.4 58.8 %reduce-scatter.2.cloned.1.call-start = ((), (), s32[]{:S(2)}) async-start(), calls=%async_computation.5 | async-start | bytes 2867200 | tf_op jit(solution)/shard_map/reduce_scatter | solution.py:519
  117.0 3.1 %collective-permute-start.4 = (bf16[2,560,512]{2,1,0:T(8,128)(2,1)}, bf16[2,560,512]{2,1,0:T(8,128)(2,1)S(1)}, u32[]{:S(2)}, u32[]{:S(2)}) collective-permute-start(bf16[2,560,512]{2,1,0:T(8,128)(2,1)} %get-tuple-element.55), channel_id=1, source_target_pairs={{0,4},{4,0},{8,12},{12,8},{16,20},{20,16},{24,28},{28,24},{32,36},... | collective-permute-start | bytes 3440648 | tf_op jit(solution)/shard_map/ppermute | solution.py:517
  117.3 4.5 %collective-permute-start.5 = (bf16[2,560,512]{2,1,0:T(8,128)(2,1)}, bf16[2,560,512]{2,1,0:T(8,128)(2,1)S(1)}, u32[]{:S(2)}, u32[]{:S(2)}) collective-permute-start(bf16[2,560,512]{2,1,0:T(8,128)(2,1)} %get-tuple-element.56), channel_id=1, source_target_pairs={{0,4},{4,0},{8,12},{12,8},{16,20},{20,16},{24,28},{28,24},{32,36},... | collective-permute-start | bytes 3440648 | tf_op jit(solution)/shard_map/ppermute | solution.py:517
  141.5 1.0 copy-start
  148.7 2.4 %collective-permute-start.6 = (bf16[4,160,512]{2,1,0:T(8,128)(2,1)}, bf16[4,160,512]{2,1,0:T(8,128)(2,1)S(1)}, u32[]{:S(2)}, u32[]{:S(2)}) collective-permute-start(bf16[4,160,512]{2,1,0:T(8,128)(2,1)} %get-tuple-element.58), channel_id=1, source_target_pairs={{0,4},{4,0},{8,12},{12,8},{16,20},{20,16},{24,28},{28,24},{32,36},... | collective-permute-start | bytes 1966088 | tf_op jit(solution)/shard_map/ppermute | solution.py:533
  153.3 14.8 %all-to-all-start.2 = ((bf16[4,160,512]{2,1,0:T(8,128)(2,1)}), bf16[4,160,512]{2,1,0:T(8,128)(2,1)S(1)}, u32[]{:S(2)}, u32[]{:S(2)}) async-start(bf16[4,160,512]{2,1,0:T(8,128)(2,1)} %add_convert_fusion.2), calls=%async_computation.3 | async-start | bytes 1310720 | tf_op jit(solution)/shard_map/all_to_all | solution.py:535
  169.4 7.5 %collective-permute-start.7 = (bf16[160,512]{1,0:T(8,128)(2,1)S(1)}, bf16[160,512]{1,0:T(8,128)(2,1)S(1)}, u32[]{:S(2)}, u32[]{:S(2)}) collective-permute-start(bf16[160,512]{1,0:T(8,128)(2,1)S(1)} %get-tuple-element.62), channel_id=1, source_target_pairs={{0,64},{4,68},{8,72},{12,76},{16,80},{20,84},{24,88},{28,92},{32,9... | collective-permute-start | bytes 491528 | tf_op jit(solution)/shard_map/ppermute | solution.py:549
  169.7 10.2 %collective-permute-start.8 = (bf16[160,512]{1,0:T(8,128)(2,1)S(1)}, bf16[160,512]{1,0:T(8,128)(2,1)S(1)}, u32[]{:S(2)}, u32[]{:S(2)}) collective-permute-start(bf16[160,512]{1,0:T(8,128)(2,1)S(1)} %get-tuple-element.64), channel_id=1, source_target_pairs={{0,128},{4,132},{8,136},{12,140},{16,144},{20,148},{24,152},{28,15... | collective-permute-start | bytes 491528 | tf_op jit(solution)/shard_map/ppermute | solution.py:549
  172.4 7.7 %collective-permute-start.9 = (bf16[160,512]{1,0:T(8,128)(2,1)S(1)}, bf16[160,512]{1,0:T(8,128)(2,1)S(1)}, u32[]{:S(2)}, u32[]{:S(2)}) collective-permute-start(bf16[160,512]{1,0:T(8,128)(2,1)S(1)} %get-tuple-element.63), channel_id=1, source_target_pairs={{0,192},{4,196},{8,200},{12,204},{16,208},{20,212},{24,216},{28,22... | collective-permute-start | bytes 491528 | tf_op jit(solution)/shard_map/ppermute | solution.py:549
Sparse Core Ops, SparseCore 0:
  125.7 34.7 reduce-scatter.1

commit v10 on v9

--- a/solution.py
+++ b/solution.py
@@ -345,7 +345,7 @@
             part.wait()
 
 
-def call(body, ins, outs, scratch=(), scalar=None, cut=None, flops=0):
+def call(body, ins, outs, scratch=(), scalar=None, cut=None, flops=0, limit=60, parts=0):
     cut = cut or {}
     extra = int(scalar is not None)
     count, made = len(ins), len(outs)
@@ -360,7 +360,7 @@
         for i in range(count):
             part = source[i].at[:, :, pl.ds(*cut[i])] if i in cut else source[i]
             got.append(Inward(part, here[i], in_sem.at[i]))
-        put = [Outward(there[i], target[i], out_sem.at[i], refs[2], 8 * i) for i in range(made)]
+        put = [Outward(there[i], target[i], out_sem.at[i], refs[2], parts * i) for i in range(made)]
         body(*lead, *got, *put, *refs[3:])
         for one in got:
             one.get()
@@ -376,9 +376,9 @@
         out_shape=[jax.ShapeDtypeStruct(shape, kind) for shape, kind in outs],
         scratch_shapes=[pltpu.VMEM(held[i], ins[i].dtype) for i in range(count)]
         + [pltpu.VMEM(shape, kind) for shape, kind in outs]
-        + [pltpu.SemaphoreType.DMA((n,)) for n in (count, made, 8 * made)]
+        + [pltpu.SemaphoreType.DMA((n,)) for n in (count, made, max(1, parts * made))]
         + [pltpu.VMEM(shape, kind) for shape, kind in scratch],
-        compiler_params=pltpu.CompilerParams(vmem_limit_bytes=60 << 20),
+        compiler_params=pltpu.CompilerParams(vmem_limit_bytes=limit << 20),
         cost_estimate=pl.CostEstimate(flops=flops, bytes_accessed=moved, transcendentals=0),
     )(*([scalar] * extra), *ins)
 
@@ -512,6 +512,7 @@
         [block, early_shape] + [sent_shape] * pieces,
         [square] * 7,
         scalar=where,
+        parts=count * narrow // turn.shape[0],
         flops=32 * rows * width * width,
     )
     came = jnp.concatenate([lax.ppermute(one, "wide", swap) for one in sent], axis=0)
@@ -528,6 +529,8 @@
         [((grid_rows, width), F32), late_shape, late_shape],
         [square, square],
         scalar=where,
+        parts=spread * narrow // turn.shape[0],
+        limit=24,
         flops=1200 * edges * width * width,
     )
     came = lax.ppermute(sent, "wide", swap)

time: 206 us -> 205 us (level)
  Pallas kernels: 38.9 us -> 36.1 us
    pallas_call x6, Pallas kernels: 38.9 us -> 36.1 us  [call(): pl.pallas_call(kernel, in_specs=[pl.BlockSpec(memory_space=pltpu.SMEM)] *...]
    all_to_all x1, waiting for transfers between devices: 10 us -> 12.5 us  [on_device(): lax.all_to_all(last, 'narrow', split_axis=0, concat_axis=0, tiled=True)]
  transfers between devices with their start and end apart: 13 -> 13, of which waited for: 12 -> 11; matrix products, arithmetic and copies ran while one was open for 4% -> 3% of each run, Pallas kernels for 7% -> 6%
where the time goes in v10:
time: 205 us; the launch traced here: 203 us
  blocking collectives  69.2 us (34%)
  waiting for transfers between devices  56 us (27%)
  Pallas kernels  36.1 us (18%)
  starting transfers between devices  18.3 us (9%)
  between operations  14.3 us (7%)
  other arithmetic  6.14 us (3%)
  local copies, waits for them, and re-layouts  3.28 us (2%)
    all_to_all x1, blocking collectives, on_device(): lax.all_to_all(payload, ('wide', 'narrow'), split_axis=0, concat_axis=0,...  52.2 us
    pallas_call x6, Pallas kernels, call(): pl.pallas_call(kernel, in_specs=[pl.BlockSpec(memory_space=pltpu.SMEM)] *...  36.1 us
    all_to_all x1, blocking collectives, on_device(): lax.all_to_all(both.astype(BF).reshape(near, chunk, width), 'wide', split...  17 us
    all_to_all x1, waiting for transfers between devices, on_device(): lax.all_to_all(returning, ('wide', 'narrow'), split_axis=0, concat_axis=0...  15.9 us
    all_to_all x1, waiting for transfers between devices, on_device(): lax.all_to_all(last, 'narrow', split_axis=0, concat_axis=0, tiled=True)  12.5 us
    ppermute x1, waiting for transfers between devices, on_device(): from_other = lax.ppermute(s_other, 'wide', cross)  6.95 us
    ppermute x1, waiting for transfers between devices, on_device(): p_other = lax.ppermute(p_src, 'wide', cross)  6.77 us
    all_to_all x1, starting transfers between devices, on_device(): lax.all_to_all(returning, ('wide', 'narrow'), split_axis=0, concat_axis=0...  6.5 us
  transfers between devices with their start and end apart: 13, of which 11 were waited for; matrix products, arithmetic and copies ran while one was open for 3% of the time, Pallas kernels for 6%

profile of v10, /device:TPU:8, one launch (start us, length us, event | category | flops | bytes accessed | tf_op | source)
XLA Modules:
  0.0 203.2 jit_solution(17339369981078633023)
XLA Ops:
  7.2 4.8 %shard_map.228 = (bf16[256,4,640]{2,1,0:T(4,128)(2,1)}, bf16[512,512]{1,0:T(8,128)(2,1)}, s32[1,512]{1,0:T(1,128)}) custom-call(s32[1,512]{1,0:T(1,128)} %bitcast.20, s32[1,512]{1,0:T(1,128)} %bitcast.21, s32[1,512]{1,0:T(1,128)} %bitcast.15, bf16[512,512]{1,0:T(8,128)(2,1)} %refs_6_.3, bf16[512,512]{1,0:T(8,128)(2,1)} %refs_5_.5, bf16[512,512]{1,0:T(8,128)(2,1)} %refs_5_.3, ...), custom_call_target="tpu_custom_call" | custom-call | bytes 2103296 | tf_op jit(solution)/shard_map/pallas_call | solution.py:372
  11.9 52.2 %all_to_all.20.refs_0_.refs_10_ = bf16[256,4,640]{2,1,0:T(4,128)(2,1)} all-to-all(bf16[256,4,640]{2,1,0:T(4,128)(2,1)} %get-tuple-element.33), channel_id=1, replica_groups=mesh['wide'=64,'narrow'=4] {'wide','narrow'}, dimensions={0} | all-to-all | bytes 2621440 | tf_op jit(solution)/shard_map/all_to_all | solution.py:436
  64.1 3.6 %shard_map.229 = (bf16[160,512]{1,0:T(8,128)(2,1)}, bf16[160,512]{1,0:T(8,128)(2,1)}, bf16[160,512]{1,0:T(8,128)(2,1)}) custom-call(bf16[256,4,640]{2,1,0:T(4,128)(2,1)} %all_to_all.20.refs_0_.refs_10_, bf16[512,512]{1,0:T(8,128)(2,1)} %refs_9_.3, bf16[160,512]{1,0:T(8,128)(2,1)} %refs_2_.1, bf16[512,512]{1,0:T(8,128)(2,1)} %refs_3_.5), custom_call_target="tpu_custom_call" | custom-call | bytes 2523136 | tf_op jit(solution)/shard_map/pallas_call | solution.py:372
  67.7 0.1 collective-permute-start
  67.8 0.1 collective-permute-start.1
  67.9 0.0 copy-done.9
  67.9 0.6 reshape.41.refs_1_
  68.5 0.0 copy-done.10
  68.5 0.6 reshape.42.refs_2_
  69.2 0.3 collective-permute-done.refs_3_
  69.4 6.8 %collective-permute-done.1.refs_5_ = bf16[160,512]{1,0:T(8,128)(2,1)S(1)} collective-permute-done((bf16[160,512]{1,0:T(8,128)(2,1)}, bf16[160,512]{1,0:T(8,128)(2,1)S(1)}, u32[]{:S(2)}, u32[]{:S(2)}) %collective-permute-start.1) | collective-permute-done | bytes 163872 | tf_op jit(solution)/shard_map/ppermute | solution.py:446
  76.2 0.7 copy-done.12
  76.9 11.2 %shard_map.230 = (bf16[160,512]{1,0:T(8,128)(2,1)}, bf16[160,512]{1,0:T(8,128)(2,1)}, bf16[160,512]{1,0:T(8,128)(2,1)}, bf16[160,512]{1,0:T(8,128)(2,1)}, bf16[1...) custom-call(s32[1]{0:T(128)} %bitcast.refs_0_, ...), custom_call_target="tpu_custom_call" | custom-call | flops 4026531840 | bytes 5285888 | tf_op jit(solution)/shard_map/pallas_call | solution.py:372
  88.0 0.1 collective-permute-start.2
  88.1 0.3 collective-permute-start.3
  88.4 1.3 collective-permute-done.2.refs_1_
  89.7 6.9 %collective-permute-done.3.refs_2_ = bf16[160,512]{1,0:T(8,128)(2,1)S(1)} collective-permute-done((bf16[160,512]{1,0:T(8,128)(2,1)}, bf16[160,512]{1,0:T(8,128)(2,1)S(1)}, u32[]{:S(2)}, u32[]{:S(2)}) %collective-permute-start.3) | collective-permute-done | bytes 163872 | tf_op jit(solution)/shard_map/ppermute | solution.py:482
  96.7 0.0 copy-done.7
  96.7 0.7 copy-done.8
  97.3 4.2 %shard_map.231 = (f32[160,512]{1,0:T(8,128)}, bf16[256,4,512]{2,1,0:T(4,128)(2,1)}, bf16[160,512]{1,0:T(8,128)(2,1)}, bf16[160,512]{1,0:T(8,128)(2,1)}) custom-call(bf16[160,512]{1,0:T(8,128)(2,1)} %get-tuple-element.36.refs_0_, bf16[160,512]{1,0:T(8,128)(2,1)} %copy-done.7, bf16[160,512]{1,0:T(8,128)(2,1)} %copy-done.8, bf16[512,512]{1,0:T(8,128)(2,1)} %refs_3_.5, ...), custom_call_target="tpu_custom_call" | custom-call | flops 503316480 | bytes 4390912 | tf_op jit(solution)/shard_map/pallas_call | solution.py:372
  101.6 6.5 %all-to-all-start.1 = ((bf16[256,4,512]{2,1,0:T(4,128)(2,1)}), bf16[256,4,512]{2,1,0:T(4,128)(2,1)S(1)}, u32[]{:S(2)}, u32[]{:S(2)}) async-start(bf16[256,4,512]{2,1,0:T(4,128)(2,1)} %get-tuple-element.51), calls=%async_computation.1 | async-start | bytes 2097152 | tf_op jit(solution)/shard_map/all_to_all | solution.py:521
  108.1 0.0 reduce-scatter.2.cloned.1.call-start
  108.1 7.5 %shard_map.232 = (bf16[160,512]{1,0:T(8,128)(2,1)}, bf16[4,560,512]{2,1,0:T(8,128)(2,1)}, bf16[2,560,512]{2,1,0:T(8,128)(2,1)}, bf16[2,560,512]{2,1,0:T(8,128)(2,1)}) custom-call(s32[1]{0:T(128)} %bitcast.refs_0_, bf16[160,512]{1,0:T(8,128)(2,1)} %get-tuple-element.34.refs_6_.refs_1_, bf16[160,512]{1,0:T(8,128)(2,1)} %get-tuple-element.41.refs_2_, ...), custom_call_target="tpu_custom_call" | custom-call | flops 1342177280 | bytes 3055616 | tf_op jit(solution)/shard_map/pallas_call | solution.py:372
  115.6 0.2 collective-permute-start.4
  115.9 0.4 collective-permute-start.5
  116.2 2.5 %collective-permute-done.4 = bf16[2,560,512]{2,1,0:T(8,128)(2,1)S(1)} collective-permute-done((bf16[2,560,512]{2,1,0:T(8,128)(2,1)}, bf16[2,560,512]{2,1,0:T(8,128)(2,1)S(1)}, u32[]{:S(2)}, u32[]{:S(2)}) %collective-permute-start.4) | collective-permute-done | bytes 1146912 | tf_op jit(solution)/shard_map/ppermute | solution.py:518
  118.7 1.6 collective-permute-done.5
  120.4 3.8 %add_convert_fusion = bf16[4,560,512]{2,1,0:T(8,128)(2,1)} fusion(bf16[4,560,512]{2,1,0:T(8,128)(2,1)} %get-tuple-element.54, bf16[2,560,512]{2,1,0:T(8,128)(2,1)S(1)} %collective-permute-done.5, bf16[2,560,512]{2,1,0:T(8,128)(2,1)S(1)} %collective-permute-done.4), kind=kLoop, calls=%fused_computation | loop fusion | flops 5734400 | bytes 6881280 | tf_op jit(solution)/shard_map/convert_element_type | solution.py:519
  124.2 0.0 reduce-scatter.2.cloned.1.call-update
  124.2 15.9 %all-to-all-done.1.refs_3_ = bf16[256,4,512]{2,1,0:T(4,128)(2,1)S(1)} async-done(((bf16[256,4,512]{2,1,0:T(4,128)(2,1)}), bf16[256,4,512]{2,1,0:T(4,128)(2,1)S(1)}, u32[]{:S(2)}, u32[]{:S(2)}) %all-to-all-start.1) | async-done | bytes 1048608 | tf_op jit(solution)/shard_map/all_to_all | solution.py:521
  140.2 4.8 %shard_map.233 = (f32[512,512]{1,0:T(8,128)}, bf16[4,160,512]{2,1,0:T(8,128)(2,1)S(1)}, bf16[4,160,512]{2,1,0:T(8,128)(2,1)S(1)}) custom-call(s32[1]{0:T(128)} %bitcast.refs_0_, s32[1,512]{1,0:T(1,128)S(1)} %copy-done.5, s32[1,512]{1,0:T(1,128)S(1)} %bitcast.16, bf16[256,4,512]{2,1,0:T(4,128)(2,1)S(1)} %all-to-all-done.1.refs_3_, ...), custom_call_target="tpu_custom_call" | custom-call | flops 161061273600 | bytes 3354624 | tf_op jit(solution)/shard_map/pallas_call | solution.py:372
  145.0 0.1 collective-permute-start.6
  145.1 2.1 %collective-permute-done.6 = bf16[4,160,512]{2,1,0:T(8,128)(2,1)S(1)} collective-permute-done((bf16[4,160,512]{2,1,0:T(8,128)(2,1)S(1)}, bf16[4,160,512]{2,1,0:T(8,128)(2,1)S(1)}, u32[]{:S(2)}, u32[]{:S(2)}) %collective-permute-start.6) | collective-permute-done | bytes 655392 | tf_op jit(solution)/shard_map/ppermute | solution.py:536
  147.2 1.0 add_convert_fusion.2
  148.2 4.8 %all-to-all-start.2 = ((bf16[4,160,512]{2,1,0:T(8,128)(2,1)}), bf16[4,160,512]{2,1,0:T(8,128)(2,1)S(1)}, u32[]{:S(2)}, u32[]{:S(2)}) async-start(bf16[4,160,512]{2,1,0:T(8,128)(2,1)} %add_convert_fusion.2), calls=%async_computation.3 | async-start | bytes 1310720 | tf_op jit(solution)/shard_map/all_to_all | solution.py:538
  153.0 12.5 %all-to-all-done.2 = bf16[4,160,512]{2,1,0:T(8,128)(2,1)S(1)} async-done(((bf16[4,160,512]{2,1,0:T(8,128)(2,1)}), bf16[4,160,512]{2,1,0:T(8,128)(2,1)S(1)}, u32[]{:S(2)}, u32[]{:S(2)}) %all-to-all-start.2) | async-done | bytes 655392 | tf_op jit(solution)/shard_map/all_to_all | solution.py:538
  165.6 0.1 convert_reduce_fusion
  165.7 0.0 reduce-scatter.2.cloned.1.call-done
  165.7 1.1 add_convert_fusion.1
  166.9 1.5 collective-permute-start.7
  168.4 2.7 %collective-permute-start.8 = (bf16[160,512]{1,0:T(8,128)(2,1)S(1)}, bf16[160,512]{1,0:T(8,128)(2,1)S(1)}, u32[]{:S(2)}, u32[]{:S(2)}) collective-permute-start(bf16[160,512]{1,0:T(8,128)(2,1)S(1)} %get-tuple-element.64), channel_id=1, source_target_pairs={{0,128},{4,132},{8,136},{12,140},{16,144},{20,148},{24,152},{28,15... | collective-permute-start | bytes 491528 | tf_op jit(solution)/shard_map/ppermute | solution.py:552
  171.1 1.5 collective-permute-start.9
  172.6 1.7 collective-permute-done.7
  174.3 4.3 %collective-permute-done.8 = bf16[160,512]{1,0:T(8,128)(2,1)S(1)} collective-permute-done((bf16[160,512]{1,0:T(8,128)(2,1)S(1)}, bf16[160,512]{1,0:T(8,128)(2,1)S(1)}, u32[]{:S(2)}, u32[]{:S(2)}) %collective-permute-start.8) | collective-permute-done | bytes 163872 | tf_op jit(solution)/shard_map/ppermute | solution.py:552
  178.6 0.0 collective-permute-done.9
  178.6 0.1 fusion.2
  178.7 17.0 %all_to_all.21 = bf16[8,20,512]{2,1,0:T(8,128)(2,1)S(1)} all-to-all(bf16[8,20,512]{2,1,0:T(8,128)(2,1)S(1)} %reshape.44), channel_id=1, replica_groups={{0,8,16,24,32,40,48,56},{4,12,20,28,36,44,52,60},{64,72,80,88,96,104,11..., dimensions={0} | all-to-all | bytes 327680 | tf_op jit(solution)/shard_map/all_to_all | solution.py:554
  195.7 0.6 reshape.45
  (24 shorter events, 0.2 us)
Async XLA Ops:
  64.1 3.8 %copy-start.9 = (s32[1280]{0:T(1024)S(1)}, s32[1280]{0:T(1024)}, u32[]{:S(2)}) copy-start(s32[1280]{0:T(1024)} %param.28) | copy-start | bytes 15364
  64.1 4.4 %copy-start.10 = (s32[1280]{0:T(1024)S(1)}, s32[1280]{0:T(1024)}, u32[]{:S(2)}) copy-start(s32[1280]{0:T(1024)} %param.29) | copy-start | bytes 15364
  67.7 1.7 collective-permute-start
  67.8 8.4 %collective-permute-start.1 = (bf16[160,512]{1,0:T(8,128)(2,1)}, bf16[160,512]{1,0:T(8,128)(2,1)S(1)}, u32[]{:S(2)}, u32[]{:S(2)}) collective-permute-start(bf16[160,512]{1,0:T(8,128)(2,1)} %get-tuple-element.35.refs_4_), channel_id=1, source_target_pairs={{0,252},{4,8},{8,4},{12,16},{16,12},{20,24},{24,20},{28,32},{32,28... | collective-permute-start | bytes 491528 | tf_op jit(solution)/shard_map/ppermute | solution.py:446
  69.4 6.8 %copy-start.11 = (bf16[160,512]{1,0:T(8,128)(2,1)}, bf16[160,512]{1,0:T(8,128)(2,1)S(1)}, u32[]{:S(2)}) copy-start(bf16[160,512]{1,0:T(8,128)(2,1)S(1)} %collective-permute-done.refs_3_) | copy-start | bytes 491524
  76.2 0.7 copy-start.12
  88.0 1.7 collective-permute-start.2
  88.1 8.5 %collective-permute-start.3 = (bf16[160,512]{1,0:T(8,128)(2,1)}, bf16[160,512]{1,0:T(8,128)(2,1)S(1)}, u32[]{:S(2)}, u32[]{:S(2)}) collective-permute-start(bf16[160,512]{1,0:T(8,128)(2,1)} %get-tuple-element.38), channel_id=1, source_target_pairs={{0,252},{4,8},{8,4},{12,16},{16,12},{20,24},{24,20},{28,32},{32,28... | collective-permute-start | bytes 491528 | tf_op jit(solution)/shard_map/ppermute | solution.py:482
  89.7 7.0 %copy-start.7 = (bf16[160,512]{1,0:T(8,128)(2,1)}, bf16[160,512]{1,0:T(8,128)(2,1)S(1)}, u32[]{:S(2)}) copy-start(bf16[160,512]{1,0:T(8,128)(2,1)S(1)} %collective-permute-done.2.refs_1_) | copy-start | bytes 491524
  96.7 0.7 copy-start.8
  101.6 38.5 %all-to-all-start.1 = ((bf16[256,4,512]{2,1,0:T(4,128)(2,1)}), bf16[256,4,512]{2,1,0:T(4,128)(2,1)S(1)}, u32[]{:S(2)}, u32[]{:S(2)}) async-start(bf16[256,4,512]{2,1,0:T(4,128)(2,1)} %get-tuple-element.51), calls=%async_computation.1 | async-start | bytes 2097152 | tf_op jit(solution)/shard_map/all_to_all | solution.py:521
  108.1 57.6 %reduce-scatter.2.cloned.1.call-start = ((), (), s32[]{:S(2)}) async-start(), calls=%async_computation.5 | async-start | bytes 2867200 | tf_op jit(solution)/shard_map/reduce_scatter | solution.py:520
  115.6 3.1 %collective-permute-start.4 = (bf16[2,560,512]{2,1,0:T(8,128)(2,1)}, bf16[2,560,512]{2,1,0:T(8,128)(2,1)S(1)}, u32[]{:S(2)}, u32[]{:S(2)}) collective-permute-start(bf16[2,560,512]{2,1,0:T(8,128)(2,1)} %get-tuple-element.55), channel_id=1, source_target_pairs={{0,4},{4,0},{8,12},{12,8},{16,20},{20,16},{24,28},{28,24},{32,36},... | collective-permute-start | bytes 3440648 | tf_op jit(solution)/shard_map/ppermute | solution.py:518
  115.9 4.5 %collective-permute-start.5 = (bf16[2,560,512]{2,1,0:T(8,128)(2,1)}, bf16[2,560,512]{2,1,0:T(8,128)(2,1)S(1)}, u32[]{:S(2)}, u32[]{:S(2)}) collective-permute-start(bf16[2,560,512]{2,1,0:T(8,128)(2,1)} %get-tuple-element.56), channel_id=1, source_target_pairs={{0,4},{4,0},{8,12},{12,8},{16,20},{20,16},{24,28},{28,24},{32,36},... | collective-permute-start | bytes 3440648 | tf_op jit(solution)/shard_map/ppermute | solution.py:518
  120.4 19.7 %copy-start.6 = (bf16[320,320]{1,0:T(8,128)(2,1)S(1)}, bf16[320,320]{1,0:T(8,128)(2,1)}, u32[]{:S(2)}) copy-start(bf16[320,320]{1,0:T(8,128)(2,1)} %constant.63.clone.refs_14_.refs_8_) | copy-start | bytes 614404
  124.2 15.9 %copy-start = (bf16[512,512]{1,0:T(8,128)(2,1)S(1)}, bf16[512,512]{1,0:T(8,128)(2,1)}, u32[]{:S(2)}) copy-start(bf16[512,512]{1,0:T(8,128)(2,1)} %refs_6_.3) | copy-start | bytes 1572868
  124.2 15.9 %copy-start.1 = (bf16[512,512]{1,0:T(8,128)(2,1)S(1)}, bf16[512,512]{1,0:T(8,128)(2,1)}, u32[]{:S(2)}) copy-start(bf16[512,512]{1,0:T(8,128)(2,1)} %refs_5_.5) | copy-start | bytes 1572868
  124.2 16.0 %copy-start.2 = (bf16[512,512]{1,0:T(8,128)(2,1)S(1)}, bf16[512,512]{1,0:T(8,128)(2,1)}, u32[]{:S(2)}) copy-start(bf16[512,512]{1,0:T(8,128)(2,1)} %refs_7_.5) | copy-start | bytes 1572868
  124.2 16.0 %copy-start.3 = (s32[512]{0:T(512)S(1)}, s32[512]{0:T(512)}, u32[]{:S(2)}) copy-start(s32[512]{0:T(512)} %param.23) | copy-start | bytes 6148
  124.2 16.0 %copy-start.4 = (bf16[512,512]{1,0:T(8,128)(2,1)S(1)}, bf16[512,512]{1,0:T(8,128)(2,1)}, u32[]{:S(2)}) copy-start(bf16[512,512]{1,0:T(8,128)(2,1)} %get-tuple-element.52.refs_4_) | copy-start | bytes 1572868
  124.2 16.0 %copy-start.5 = (s32[1,512]{1,0:T(1,128)S(1)}, s32[1,512]{1,0:T(1,128)}, u32[]{:S(2)}) copy-start(s32[1,512]{1,0:T(1,128)} %get-tuple-element.50.refs_1_) | copy-start | bytes 6148
  145.0 2.2 %collective-permute-start.6 = (bf16[4,160,512]{2,1,0:T(8,128)(2,1)S(1)}, bf16[4,160,512]{2,1,0:T(8,128)(2,1)S(1)}, u32[]{:S(2)}, u32[]{:S(2)}) collective-permute-start(bf16[4,160,512]{2,1,0:T(8,128)(2,1)S(1)} %get-tuple-element.58), channel_id=1, source_target_pairs={{0,4},{4,0},{8,12},{12,8},{16,20},{20,16},{24,28},{28,24},{32,36},... | collective-permute-start | bytes 1966088 | tf_op jit(solution)/shard_map/ppermute | solution.py:536
  148.2 17.4 %all-to-all-start.2 = ((bf16[4,160,512]{2,1,0:T(8,128)(2,1)}), bf16[4,160,512]{2,1,0:T(8,128)(2,1)S(1)}, u32[]{:S(2)}, u32[]{:S(2)}) async-start(bf16[4,160,512]{2,1,0:T(8,128)(2,1)} %add_convert_fusion.2), calls=%async_computation.3 | async-start | bytes 1310720 | tf_op jit(solution)/shard_map/all_to_all | solution.py:538
  166.9 7.4 %collective-permute-start.7 = (bf16[160,512]{1,0:T(8,128)(2,1)S(1)}, bf16[160,512]{1,0:T(8,128)(2,1)S(1)}, u32[]{:S(2)}, u32[]{:S(2)}) collective-permute-start(bf16[160,512]{1,0:T(8,128)(2,1)S(1)} %get-tuple-element.62), channel_id=1, source_target_pairs={{0,64},{4,68},{8,72},{12,76},{16,80},{20,84},{24,88},{28,92},{32,9... | collective-permute-start | bytes 491528 | tf_op jit(solution)/shard_map/ppermute | solution.py:552
  168.4 10.2 %collective-permute-start.8 = (bf16[160,512]{1,0:T(8,128)(2,1)S(1)}, bf16[160,512]{1,0:T(8,128)(2,1)S(1)}, u32[]{:S(2)}, u32[]{:S(2)}) collective-permute-start(bf16[160,512]{1,0:T(8,128)(2,1)S(1)} %get-tuple-element.64), channel_id=1, source_target_pairs={{0,128},{4,132},{8,136},{12,140},{16,144},{20,148},{24,152},{28,15... | collective-permute-start | bytes 491528 | tf_op jit(solution)/shard_map/ppermute | solution.py:552
  171.1 7.5 %collective-permute-start.9 = (bf16[160,512]{1,0:T(8,128)(2,1)S(1)}, bf16[160,512]{1,0:T(8,128)(2,1)S(1)}, u32[]{:S(2)}, u32[]{:S(2)}) collective-permute-start(bf16[160,512]{1,0:T(8,128)(2,1)S(1)} %get-tuple-element.63), channel_id=1, source_target_pairs={{0,192},{4,196},{8,200},{12,204},{16,208},{20,212},{24,216},{28,22... | collective-permute-start | bytes 491528 | tf_op jit(solution)/shard_map/ppermute | solution.py:552
Sparse Core Ops, SparseCore 0:
  124.3 37.1 reduce-scatter.1

commit v11 on v10

--- a/solution.py
+++ b/solution.py
@@ -516,7 +516,8 @@
         flops=32 * rows * width * width,
     )
     came = jnp.concatenate([lax.ppermute(one, "wide", swap) for one in sent], axis=0)
-    early = (kept.astype(F32) + came.astype(F32)).astype(BF)
+    front = late // (2 * half) * chunk
+    early = (kept.astype(F32) + came.astype(F32)).astype(BF)[:, front - start // (2 * narrow) :]
     early = lax.psum_scatter(early, "narrow", scatter_dimension=0, tiled=True)[0]
     returned = lax.all_to_all(
         returning, ("wide", "narrow"), split_axis=0, concat_axis=0, tiled=True
@@ -538,7 +539,7 @@
     last = lax.all_to_all(last, "narrow", split_axis=0, concat_axis=0, tiled=True)
     last = jnp.sum(last.astype(F32), axis=0)[: near * chunk]
     early, last = lax.optimization_barrier((early, last))
-    early = jnp.pad(early, ((start // (2 * narrow), 0), (0, 0))).astype(F32)
+    early = jnp.pad(early, ((front, 0), (0, 0))).astype(F32)
     early += jnp.pad(last, ((0, early.shape[0] - last.shape[0]), (0, 0)))
     both = early.astype(BF).reshape(far, near * chunk, width)
     x = lax.axis_index("wide") // (2 * near)

time: 205 us -> 203 us (level)
  no operation moved by 1% of the time
where the time goes in v11:
time: 203 us; the launch traced here: 202 us
  blocking collectives  69 us (34%)
  waiting for transfers between devices  54.7 us (27%)
  Pallas kernels  36.1 us (18%)
  starting transfers between devices  18.3 us (9%)
  between operations  14.2 us (7%)
  other arithmetic  5.96 us (3%)
  local copies, waits for them, and re-layouts  3.28 us (2%)
    all_to_all x1, blocking collectives, on_device(): lax.all_to_all(payload, ('wide', 'narrow'), split_axis=0, concat_axis=0,...  52.2 us
    pallas_call x6, Pallas kernels, call(): pl.pallas_call(kernel, in_specs=[pl.BlockSpec(memory_space=pltpu.SMEM)] *...  36.1 us
    all_to_all x1, blocking collectives, on_device(): lax.all_to_all(both.astype(BF).reshape(near, chunk, width), 'wide', split...  16.8 us
    all_to_all x1, waiting for transfers between devices, on_device(): lax.all_to_all(returning, ('wide', 'narrow'), split_axis=0, concat_axis=0...  16 us
    all_to_all x1, waiting for transfers between devices, on_device(): lax.all_to_all(last, 'narrow', split_axis=0, concat_axis=0, tiled=True)  11.1 us
    ppermute x1, waiting for transfers between devices, on_device(): from_other = lax.ppermute(s_other, 'wide', cross)  6.95 us
    ppermute x1, waiting for transfers between devices, on_device(): p_other = lax.ppermute(p_src, 'wide', cross)  6.77 us
    all_to_all x1, starting transfers between devices, on_device(): lax.all_to_all(returning, ('wide', 'narrow'), split_axis=0, concat_axis=0...  6.5 us
  transfers between devices with their start and end apart: 13, of which 11 were waited for; matrix products, arithmetic and copies ran while one was open for 3% of the time, Pallas kernels for 6%

profile of v11, /device:TPU:8, one launch (start us, length us, event | category | flops | bytes accessed | tf_op | source)
XLA Modules:
  0.0 201.6 jit_solution(16094405613803115280)
XLA Ops:
  7.2 4.8 %shard_map.228 = (bf16[256,4,640]{2,1,0:T(4,128)(2,1)}, bf16[512,512]{1,0:T(8,128)(2,1)}, s32[1,512]{1,0:T(1,128)}) custom-call(s32[1,512]{1,0:T(1,128)} %bitcast.20, s32[1,512]{1,0:T(1,128)} %bitcast.21, s32[1,512]{1,0:T(1,128)} %bitcast.15, bf16[512,512]{1,0:T(8,128)(2,1)} %refs_6_.3, bf16[512,512]{1,0:T(8,128)(2,1)} %refs_5_.5, bf16[512,512]{1,0:T(8,128)(2,1)} %refs_5_.3, ...), custom_call_target="tpu_custom_call" | custom-call | bytes 2103296 | tf_op jit(solution)/shard_map/pallas_call | solution.py:372
  11.9 52.2 %all_to_all.20.refs_0_.refs_10_ = bf16[256,4,640]{2,1,0:T(4,128)(2,1)} all-to-all(bf16[256,4,640]{2,1,0:T(4,128)(2,1)} %get-tuple-element.33), channel_id=1, replica_groups=mesh['wide'=64,'narrow'=4] {'wide','narrow'}, dimensions={0} | all-to-all | bytes 2621440 | tf_op jit(solution)/shard_map/all_to_all | solution.py:436
  64.1 3.6 %shard_map.229 = (bf16[160,512]{1,0:T(8,128)(2,1)}, bf16[160,512]{1,0:T(8,128)(2,1)}, bf16[160,512]{1,0:T(8,128)(2,1)}) custom-call(bf16[256,4,640]{2,1,0:T(4,128)(2,1)} %all_to_all.20.refs_0_.refs_10_, bf16[512,512]{1,0:T(8,128)(2,1)} %refs_9_.3, bf16[160,512]{1,0:T(8,128)(2,1)} %refs_2_.1, bf16[512,512]{1,0:T(8,128)(2,1)} %refs_3_.5), custom_call_target="tpu_custom_call" | custom-call | bytes 2523136 | tf_op jit(solution)/shard_map/pallas_call | solution.py:372
  67.7 0.1 collective-permute-start
  67.8 0.1 collective-permute-start.1
  67.9 0.0 copy-done.9
  67.9 0.6 reshape.41.refs_1_
  68.5 0.6 reshape.42.refs_2_
  69.2 0.3 collective-permute-done.refs_3_
  69.4 6.8 %collective-permute-done.1.refs_5_ = bf16[160,512]{1,0:T(8,128)(2,1)S(1)} collective-permute-done((bf16[160,512]{1,0:T(8,128)(2,1)}, bf16[160,512]{1,0:T(8,128)(2,1)S(1)}, u32[]{:S(2)}, u32[]{:S(2)}) %collective-permute-start.1) | collective-permute-done | bytes 163872 | tf_op jit(solution)/shard_map/ppermute | solution.py:446
  76.2 0.0 copy-done.11
  76.2 0.7 copy-done.12
  76.9 11.2 %shard_map.230 = (bf16[160,512]{1,0:T(8,128)(2,1)}, bf16[160,512]{1,0:T(8,128)(2,1)}, bf16[160,512]{1,0:T(8,128)(2,1)}, bf16[160,512]{1,0:T(8,128)(2,1)}, bf16[1...) custom-call(s32[1]{0:T(128)} %bitcast.refs_0_, ...), custom_call_target="tpu_custom_call" | custom-call | flops 4026531840 | bytes 5285888 | tf_op jit(solution)/shard_map/pallas_call | solution.py:372
  88.0 0.1 collective-permute-start.2
  88.1 0.3 collective-permute-start.3
  88.4 1.3 collective-permute-done.2.refs_1_
  89.7 6.9 %collective-permute-done.3.refs_2_ = bf16[160,512]{1,0:T(8,128)(2,1)S(1)} collective-permute-done((bf16[160,512]{1,0:T(8,128)(2,1)}, bf16[160,512]{1,0:T(8,128)(2,1)S(1)}, u32[]{:S(2)}, u32[]{:S(2)}) %collective-permute-start.3) | collective-permute-done | bytes 163872 | tf_op jit(solution)/shard_map/ppermute | solution.py:482
  96.7 0.0 copy-done.7
  96.7 0.7 copy-done.8
  97.3 4.2 %shard_map.231 = (f32[160,512]{1,0:T(8,128)}, bf16[256,4,512]{2,1,0:T(4,128)(2,1)}, bf16[160,512]{1,0:T(8,128)(2,1)}, bf16[160,512]{1,0:T(8,128)(2,1)}) custom-call(bf16[160,512]{1,0:T(8,128)(2,1)} %get-tuple-element.36.refs_0_, bf16[160,512]{1,0:T(8,128)(2,1)} %copy-done.7, bf16[160,512]{1,0:T(8,128)(2,1)} %copy-done.8, bf16[512,512]{1,0:T(8,128)(2,1)} %refs_3_.5, ...), custom_call_target="tpu_custom_call" | custom-call | flops 503316480 | bytes 4390912 | tf_op jit(solution)/shard_map/pallas_call | solution.py:372
  101.6 6.5 %all-to-all-start.1 = ((bf16[256,4,512]{2,1,0:T(4,128)(2,1)}), bf16[256,4,512]{2,1,0:T(4,128)(2,1)S(1)}, u32[]{:S(2)}, u32[]{:S(2)}) async-start(bf16[256,4,512]{2,1,0:T(4,128)(2,1)} %get-tuple-element.51), calls=%async_computation.1 | async-start | bytes 2097152 | tf_op jit(solution)/shard_map/all_to_all | solution.py:522
  108.1 0.0 reduce-scatter.2.cloned.1.call-start
  108.1 7.5 %shard_map.232 = (bf16[160,512]{1,0:T(8,128)(2,1)}, bf16[4,560,512]{2,1,0:T(8,128)(2,1)}, bf16[2,560,512]{2,1,0:T(8,128)(2,1)}, bf16[2,560,512]{2,1,0:T(8,128)(2,1)}) custom-call(s32[1]{0:T(128)} %bitcast.refs_0_, bf16[160,512]{1,0:T(8,128)(2,1)} %get-tuple-element.34.refs_6_.refs_1_, bf16[160,512]{1,0:T(8,128)(2,1)} %get-tuple-element.41.refs_2_, ...), custom_call_target="tpu_custom_call" | custom-call | flops 1342177280 | bytes 3055616 | tf_op jit(solution)/shard_map/pallas_call | solution.py:372
  115.6 0.2 collective-permute-start.4
  115.9 0.4 collective-permute-start.5
  116.2 2.5 %collective-permute-done.4 = bf16[2,560,512]{2,1,0:T(8,128)(2,1)S(1)} collective-permute-done((bf16[2,560,512]{2,1,0:T(8,128)(2,1)}, bf16[2,560,512]{2,1,0:T(8,128)(2,1)S(1)}, u32[]{:S(2)}, u32[]{:S(2)}) %collective-permute-start.4) | collective-permute-done | bytes 1146912 | tf_op jit(solution)/shard_map/ppermute | solution.py:518
  118.7 1.6 collective-permute-done.5
  120.4 3.6 %add_convert_fusion = bf16[4,520,512]{2,1,0:T(8,128)(2,1)} fusion(bf16[4,560,512]{2,1,0:T(8,128)(2,1)} %get-tuple-element.54, bf16[2,560,512]{2,1,0:T(8,128)(2,1)S(1)} %collective-permute-done.5, bf16[2,560,512]{2,1,0:T(8,128)(2,1)S(1)} %collective-permute-done.4), kind=kLoop, calls=%fused_computation | loop fusion | flops 7454720 | bytes 6553600 | tf_op jit(solution)/shard_map/convert_element_type | solution.py:520
  124.0 0.0 reduce-scatter.2.cloned.1.call-update
  124.1 16.0 %all-to-all-done.1.refs_3_ = bf16[256,4,512]{2,1,0:T(4,128)(2,1)S(1)} async-done(((bf16[256,4,512]{2,1,0:T(4,128)(2,1)}), bf16[256,4,512]{2,1,0:T(4,128)(2,1)S(1)}, u32[]{:S(2)}, u32[]{:S(2)}) %all-to-all-start.1) | async-done | bytes 1048608 | tf_op jit(solution)/shard_map/all_to_all | solution.py:522
  140.2 4.8 %shard_map.233 = (f32[512,512]{1,0:T(8,128)}, bf16[4,160,512]{2,1,0:T(8,128)(2,1)S(1)}, bf16[4,160,512]{2,1,0:T(8,128)(2,1)S(1)}) custom-call(s32[1]{0:T(128)} %bitcast.refs_0_, s32[1,512]{1,0:T(1,128)S(1)} %copy-done.5, s32[1,512]{1,0:T(1,128)S(1)} %bitcast.16, bf16[256,4,512]{2,1,0:T(4,128)(2,1)S(1)} %all-to-all-done.1.refs_3_, ...), custom_call_target="tpu_custom_call" | custom-call | flops 161061273600 | bytes 3354624 | tf_op jit(solution)/shard_map/pallas_call | solution.py:372
  145.0 0.1 collective-permute-start.6
  145.1 2.1 %collective-permute-done.6 = bf16[4,160,512]{2,1,0:T(8,128)(2,1)S(1)} collective-permute-done((bf16[4,160,512]{2,1,0:T(8,128)(2,1)S(1)}, bf16[4,160,512]{2,1,0:T(8,128)(2,1)S(1)}, u32[]{:S(2)}, u32[]{:S(2)}) %collective-permute-start.6) | collective-permute-done | bytes 655392 | tf_op jit(solution)/shard_map/ppermute | solution.py:537
  147.2 1.0 add_convert_fusion.2
  148.2 4.8 %all-to-all-start.2 = ((bf16[4,160,512]{2,1,0:T(8,128)(2,1)}), bf16[4,160,512]{2,1,0:T(8,128)(2,1)S(1)}, u32[]{:S(2)}, u32[]{:S(2)}) async-start(bf16[4,160,512]{2,1,0:T(8,128)(2,1)} %add_convert_fusion.2), calls=%async_computation.3 | async-start | bytes 1310720 | tf_op jit(solution)/shard_map/all_to_all | solution.py:539
  153.0 11.1 %all-to-all-done.2 = bf16[4,160,512]{2,1,0:T(8,128)(2,1)S(1)} async-done(((bf16[4,160,512]{2,1,0:T(8,128)(2,1)}), bf16[4,160,512]{2,1,0:T(8,128)(2,1)S(1)}, u32[]{:S(2)}, u32[]{:S(2)}) %all-to-all-start.2) | async-done | bytes 655392 | tf_op jit(solution)/shard_map/all_to_all | solution.py:539
  164.1 0.1 convert_reduce_fusion
  164.2 0.0 reduce-scatter.2.cloned.1.call-done
  164.3 1.1 add_convert_fusion.1
  165.4 1.5 collective-permute-start.7
  166.9 2.7 %collective-permute-start.8 = (bf16[160,512]{1,0:T(8,128)(2,1)S(1)}, bf16[160,512]{1,0:T(8,128)(2,1)S(1)}, u32[]{:S(2)}, u32[]{:S(2)}) collective-permute-start(bf16[160,512]{1,0:T(8,128)(2,1)S(1)} %get-tuple-element.64), channel_id=1, source_target_pairs={{0,128},{4,132},{8,136},{12,140},{16,144},{20,148},{24,152},{28,15... | collective-permute-start | bytes 491528 | tf_op jit(solution)/shard_map/ppermute | solution.py:553
  169.6 1.5 collective-permute-start.9
  171.1 1.8 collective-permute-done.7
  172.9 4.2 %collective-permute-done.8 = bf16[160,512]{1,0:T(8,128)(2,1)S(1)} collective-permute-done((bf16[160,512]{1,0:T(8,128)(2,1)S(1)}, bf16[160,512]{1,0:T(8,128)(2,1)S(1)}, u32[]{:S(2)}, u32[]{:S(2)}) %collective-permute-start.8) | collective-permute-done | bytes 163872 | tf_op jit(solution)/shard_map/ppermute | solution.py:553
  177.1 0.0 collective-permute-done.9
  177.1 0.1 fusion.2
  177.2 16.8 %all_to_all.21 = bf16[8,20,512]{2,1,0:T(8,128)(2,1)S(1)} all-to-all(bf16[8,20,512]{2,1,0:T(8,128)(2,1)S(1)} %reshape.44), channel_id=1, replica_groups={{0,8,16,24,32,40,48,56},{4,12,20,28,36,44,52,60},{64,72,80,88,96,104,11..., dimensions={0} | all-to-all | bytes 327680 | tf_op jit(solution)/shard_map/all_to_all | solution.py:555
  194.1 0.6 reshape.45
  (24 shorter events, 0.2 us)
Async XLA Ops:
  64.1 3.8 %copy-start.9 = (s32[1280]{0:T(1024)S(1)}, s32[1280]{0:T(1024)}, u32[]{:S(2)}) copy-start(s32[1280]{0:T(1024)} %param.28) | copy-start | bytes 15364
  64.1 4.4 %copy-start.10 = (s32[1280]{0:T(1024)S(1)}, s32[1280]{0:T(1024)}, u32[]{:S(2)}) copy-start(s32[1280]{0:T(1024)} %param.29) | copy-start | bytes 15364
  67.7 1.7 collective-permute-start
  67.8 8.4 %collective-permute-start.1 = (bf16[160,512]{1,0:T(8,128)(2,1)}, bf16[160,512]{1,0:T(8,128)(2,1)S(1)}, u32[]{:S(2)}, u32[]{:S(2)}) collective-permute-start(bf16[160,512]{1,0:T(8,128)(2,1)} %get-tuple-element.35.refs_4_), channel_id=1, source_target_pairs={{0,252},{4,8},{8,4},{12,16},{16,12},{20,24},{24,20},{28,32},{32,28... | collective-permute-start | bytes 491528 | tf_op jit(solution)/shard_map/ppermute | solution.py:446
  69.4 6.8 %copy-start.11 = (bf16[160,512]{1,0:T(8,128)(2,1)}, bf16[160,512]{1,0:T(8,128)(2,1)S(1)}, u32[]{:S(2)}) copy-start(bf16[160,512]{1,0:T(8,128)(2,1)S(1)} %collective-permute-done.refs_3_) | copy-start | bytes 491524
  76.2 0.7 copy-start.12
  88.0 1.7 collective-permute-start.2
  88.1 8.5 %collective-permute-start.3 = (bf16[160,512]{1,0:T(8,128)(2,1)}, bf16[160,512]{1,0:T(8,128)(2,1)S(1)}, u32[]{:S(2)}, u32[]{:S(2)}) collective-permute-start(bf16[160,512]{1,0:T(8,128)(2,1)} %get-tuple-element.38), channel_id=1, source_target_pairs={{0,252},{4,8},{8,4},{12,16},{16,12},{20,24},{24,20},{28,32},{32,28... | collective-permute-start | bytes 491528 | tf_op jit(solution)/shard_map/ppermute | solution.py:482
  89.7 7.0 %copy-start.7 = (bf16[160,512]{1,0:T(8,128)(2,1)}, bf16[160,512]{1,0:T(8,128)(2,1)S(1)}, u32[]{:S(2)}) copy-start(bf16[160,512]{1,0:T(8,128)(2,1)S(1)} %collective-permute-done.2.refs_1_) | copy-start | bytes 491524
  96.7 0.7 copy-start.8
  101.6 38.5 %all-to-all-start.1 = ((bf16[256,4,512]{2,1,0:T(4,128)(2,1)}), bf16[256,4,512]{2,1,0:T(4,128)(2,1)S(1)}, u32[]{:S(2)}, u32[]{:S(2)}) async-start(bf16[256,4,512]{2,1,0:T(4,128)(2,1)} %get-tuple-element.51), calls=%async_computation.1 | async-start | bytes 2097152 | tf_op jit(solution)/shard_map/all_to_all | solution.py:522
  108.1 56.2 %reduce-scatter.2.cloned.1.call-start = ((), (), s32[]{:S(2)}) async-start(), calls=%async_computation.5 | async-start | bytes 2662400 | tf_op jit(solution)/shard_map/reduce_scatter | solution.py:521
  115.6 3.1 %collective-permute-start.4 = (bf16[2,560,512]{2,1,0:T(8,128)(2,1)}, bf16[2,560,512]{2,1,0:T(8,128)(2,1)S(1)}, u32[]{:S(2)}, u32[]{:S(2)}) collective-permute-start(bf16[2,560,512]{2,1,0:T(8,128)(2,1)} %get-tuple-element.55), channel_id=1, source_target_pairs={{0,4},{4,0},{8,12},{12,8},{16,20},{20,16},{24,28},{28,24},{32,36},... | collective-permute-start | bytes 3440648 | tf_op jit(solution)/shard_map/ppermute | solution.py:518
  115.9 4.5 %collective-permute-start.5 = (bf16[2,560,512]{2,1,0:T(8,128)(2,1)}, bf16[2,560,512]{2,1,0:T(8,128)(2,1)S(1)}, u32[]{:S(2)}, u32[]{:S(2)}) collective-permute-start(bf16[2,560,512]{2,1,0:T(8,128)(2,1)} %get-tuple-element.56), channel_id=1, source_target_pairs={{0,4},{4,0},{8,12},{12,8},{16,20},{20,16},{24,28},{28,24},{32,36},... | collective-permute-start | bytes 3440648 | tf_op jit(solution)/shard_map/ppermute | solution.py:518
  120.4 19.7 %copy-start.6 = (bf16[320,320]{1,0:T(8,128)(2,1)S(1)}, bf16[320,320]{1,0:T(8,128)(2,1)}, u32[]{:S(2)}) copy-start(bf16[320,320]{1,0:T(8,128)(2,1)} %constant.63.clone.refs_14_.refs_8_) | copy-start | bytes 614404
  124.0 16.1 %copy-start = (bf16[512,512]{1,0:T(8,128)(2,1)S(1)}, bf16[512,512]{1,0:T(8,128)(2,1)}, u32[]{:S(2)}) copy-start(bf16[512,512]{1,0:T(8,128)(2,1)} %refs_6_.3) | copy-start | bytes 1572868
  124.0 16.1 %copy-start.1 = (bf16[512,512]{1,0:T(8,128)(2,1)S(1)}, bf16[512,512]{1,0:T(8,128)(2,1)}, u32[]{:S(2)}) copy-start(bf16[512,512]{1,0:T(8,128)(2,1)} %refs_5_.5) | copy-start | bytes 1572868
  124.0 16.1 %copy-start.2 = (bf16[512,512]{1,0:T(8,128)(2,1)S(1)}, bf16[512,512]{1,0:T(8,128)(2,1)}, u32[]{:S(2)}) copy-start(bf16[512,512]{1,0:T(8,128)(2,1)} %refs_7_.5) | copy-start | bytes 1572868
  124.0 16.1 %copy-start.3 = (s32[512]{0:T(512)S(1)}, s32[512]{0:T(512)}, u32[]{:S(2)}) copy-start(s32[512]{0:T(512)} %param.23) | copy-start | bytes 6148
  124.0 16.1 %copy-start.4 = (bf16[512,512]{1,0:T(8,128)(2,1)S(1)}, bf16[512,512]{1,0:T(8,128)(2,1)}, u32[]{:S(2)}) copy-start(bf16[512,512]{1,0:T(8,128)(2,1)} %get-tuple-element.52.refs_4_) | copy-start | bytes 1572868
  124.0 16.1 %copy-start.5 = (s32[1,512]{1,0:T(1,128)S(1)}, s32[1,512]{1,0:T(1,128)}, u32[]{:S(2)}) copy-start(s32[1,512]{1,0:T(1,128)} %get-tuple-element.50.refs_1_) | copy-start | bytes 6148
  145.0 2.2 %collective-permute-start.6 = (bf16[4,160,512]{2,1,0:T(8,128)(2,1)S(1)}, bf16[4,160,512]{2,1,0:T(8,128)(2,1)S(1)}, u32[]{:S(2)}, u32[]{:S(2)}) collective-permute-start(bf16[4,160,512]{2,1,0:T(8,128)(2,1)S(1)} %get-tuple-element.58), channel_id=1, source_target_pairs={{0,4},{4,0},{8,12},{12,8},{16,20},{20,16},{24,28},{28,24},{32,36},... | collective-permute-start | bytes 1966088 | tf_op jit(solution)/shard_map/ppermute | solution.py:537
  148.2 15.9 %all-to-all-start.2 = ((bf16[4,160,512]{2,1,0:T(8,128)(2,1)}), bf16[4,160,512]{2,1,0:T(8,128)(2,1)S(1)}, u32[]{:S(2)}, u32[]{:S(2)}) async-start(bf16[4,160,512]{2,1,0:T(8,128)(2,1)} %add_convert_fusion.2), calls=%async_computation.3 | async-start | bytes 1310720 | tf_op jit(solution)/shard_map/all_to_all | solution.py:539
  165.4 7.5 %collective-permute-start.7 = (bf16[160,512]{1,0:T(8,128)(2,1)S(1)}, bf16[160,512]{1,0:T(8,128)(2,1)S(1)}, u32[]{:S(2)}, u32[]{:S(2)}) collective-permute-start(bf16[160,512]{1,0:T(8,128)(2,1)S(1)} %get-tuple-element.62), channel_id=1, source_target_pairs={{0,64},{4,68},{8,72},{12,76},{16,80},{20,84},{24,88},{28,92},{32,9... | collective-permute-start | bytes 491528 | tf_op jit(solution)/shard_map/ppermute | solution.py:553
  166.9 10.2 %collective-permute-start.8 = (bf16[160,512]{1,0:T(8,128)(2,1)S(1)}, bf16[160,512]{1,0:T(8,128)(2,1)S(1)}, u32[]{:S(2)}, u32[]{:S(2)}) collective-permute-start(bf16[160,512]{1,0:T(8,128)(2,1)S(1)} %get-tuple-element.64), channel_id=1, source_target_pairs={{0,128},{4,132},{8,136},{12,140},{16,144},{20,148},{24,152},{28,15... | collective-permute-start | bytes 491528 | tf_op jit(solution)/shard_map/ppermute | solution.py:553
  169.6 7.5 %collective-permute-start.9 = (bf16[160,512]{1,0:T(8,128)(2,1)S(1)}, bf16[160,512]{1,0:T(8,128)(2,1)S(1)}, u32[]{:S(2)}, u32[]{:S(2)}) collective-permute-start(bf16[160,512]{1,0:T(8,128)(2,1)S(1)} %get-tuple-element.63), channel_id=1, source_target_pairs={{0,192},{4,196},{8,200},{12,204},{16,208},{20,212},{24,216},{28,22... | collective-permute-start | bytes 491528 | tf_op jit(solution)/shard_map/ppermute | solution.py:553
Sparse Core Ops, SparseCore 0:
  124.2 34.3 reduce-scatter.1
